TPU v7x, 512 devices: a whole 4x8x8 slice. The times are simulated.
512 devices in a mesh: tm: 32 (over x_lo, y, core), mp: 16 (over x_hi, z).
Axes of the slice: x: 4 (x_hi: 2, x_lo: 2; x = x_hi * 2 + x_lo), y: 8, z: 8, core: 2. Of those that a mesh axis runs over, the one named last changes fastest.
Arguments:
- tokens: bfloat16 [65536, 1024], P('tm', 'mp'), may hold values from -45 to 45
- ln_conv_gain: float32 [1024], replicated, may hold values from 0.25 to 1.75
- glu_weight: bfloat16 [1024, 2, 1024], P(None, None, 'mp'), may hold values from -0.1875 to 0.1875
- depth_weight: float32 [31, 1024], P(None, 'mp'), may hold values from -1 to 1
- bn_gain: float32 [1024], P('mp'), may hold values from 0.25 to 1.75
- bn_shift: float32 [1024], P('mp'), may hold values from -1 to 1
- conv_out_weight: bfloat16 [1024, 1024], P(None, 'mp'), may hold values from -0.1875 to 0.1875
- ln_ff_gain: float32 [1024], replicated, may hold values from 0.25 to 1.75
- ff_in_weight: bfloat16 [1024, 4096], P(None, 'mp'), may hold values from -0.1875 to 0.1875
- ff_out_weight: bfloat16 [4096, 1024], P('mp'), may hold values from -0.125 to 0.125
Outputs:
- block_out: bfloat16 [65536, 1024], P('tm', 'mp')
All inputs are finite; a program needn't handle non-finite values.
Results may differ from a plain program's by a relative error of at most 0.009.
Values may be sent and summed in bfloat16 or wider, within the bound.
No kernel may reach another device: no remote copies, remote signals or barrier semaphores. Data moves between devices by JAX's collectives and lax.ppermute only.
A program may use at most 64 MiB of HBM per device.

v0:
```python
import jax
import jax.numpy as jnp
from jax import lax
from jax.sharding import PartitionSpec as P


def with_halo(x, sides, width):
    for axis, dim in sides:
        size, length = (lax.axis_size(axis), x.shape[dim])
        up = [(i, (i + 1) % size) for i in range(size - 1)]
        down = [(j, i) for i, j in up]
        last = lax.slice_in_dim(x, length - width, length, axis=dim)
        leading = lax.slice_in_dim(x, 0, width, axis=dim)
        before = lax.ppermute(last, axis, up)
        after = lax.ppermute(leading, axis, down)
        x = jnp.concatenate([before, x, after], axis=dim)
    return x


def layer_norm(values, scale_gain):
    centre = jnp.mean(values, axis=-1, keepdims=True)
    spread = jnp.mean((values - centre) * (values - centre), axis=-1, keepdims=True)
    return (values - centre) * lax.rsqrt(spread + 1e-05) * scale_gain


def make_adder(matrix, piece):
    return lax.dot_general(
        piece, matrix, (((0,), (0,)), ((), ())), preferred_element_type=jnp.float32
    )


def body(
    tokens,
    ln_conv_gain,
    glu_weight,
    depth_weight,
    bn_gain,
    bn_shift,
    conv_out_weight,
    ln_ff_gain,
    ff_in_weight,
    ff_out_weight,
):
    frames = tokens.shape[0]
    local_width = tokens.shape[1]
    full_width = ln_conv_gain.shape[0]
    total_frames = frames * lax.axis_size("tm")
    whole = lax.all_gather(tokens, "mp", axis=1, tiled=True)
    normed = layer_norm(whole.astype(jnp.float32), ln_conv_gain).astype(jnp.bfloat16)
    paired = lax.dot_general(
        glu_weight.reshape(full_width, 2 * local_width),
        normed,
        (((0,), (1,)), ((), ())),
        preferred_element_type=jnp.float32,
    )
    gated = (paired[:local_width] * jax.nn.sigmoid(paired[local_width:])).astype(jnp.bfloat16)
    kernel_taps = depth_weight.shape[0]
    half_span = (kernel_taps - 1) // 2
    padded = with_halo(gated, (("tm", 1),), half_span).astype(jnp.float32)
    tap_weights = depth_weight.T
    convolved = jnp.zeros((local_width, frames), jnp.float32)
    for offset in range(kernel_taps):
        convolved = (
            convolved + tap_weights[:, offset : offset + 1] * padded[:, offset : offset + frames]
        )
    channel_sum = lax.psum(jnp.sum(convolved, axis=1), "tm")
    channel_mean = channel_sum / total_frames
    centred = convolved - channel_mean[:, None]
    variance = lax.psum(jnp.sum(centred * centred, axis=1), "tm") / total_frames
    normal_bn = (
        centred * lax.rsqrt(variance + 1e-05)[:, None] * bn_gain[:, None] + bn_shift[:, None]
    )
    activated = (normal_bn * jax.nn.sigmoid(normal_bn)).astype(jnp.bfloat16)
    mixed = make_adder(conv_out_weight, lax.all_gather(activated, "mp", axis=0, tiled=True))
    block_cols = (tokens.astype(jnp.float32) + mixed).astype(jnp.bfloat16)
    block_whole = lax.all_gather(block_cols, "mp", axis=1, tiled=True)
    normed_ff = layer_norm(block_whole.astype(jnp.float32), ln_ff_gain).astype(jnp.bfloat16)
    pre_act = jnp.dot(normed_ff, ff_in_weight, preferred_element_type=jnp.float32)
    hidden = (pre_act * jax.nn.sigmoid(pre_act)).astype(jnp.bfloat16)
    reduced = (
        lax.psum_scatter(
            lax.dot_general(
                ff_out_weight, hidden, (((0,), (1,)), ((), ())), preferred_element_type=jnp.float32
            ).astype(jnp.bfloat16),
            "mp",
            scatter_dimension=0,
            tiled=True,
        )
        .astype(jnp.float32)
        .T
    )
    return (block_cols.astype(jnp.float32) + 0.5 * reduced).astype(jnp.bfloat16)


def solution(mesh):
    in_specs = (
        P("tm", "mp"),
        P(),
        P(None, None, "mp"),
        P(None, "mp"),
        P("mp"),
        P("mp"),
        P(None, "mp"),
        P(),
        P(None, "mp"),
        P("mp", None),
    )
    out_specs = P("tm", "mp")
    return jax.shard_map(body, mesh=mesh, in_specs=in_specs, out_specs=out_specs, check_vma=False)
```

profile of v0, /device:TPU:1, one launch (start us, length us, event | category | flops | bytes accessed | tf_op | source)
XLA Modules:
  0.0 681.7 jit_solution(13901758034869463315)
XLA Ops:
  6.5 0.7 all-gather.4.cloned.1.call-update
  7.3 0.0 all-gather.6.cloned.1.call-start
  7.3 1.0 slice_bitcast_fusion.30
  8.3 110.6 %all-gather.4.cloned.1.call-done = bf16[2048,1024]{0,1:T(8,128)(2,1)} async-done(((bf16[2048,64]{0,1:T(8,128)(2,1)}), bf16[2048,1024]{0,1:T(8,128)(2,1)}) %all-gather.4.cloned.1.call-update) | async-done | bytes 4194320 | tf_op jit(solution)/shard_map/all_gather | solution.py:48
  119.0 3.0 convert_reduce_fusion.1
  122.0 0.5 copy-done.1
  122.4 1.1 fusion.7
  123.6 1.6 fusion.20
  125.2 0.1 fusion.64
  125.4 0.1 fusion.68
  125.4 5.7 collective-permute-start.1
  131.2 3.0 collective-permute-start
  134.2 1.0 slice_bitcast_fusion.29
  135.2 0.3 concatenate.3
  135.5 5.1 fusion.66
  140.7 52.5 %psum.14 = f32[64]{0:T(128)S(1)} all-reduce(f32[64]{0:T(128)S(1)} %get-tuple-element.5), channel_id=1, replica_groups=mesh['tm'=32,'mp'=16] {'tm'}, use_global_device_ids=true, to_apply=%region_3.0 | all-reduce | flops 64 | bytes 512 | tf_op jit(solution)/shard_map/psum | solution.py:66
  193.2 0.2 multiply_reduce_fusion
  193.4 54.8 %psum.15 = f32[64]{0:T(128)S(1)} all-reduce(f32[64]{0:T(128)S(1)} %multiply_reduce_fusion), channel_id=1, replica_groups=mesh['tm'=32,'mp'=16] {'tm'}, use_global_device_ids=true, to_apply=%region_5.0 | all-reduce | flops 64 | bytes 512 | tf_op jit(solution)/shard_map/psum | solution.py:69
  248.3 1.1 multiply_convert_fusion.1
  249.4 0.0 all-gather.6.cloned.1.call-update
  249.4 0.0 all-gather.8.cloned.1.call-start
  249.5 95.4 %all-gather.6.cloned.1.call-done = bf16[1024,2048]{1,0:T(8,128)(2,1)} async-done(((bf16[64,2048]{1,0:T(8,128)(2,1)}), bf16[1024,2048]{1,0:T(8,128)(2,1)}) %all-gather.6.cloned.1.call-update) | async-done | bytes 4194320 | tf_op jit(solution)/shard_map/all_gather | solution.py:74
  344.9 3.7 fusion.23
  348.6 0.0 all-gather.8.cloned.1.call-update
  348.7 0.2 reduce-scatter.2.cloned.1.call-start
  348.9 101.9 %all-gather.8.cloned.1.call-done = bf16[2048,1024]{0,1:T(8,128)(2,1)} async-done(((bf16[2048,64]{0,1:T(8,128)(2,1)}), bf16[2048,1024]{0,1:T(8,128)(2,1)}) %all-gather.8.cloned.1.call-update) | async-done | bytes 4194320 | tf_op jit(solution)/shard_map/all_gather | solution.py:76
  450.8 3.0 convert_reduce_fusion
  453.8 0.5 copy-done.2
  454.3 1.1 fusion.4
  455.4 8.5 %convert_bitcast_fusion = bf16[1024,2048]{1,0:T(8,128)(2,1)} fusion(bf16[256,1024]{1,0:T(8,128)(2,1)S(1)} %copy-done, bf16[1024,256]{1,0:T(8,128)(2,1)S(1)} %copy-done.8, bf16[2048,1024]{0,1:T(8,128)(2,1)} %all-gather.8.cloned.1.call-done, f32[1024]{0:T(1024)S(1)} %copy-done.11, f32[2048]{0:T(1024)S(1)} %add_rsqrt_fusion, f32[2048]{0:T(1024)S(1)} %broadcast_multiply_fusion), kind=kOutput, calls=%fused_computation.16 | convolution fusion | flops 2162688000 | bytes 9457664 | tf_op jit(solution)/shard_map/dot_general | solution.py:82
  464.0 209.5 %reduce-scatter.2.cloned.1.call-done = bf16[64,2048]{1,0:T(8,128)(2,1)} async-done(((bf16[1024,2048]{1,0:T(8,128)(2,1)}), bf16[64,2048]{1,0:T(8,128)(2,1)}) %reduce-scatter.2.cloned.1.call-update) | async-done | bytes 262160 | tf_op jit(solution)/shard_map/reduce_scatter | solution.py:81
  673.5 1.7 fusion.63
  (33 shorter events, 0.2 us)
Async XLA Ops:
  6.5 448.9 %copy-start = (bf16[256,1024]{1,0:T(8,128)(2,1)S(1)}, bf16[256,1024]{1,0:T(8,128)(2,1)}, u32[]{:S(2)}) copy-start(bf16[256,1024]{1,0:T(8,128)(2,1)} %param.19) | copy-start | bytes 1572868
  6.5 112.4 %all-gather.4.cloned.1.call-start = ((), (), s32[]{:S(2)}) async-start(), calls=%async_computation.1 | async-start | bytes 4456448 | tf_op jit(solution)/shard_map/all_gather | solution.py:48
  7.3 337.6 %all-gather.6.cloned.1.call-start = ((), (), s32[]{:S(2)}) async-start(), calls=%async_computation.2 | async-start | bytes 4456448 | tf_op jit(solution)/shard_map/all_gather | solution.py:74
  8.3 115.3 %copy-start.10 = (f32[1024]{0:T(1024)S(1)}, f32[1024]{0:T(1024)}, u32[]{:S(2)}) copy-start(f32[1024]{0:T(1024)} %param.11) | copy-start | bytes 12292
  119.0 3.4 copy-start.1
  119.0 4.6 copy-start.9
  125.4 9.7 %collective-permute-start.1 = (bf16[64,15]{1,0:T(8,128)(2,1)S(1)}, bf16[64,15]{1,0:T(8,128)(2,1)S(1)}, u32[]{:S(2)}, u32[]{:S(2)}) collective-permute-start(bf16[64,15]{1,0:T(8,128)(2,1)S(1)} %get-tuple-element.7), channel_id=1, source_target_pairs={{16,0},{32,16},{48,32},{64,48},{80,64},{96,80},{112,96},{128,112},... | collective-permute-start | bytes 5768 | tf_op jit(solution)/shard_map/ppermute | solution.py:15
  131.2 4.0 collective-permute-start
  135.5 112.8 %copy-start.6 = (f32[64]{0:T(128)S(1)}, f32[64]{0:T(128)}, u32[]{:S(2)}) copy-start(f32[64]{0:T(128)} %param.15) | copy-start | bytes 772
  135.5 112.8 %copy-start.7 = (f32[64]{0:T(128)S(1)}, f32[64]{0:T(128)}, u32[]{:S(2)}) copy-start(f32[64]{0:T(128)} %param.14) | copy-start | bytes 772
  135.5 209.4 %copy-start.4 = (bf16[2048,64]{0,1:T(8,128)(2,1)S(1)}, bf16[2048,64]{0,1:T(8,128)(2,1)}, u32[]{:S(2)}) copy-start(bf16[2048,64]{0,1:T(8,128)(2,1)} %param.10) | copy-start | bytes 786436
  135.5 209.4 %copy-start.5 = (bf16[1024,64]{0,1:T(8,128)(2,1)S(1)}, bf16[1024,64]{0,1:T(8,128)(2,1)}, u32[]{:S(2)}) copy-start(bf16[1024,64]{0,1:T(8,128)(2,1)} %param.16) | copy-start | bytes 393220
  249.4 201.4 %all-gather.8.cloned.1.call-start = ((), (), s32[]{:S(2)}) async-start(), calls=%async_computation.3 | async-start | bytes 4456448 | tf_op jit(solution)/shard_map/all_gather | solution.py:76
  348.6 106.8 %copy-start.11 = (f32[1024]{0:T(1024)S(1)}, f32[1024]{0:T(1024)}, u32[]{:S(2)}) copy-start(f32[1024]{0:T(1024)} %param.17) | copy-start | bytes 12292
  348.7 324.8 %reduce-scatter.2.cloned.1.call-start = ((), (), s32[]{:S(2)}) async-start(), calls=%async_computation.4 | async-start | bytes 4456448 | tf_op jit(solution)/shard_map/reduce_scatter | solution.py:81
  450.8 3.4 copy-start.2
  450.8 4.6 copy-start.8
  464.0 209.5 %copy-start.3 = (bf16[2048,64]{0,1:T(8,128)(2,1)S(1)}, bf16[2048,64]{0,1:T(8,128)(2,1)}, u32[]{:S(2)}) copy-start(bf16[2048,64]{0,1:T(8,128)(2,1)} %fusion.23) | copy-start | bytes 786436
Sparse Core Ops, SparseCore 0:
  10.5 108.3 all-gather.3
  249.5 95.3 all-gather.5
  348.8 101.9 all-gather.7
  464.1 209.3 reduce-scatter.1
where the time goes:
time: 686 us; the launch traced here: 682 us
  waiting for transfers between devices  518 us (76%)
  blocking collectives  107 us (16%)
  other arithmetic  16.7 us (2%)
  matrix products  13.9 us (2%)
  between operations  13.3 us (2%)
  starting transfers between devices  9.02 us (1%)
    reduce_scatter x1, waiting for transfers between devices, body(): lax.psum_scatter(lax.dot_general(ff_out_weight, hidden, (((0,), (1,)), ((...  209 us
    all_gather x1, waiting for transfers between devices, body(): whole = lax.all_gather(tokens, 'mp', axis=1, tiled=True)  111 us
    all_gather x1, waiting for transfers between devices, body(): block_whole = lax.all_gather(block_cols, 'mp', axis=1, tiled=True)  102 us
    all_gather x1, waiting for transfers between devices, body(): lax.all_gather(activated, 'mp', axis=0, tiled=True)  95.4 us
    psum x1, blocking collectives, body(): variance = lax.psum(jnp.sum(centred * centred, axis=1), 'tm') / total_frames  54.8 us
    psum x1, blocking collectives, body(): channel_sum = lax.psum(jnp.sum(convolved, axis=1), 'tm')  52.5 us
  transfers between devices with their start and end apart: 6, of which 4 were waited for; matrix products, arithmetic and copies ran while one was open for 0% of the time, Pallas kernels for 0%

commit v1 on v0

v1 whole, which is shorter than its diff:
```python
import jax
import jax.numpy as jnp
from jax import lax
from jax.sharding import Mesh, PartitionSpec as P

XLO, Y, CORE, XHI, Z = ("xlo", "y", "core", "xhi", "z")
BF, F32 = (jnp.bfloat16, jnp.float32)


def swap(x, axis):
    return lax.ppermute(x, axis, [(0, 1), (1, 0)])


def ordered(index, own, other):
    first = index == 0
    return jnp.where(first, own, other), jnp.where(first, other, own)


def group_gather(x, core, xhi):
    across = swap(x, XHI)
    beside = swap(x, CORE)
    far = swap(across, CORE)
    near = ordered(xhi, x, across)
    away = ordered(xhi, beside, far)
    return [[ordered(core, near[h], away[h])[c] for h in range(2)] for c in range(2)]


def split3(x):
    hi = x.astype(BF)
    rest = x - hi.astype(F32)
    mid = rest.astype(BF)
    return hi, mid, (rest - mid.astype(F32)).astype(BF)


def layer_norm(values, gain, axis):
    centre = jnp.mean(values, axis=axis, keepdims=True)
    spread = jnp.mean((values - centre) * (values - centre), axis=axis, keepdims=True)
    return (values - centre) * lax.rsqrt(spread + 1e-05) * gain


def combine(mean, square, count, axes):
    n = lax.axis_size(axes)
    stats = jnp.stack([mean, square])
    stats = lax.all_to_all(
        jnp.broadcast_to(stats[None], (n,) + stats.shape), axes, 0, 0, tiled=True
    )
    whole = jnp.mean(stats[:, 0], axis=0)
    apart = stats[:, 0] - whole
    return whole, jnp.sum(stats[:, 1], axis=0) + count * jnp.sum(apart * apart, axis=0)


def body(
    tokens,
    ln_conv_gain,
    glu_weight,
    depth_weight,
    bn_gain,
    bn_shift,
    conv_out_weight,
    ln_ff_gain,
    ff_in_weight,
    ff_out_weight,
):
    core, xhi = (lax.axis_index(CORE), lax.axis_index(XHI))
    nz = lax.axis_size(Z)
    frames, width = tokens.shape
    full = ln_conv_gain.shape[0]
    half = width // 2
    run = frames // nz
    taps = depth_weight.shape[0]
    span = (taps - 1) // 2
    total = frames * lax.axis_size((XLO, Y, CORE))

    def mine(x, axis, size):
        return lax.dynamic_slice_in_dim(x, core * size, size, axis=axis)

    glu = mine(glu_weight.transpose(1, 2, 0), 1, half).reshape(2 * half, full)
    conv_out = mine(conv_out_weight.T, 0, half)
    small = jnp.concatenate([depth_weight, bn_gain[None], bn_shift[None]], axis=0)
    small = mine(small.T, 0, half)
    small = jnp.concatenate(split3(small), axis=1)
    small = jnp.pad(small, ((0, 0), (0, 128 - small.shape[1]))).reshape(-1, full)
    first = lax.all_gather(jnp.concatenate([glu, conv_out, small], axis=0), Z)
    units = ff_in_weight.shape[1] // 2
    ff_in = mine(ff_in_weight, 1, units).T
    ff_out = mine(ff_out_weight, 0, units)
    second = lax.all_gather(jnp.concatenate([ff_in, ff_out], axis=0), Z)

    glu = first[:, : 2 * half].reshape(nz, 2, half, full).transpose(1, 0, 2, 3).reshape(-1, full)
    conv_out = first[:, 2 * half : 3 * half].reshape(-1, full)
    small = first[:, 3 * half :].reshape(nz * half, 128).astype(F32)
    n = taps + 2
    small = small[:, :n] + (small[:, n : 2 * n] + small[:, 2 * n : 3 * n])
    tap_weights, gain, shift = (small[:, :taps], small[:, taps], small[:, taps + 1])
    ff_in = second[:, :units].reshape(-1, full)
    ff_out = second[:, units:].reshape(-1, full)

    tok = tokens.T
    tm = lax.axis_size((XLO, Y, CORE))
    up = [(i, i + 1) for i in range(tm - 1)]
    left = lax.ppermute(tok[:, frames - span :], (XLO, Y, CORE), up)
    right = lax.ppermute(tok[:, :span], (XLO, Y, CORE), [(j, i) for i, j in up])
    lefts = [left] + [tok[:, k * run - span : k * run] for k in range(1, nz)]
    rights = [tok[:, k * run : k * run + span] for k in range(1, nz)] + [right]
    pad = jnp.zeros((width, 128 - 2 * span), BF)
    parts = [
        jnp.concatenate([tok[:, k * run : (k + 1) * run], lefts[k], rights[k], pad], axis=1)
        for k in range(nz)
    ]
    parts = lax.all_to_all(jnp.stack(parts), Z, 0, 0, tiled=True)
    here = group_gather(parts.reshape(nz * width, run + 128), core, xhi)
    whole = jnp.concatenate([jnp.concatenate(c, axis=0) for c in here], axis=1)
    normed = layer_norm(whole.astype(F32), ln_conv_gain[:, None], 0).astype(BF)
    paired = jnp.dot(glu, normed, preferred_element_type=F32)
    mid = nz * half
    gated = (paired[:mid] * jax.nn.sigmoid(paired[mid:])).astype(BF)
    gated = gated.reshape(mid, 2, run + 128).astype(F32)
    window = jnp.concatenate(
        [gated[:, :, run : run + span], gated[:, :, :run], gated[:, :, run + span : run + 2 * span]],
        axis=2,
    )
    convolved = jnp.zeros((mid, 2, run), F32)
    for j in range(taps):
        convolved = convolved + tap_weights[:, j][:, None, None] * window[:, :, j : j + run]
    convolved = convolved.reshape(mid, 2 * run)
    mean = jnp.mean(convolved, axis=1)
    apart = convolved - mean[:, None]
    square = jnp.sum(apart * apart, axis=1)
    count = 2 * run
    mean, square = combine(mean, square, count, (Z,))
    mean, square = combine(mean, square, count * nz, (XLO, Y))
    variance = square / total
    normal_bn = (convolved - mean[:, None]) * lax.rsqrt(variance + 1e-05)[:, None] * gain[
        :, None
    ] + shift[:, None]
    activated = (normal_bn * jax.nn.sigmoid(normal_bn)).astype(BF)

    def natural(blocks):
        cols = blocks[0][0].shape[1]
        x = jnp.stack([jnp.stack([b.reshape(nz, half, cols) for b in c]) for c in blocks])
        return x.transpose(1, 2, 0, 3, 4).reshape(full, cols)

    mixed = jnp.dot(
        conv_out, natural(group_gather(activated, core, xhi)), preferred_element_type=F32
    )
    rows = lax.dynamic_slice_in_dim(whole, xhi * nz * width, nz * width, axis=0)
    rows = rows.reshape(nz, width, 2, run + 128)[..., :run]
    residual = mine(rows, 1, half).reshape(mid, 2 * run)
    block = (residual.astype(F32) + mixed).astype(BF)
    block = natural(group_gather(block, core, xhi))
    normed_ff = layer_norm(block.astype(F32), ln_ff_gain[:, None], 0).astype(BF)
    pre_act = jnp.dot(ff_in, normed_ff, preferred_element_type=F32)
    hidden = (pre_act * jax.nn.sigmoid(pre_act)).astype(BF)
    partial = lax.dot_general(
        ff_out, hidden, (((0,), (0,)), ((), ())), preferred_element_type=F32
    )
    keep, give = ordered(core, partial[:, :run], partial[:, run:])
    keep = keep + swap(give.astype(BF), CORE).astype(F32)
    keep, give = ordered(xhi, keep[: full // 2], keep[full // 2 :])
    keep = keep + swap(give.astype(BF), XHI).astype(F32)
    block = lax.dynamic_slice(block, (xhi * (full // 2), core * run), (full // 2, run))
    out = (block.astype(F32) + 0.5 * keep).astype(BF)
    out = lax.all_to_all(out.reshape(nz, width, run), Z, 0, 0, tiled=True)
    return out.transpose(1, 0, 2).reshape(width, frames).T


def solution(mesh):
    fine = Mesh(mesh.devices.reshape(2, 8, 2, 2, 8), (XLO, Y, CORE, XHI, Z))
    tm, mp = ((XLO, Y, CORE), (XHI, Z))
    in_specs = (
        P(tm, mp),
        P(),
        P(None, None, mp),
        P(None, mp),
        P(mp),
        P(mp),
        P(None, mp),
        P(),
        P(None, mp),
        P(mp, None),
    )
    return jax.shard_map(body, mesh=fine, in_specs=in_specs, out_specs=P(tm, mp), check_vma=False)
```

time: 686 us -> 201 us (0.29)
  waiting for transfers between devices: 518 us -> 26.6 us
  blocking collectives: 107 us -> 46.5 us
  starting transfers between devices: 9.02 us -> 60.1 us
  local copies, waits for them, and re-layouts: 3.26 us -> 23.8 us
    all_gather x3 -> x2, waiting for transfers between devices: 308 us -> 0.04 us  [the longest x1 0.02 us: body(): first = lax.all_gather(jnp.concatenate([glu, conv_out, small], axis=0), Z)]
    reduce_scatter x1 -> x0, waiting for transfers between devices: 209 us -> none  [body(): lax.psum_scatter(lax.dot_general(ff_out_weight, hidden, (((0,), (1,)), ((...]
    psum x2 -> x0, blocking collectives: 107 us -> none  [the longest x1 54.8 us: body(): variance = lax.psum(jnp.sum(centred * centred, axis=1), 'tm') / total_frames]
    all_to_all x0 -> x3, blocking collectives: none -> 46.5 us  [the longest x1 24.7 us: body(): parts = lax.all_to_all(jnp.stack(parts), Z, 0, 0, tiled=True)]
    ppermute x2 -> x13, starting transfers between devices: 8.72 us -> 53.4 us  [the longest x11 42.7 us: swap(): return lax.ppermute(x, axis, [(0, 1), (1, 0)])]
    ppermute x2 -> x13, waiting for transfers between devices: 0.01 us -> 19.6 us  [the longest x11 19.4 us: swap(): return lax.ppermute(x, axis, [(0, 1), (1, 0)])]
    slice x1 -> x12, local copies, waits for them, and re-layouts: 0.08 us -> 13.5 us  [the longest x1 4.8 us: body(): ff_in = second[:, :units].reshape(-1, full)]
    all_to_all x0 -> x1, waiting for transfers between devices: none -> 6.93 us  [combine(): lax.all_to_all(jnp.broadcast_to(stats[None], (n,) + stats.shape), axes, 0...]
  transfers between devices with their start and end apart: 6 -> 16, of which waited for: 4 -> 9; matrix products, arithmetic and copies ran while one was open for 0% -> 14% of each run, Pallas kernels for 0% -> 0%
where the time goes in v1:
time: 201 us; the launch traced here: 199 us
  starting transfers between devices  60.1 us (30%)
  blocking collectives  46.5 us (23%)
  waiting for transfers between devices  26.6 us (13%)
  local copies, waits for them, and re-layouts  23.8 us (12%)
  other arithmetic  20.1 us (10%)
  between operations  14 us (7%)
  matrix products  7.69 us (4%)
    ppermute x11, starting transfers between devices, swap(): return lax.ppermute(x, axis, [(0, 1), (1, 0)])  42.7 us
    all_to_all x1, blocking collectives, body(): parts = lax.all_to_all(jnp.stack(parts), Z, 0, 0, tiled=True)  24.7 us
    ppermute x11, waiting for transfers between devices, swap(): return lax.ppermute(x, axis, [(0, 1), (1, 0)])  19.4 us
    all_to_all x1, blocking collectives, body(): out = lax.all_to_all(out.reshape(nz, width, run), Z, 0, 0, tiled=True)  12.6 us
    all_to_all x1, blocking collectives, combine(): lax.all_to_all(jnp.broadcast_to(stats[None], (n,) + stats.shape), axes, 0...  9.21 us
    ppermute x1, starting transfers between devices, body(): right = lax.ppermute(tok[:, :span], (XLO, Y, CORE), [(j, i) for i, j in up])  8.79 us
    reduce_sum x1, other arithmetic, body(): mean = jnp.mean(convolved, axis=1)  7.95 us
    all_to_all x1, waiting for transfers between devices, combine(): lax.all_to_all(jnp.broadcast_to(stats[None], (n,) + stats.shape), axes, 0...  6.93 us
  transfers between devices with their start and end apart: 16, of which 9 were waited for; matrix products, arithmetic and copies ran while one was open for 14% of the time, Pallas kernels for 0%

profile of v1, /device:TPU:1, one launch (start us, length us, event | category | flops | bytes accessed | tf_op | source)
XLA Modules:
  0.0 198.8 jit_solution(2467756296888743444)
XLA Ops:
  12.7 8.8 %collective-permute-start.1 = (bf16[64,15]{1,0:T(8,128)(2,1)S(1)}, bf16[64,15]{1,0:T(8,128)(2,1)S(1)}, u32[]{:S(2)}, u32[]{:S(2)}) collective-permute-start(bf16[64,15]{1,0:T(8,128)(2,1)S(1)} %get-tuple-element.73), channel_id=1, source_target_pairs={{16,0},{32,16},{48,32},{64,48},{80,64},{96,80},{112,96},{128,112},... | collective-permute-start | bytes 5768 | tf_op jit(solution)/shard_map/ppermute | solution.py:102
  21.5 1.9 collective-permute-start
  25.3 24.7 %all_to_all.20 = bf16[8,64,384]{2,1,0:T(8,128)(2,1)S(1)} all-to-all(bf16[8,64,384]{2,1,0:T(8,128)(2,1)S(1)} %fusion.120), channel_id=1, replica_groups=mesh['xlo'=2,'y'=8,'core'=2,'xhi'=2,'z'=8] {'z'}, dimensions={0} | all-to-all | bytes 786432 | tf_op jit(solution)/shard_map/all_to_all | solution.py:110
  50.0 4.7 %collective-permute-start.2 = (bf16[512,384]{1,0:T(8,128)(2,1)S(1)}, bf16[512,384]{1,0:T(8,128)(2,1)S(1)}, u32[]{:S(2)}, u32[]{:S(2)}) collective-permute-start(bf16[512,384]{1,0:T(8,128)(2,1)S(1)} %bitcast.130), channel_id=1, source_target_pairs={{0,8},{8,0},{1,9},{9,1},{2,10},{10,2},{3,11},{11,3},{4,12},{12,4},... | collective-permute-start | bytes 1179656 | tf_op jit(solution)/shard_map/ppermute | solution.py:11
  54.7 2.6 %collective-permute-start.3 = (bf16[512,384]{1,0:T(8,128)(2,1)S(1)}, bf16[512,384]{1,0:T(8,128)(2,1)S(1)}, u32[]{:S(2)}, u32[]{:S(2)}) collective-permute-start(bf16[512,384]{1,0:T(8,128)(2,1)S(1)} %bitcast.131), channel_id=1, source_target_pairs={{0,16},{16,0},{1,17},{17,1},{2,18},{18,2},{3,19},{19,3},{4,20},{20... | collective-permute-start | bytes 1179656 | tf_op jit(solution)/shard_map/ppermute | solution.py:11
  57.3 6.3 %collective-permute-done.2 = bf16[512,384]{1,0:T(8,128)(2,1)S(1)} collective-permute-done((bf16[512,384]{1,0:T(8,128)(2,1)S(1)}, bf16[512,384]{1,0:T(8,128)(2,1)S(1)}, u32[]{:S(2)}, u32[]{:S(2)}) %collective-permute-start.2) | collective-permute-done | bytes 393248 | tf_op jit(solution)/shard_map/ppermute | solution.py:11
  63.6 3.3 %collective-permute-start.4 = (bf16[512,384]{1,0:T(8,128)(2,1)S(1)}, bf16[512,384]{1,0:T(8,128)(2,1)S(1)}, u32[]{:S(2)}, u32[]{:S(2)}) collective-permute-start(bf16[512,384]{1,0:T(8,128)(2,1)S(1)} %collective-permute-done.2), channel_id=1, source_target_pairs={{0,16},{16,0},{1,17},{17,1},{2,18},{18,2},{3,19},{19,3},{4,20},{20... | collective-permute-start | bytes 1179656 | tf_op jit(solution)/shard_map/ppermute | solution.py:11
  69.4 1.2 slice-done
  72.1 1.2 copy-done.1
  73.4 1.2 copy.57
  78.9 1.4 slice_reduce_fusion.1
  80.4 8.0 %fusion.135 = (f32[256]{0:T(256)S(1)}, f32[256,2,256]{2,0,1:T(8,128)S(1)}) fusion(f32[256,2,15]{2,0,1:T(8,128)S(1)} %copy-done.2, f32[256,2,256]{2,0,1:T(8,128)S(1)} %copy.76, f32[256]{0:T(256)S(1)} %get-tuple-element.7, f32[256]{0:T(256)S(1)} %get-tuple-element.8, f32[256]{0:T(256)S(1)} %get-tuple-element.9, f32[256]{0:T(256)S(1)} %get-tuple-element.10, ...), kind=kLoop, calls=%fused_computation.310 | loop fusion | flops 12058368 | bytes 1142784 | tf_op jit(solution)/shard_map/reduce_sum | solution.py:126
  88.6 9.2 %all_to_all.21 = f32[8,2,256]{2,1,0:T(2,128)S(1)} all-to-all(f32[8,2,256]{2,1,0:T(2,128)S(1)} %broadcast_in_dim.13), channel_id=1, replica_groups=mesh['xlo'=2,'y'=8,'core'=2,'xhi'=2,'z'=8] {'z'}, dimensions={0} | all-to-all | bytes 32768 | tf_op jit(solution)/shard_map/all_to_all | solution.py:44
  98.5 6.7 %all-to-all-start.2 = ((f32[16,2,256]{2,1,0:T(2,128)}), f32[16,2,256]{2,1,0:T(2,128)S(1)}, u32[]{:S(2)}, u32[]{:S(2)}) async-start(f32[16,2,256]{2,1,0:T(2,128)} %broadcast_in_dim.14), calls=%async_computation.2 | async-start | bytes 65536 | tf_op jit(solution)/shard_map/all_to_all | solution.py:44
  105.6 6.9 %all-to-all-done.2 = f32[16,2,256]{2,1,0:T(2,128)S(1)} async-done(((f32[16,2,256]{2,1,0:T(2,128)}), f32[16,2,256]{2,1,0:T(2,128)S(1)}, u32[]{:S(2)}, u32[]{:S(2)}) %all-to-all-start.2) | async-done | bytes 32800 | tf_op jit(solution)/shard_map/all_to_all | solution.py:44
  113.6 4.7 %collective-permute-start.5 = (bf16[256,512]{1,0:T(8,128)(2,1)}, bf16[256,512]{1,0:T(8,128)(2,1)}, u32[]{:S(2)}, u32[]{:S(2)}) collective-permute-start(bf16[256,512]{1,0:T(8,128)(2,1)} %multiply_convert_fusion.2), channel_id=1, source_target_pairs={{0,8},{8,0},{1,9},{9,1},{2,10},{10,2},{3,11},{11,3},{4,12},{12,4},... | collective-permute-start | bytes 786440 | tf_op jit(solution)/shard_map/ppermute | solution.py:11
  118.2 5.1 %collective-permute-start.6 = (bf16[256,512]{1,0:T(8,128)(2,1)}, bf16[256,512]{1,0:T(8,128)(2,1)}, u32[]{:S(2)}, u32[]{:S(2)}) collective-permute-start(bf16[256,512]{1,0:T(8,128)(2,1)} %multiply_convert_fusion.2), channel_id=1, source_target_pairs={{0,16},{16,0},{1,17},{17,1},{2,18},{18,2},{3,19},{19,3},{4,20},{20... | collective-permute-start | bytes 786440 | tf_op jit(solution)/shard_map/ppermute | solution.py:11
  123.4 5.1 %collective-permute-start.7 = (bf16[256,512]{1,0:T(8,128)(2,1)}, bf16[256,512]{1,0:T(8,128)(2,1)}, u32[]{:S(2)}, u32[]{:S(2)}) collective-permute-start(bf16[256,512]{1,0:T(8,128)(2,1)} %collective-permute-done.5), channel_id=1, source_target_pairs={{0,16},{16,0},{1,17},{17,1},{2,18},{18,2},{3,19},{19,3},{4,20},{20... | collective-permute-start | bytes 786440 | tf_op jit(solution)/shard_map/ppermute | solution.py:11
  130.0 1.7 broadcast_select_fusion.23
  133.1 4.7 %collective-permute-start.8 = (bf16[256,512]{1,0:T(8,128)(2,1)S(1)}, bf16[256,512]{1,0:T(8,128)(2,1)S(1)}, u32[]{:S(2)}, u32[]{:S(2)}) collective-permute-start(bf16[256,512]{1,0:T(8,128)(2,1)S(1)} %fusion.15), channel_id=1, source_target_pairs={{0,8},{8,0},{1,9},{9,1},{2,10},{10,2},{3,11},{11,3},{4,12},{12,4},... | collective-permute-start | bytes 786440 | tf_op jit(solution)/shard_map/ppermute | solution.py:11
  137.8 2.6 %collective-permute-start.9 = (bf16[256,512]{1,0:T(8,128)(2,1)S(1)}, bf16[256,512]{1,0:T(8,128)(2,1)S(1)}, u32[]{:S(2)}, u32[]{:S(2)}) collective-permute-start(bf16[256,512]{1,0:T(8,128)(2,1)S(1)} %fusion.15), channel_id=1, source_target_pairs={{0,16},{16,0},{1,17},{17,1},{2,18},{18,2},{3,19},{19,3},{4,20},{20... | collective-permute-start | bytes 786440 | tf_op jit(solution)/shard_map/ppermute | solution.py:11
  140.4 3.7 %collective-permute-done.8 = bf16[256,512]{1,0:T(8,128)(2,1)S(1)} collective-permute-done((bf16[256,512]{1,0:T(8,128)(2,1)S(1)}, bf16[256,512]{1,0:T(8,128)(2,1)S(1)}, u32[]{:S(2)}, u32[]{:S(2)}) %collective-permute-start.8) | collective-permute-done | bytes 262176 | tf_op jit(solution)/shard_map/ppermute | solution.py:11
  144.1 3.1 %collective-permute-start.10 = (bf16[256,512]{1,0:T(8,128)(2,1)S(1)}, bf16[256,512]{1,0:T(8,128)(2,1)S(1)}, u32[]{:S(2)}, u32[]{:S(2)}) collective-permute-start(bf16[256,512]{1,0:T(8,128)(2,1)S(1)} %collective-permute-done.8), channel_id=1, source_target_pairs={{0,16},{16,0},{1,17},{17,1},{2,18},{18,2},{3,19},{19,3},{4,20},{20... | collective-permute-start | bytes 786440 | tf_op jit(solution)/shard_map/ppermute | solution.py:11
  149.5 4.8 %fusion.139 = (bf16[8,128,1024]{2,1,0:T(8,128)(2,1)}, bf16[8,128,1024]{2,1,0:T(8,128)(2,1)}) fusion(bf16[8,256,1024]{2,1,0:T(8,128)(2,1)} %bitcast.118), kind=kLoop, calls=%fused_computation.312 | loop fusion | bytes 8388608 | tf_op jit(solution)/shard_map/slice | solution.py:95
  154.3 6.1 %fusion.16 = f32[1024,512]{1,0:T(8,128)} fusion(bf16[1024,1024]{1,0:T(8,128)(2,1)} %bitcast.128, bf16[1024,1024]{1,0:T(8,128)(2,1)} %bitcast.127, bf16[1024,512]{1,0:T(8,128)(2,1)S(1)} %bitcast.132), kind=kOutput, calls=%fused_computation.78 | convolution fusion | flops 2150105088 | bytes 7340032 | tf_op jit(solution)/shard_map/dot_general | solution.py:154
  160.4 1.6 select_convert_fusion
  162.0 2.3 %collective-permute-start.11 = (bf16[1024,256]{1,0:T(8,128)(2,1)S(1)}, bf16[1024,256]{1,0:T(8,128)(2,1)S(1)}, u32[]{:S(2)}, u32[]{:S(2)}) collective-permute-start(bf16[1024,256]{1,0:T(8,128)(2,1)S(1)} %select_convert_fusion), channel_id=1, source_target_pairs={{0,16},{16,0},{1,17},{17,1},{2,18},{18,2},{3,19},{19,3},{4,20},{20... | collective-permute-start | bytes 1572872 | tf_op jit(solution)/shard_map/ppermute | solution.py:11
  164.3 1.5 collective-permute-done.11
  165.8 1.7 convert_add_fusion
  167.6 4.7 %collective-permute-start.12 = (bf16[512,256]{1,0:T(8,128)(2,1)S(1)}, bf16[512,256]{1,0:T(8,128)(2,1)S(1)}, u32[]{:S(2)}, u32[]{:S(2)}) collective-permute-start(bf16[512,256]{1,0:T(8,128)(2,1)S(1)} %select_convert_fusion.1), channel_id=1, source_target_pairs={{0,8},{8,0},{1,9},{9,1},{2,10},{10,2},{3,11},{11,3},{4,12},{12,4},... | collective-permute-start | bytes 786440 | tf_op jit(solution)/shard_map/ppermute | solution.py:11
  172.4 6.1 %collective-permute-done.12 = bf16[512,256]{1,0:T(8,128)(2,1)S(1)} collective-permute-done((bf16[512,256]{1,0:T(8,128)(2,1)S(1)}, bf16[512,256]{1,0:T(8,128)(2,1)S(1)}, u32[]{:S(2)}, u32[]{:S(2)}) %collective-permute-start.12) | collective-permute-done | bytes 262176 | tf_op jit(solution)/shard_map/ppermute | solution.py:11
  178.7 12.6 %all_to_all.22 = bf16[8,64,256]{2,1,0:T(8,128)(2,1)S(1)} all-to-all(bf16[8,64,256]{2,1,0:T(8,128)(2,1)S(1)} %bitcast.142), channel_id=1, replica_groups=mesh['xlo'=2,'y'=8,'core'=2,'xhi'=2,'z'=8] {'z'}, dimensions={0} | all-to-all | bytes 524288 | tf_op jit(solution)/shard_map/all_to_all | solution.py:163
  (110 shorter events, 24.8 us)
Async XLA Ops:
  6.5 60.3 %copy-start = (bf16[1024,256]{1,0:T(8,128)(2,1)S(1)}, bf16[1024,256]{1,0:T(8,128)(2,1)}, u32[]{:S(2)}) copy-start(bf16[1024,256]{1,0:T(8,128)(2,1)} %param.18) | copy-start | bytes 1572868
  6.5 62.9 %all-gather.8.cloned.1.call-start = ((), (), s32[]{:S(2)}) async-start(), calls=%async_computation.5 | async-start | bytes 1916928 | tf_op jit(solution)/shard_map/all_gather | solution.py:83
  11.5 55.5 %copy-start.3 = (bf16[256,1024]{1,0:T(8,128)(2,1)S(1)}, bf16[256,1024]{1,0:T(8,128)(2,1)}, u32[]{:S(2)}) copy-start(bf16[256,1024]{1,0:T(8,128)(2,1)} %param.19) | copy-start | bytes 1572868
  11.6 137.9 %all-gather.6.cloned.1.call-start = ((), (), s32[]{:S(2)}) async-start(), calls=%async_computation.4 | async-start | bytes 4718592 | tf_op jit(solution)/shard_map/all_gather | solution.py:87
  12.7 12.5 %collective-permute-start.1 = (bf16[64,15]{1,0:T(8,128)(2,1)S(1)}, bf16[64,15]{1,0:T(8,128)(2,1)S(1)}, u32[]{:S(2)}, u32[]{:S(2)}) collective-permute-start(bf16[64,15]{1,0:T(8,128)(2,1)S(1)} %get-tuple-element.73), channel_id=1, source_target_pairs={{16,0},{32,16},{48,32},{64,48},{80,64},{96,80},{112,96},{128,112},... | collective-permute-start | bytes 5768 | tf_op jit(solution)/shard_map/ppermute | solution.py:102
  21.5 3.1 %collective-permute-start = (bf16[64,15]{1,0:T(8,128)(2,1)S(1)}, bf16[64,15]{1,0:T(8,128)(2,1)S(1)}, u32[]{:S(2)}, u32[]{:S(2)}) collective-permute-start(bf16[64,15]{1,0:T(8,128)(2,1)S(1)} %get-tuple-element.87), channel_id=1, source_target_pairs={{0,16},{16,32},{32,48},{48,64},{64,80},{80,96},{96,112},{112,128},... | collective-permute-start | bytes 5768 | tf_op jit(solution)/shard_map/ppermute | solution.py:101
  50.0 13.6 %collective-permute-start.2 = (bf16[512,384]{1,0:T(8,128)(2,1)S(1)}, bf16[512,384]{1,0:T(8,128)(2,1)S(1)}, u32[]{:S(2)}, u32[]{:S(2)}) collective-permute-start(bf16[512,384]{1,0:T(8,128)(2,1)S(1)} %bitcast.130), channel_id=1, source_target_pairs={{0,8},{8,0},{1,9},{9,1},{2,10},{10,2},{3,11},{11,3},{4,12},{12,4},... | collective-permute-start | bytes 1179656 | tf_op jit(solution)/shard_map/ppermute | solution.py:11
  54.7 13.3 %collective-permute-start.3 = (bf16[512,384]{1,0:T(8,128)(2,1)S(1)}, bf16[512,384]{1,0:T(8,128)(2,1)S(1)}, u32[]{:S(2)}, u32[]{:S(2)}) collective-permute-start(bf16[512,384]{1,0:T(8,128)(2,1)S(1)} %bitcast.131), channel_id=1, source_target_pairs={{0,16},{16,0},{1,17},{17,1},{2,18},{18,2},{3,19},{19,3},{4,20},{20... | collective-permute-start | bytes 1179656 | tf_op jit(solution)/shard_map/ppermute | solution.py:11
  63.6 4.6 %collective-permute-start.4 = (bf16[512,384]{1,0:T(8,128)(2,1)S(1)}, bf16[512,384]{1,0:T(8,128)(2,1)S(1)}, u32[]{:S(2)}, u32[]{:S(2)}) collective-permute-start(bf16[512,384]{1,0:T(8,128)(2,1)S(1)} %collective-permute-done.2), channel_id=1, source_target_pairs={{0,16},{16,0},{1,17},{17,1},{2,18},{18,2},{3,19},{19,3},{4,20},{20... | collective-permute-start | bytes 1179656 | tf_op jit(solution)/shard_map/ppermute | solution.py:11
  69.4 1.4 copy-start.5
  69.4 1.2 slice-start
  71.9 1.5 copy-start.1
  77.9 2.5 %copy-start.2 = (f32[256,2,15]{2,0,1:T(8,128)S(1)}, f32[256,2,15]{2,0,1:T(8,128)}, u32[]{:S(2)}) copy-start(f32[256,2,15]{2,0,1:T(8,128)} %copy.77) | copy-start | bytes 92164
  98.5 14.0 %all-to-all-start.2 = ((f32[16,2,256]{2,1,0:T(2,128)}), f32[16,2,256]{2,1,0:T(2,128)S(1)}, u32[]{:S(2)}, u32[]{:S(2)}) async-start(f32[16,2,256]{2,1,0:T(2,128)} %broadcast_in_dim.14), calls=%async_computation.2 | async-start | bytes 65536 | tf_op jit(solution)/shard_map/all_to_all | solution.py:44
  113.6 9.8 %collective-permute-start.5 = (bf16[256,512]{1,0:T(8,128)(2,1)}, bf16[256,512]{1,0:T(8,128)(2,1)}, u32[]{:S(2)}, u32[]{:S(2)}) collective-permute-start(bf16[256,512]{1,0:T(8,128)(2,1)} %multiply_convert_fusion.2), channel_id=1, source_target_pairs={{0,8},{8,0},{1,9},{9,1},{2,10},{10,2},{3,11},{11,3},{4,12},{12,4},... | collective-permute-start | bytes 786440 | tf_op jit(solution)/shard_map/ppermute | solution.py:11
  118.2 11.1 %collective-permute-start.6 = (bf16[256,512]{1,0:T(8,128)(2,1)}, bf16[256,512]{1,0:T(8,128)(2,1)}, u32[]{:S(2)}, u32[]{:S(2)}) collective-permute-start(bf16[256,512]{1,0:T(8,128)(2,1)} %multiply_convert_fusion.2), channel_id=1, source_target_pairs={{0,16},{16,0},{1,17},{17,1},{2,18},{18,2},{3,19},{19,3},{4,20},{20... | collective-permute-start | bytes 786440 | tf_op jit(solution)/shard_map/ppermute | solution.py:11
  123.4 6.6 %collective-permute-start.7 = (bf16[256,512]{1,0:T(8,128)(2,1)}, bf16[256,512]{1,0:T(8,128)(2,1)}, u32[]{:S(2)}, u32[]{:S(2)}) collective-permute-start(bf16[256,512]{1,0:T(8,128)(2,1)} %collective-permute-done.5), channel_id=1, source_target_pairs={{0,16},{16,0},{1,17},{17,1},{2,18},{18,2},{3,19},{19,3},{4,20},{20... | collective-permute-start | bytes 786440 | tf_op jit(solution)/shard_map/ppermute | solution.py:11
  131.7 1.0 slice-start.1
  131.8 15.4 %copy-start.4 = (f32[1024]{0:T(1024)S(1)}, f32[1024]{0:T(1024)}, u32[]{:S(2)}) copy-start(f32[1024]{0:T(1024)} %param.17) | copy-start | bytes 12292
  133.1 10.9 %collective-permute-start.8 = (bf16[256,512]{1,0:T(8,128)(2,1)S(1)}, bf16[256,512]{1,0:T(8,128)(2,1)S(1)}, u32[]{:S(2)}, u32[]{:S(2)}) collective-permute-start(bf16[256,512]{1,0:T(8,128)(2,1)S(1)} %fusion.15), channel_id=1, source_target_pairs={{0,8},{8,0},{1,9},{9,1},{2,10},{10,2},{3,11},{11,3},{4,12},{12,4},... | collective-permute-start | bytes 786440 | tf_op jit(solution)/shard_map/ppermute | solution.py:11
  137.8 9.4 %collective-permute-start.9 = (bf16[256,512]{1,0:T(8,128)(2,1)S(1)}, bf16[256,512]{1,0:T(8,128)(2,1)S(1)}, u32[]{:S(2)}, u32[]{:S(2)}) collective-permute-start(bf16[256,512]{1,0:T(8,128)(2,1)S(1)} %fusion.15), channel_id=1, source_target_pairs={{0,16},{16,0},{1,17},{17,1},{2,18},{18,2},{3,19},{19,3},{4,20},{20... | collective-permute-start | bytes 786440 | tf_op jit(solution)/shard_map/ppermute | solution.py:11
  144.1 4.2 %collective-permute-start.10 = (bf16[256,512]{1,0:T(8,128)(2,1)S(1)}, bf16[256,512]{1,0:T(8,128)(2,1)S(1)}, u32[]{:S(2)}, u32[]{:S(2)}) collective-permute-start(bf16[256,512]{1,0:T(8,128)(2,1)S(1)} %collective-permute-done.8), channel_id=1, source_target_pairs={{0,16},{16,0},{1,17},{17,1},{2,18},{18,2},{3,19},{19,3},{4,20},{20... | collective-permute-start | bytes 786440 | tf_op jit(solution)/shard_map/ppermute | solution.py:11
  162.0 3.8 %collective-permute-start.11 = (bf16[1024,256]{1,0:T(8,128)(2,1)S(1)}, bf16[1024,256]{1,0:T(8,128)(2,1)S(1)}, u32[]{:S(2)}, u32[]{:S(2)}) collective-permute-start(bf16[1024,256]{1,0:T(8,128)(2,1)S(1)} %select_convert_fusion), channel_id=1, source_target_pairs={{0,16},{16,0},{1,17},{17,1},{2,18},{18,2},{3,19},{19,3},{4,20},{20... | collective-permute-start | bytes 1572872 | tf_op jit(solution)/shard_map/ppermute | solution.py:11
  167.6 10.9 %collective-permute-start.12 = (bf16[512,256]{1,0:T(8,128)(2,1)S(1)}, bf16[512,256]{1,0:T(8,128)(2,1)S(1)}, u32[]{:S(2)}, u32[]{:S(2)}) collective-permute-start(bf16[512,256]{1,0:T(8,128)(2,1)S(1)} %select_convert_fusion.1), channel_id=1, source_target_pairs={{0,8},{8,0},{1,9},{9,1},{2,10},{10,2},{3,11},{11,3},{4,12},{12,4},... | collective-permute-start | bytes 786440 | tf_op jit(solution)/shard_map/ppermute | solution.py:11
Sparse Core Ops, SparseCore 0:
  11.7 52.1 all-gather.7
  68.1 56.8 all-gather.5

commit v2 on v1

v2 whole, which is shorter than its diff:
```python
import jax
import jax.numpy as jnp
from jax import lax
from jax.experimental import pallas as pl
from jax.experimental.pallas import tpu as pltpu
from jax.sharding import Mesh, PartitionSpec as P

XLO, Y, CORE, XHI, Z = ("xlo", "y", "core", "xhi", "z")
BF, F32 = (jnp.bfloat16, jnp.float32)
EPS = 1e-05
LANES = 128
SPAN = 15
VMEM = pl.BlockSpec(memory_space=pltpu.VMEM)
SMEM = pl.BlockSpec(memory_space=pltpu.SMEM)
ANY = pl.BlockSpec(memory_space=pl.ANY)
PARAMS = pltpu.CompilerParams(vmem_limit_bytes=40 << 20)


def shape(dims, dtype):
    return jax.ShapeDtypeStruct(dims, dtype)


def swap(x, axis):
    return lax.ppermute(x, axis, [(0, 1), (1, 0)])


def group_gather(x):
    across = swap(x, XHI)
    beside = swap(x, CORE)
    return x, across, beside, swap(across, CORE)


def split3(x):
    hi = x.astype(BF)
    rest = x - hi.astype(F32)
    mid = rest.astype(BF)
    return hi, mid, (rest - mid.astype(F32)).astype(BF)


def norm_rows(x, gain):
    inv = 1.0 / x.shape[0]
    centred = x - jnp.sum(x, axis=0, keepdims=True) * inv
    spread = jnp.sum(centred * centred, axis=0, keepdims=True) * inv
    return (centred * lax.rsqrt(spread + EPS) * gain).astype(BF)


def at(start, size, step):
    return pl.ds(pl.multiple_of(start, step), size)


def pack_kernel(tok, left, right, out):
    lane = lax.broadcasted_iota(jnp.int32, (16, LANES), 1)
    nz = out.shape[0]
    for z in range(nz):
        out[z, 0:64] = tok[:, 2 * z * LANES : (2 * z + 1) * LANES]
        out[z, 64:128] = tok[:, (2 * z + 1) * LANES : (2 * z + 2) * LANES]
        packed = jnp.zeros((16, LANES), F32)
        for i in range(4):
            rows = slice(16 * i, 16 * i + 16)
            if z == 0:
                before = left[rows]
            else:
                before = tok[rows, (2 * z - 1) * LANES : 2 * z * LANES]
            if z == nz - 1:
                after = right[rows]
            else:
                after = tok[rows, (2 * z + 2) * LANES : (2 * z + 3) * LANES]
            low = pltpu.roll(before.astype(F32), (32 * i + SPAN) % LANES, 1)
            high = pltpu.roll(after.astype(F32), 32 * i + SPAN, 1)
            packed = jnp.where((lane >= 32 * i) & (lane < 32 * i + SPAN), low, packed)
            packed = jnp.where(
                (lane >= 32 * i + SPAN) & (lane < 32 * i + 2 * SPAN), high, packed
            )
        out[z, 128:144] = packed.astype(BF)


def conv_kernel(
    place, own, across, beside, far, glu, small, gain,
    conv, stats, par, res,
    tok, edge, win, taps,
):
    core, xhi = place[0], place[1]
    lane = lax.broadcasted_iota(jnp.int32, (16, LANES), 1)
    nz = glu.shape[0]
    for near, away, side in ((own, beside, xhi), (across, far, 1 - xhi)):
        for z in range(nz):
            row = side * (64 * nz) + 64 * z
            for c, blk in ((0, near), (1, away)):
                tok[at(row, 64, 64), 256 * c : 256 * c + 128] = blk[z, 0:64]
                tok[at(row, 64, 64), 256 * c + 128 : 256 * c + 256] = blk[z, 64:128]
            one = near[z, 128:144].astype(F32)
            two = away[z, 128:144].astype(F32)
            for i in range(4):
                low = pltpu.roll(one, (LANES - 32 * i) % LANES, 1)
                high = pltpu.roll(two, (LANES + 32 - 32 * i) % LANES, 1)
                part = jnp.where(lane < 32, low, jnp.where(lane < 64, high, 0.0))
                edge[at(row + 16 * i, 16, 16), :] = part
    for z in range(nz):
        row = xhi * (64 * nz) + 64 * z + 32 * core
        res[32 * z : 32 * z + 32, :] = tok[at(row, 32, 32), :]

    for z in range(nz):
        s = small[z].astype(F32)
        for i in range(2):
            hi = s[:, LANES * i : LANES * (i + 1)]
            mid = s[:, LANES * (2 + i) : LANES * (3 + i)]
            low = s[:, LANES * (4 + i) : LANES * (5 + i)]
            taps[32 * z + 16 * i : 32 * z + 16 * i + 16, :] = hi + (mid + low)
    table = [taps[0:128, :].T, taps[128:256, :].T]
    for h in range(2):
        par[:, LANES * h : LANES * (h + 1)] = table[h][31:39]

    weight = glu[...].reshape(glu.shape[0] * glu.shape[1], glu.shape[2])
    scale = gain[...]
    for c in range(3):
        x = edge[...] if c == 2 else tok[:, 256 * c : 256 * (c + 1)].astype(F32)
        paired = jnp.dot(weight, norm_rows(x, scale), preferred_element_type=F32)
        cols = x.shape[1]
        paired = paired.reshape(nz, 2, 32, cols)
        gated = (paired[:, 0] * jax.nn.sigmoid(paired[:, 1])).astype(BF).astype(F32)
        gated = gated.reshape(32 * nz, cols).T
        if c < 2:
            win[c, 16:272, :] = gated
        else:
            for r in range(2):
                win[r, 1:16, :] = gated[32 * r : 32 * r + 15]
                win[r, 272:287, :] = gated[32 * r + 15 : 32 * r + 30]

    step = 64
    for h in range(2):
        cols = slice(LANES * h, LANES * (h + 1))
        total = jnp.zeros((1, LANES), F32)
        for r in range(2):
            for k in range(256 // step):
                acc = jnp.zeros((step, LANES), F32)
                for j in range(31):
                    first = step * k + 1 + j
                    acc = acc + table[h][j : j + 1] * win[r, first : first + step, cols]
                conv[256 * r + step * k : 256 * r + step * (k + 1), cols] = acc
                total = total + jnp.sum(acc, axis=0, keepdims=True)
        mean = total * (1.0 / 512)
        apart = conv[:, cols] - mean
        square = jnp.sum(apart * apart, axis=0, keepdims=True)
        n = stats.shape[0]
        stats[:, h : h + 1, :] = jnp.broadcast_to(mean[None], (n, 1, LANES))
        stats[:, 2 + h : 3 + h, :] = jnp.broadcast_to(square[None], (n, 1, LANES))


def bn_kernel(conv, stats, par, out):
    n, frames = stats.shape[0], conv.shape[0]
    s = stats[...]
    total = jnp.sum(s, axis=0)
    mean = total * (1.0 / n)
    apart = s - mean[None]
    apart = jnp.sum(apart * apart, axis=0)
    for h in range(2):
        cols = slice(LANES * h, LANES * (h + 1))
        square = total[2 + h : 3 + h] + frames * apart[h : h + 1]
        scale = lax.rsqrt(square * (1.0 / (n * frames)) + EPS) * par[0:1, cols]
        value = (conv[:, cols] - mean[h : h + 1]) * scale + par[1:2, cols]
        out[cols, :] = (value * jax.nn.sigmoid(value)).T.astype(BF)


def place_blocks(place, own, across, beside, far, whole):
    core, xhi = place[0], place[1]
    nz, half = 8, 256
    for blk, c, x in ((own, core, xhi), (across, core, 1 - xhi)):
        for z in range(nz):
            row = x * 512 + 64 * z + 32 * c
            whole[at(row, 32, 32), :] = blk[32 * z : 32 * z + 32, :]
    for blk, c, x in ((beside, 1 - core, xhi), (far, 1 - core, 1 - xhi)):
        for z in range(nz):
            row = x * 512 + 64 * z + 32 * c
            whole[at(row, 32, 32), :half] = blk[32 * z : 32 * z + 32, half:]
            whole[at(row, 32, 32), half:] = blk[32 * z : 32 * z + 32, :half]


def mix_kernel(place, own, across, beside, far, weight, res, out, whole):
    place_blocks(place, own, across, beside, far, whole)
    w = weight[...].reshape(256, weight.shape[2])
    mixed = jnp.dot(w, whole[...], preferred_element_type=F32)
    out[...] = (res[...].astype(F32) + mixed).astype(BF)


def ff_kernel(
    place, own, across, beside, far, weights, gain,
    keep, give, res,
    whole, normed, hidden, w, sem,
):
    copy = pltpu.make_async_copy(weights, w, sem)
    copy.start()
    place_blocks(place, own, across, beside, far, whole)
    half = 256
    res[...] = whole[at(place[1] * 512, 512, 512), :half]
    for c in range(2):
        cols = slice(half * c, half * (c + 1))
        normed[:, cols] = norm_rows(whole[:, cols].astype(F32), gain[...])
    copy.wait()
    for z in range(0, 8, 2):
        rows = [jnp.concatenate([w[z + i, k] for k in range(8)], axis=1) for i in range(2)]
        value = jnp.dot(
            jnp.concatenate(rows, axis=0), normed[...], preferred_element_type=F32
        )
        hidden[LANES * z : LANES * (z + 2), :] = (value * jax.nn.sigmoid(value)).astype(BF)
    for k in range(0, 8, 2):
        rows = [jnp.concatenate([w[z, 8 + k + i] for z in range(8)], axis=1) for i in range(2)]
        value = jnp.dot(
            jnp.concatenate(rows, axis=0), hidden[...], preferred_element_type=F32
        )
        keep[LANES * k : LANES * (k + 2), :] = value[:, :half]
        give[LANES * k : LANES * (k + 2), :] = value[:, half:].astype(BF)


def body(
    tokens,
    ln_conv_gain,
    glu_weight,
    depth_weight,
    bn_gain,
    bn_shift,
    conv_out_weight,
    ln_ff_gain,
    ff_in_weight,
    ff_out_weight,
):
    core, xhi = (lax.axis_index(CORE), lax.axis_index(XHI))
    place = jnp.stack([core, xhi]).astype(jnp.int32)
    nz = lax.axis_size(Z)
    frames, width = tokens.shape
    full = ln_conv_gain.shape[0]
    half = width // 2
    run = frames // nz

    def mine(x, axis, size):
        return lax.dynamic_slice_in_dim(x, core * size, size, axis=axis)

    glu = mine(glu_weight.transpose(1, 2, 0), 1, half).reshape(2 * half, full)
    conv_out = mine(conv_out_weight.T, 0, half)
    small = jnp.concatenate([depth_weight, bn_gain[None], bn_shift[None]], axis=0)
    small = mine(small.T, 0, half)
    small = jnp.pad(small, ((0, 0), (0, LANES - small.shape[1])))
    small = [p[16 * i : 16 * i + 16] for p in split3(small) for i in range(2)]
    small = jnp.pad(jnp.concatenate(small, axis=1), ((0, 0), (0, full - 6 * LANES)))
    first = lax.all_gather(jnp.concatenate([glu, conv_out, small], axis=0), Z)

    tok = tokens.T
    tm = lax.axis_size((XLO, Y, CORE))
    up = [(i, i + 1) for i in range(tm - 1)]
    left = lax.ppermute(tok[:, frames - LANES :], (XLO, Y, CORE), up)
    right = lax.ppermute(tok[:, :LANES], (XLO, Y, CORE), [(j, i) for i, j in up])
    parts = pl.pallas_call(
        pack_kernel,
        out_shape=shape((nz, 144, LANES), BF),
        in_specs=[VMEM] * 3,
        out_specs=VMEM,
        compiler_params=PARAMS,
        name="pack",
    )(tok, left, right)
    parts = lax.all_to_all(parts, Z, 0, 0, tiled=True)

    ff_in_weight, ff_out_weight, parts = lax.optimization_barrier(
        (ff_in_weight, ff_out_weight, parts)
    )
    ff_in = mine(ff_in_weight, 1, LANES).reshape(8, LANES, LANES).transpose(0, 2, 1)
    ff_out = mine(ff_out_weight, 0, LANES).reshape(LANES, 8, LANES).transpose(1, 2, 0)
    second = lax.all_gather(jnp.concatenate([ff_in, ff_out], axis=0), Z)

    whole = group_gather(parts)
    peers = lax.axis_size((XLO, Y, Z))
    conv, stats, par, res = pl.pallas_call(
        conv_kernel,
        out_shape=(
            shape((2 * run, 256), F32),
            shape((peers, 4, LANES), F32),
            shape((8, 256), F32),
            shape((256, 2 * run), BF),
        ),
        grid=(1,),
        in_specs=[SMEM]
        + [VMEM] * 4
        + [
            pl.BlockSpec((nz, 64, full), lambda i: (0, 0, 0)),
            pl.BlockSpec((nz, 16, full), lambda i: (0, 6, 0)),
            VMEM,
        ],
        out_specs=(VMEM,) * 4,
        scratch_shapes=[
            pltpu.VMEM((full, 2 * run), BF),
            pltpu.VMEM((full, LANES), F32),
            pltpu.VMEM((2, run + 40, 256), F32),
            pltpu.VMEM((256, LANES), F32),
        ],
        compiler_params=PARAMS,
        name="conv",
    )(place, *whole, first, first, ln_conv_gain[:, None])
    stats = lax.all_to_all(stats, (XLO, Y, Z), 0, 0, tiled=True)
    activated = pl.pallas_call(
        bn_kernel,
        out_shape=shape((256, 2 * run), BF),
        in_specs=[VMEM] * 3,
        out_specs=VMEM,
        compiler_params=PARAMS,
        name="bn",
    )(conv, stats, par)
    block = pl.pallas_call(
        mix_kernel,
        out_shape=shape((256, 2 * run), BF),
        grid=(1,),
        in_specs=[SMEM]
        + [VMEM] * 4
        + [pl.BlockSpec((nz, 32, full), lambda i: (0, 2, 0)), VMEM],
        out_specs=VMEM,
        scratch_shapes=[pltpu.VMEM((full, 2 * run), BF)],
        compiler_params=PARAMS,
        name="mix",
    )(place, *group_gather(activated), first, res)
    keep, give, res = pl.pallas_call(
        ff_kernel,
        out_shape=(
            shape((full, run), F32),
            shape((full, run), BF),
            shape((full // 2, run), BF),
        ),
        in_specs=[SMEM] + [VMEM] * 4 + [ANY, VMEM],
        out_specs=(VMEM,) * 3,
        scratch_shapes=[
            pltpu.VMEM((full, 2 * run), BF),
            pltpu.VMEM((full, 2 * run), BF),
            pltpu.VMEM((full, 2 * run), BF),
            pltpu.VMEM((8, 16, LANES, LANES), BF),
            pltpu.SemaphoreType.DMA,
        ],
        compiler_params=PARAMS,
        name="ff",
    )(place, *group_gather(block), second, ln_ff_gain[:, None])
    other = swap(give, CORE)
    size = full // 2

    def part(x, index):
        return lax.dynamic_slice_in_dim(x, index * size, size, axis=0).astype(F32)

    give = (part(keep, 1 - xhi) + part(other, 1 - xhi)).astype(BF)
    keep = part(keep, xhi) + part(other, xhi) + swap(give, XHI).astype(F32)
    out = (res.astype(F32) + 0.5 * keep).astype(BF)
    out = lax.all_to_all(out.reshape(nz, width, run), Z, 0, 0, tiled=True)
    return out.transpose(1, 0, 2).reshape(width, frames).T


def solution(mesh):
    fine = Mesh(mesh.devices.reshape(2, 8, 2, 2, 8), (XLO, Y, CORE, XHI, Z))
    tm, mp = ((XLO, Y, CORE), (XHI, Z))
    in_specs = (
        P(tm, mp),
        P(),
        P(None, None, mp),
        P(None, mp),
        P(mp),
        P(mp),
        P(None, mp),
        P(),
        P(None, mp),
        P(mp, None),
    )
    return jax.shard_map(body, mesh=fine, in_specs=in_specs, out_specs=P(tm, mp), check_vma=False)
```

time: 201 us -> 175 us (0.87)
  other arithmetic: 20.1 us -> 1.11 us
  Pallas kernels: 0 us -> 12.2 us
  local copies, waits for them, and re-layouts: 23.8 us -> 13.2 us
  waiting for transfers between devices: 26.6 us -> 36.7 us
  blocking collectives: 46.5 us -> 37.1 us
  matrix products: 7.69 us -> 0 us
    slice x12 -> x1, local copies, waits for them, and re-layouts: 13.5 us -> 0.74 us  [body(): tok[:, :LANES]]
    pallas_call x0 -> x5, Pallas kernels: none -> 12.2 us  [the longest x1 5.08 us: body(): pl.pallas_call(conv_kernel, out_shape=(shape((2 * run, 256), F32), shape(...]
    all_to_all x2 -> x1, blocking collectives: 34 us -> 24.2 us  [body(): stats = lax.all_to_all(stats, (XLO, Y, Z), 0, 0, tiled=True)]
    reduce_sum x10 -> x0, other arithmetic: 9.77 us -> none  [the longest x1 7.95 us: body(): mean = jnp.mean(convolved, axis=1)]
    all_to_all x1, waiting for transfers between devices: 6.93 us -> 15.1 us  [body(): parts = lax.all_to_all(parts, Z, 0, 0, tiled=True)]
    dot_general x3 -> x0, matrix products: 7.69 us -> none  [the longest x1 6.12 us: body(): lax.dot_general(ff_out, hidden, (((0,), (0,)), ((), ())), preferred_eleme...]
    convert_element_type x10 -> x3, other arithmetic: 3.64 us -> 0.2 us  [the longest x1 0.14 us: body(): out = (res.astype(F32) + 0.5 * keep).astype(BF)]
    ppermute x11, starting transfers between devices: 42.7 us -> 40.1 us  [swap(): return lax.ppermute(x, axis, [(0, 1), (1, 0)])]
  transfers between devices with their start and end apart: 16 -> 16, of which waited for: 9 -> 9; matrix products, arithmetic and copies ran while one was open for 14% -> 2% of each run, Pallas kernels for 0% -> 4%
where the time goes in v2:
time: 175 us; the launch traced here: 173 us
  starting transfers between devices  59 us (34%)
  blocking collectives  37.1 us (21%)
  waiting for transfers between devices  36.7 us (21%)
  between operations  13.7 us (8%)
  local copies, waits for them, and re-layouts  13.2 us (8%)
  Pallas kernels  12.2 us (7%)
    ppermute x11, starting transfers between devices, swap(): return lax.ppermute(x, axis, [(0, 1), (1, 0)])  40.1 us
    all_to_all x1, blocking collectives, body(): stats = lax.all_to_all(stats, (XLO, Y, Z), 0, 0, tiled=True)  24.2 us
    ppermute x11, waiting for transfers between devices, swap(): return lax.ppermute(x, axis, [(0, 1), (1, 0)])  20.7 us
    all_to_all x1, waiting for transfers between devices, body(): parts = lax.all_to_all(parts, Z, 0, 0, tiled=True)  15.1 us
    all_to_all x1, blocking collectives, body(): out = lax.all_to_all(out.reshape(nz, width, run), Z, 0, 0, tiled=True)  13 us
    all_to_all x1, starting transfers between devices, body(): parts = lax.all_to_all(parts, Z, 0, 0, tiled=True)  8.79 us
    unnamed x20, local copies, waits for them, and re-layouts  5.55 us
    ppermute x1, starting transfers between devices, body(): lax.ppermute(tok[:, :LANES], (XLO, Y, CORE), [(j, i) for i, j in up])  5.48 us
  transfers between devices with their start and end apart: 16, of which 9 were waited for; matrix products, arithmetic and copies ran while one was open for 2% of the time, Pallas kernels for 4%

profile of v2, /device:TPU:1, one launch (start us, length us, event | category | flops | bytes accessed | tf_op | source)
XLA Modules:
  0.0 173.0 jit_solution(16278302606223973674)
XLA Ops:
  9.1 0.9 constant_dynamic-slice_fusion.2
  12.3 4.6 %collective-permute-start = (bf16[64,128]{1,0:T(8,128)(2,1)S(1)}, bf16[64,128]{1,0:T(8,128)(2,1)S(1)}, u32[]{:S(2)}, u32[]{:S(2)}) collective-permute-start(bf16[64,128]{1,0:T(8,128)(2,1)S(1)} %get-tuple-element.26), channel_id=1, source_target_pairs={{0,16},{16,32},{32,48},{48,64},{64,80},{80,96},{96,112},{112,128},... | collective-permute-start | bytes 49160 | tf_op jit(solution)/shard_map/ppermute | solution.py:249
  16.9 5.5 %collective-permute-start.1 = (bf16[64,128]{1,0:T(8,128)(2,1)S(1)}, bf16[64,128]{1,0:T(8,128)(2,1)S(1)}, u32[]{:S(2)}, u32[]{:S(2)}) collective-permute-start(bf16[64,128]{1,0:T(8,128)(2,1)S(1)} %get-tuple-element.25), channel_id=1, source_target_pairs={{16,0},{32,16},{48,32},{64,48},{80,64},{96,80},{112,96},{128,112},... | collective-permute-start | bytes 49160 | tf_op jit(solution)/shard_map/ppermute | solution.py:250
  23.2 0.9 copy-done.4
  25.0 8.8 %all-to-all-start = ((bf16[8,144,128]{2,1,0:T(8,128)(2,1)}), bf16[8,144,128]{2,1,0:T(8,128)(2,1)S(1)}, u32[]{:S(2)}, u32[]{:S(2)}) async-start(bf16[8,144,128]{2,1,0:T(8,128)(2,1)} %pack.1), calls=%async_computation | async-start | bytes 589824 | tf_op jit(solution)/shard_map/all_to_all | solution.py:259
  33.8 15.1 %all-to-all-done.own = bf16[8,144,128]{2,1,0:T(8,128)(2,1)S(1)} async-done(((bf16[8,144,128]{2,1,0:T(8,128)(2,1)}), bf16[8,144,128]{2,1,0:T(8,128)(2,1)S(1)}, u32[]{:S(2)}, u32[]{:S(2)}) %all-to-all-start) | async-done | bytes 294944 | tf_op jit(solution)/shard_map/all_to_all | solution.py:259
  48.9 1.3 copy.24
  50.5 1.0 copy.26
  51.5 4.7 %collective-permute-start.2 = (bf16[8,144,128]{2,1,0:T(8,128)(2,1)S(1)}, bf16[8,144,128]{2,1,0:T(8,128)(2,1)S(1)}, u32[]{:S(2)}, u32[]{:S(2)}) collective-permute-start(bf16[8,144,128]{2,1,0:T(8,128)(2,1)S(1)} %all-to-all-done.own), channel_id=1, source_target_pairs={{0,8},{8,0},{1,9},{9,1},{2,10},{10,2},{3,11},{11,3},{4,12},{12,4},... | collective-permute-start | bytes 884744 | tf_op jit(solution)/shard_map/ppermute | solution.py:24
  56.2 1.9 %collective-permute-start.3 = (bf16[8,144,128]{2,1,0:T(8,128)(2,1)S(1)}, bf16[8,144,128]{2,1,0:T(8,128)(2,1)S(1)}, u32[]{:S(2)}, u32[]{:S(2)}) collective-permute-start(bf16[8,144,128]{2,1,0:T(8,128)(2,1)S(1)} %all-to-all-done.own), channel_id=1, source_target_pairs={{0,16},{16,0},{1,17},{17,1},{2,18},{18,2},{3,19},{19,3},{4,20},{20... | collective-permute-start | bytes 884744 | tf_op jit(solution)/shard_map/ppermute | solution.py:24
  58.1 5.8 %collective-permute-done.2.across = bf16[8,144,128]{2,1,0:T(8,128)(2,1)S(1)} collective-permute-done((bf16[8,144,128]{2,1,0:T(8,128)(2,1)S(1)}, bf16[8,144,128]{2,1,0:T(8,128)(2,1)S(1)}, u32[]{:S(2)}, u32[]{:S(2)}) %collective-permute-start.2) | collective-permute-done | bytes 294944 | tf_op jit(solution)/shard_map/ppermute | solution.py:24
  63.9 2.3 %collective-permute-start.4 = (bf16[8,144,128]{2,1,0:T(8,128)(2,1)S(1)}, bf16[8,144,128]{2,1,0:T(8,128)(2,1)S(1)}, u32[]{:S(2)}, u32[]{:S(2)}) collective-permute-start(bf16[8,144,128]{2,1,0:T(8,128)(2,1)S(1)} %collective-permute-done.2.across), channel_id=1, source_target_pairs={{0,16},{16,0},{1,17},{17,1},{2,18},{18,2},{3,19},{19,3},{4,20},{20... | collective-permute-start | bytes 884744 | tf_op jit(solution)/shard_map/ppermute | solution.py:24
  66.6 0.9 collective-permute-done.4.far
  67.5 1.5 copy-done.1
  69.0 5.1 %conv.1 = (f32[512,256]{1,0:T(8,128)S(1)}, f32[128,4,128]{2,1,0:T(4,128)S(1)}, f32[8,256]{1,0:T(8,128)S(1)}, bf16[256,512]{1,0:T(8,128)(2,1)S(1)}) custom-call(s32[2]{0:T(128)S(1)} %pad_add_fusion.place, bf16[8,144,128]{2,1,0:T(8,128)(2,1)S(1)} %all-to-all-done.own, bf16[8,144,128]{2,1,0:T(8,128)(2,1)S(1)} %collective-permute-done.2.across, ...), custom_call_target="tpu_custom_call" | custom-call | tf_op jit(solution)/shard_map/conv/pallas_call | solution.py:270
  74.1 24.2 %all_to_all.15.stats = f32[128,4,128]{2,1,0:T(4,128)S(1)} all-to-all(f32[128,4,128]{2,1,0:T(4,128)S(1)} %get-tuple-element.17), channel_id=1, replica_groups=mesh['xlo'=2,'y'=8,'core'=2,'xhi'=2,'z'=8] {'xlo','y','z'}, dimensions={0} | all-to-all | bytes 524288 | tf_op jit(solution)/shard_map/all_to_all | solution.py:296
  98.7 4.4 %collective-permute-start.5 = (bf16[256,512]{1,0:T(8,128)(2,1)S(1)}, bf16[256,512]{1,0:T(8,128)(2,1)S(1)}, u32[]{:S(2)}, u32[]{:S(2)}) collective-permute-start(bf16[256,512]{1,0:T(8,128)(2,1)S(1)} %bn.1.own), channel_id=1, source_target_pairs={{0,8},{8,0},{1,9},{9,1},{2,10},{10,2},{3,11},{11,3},{4,12},{12,4},... | collective-permute-start | bytes 786440 | tf_op jit(solution)/shard_map/ppermute | solution.py:24
  103.1 4.8 %collective-permute-start.6 = (bf16[256,512]{1,0:T(8,128)(2,1)S(1)}, bf16[256,512]{1,0:T(8,128)(2,1)S(1)}, u32[]{:S(2)}, u32[]{:S(2)}) collective-permute-start(bf16[256,512]{1,0:T(8,128)(2,1)S(1)} %bn.1.own), channel_id=1, source_target_pairs={{0,16},{16,0},{1,17},{17,1},{2,18},{18,2},{3,19},{19,3},{4,20},{20... | collective-permute-start | bytes 786440 | tf_op jit(solution)/shard_map/ppermute | solution.py:24
  108.0 5.1 %collective-permute-start.7 = (bf16[256,512]{1,0:T(8,128)(2,1)S(1)}, bf16[256,512]{1,0:T(8,128)(2,1)S(1)}, u32[]{:S(2)}, u32[]{:S(2)}) collective-permute-start(bf16[256,512]{1,0:T(8,128)(2,1)S(1)} %collective-permute-done.5.across), channel_id=1, source_target_pairs={{0,16},{16,0},{1,17},{17,1},{2,18},{18,2},{3,19},{19,3},{4,20},{20... | collective-permute-start | bytes 786440 | tf_op jit(solution)/shard_map/ppermute | solution.py:24
  113.1 1.1 collective-permute-done.7.far
  114.2 1.0 mix.1.own
  115.3 4.4 %collective-permute-start.8 = (bf16[256,512]{1,0:T(8,128)(2,1)S(1)}, bf16[256,512]{1,0:T(8,128)(2,1)S(1)}, u32[]{:S(2)}, u32[]{:S(2)}) collective-permute-start(bf16[256,512]{1,0:T(8,128)(2,1)S(1)} %mix.1.own), channel_id=1, source_target_pairs={{0,8},{8,0},{1,9},{9,1},{2,10},{10,2},{3,11},{11,3},{4,12},{12,4},... | collective-permute-start | bytes 786440 | tf_op jit(solution)/shard_map/ppermute | solution.py:24
  119.6 2.6 %collective-permute-start.9 = (bf16[256,512]{1,0:T(8,128)(2,1)S(1)}, bf16[256,512]{1,0:T(8,128)(2,1)S(1)}, u32[]{:S(2)}, u32[]{:S(2)}) collective-permute-start(bf16[256,512]{1,0:T(8,128)(2,1)S(1)} %mix.1.own), channel_id=1, source_target_pairs={{0,16},{16,0},{1,17},{17,1},{2,18},{18,2},{3,19},{19,3},{4,20},{20... | collective-permute-start | bytes 786440 | tf_op jit(solution)/shard_map/ppermute | solution.py:24
  122.2 4.0 %collective-permute-done.8.across = bf16[256,512]{1,0:T(8,128)(2,1)S(1)} collective-permute-done((bf16[256,512]{1,0:T(8,128)(2,1)S(1)}, bf16[256,512]{1,0:T(8,128)(2,1)S(1)}, u32[]{:S(2)}, u32[]{:S(2)}) %collective-permute-start.8) | collective-permute-done | bytes 262176 | tf_op jit(solution)/shard_map/ppermute | solution.py:24
  126.2 3.3 %collective-permute-start.10 = (bf16[256,512]{1,0:T(8,128)(2,1)S(1)}, bf16[256,512]{1,0:T(8,128)(2,1)S(1)}, u32[]{:S(2)}, u32[]{:S(2)}) collective-permute-start(bf16[256,512]{1,0:T(8,128)(2,1)S(1)} %collective-permute-done.8.across), channel_id=1, source_target_pairs={{0,16},{16,0},{1,17},{17,1},{2,18},{18,2},{3,19},{19,3},{4,20},{20... | collective-permute-start | bytes 786440 | tf_op jit(solution)/shard_map/ppermute | solution.py:24
  130.4 2.2 %copy-done.3 = bf16[128,128,128]{2,1,0:T(8,128)(2,1)S(1)} copy-done((bf16[128,128,128]{2,1,0:T(8,128)(2,1)S(1)}, bf16[128,128,128]{2,1,0:T(8,128)(2,1)}, u32[]{:S(2)}) %copy-start.3) | copy-done | bytes 4194328
  132.6 4.8 %ff.1 = (f32[1024,256]{1,0:T(8,128)S(1)}, bf16[1024,256]{1,0:T(8,128)(2,1)}, bf16[512,256]{1,0:T(8,128)(2,1)S(1)}) custom-call(s32[2]{0:T(128)S(1)} %pad_add_fusion.place, bf16[256,512]{1,0:T(8,128)(2,1)S(1)} %mix.1.own, bf16[256,512]{1,0:T(8,128)(2,1)S(1)} %collective-permute-done.8.across, bf16[256,512]{1,0:T(8,128)(2,1)S(1)} %collective-permute-done.9.beside, ...), custom_call_target="tpu_custom_call" | custom-call | tf_op jit(solution)/shard_map/ff/pallas_call | solution.py:317
  137.4 2.3 %collective-permute-start.11 = (bf16[1024,256]{1,0:T(8,128)(2,1)}, bf16[1024,256]{1,0:T(8,128)(2,1)S(1)}, u32[]{:S(2)}, u32[]{:S(2)}) collective-permute-start(bf16[1024,256]{1,0:T(8,128)(2,1)} %get-tuple-element.24), channel_id=1, source_target_pairs={{0,16},{16,0},{1,17},{17,1},{2,18},{18,2},{3,19},{19,3},{4,20},{20... | collective-permute-start | bytes 1572872 | tf_op jit(solution)/shard_map/ppermute | solution.py:24
  139.7 1.7 collective-permute-done.11
  141.5 4.4 %collective-permute-start.12 = (bf16[512,256]{1,0:T(8,128)(2,1)S(1)}, bf16[512,256]{1,0:T(8,128)(2,1)S(1)}, u32[]{:S(2)}, u32[]{:S(2)}) collective-permute-start(bf16[512,256]{1,0:T(8,128)(2,1)S(1)} %add_convert_fusion.1), channel_id=1, source_target_pairs={{0,8},{8,0},{1,9},{9,1},{2,10},{10,2},{3,11},{11,3},{4,12},{12,4},... | collective-permute-start | bytes 786440 | tf_op jit(solution)/shard_map/ppermute | solution.py:24
  145.8 6.5 %collective-permute-done.12 = bf16[512,256]{1,0:T(8,128)(2,1)S(1)} collective-permute-done((bf16[512,256]{1,0:T(8,128)(2,1)S(1)}, bf16[512,256]{1,0:T(8,128)(2,1)S(1)}, u32[]{:S(2)}, u32[]{:S(2)}) %collective-permute-start.12) | collective-permute-done | bytes 262176 | tf_op jit(solution)/shard_map/ppermute | solution.py:24
  152.5 13.0 %all_to_all.16 = bf16[8,64,256]{2,1,0:T(8,128)(2,1)S(1)} all-to-all(bf16[8,64,256]{2,1,0:T(8,128)(2,1)S(1)} %bitcast.36), channel_id=1, replica_groups=mesh['xlo'=2,'y'=8,'core'=2,'xhi'=2,'z'=8] {'z'}, dimensions={0} | all-to-all | bytes 524288 | tf_op jit(solution)/shard_map/all_to_all | solution.py:345
  (51 shorter events, 9.4 us)
Async XLA Ops:
  6.5 43.9 %copy-start = (bf16[1024,256]{1,0:T(8,128)(2,1)S(1)}, bf16[1024,256]{1,0:T(8,128)(2,1)}, u32[]{:S(2)}) copy-start(bf16[1024,256]{1,0:T(8,128)(2,1)} %param.18) | copy-start | bytes 1572868
  6.5 59.7 %copy-start.5 = (f32[1024]{0:T(1024)S(1)}, f32[1024]{0:T(1024)}, u32[]{:S(2)}) copy-start(f32[1024]{0:T(1024)} %param.11) | copy-start | bytes 12292
  6.5 60.9 %all-gather.5.cloned.1.call-start = ((), (), s32[]{:S(2)}) async-start(), calls=%async_computation.3 | async-start | bytes 2064384 | tf_op jit(solution)/shard_map/all_gather | solution.py:244
  12.3 10.1 %collective-permute-start = (bf16[64,128]{1,0:T(8,128)(2,1)S(1)}, bf16[64,128]{1,0:T(8,128)(2,1)S(1)}, u32[]{:S(2)}, u32[]{:S(2)}) collective-permute-start(bf16[64,128]{1,0:T(8,128)(2,1)S(1)} %get-tuple-element.26), channel_id=1, source_target_pairs={{0,16},{16,32},{32,48},{48,64},{64,80},{80,96},{96,112},{112,128},... | collective-permute-start | bytes 49160 | tf_op jit(solution)/shard_map/ppermute | solution.py:249
  16.9 6.3 %collective-permute-start.1 = (bf16[64,128]{1,0:T(8,128)(2,1)S(1)}, bf16[64,128]{1,0:T(8,128)(2,1)S(1)}, u32[]{:S(2)}, u32[]{:S(2)}) collective-permute-start(bf16[64,128]{1,0:T(8,128)(2,1)S(1)} %get-tuple-element.25), channel_id=1, source_target_pairs={{16,0},{32,16},{48,32},{64,48},{80,64},{96,80},{112,96},{128,112},... | collective-permute-start | bytes 49160 | tf_op jit(solution)/shard_map/ppermute | solution.py:250
  23.2 0.9 copy-start.4
  25.0 23.9 %all-to-all-start = ((bf16[8,144,128]{2,1,0:T(8,128)(2,1)}), bf16[8,144,128]{2,1,0:T(8,128)(2,1)S(1)}, u32[]{:S(2)}, u32[]{:S(2)}) async-start(bf16[8,144,128]{2,1,0:T(8,128)(2,1)} %pack.1), calls=%async_computation | async-start | bytes 589824 | tf_op jit(solution)/shard_map/all_to_all | solution.py:259
  33.8 96.6 %all-gather.7.cloned.1.call-start = ((), (), s32[]{:S(2)}) async-start(), calls=%async_computation.4 | async-start | bytes 4718592 | tf_op jit(solution)/shard_map/all_gather | solution.py:266
  51.5 12.4 %collective-permute-start.2 = (bf16[8,144,128]{2,1,0:T(8,128)(2,1)S(1)}, bf16[8,144,128]{2,1,0:T(8,128)(2,1)S(1)}, u32[]{:S(2)}, u32[]{:S(2)}) collective-permute-start(bf16[8,144,128]{2,1,0:T(8,128)(2,1)S(1)} %all-to-all-done.own), channel_id=1, source_target_pairs={{0,8},{8,0},{1,9},{9,1},{2,10},{10,2},{3,11},{11,3},{4,12},{12,4},... | collective-permute-start | bytes 884744 | tf_op jit(solution)/shard_map/ppermute | solution.py:24
  56.2 10.4 %collective-permute-start.3 = (bf16[8,144,128]{2,1,0:T(8,128)(2,1)S(1)}, bf16[8,144,128]{2,1,0:T(8,128)(2,1)S(1)}, u32[]{:S(2)}, u32[]{:S(2)}) collective-permute-start(bf16[8,144,128]{2,1,0:T(8,128)(2,1)S(1)} %all-to-all-done.own), channel_id=1, source_target_pairs={{0,16},{16,0},{1,17},{17,1},{2,18},{18,2},{3,19},{19,3},{4,20},{20... | collective-permute-start | bytes 884744 | tf_op jit(solution)/shard_map/ppermute | solution.py:24
  63.9 3.5 %collective-permute-start.4 = (bf16[8,144,128]{2,1,0:T(8,128)(2,1)S(1)}, bf16[8,144,128]{2,1,0:T(8,128)(2,1)S(1)}, u32[]{:S(2)}, u32[]{:S(2)}) collective-permute-start(bf16[8,144,128]{2,1,0:T(8,128)(2,1)S(1)} %collective-permute-done.2.across), channel_id=1, source_target_pairs={{0,16},{16,0},{1,17},{17,1},{2,18},{18,2},{3,19},{19,3},{4,20},{20... | collective-permute-start | bytes 884744 | tf_op jit(solution)/shard_map/ppermute | solution.py:24
  67.5 1.5 copy-start.1
  69.0 45.3 %copy-start.2 = (bf16[896,1024]{1,0:T(8,128)(2,1)S(1)}, bf16[896,1024]{1,0:T(8,128)(2,1)}, u32[]{:S(2)}) copy-start(bf16[896,1024]{1,0:T(8,128)(2,1)} %all-gather.5.cloned.1.call-done) | copy-start | bytes 5505028
  69.0 60.5 %copy-start.6 = (f32[1024]{0:T(1024)S(1)}, f32[1024]{0:T(1024)}, u32[]{:S(2)}) copy-start(f32[1024]{0:T(1024)} %param.17) | copy-start | bytes 12292
  98.7 9.3 %collective-permute-start.5 = (bf16[256,512]{1,0:T(8,128)(2,1)S(1)}, bf16[256,512]{1,0:T(8,128)(2,1)S(1)}, u32[]{:S(2)}, u32[]{:S(2)}) collective-permute-start(bf16[256,512]{1,0:T(8,128)(2,1)S(1)} %bn.1.own), channel_id=1, source_target_pairs={{0,8},{8,0},{1,9},{9,1},{2,10},{10,2},{3,11},{11,3},{4,12},{12,4},... | collective-permute-start | bytes 786440 | tf_op jit(solution)/shard_map/ppermute | solution.py:24
  103.1 9.9 %collective-permute-start.6 = (bf16[256,512]{1,0:T(8,128)(2,1)S(1)}, bf16[256,512]{1,0:T(8,128)(2,1)S(1)}, u32[]{:S(2)}, u32[]{:S(2)}) collective-permute-start(bf16[256,512]{1,0:T(8,128)(2,1)S(1)} %bn.1.own), channel_id=1, source_target_pairs={{0,16},{16,0},{1,17},{17,1},{2,18},{18,2},{3,19},{19,3},{4,20},{20... | collective-permute-start | bytes 786440 | tf_op jit(solution)/shard_map/ppermute | solution.py:24
  108.0 6.2 %collective-permute-start.7 = (bf16[256,512]{1,0:T(8,128)(2,1)S(1)}, bf16[256,512]{1,0:T(8,128)(2,1)S(1)}, u32[]{:S(2)}, u32[]{:S(2)}) collective-permute-start(bf16[256,512]{1,0:T(8,128)(2,1)S(1)} %collective-permute-done.5.across), channel_id=1, source_target_pairs={{0,16},{16,0},{1,17},{17,1},{2,18},{18,2},{3,19},{19,3},{4,20},{20... | collective-permute-start | bytes 786440 | tf_op jit(solution)/shard_map/ppermute | solution.py:24
  115.3 10.9 %collective-permute-start.8 = (bf16[256,512]{1,0:T(8,128)(2,1)S(1)}, bf16[256,512]{1,0:T(8,128)(2,1)S(1)}, u32[]{:S(2)}, u32[]{:S(2)}) collective-permute-start(bf16[256,512]{1,0:T(8,128)(2,1)S(1)} %mix.1.own), channel_id=1, source_target_pairs={{0,8},{8,0},{1,9},{9,1},{2,10},{10,2},{3,11},{11,3},{4,12},{12,4},... | collective-permute-start | bytes 786440 | tf_op jit(solution)/shard_map/ppermute | solution.py:24
  119.6 10.1 %collective-permute-start.9 = (bf16[256,512]{1,0:T(8,128)(2,1)S(1)}, bf16[256,512]{1,0:T(8,128)(2,1)S(1)}, u32[]{:S(2)}, u32[]{:S(2)}) collective-permute-start(bf16[256,512]{1,0:T(8,128)(2,1)S(1)} %mix.1.own), channel_id=1, source_target_pairs={{0,16},{16,0},{1,17},{17,1},{2,18},{18,2},{3,19},{19,3},{4,20},{20... | collective-permute-start | bytes 786440 | tf_op jit(solution)/shard_map/ppermute | solution.py:24
  126.2 4.3 %collective-permute-start.10 = (bf16[256,512]{1,0:T(8,128)(2,1)S(1)}, bf16[256,512]{1,0:T(8,128)(2,1)S(1)}, u32[]{:S(2)}, u32[]{:S(2)}) collective-permute-start(bf16[256,512]{1,0:T(8,128)(2,1)S(1)} %collective-permute-done.8.across), channel_id=1, source_target_pairs={{0,16},{16,0},{1,17},{17,1},{2,18},{18,2},{3,19},{19,3},{4,20},{20... | collective-permute-start | bytes 786440 | tf_op jit(solution)/shard_map/ppermute | solution.py:24
  130.4 2.2 %copy-start.3 = (bf16[128,128,128]{2,1,0:T(8,128)(2,1)S(1)}, bf16[128,128,128]{2,1,0:T(8,128)(2,1)}, u32[]{:S(2)}) copy-start(bf16[128,128,128]{2,1,0:T(8,128)(2,1)} %all-gather.7.cloned.1.call-done) | copy-start | bytes 12582916
  137.4 4.0 %collective-permute-start.11 = (bf16[1024,256]{1,0:T(8,128)(2,1)}, bf16[1024,256]{1,0:T(8,128)(2,1)S(1)}, u32[]{:S(2)}, u32[]{:S(2)}) collective-permute-start(bf16[1024,256]{1,0:T(8,128)(2,1)} %get-tuple-element.24), channel_id=1, source_target_pairs={{0,16},{16,0},{1,17},{17,1},{2,18},{18,2},{3,19},{19,3},{4,20},{20... | collective-permute-start | bytes 1572872 | tf_op jit(solution)/shard_map/ppermute | solution.py:24
  141.5 10.9 %collective-permute-start.12 = (bf16[512,256]{1,0:T(8,128)(2,1)S(1)}, bf16[512,256]{1,0:T(8,128)(2,1)S(1)}, u32[]{:S(2)}, u32[]{:S(2)}) collective-permute-start(bf16[512,256]{1,0:T(8,128)(2,1)S(1)} %add_convert_fusion.1), channel_id=1, source_target_pairs={{0,8},{8,0},{1,9},{9,1},{2,10},{10,2},{3,11},{11,3},{4,12},{12,4},... | collective-permute-start | bytes 786440 | tf_op jit(solution)/shard_map/ppermute | solution.py:24
Sparse Core Ops, SparseCore 0:
  11.7 50.3 all-gather.4
  64.1 65.0 all-gather.6

commit v3 on v2

--- a/solution.py
+++ b/solution.py
@@ -30,13 +30,6 @@
     return x, across, beside, swap(across, CORE)
 
 
-def split3(x):
-    hi = x.astype(BF)
-    rest = x - hi.astype(F32)
-    mid = rest.astype(BF)
-    return hi, mid, (rest - mid.astype(F32)).astype(BF)
-
-
 def norm_rows(x, gain):
     inv = 1.0 / x.shape[0]
     centred = x - jnp.sum(x, axis=0, keepdims=True) * inv
@@ -46,6 +39,41 @@
 
 def at(start, size, step):
     return pl.ds(pl.multiple_of(start, step), size)
+
+
+def weight_kernel(place, glu, depth, gain, shift, out, table):
+    core = place[0]
+    lane = lax.broadcasted_iota(jnp.int32, table.shape, 1)
+    table[...] = jnp.zeros_like(table)
+    width, taps = depth.shape[1], depth.shape[0]
+    table[0:taps, 0:width] = depth[...]
+    table[taps : taps + 1, 0:width] = gain[...]
+    table[taps + 1 : taps + 2, 0:width] = shift[...]
+    rest = jnp.where(core == 0, table[...], pltpu.roll(table[...], LANES - 32, 1))
+    rest = jnp.where(lane < 32, rest, 0.0)
+    packed = jnp.zeros_like(rest)
+    for i in range(3):
+        piece = rest.astype(BF).astype(F32)
+        packed = packed + (piece if i == 0 else pltpu.roll(piece, 32 * i, 1))
+        rest = rest - piece
+    nz = out.shape[0]
+    for k in range(8):
+        for v in range(2):
+            tile = glu[v, at(32 * core, 32, 32), LANES * k : LANES * (k + 1)]
+            for z in range(nz):
+                out[z, 64 * k + 32 * v : 64 * k + 32 * v + 32] = tile
+    for z in range(nz):
+        out[z, 512:560] = packed.astype(BF)
+
+
+def block_kernel(place, ff_in, ff_out, conv_out, out):
+    half = at(place[0] * LANES, LANES, LANES)
+    for k in range(8):
+        tile = slice(LANES * k, LANES * (k + 1))
+        out[k] = ff_in[tile, half].astype(F32).T.astype(BF)
+        out[8 + k] = ff_out[half, tile].astype(F32).T.astype(BF)
+        rows = slice(32 * (k % 4), 32 * (k % 4) + 32)
+        out[16 + k // 4, rows, :] = conv_out[at(place[0] * 32, 32, 32), tile]
 
 
 def pack_kernel(tok, left, right, out):
@@ -75,9 +103,9 @@
 
 
 def conv_kernel(
-    place, own, across, beside, far, glu, small, gain,
+    place, own, across, beside, far, glu, gain,
     conv, stats, par, res,
-    tok, edge, win, taps,
+    tok, edge, win, weight,
 ):
     core, xhi = place[0], place[1]
     lane = lax.broadcasted_iota(jnp.int32, (16, LANES), 1)
@@ -99,22 +127,25 @@
         row = xhi * (64 * nz) + 64 * z + 32 * core
         res[32 * z : 32 * z + 32, :] = tok[at(row, 32, 32), :]
 
+    table = []
+    lane = lax.broadcasted_iota(jnp.int32, (48, LANES), 1)
+    for h in range(2):
+        total = jnp.zeros((48, LANES), F32)
+        for i in range(4):
+            x = glu[4 * h + i, 512:560].astype(F32)
+            x = x + (pltpu.roll(x, LANES - 32, 1) + pltpu.roll(x, LANES - 64, 1))
+            x = jnp.where(lane < 32, x, 0.0)
+            total = total + (x if i == 0 else pltpu.roll(x, 32 * i, 1))
+        par[:, LANES * h : LANES * (h + 1)] = total[31:39]
+        table.append(total)
     for z in range(nz):
-        s = small[z].astype(F32)
-        for i in range(2):
-            hi = s[:, LANES * i : LANES * (i + 1)]
-            mid = s[:, LANES * (2 + i) : LANES * (3 + i)]
-            low = s[:, LANES * (4 + i) : LANES * (5 + i)]
-            taps[32 * z + 16 * i : 32 * z + 16 * i + 16, :] = hi + (mid + low)
-    table = [taps[0:128, :].T, taps[128:256, :].T]
-    for h in range(2):
-        par[:, LANES * h : LANES * (h + 1)] = table[h][31:39]
-
-    weight = glu[...].reshape(glu.shape[0] * glu.shape[1], glu.shape[2])
+        for k in range(8):
+            weight[64 * z : 64 * z + 64, LANES * k : LANES * (k + 1)] = glu[z, 64 * k : 64 * k + 64]
+
     scale = gain[...]
     for c in range(3):
         x = edge[...] if c == 2 else tok[:, 256 * c : 256 * (c + 1)].astype(F32)
-        paired = jnp.dot(weight, norm_rows(x, scale), preferred_element_type=F32)
+        paired = jnp.dot(weight[...], norm_rows(x, scale), preferred_element_type=F32)
         cols = x.shape[1]
         paired = paired.reshape(nz, 2, 32, cols)
         gated = (paired[:, 0] * jax.nn.sigmoid(paired[:, 1])).astype(BF).astype(F32)
@@ -175,23 +206,25 @@
             whole[at(row, 32, 32), half:] = blk[32 * z : 32 * z + 32, :half]
 
 
-def mix_kernel(place, own, across, beside, far, weight, res, out, whole):
+def mix_kernel(place, own, across, beside, far, blocks, res, out, whole, weight):
     place_blocks(place, own, across, beside, far, whole)
-    w = weight[...].reshape(256, weight.shape[2])
-    mixed = jnp.dot(w, whole[...], preferred_element_type=F32)
+    for z in range(8):
+        for k in range(8):
+            rows = slice(32 * (k % 4), 32 * (k % 4) + 32)
+            weight[32 * z : 32 * z + 32, LANES * k : LANES * (k + 1)] = blocks[z, k // 4, rows, :]
+    mixed = jnp.dot(weight[...], whole[...], preferred_element_type=F32)
     out[...] = (res[...].astype(F32) + mixed).astype(BF)
 
 
 def ff_kernel(
     place, own, across, beside, far, weights, gain,
-    keep, give, res,
+    keep, give,
     whole, normed, hidden, w, sem,
 ):
-    copy = pltpu.make_async_copy(weights, w, sem)
+    copy = pltpu.make_async_copy(weights.at[:, 0:16], w, sem)
     copy.start()
     place_blocks(place, own, across, beside, far, whole)
     half = 256
-    res[...] = whole[at(place[1] * 512, 512, 512), :half]
     for c in range(2):
         cols = slice(half * c, half * (c + 1))
         normed[:, cols] = norm_rows(whole[:, cols].astype(F32), gain[...])
@@ -207,8 +240,10 @@
         value = jnp.dot(
             jnp.concatenate(rows, axis=0), hidden[...], preferred_element_type=F32
         )
-        keep[LANES * k : LANES * (k + 2), :] = value[:, :half]
-        give[LANES * k : LANES * (k + 2), :] = value[:, half:].astype(BF)
+        rows = slice(LANES * k, LANES * (k + 2))
+        mine = jnp.where(place[1] == k // 4, 1.0, 0.0)
+        keep[rows, :] = 0.5 * value[:, :half] + mine * whole[rows, :half].astype(F32)
+        give[rows, :] = (0.5 * value[:, half:]).astype(BF)
 
 
 def body(
@@ -228,26 +263,22 @@
     nz = lax.axis_size(Z)
     frames, width = tokens.shape
     full = ln_conv_gain.shape[0]
-    half = width // 2
     run = frames // nz
-
-    def mine(x, axis, size):
-        return lax.dynamic_slice_in_dim(x, core * size, size, axis=axis)
-
-    glu = mine(glu_weight.transpose(1, 2, 0), 1, half).reshape(2 * half, full)
-    conv_out = mine(conv_out_weight.T, 0, half)
-    small = jnp.concatenate([depth_weight, bn_gain[None], bn_shift[None]], axis=0)
-    small = mine(small.T, 0, half)
-    small = jnp.pad(small, ((0, 0), (0, LANES - small.shape[1])))
-    small = [p[16 * i : 16 * i + 16] for p in split3(small) for i in range(2)]
-    small = jnp.pad(jnp.concatenate(small, axis=1), ((0, 0), (0, full - 6 * LANES)))
-    first = lax.all_gather(jnp.concatenate([glu, conv_out, small], axis=0), Z)
 
     tok = tokens.T
     tm = lax.axis_size((XLO, Y, CORE))
     up = [(i, i + 1) for i in range(tm - 1)]
     left = lax.ppermute(tok[:, frames - LANES :], (XLO, Y, CORE), up)
     right = lax.ppermute(tok[:, :LANES], (XLO, Y, CORE), [(j, i) for i, j in up])
+    glu = pl.pallas_call(
+        weight_kernel,
+        out_shape=shape((nz, 560, LANES), BF),
+        in_specs=[SMEM] + [VMEM] * 4,
+        out_specs=VMEM,
+        scratch_shapes=[pltpu.VMEM((48, LANES), F32)],
+        compiler_params=PARAMS,
+        name="weights",
+    )(place, glu_weight.transpose(1, 2, 0), depth_weight, bn_gain[None], bn_shift[None])
     parts = pl.pallas_call(
         pack_kernel,
         out_shape=shape((nz, 144, LANES), BF),
@@ -256,14 +287,20 @@
         compiler_params=PARAMS,
         name="pack",
     )(tok, left, right)
+    parts, glu = lax.optimization_barrier((parts, glu))
     parts = lax.all_to_all(parts, Z, 0, 0, tiled=True)
-
-    ff_in_weight, ff_out_weight, parts = lax.optimization_barrier(
-        (ff_in_weight, ff_out_weight, parts)
-    )
-    ff_in = mine(ff_in_weight, 1, LANES).reshape(8, LANES, LANES).transpose(0, 2, 1)
-    ff_out = mine(ff_out_weight, 0, LANES).reshape(LANES, 8, LANES).transpose(1, 2, 0)
-    second = lax.all_gather(jnp.concatenate([ff_in, ff_out], axis=0), Z)
+    glu = lax.all_to_all(glu, Z, 0, 0, tiled=True)
+
+    blocks = pl.pallas_call(
+        block_kernel,
+        out_shape=shape((18, LANES, LANES), BF),
+        in_specs=[SMEM] + [VMEM] * 3,
+        out_specs=VMEM,
+        compiler_params=PARAMS,
+        name="blocks",
+    )(place, ff_in_weight, ff_out_weight, conv_out_weight.T)
+    blocks, parts = lax.optimization_barrier((blocks, parts))
+    blocks = lax.all_gather(blocks, Z)
 
     whole = group_gather(parts)
     peers = lax.axis_size((XLO, Y, Z))
@@ -275,24 +312,17 @@
             shape((8, 256), F32),
             shape((256, 2 * run), BF),
         ),
-        grid=(1,),
-        in_specs=[SMEM]
-        + [VMEM] * 4
-        + [
-            pl.BlockSpec((nz, 64, full), lambda i: (0, 0, 0)),
-            pl.BlockSpec((nz, 16, full), lambda i: (0, 6, 0)),
-            VMEM,
-        ],
+        in_specs=[SMEM] + [VMEM] * 6,
         out_specs=(VMEM,) * 4,
         scratch_shapes=[
             pltpu.VMEM((full, 2 * run), BF),
             pltpu.VMEM((full, LANES), F32),
             pltpu.VMEM((2, run + 40, 256), F32),
-            pltpu.VMEM((256, LANES), F32),
+            pltpu.VMEM((512, full), BF),
         ],
         compiler_params=PARAMS,
         name="conv",
-    )(place, *whole, first, first, ln_conv_gain[:, None])
+    )(place, *whole, glu, ln_conv_gain[:, None])
     stats = lax.all_to_all(stats, (XLO, Y, Z), 0, 0, tiled=True)
     activated = pl.pallas_call(
         bn_kernel,
@@ -308,21 +338,17 @@
         grid=(1,),
         in_specs=[SMEM]
         + [VMEM] * 4
-        + [pl.BlockSpec((nz, 32, full), lambda i: (0, 2, 0)), VMEM],
-        out_specs=VMEM,
-        scratch_shapes=[pltpu.VMEM((full, 2 * run), BF)],
+        + [pl.BlockSpec((nz, 2, LANES, LANES), lambda i: (0, 8, 0, 0)), VMEM],
+        out_specs=VMEM,
+        scratch_shapes=[pltpu.VMEM((full, 2 * run), BF), pltpu.VMEM((256, full), BF)],
         compiler_params=PARAMS,
         name="mix",
-    )(place, *group_gather(activated), first, res)
-    keep, give, res = pl.pallas_call(
+    )(place, *group_gather(activated), blocks, res)
+    keep, give = pl.pallas_call(
         ff_kernel,
-        out_shape=(
-            shape((full, run), F32),
-            shape((full, run), BF),
-            shape((full // 2, run), BF),
-        ),
+        out_shape=(shape((full, run), F32), shape((full, run), BF)),
         in_specs=[SMEM] + [VMEM] * 4 + [ANY, VMEM],
-        out_specs=(VMEM,) * 3,
+        out_specs=(VMEM,) * 2,
         scratch_shapes=[
             pltpu.VMEM((full, 2 * run), BF),
             pltpu.VMEM((full, 2 * run), BF),
@@ -330,19 +356,12 @@
             pltpu.VMEM((8, 16, LANES, LANES), BF),
             pltpu.SemaphoreType.DMA,
         ],
-        compiler_params=PARAMS,
+        compiler_params=pltpu.CompilerParams(vmem_limit_bytes=58 << 20),
         name="ff",
-    )(place, *group_gather(block), second, ln_ff_gain[:, None])
-    other = swap(give, CORE)
-    size = full // 2
-
-    def part(x, index):
-        return lax.dynamic_slice_in_dim(x, index * size, size, axis=0).astype(F32)
-
-    give = (part(keep, 1 - xhi) + part(other, 1 - xhi)).astype(BF)
-    keep = part(keep, xhi) + part(other, xhi) + swap(give, XHI).astype(F32)
-    out = (res.astype(F32) + 0.5 * keep).astype(BF)
-    out = lax.all_to_all(out.reshape(nz, width, run), Z, 0, 0, tiled=True)
+    )(place, *group_gather(block), blocks, ln_ff_gain[:, None])
+    keep = (keep + swap(give, CORE).astype(F32)).astype(BF)
+    keep = lax.all_to_all(keep.reshape(2 * nz, width, run), (XHI, Z), 0, 0, tiled=True)
+    out = (keep[:nz].astype(F32) + keep[nz:].astype(F32)).astype(BF)
     return out.transpose(1, 0, 2).reshape(width, frames).T
 
 

time: 175 us -> 194 us (1.11)
  waiting for transfers between devices: 36.7 us -> 47.8 us
  blocking collectives: 37.1 us -> 46.6 us
  Pallas kernels: 12.2 us -> 17.8 us
  local copies, waits for them, and re-layouts: 13.2 us -> 9.49 us
  starting transfers between devices: 59 us -> 55.5 us
    all_to_all x0 -> x1, waiting for transfers between devices: none -> 24.2 us  [body(): glu = lax.all_to_all(glu, Z, 0, 0, tiled=True)]
    ppermute x11 -> x10, waiting for transfers between devices: 20.7 us -> 13.7 us  [swap(): return lax.ppermute(x, axis, [(0, 1), (1, 0)])]
    all_to_all x1, blocking collectives: 13 us -> 19.2 us  [body(): lax.all_to_all(keep.reshape(2 * nz, width, run), (XHI, Z), 0, 0, tiled=True)]
    all_to_all x1, waiting for transfers between devices: 15.1 us -> 9.94 us  [body(): parts = lax.all_to_all(parts, Z, 0, 0, tiled=True)]
    ppermute x11 -> x10, starting transfers between devices: 40.1 us -> 35.3 us  [swap(): return lax.ppermute(x, axis, [(0, 1), (1, 0)])]
    all_to_all x0 -> x1, starting transfers between devices: none -> 3.57 us  [body(): glu = lax.all_to_all(glu, Z, 0, 0, tiled=True)]
    pallas_call x0 -> x2, Pallas kernels: none -> 3.35 us  [the longest x1 1.77 us: body(): pl.pallas_call(weight_kernel, out_shape=shape((nz, 560, LANES), BF), in_s...]
    all_to_all x1, blocking collectives: 24.2 us -> 27.4 us  [body(): stats = lax.all_to_all(stats, (XLO, Y, Z), 0, 0, tiled=True)]
  transfers between devices with their start and end apart: 16 -> 15, of which waited for: 9 -> 7; matrix products, arithmetic and copies ran while one was open for 2% -> 1% of each run, Pallas kernels for 4% -> 5%
where the time goes in v3:
time: 194 us; the launch traced here: 192 us
  starting transfers between devices  55.5 us (29%)
  waiting for transfers between devices  47.8 us (25%)
  blocking collectives  46.6 us (24%)
  Pallas kernels  17.8 us (9%)
  between operations  13.7 us (7%)
  local copies, waits for them, and re-layouts  9.49 us (5%)
    ppermute x10, starting transfers between devices, swap(): return lax.ppermute(x, axis, [(0, 1), (1, 0)])  35.3 us
    all_to_all x1, blocking collectives, body(): stats = lax.all_to_all(stats, (XLO, Y, Z), 0, 0, tiled=True)  27.4 us
    all_to_all x1, waiting for transfers between devices, body(): glu = lax.all_to_all(glu, Z, 0, 0, tiled=True)  24.2 us
    all_to_all x1, blocking collectives, body(): lax.all_to_all(keep.reshape(2 * nz, width, run), (XHI, Z), 0, 0, tiled=True)  19.2 us
    ppermute x10, waiting for transfers between devices, swap(): return lax.ppermute(x, axis, [(0, 1), (1, 0)])  13.7 us
    all_to_all x1, waiting for transfers between devices, body(): parts = lax.all_to_all(parts, Z, 0, 0, tiled=True)  9.94 us
    pallas_call x1, Pallas kernels, body(): pl.pallas_call(ff_kernel, out_shape=(shape((full, run), F32), shape((full...  7.17 us
    unnamed x32, local copies, waits for them, and re-layouts  6.72 us
  transfers between devices with their start and end apart: 15, of which 7 were waited for; matrix products, arithmetic and copies ran while one was open for 1% of the time, Pallas kernels for 5%

profile of v3, /device:TPU:1, one launch (start us, length us, event | category | flops | bytes accessed | tf_op | source)
XLA Modules:
  0.0 192.4 jit_solution(15235571745680536909)
XLA Ops:
  7.3 4.6 %collective-permute-start = (bf16[64,128]{1,0:T(8,128)(2,1)S(1)}, bf16[64,128]{1,0:T(8,128)(2,1)S(1)}, u32[]{:S(2)}, u32[]{:S(2)}) collective-permute-start(bf16[64,128]{1,0:T(8,128)(2,1)S(1)} %get-tuple-element.26), channel_id=1, source_target_pairs={{0,16},{16,32},{32,48},{48,64},{64,80},{80,96},{96,112},{112,128},... | collective-permute-start | bytes 49160 | tf_op jit(solution)/shard_map/ppermute | solution.py:271
  11.9 5.5 %collective-permute-start.1 = (bf16[64,128]{1,0:T(8,128)(2,1)S(1)}, bf16[64,128]{1,0:T(8,128)(2,1)S(1)}, u32[]{:S(2)}, u32[]{:S(2)}) collective-permute-start(bf16[64,128]{1,0:T(8,128)(2,1)S(1)} %get-tuple-element.25), channel_id=1, source_target_pairs={{16,0},{32,16},{48,32},{64,48},{80,64},{96,80},{112,96},{128,112},... | collective-permute-start | bytes 49160 | tf_op jit(solution)/shard_map/ppermute | solution.py:272
  17.5 0.9 copy-done.5
  20.5 1.8 weights.1
  23.1 6.5 %all-to-all-start = ((bf16[8,144,128]{2,1,0:T(8,128)(2,1)}), bf16[8,144,128]{2,1,0:T(8,128)(2,1)S(1)}, u32[]{:S(2)}, u32[]{:S(2)}) async-start(bf16[8,144,128]{2,1,0:T(8,128)(2,1)} %pack.1), calls=%async_computation | async-start | bytes 589824 | tf_op jit(solution)/shard_map/all_to_all | solution.py:291
  29.7 1.6 blocks.1
  31.2 9.9 %all-to-all-done.own = bf16[8,144,128]{2,1,0:T(8,128)(2,1)S(1)} async-done(((bf16[8,144,128]{2,1,0:T(8,128)(2,1)}), bf16[8,144,128]{2,1,0:T(8,128)(2,1)S(1)}, u32[]{:S(2)}, u32[]{:S(2)}) %all-to-all-start) | async-done | bytes 294944 | tf_op jit(solution)/shard_map/all_to_all | solution.py:291
  41.2 3.6 %all-to-all-start.1 = ((bf16[8,560,128]{2,1,0:T(8,128)(2,1)}), bf16[8,560,128]{2,1,0:T(8,128)(2,1)S(1)}, u32[]{:S(2)}, u32[]{:S(2)}) async-start(bf16[8,560,128]{2,1,0:T(8,128)(2,1)} %weights.1), calls=%async_computation.1 | async-start | bytes 2293760 | tf_op jit(solution)/shard_map/all_to_all | solution.py:292
  44.8 4.7 %collective-permute-start.2 = (bf16[8,144,128]{2,1,0:T(8,128)(2,1)S(1)}, bf16[8,144,128]{2,1,0:T(8,128)(2,1)S(1)}, u32[]{:S(2)}, u32[]{:S(2)}) collective-permute-start(bf16[8,144,128]{2,1,0:T(8,128)(2,1)S(1)} %all-to-all-done.own), channel_id=1, source_target_pairs={{0,8},{8,0},{1,9},{9,1},{2,10},{10,2},{3,11},{11,3},{4,12},{12,4},... | collective-permute-start | bytes 884744 | tf_op jit(solution)/shard_map/ppermute | solution.py:24
  49.5 1.9 collective-permute-start.3
  51.4 5.3 %collective-permute-done.2.across = bf16[8,144,128]{2,1,0:T(8,128)(2,1)S(1)} collective-permute-done((bf16[8,144,128]{2,1,0:T(8,128)(2,1)S(1)}, bf16[8,144,128]{2,1,0:T(8,128)(2,1)S(1)}, u32[]{:S(2)}, u32[]{:S(2)}) %collective-permute-start.2) | collective-permute-done | bytes 294944 | tf_op jit(solution)/shard_map/ppermute | solution.py:24
  56.7 1.9 collective-permute-start.4
  58.8 1.3 collective-permute-done.4.far
  60.1 24.2 %all-to-all-done.1.glu = bf16[8,560,128]{2,1,0:T(8,128)(2,1)S(1)} async-done(((bf16[8,560,128]{2,1,0:T(8,128)(2,1)}), bf16[8,560,128]{2,1,0:T(8,128)(2,1)S(1)}, u32[]{:S(2)}, u32[]{:S(2)}) %all-to-all-start.1) | async-done | bytes 1146912 | tf_op jit(solution)/shard_map/all_to_all | solution.py:292
  84.3 4.9 %conv.1 = (f32[512,256]{1,0:T(8,128)S(1)}, f32[128,4,128]{2,1,0:T(4,128)S(1)}, f32[8,256]{1,0:T(8,128)S(1)}, bf16[256,512]{1,0:T(8,128)(2,1)S(1)}) custom-call(s32[2]{0:T(128)S(1)} %pad_add_fusion.place, bf16[8,144,128]{2,1,0:T(8,128)(2,1)S(1)} %all-to-all-done.own, bf16[8,144,128]{2,1,0:T(8,128)(2,1)S(1)} %collective-permute-done.2.across, ...), custom_call_target="tpu_custom_call" | custom-call | tf_op jit(solution)/shard_map/conv/pallas_call | solution.py:307
  89.2 27.4 %all_to_all.20.stats = f32[128,4,128]{2,1,0:T(4,128)S(1)} all-to-all(f32[128,4,128]{2,1,0:T(4,128)S(1)} %get-tuple-element.19), channel_id=1, replica_groups=mesh['xlo'=2,'y'=8,'core'=2,'xhi'=2,'z'=8] {'xlo','y','z'}, dimensions={0} | all-to-all | bytes 524288 | tf_op jit(solution)/shard_map/all_to_all | solution.py:326
  117.1 4.4 %collective-permute-start.5 = (bf16[256,512]{1,0:T(8,128)(2,1)S(1)}, bf16[256,512]{1,0:T(8,128)(2,1)S(1)}, u32[]{:S(2)}, u32[]{:S(2)}) collective-permute-start(bf16[256,512]{1,0:T(8,128)(2,1)S(1)} %bn.1.own), channel_id=1, source_target_pairs={{0,8},{8,0},{1,9},{9,1},{2,10},{10,2},{3,11},{11,3},{4,12},{12,4},... | collective-permute-start | bytes 786440 | tf_op jit(solution)/shard_map/ppermute | solution.py:24
  121.5 5.2 %collective-permute-start.6 = (bf16[256,512]{1,0:T(8,128)(2,1)S(1)}, bf16[256,512]{1,0:T(8,128)(2,1)S(1)}, u32[]{:S(2)}, u32[]{:S(2)}) collective-permute-start(bf16[256,512]{1,0:T(8,128)(2,1)S(1)} %bn.1.own), channel_id=1, source_target_pairs={{0,16},{16,0},{1,17},{17,1},{2,18},{18,2},{3,19},{19,3},{4,20},{20... | collective-permute-start | bytes 786440 | tf_op jit(solution)/shard_map/ppermute | solution.py:24
  126.8 5.0 %collective-permute-start.7 = (bf16[256,512]{1,0:T(8,128)(2,1)S(1)}, bf16[256,512]{1,0:T(8,128)(2,1)S(1)}, u32[]{:S(2)}, u32[]{:S(2)}) collective-permute-start(bf16[256,512]{1,0:T(8,128)(2,1)S(1)} %collective-permute-done.5.across), channel_id=1, source_target_pairs={{0,16},{16,0},{1,17},{17,1},{2,18},{18,2},{3,19},{19,3},{4,20},{20... | collective-permute-start | bytes 786440 | tf_op jit(solution)/shard_map/ppermute | solution.py:24
  131.8 1.1 collective-permute-done.7.far
  133.0 2.3 %copy-done = bf16[144,128,128]{2,1,0:T(8,128)(2,1)S(1)} copy-done((bf16[144,128,128]{2,1,0:T(8,128)(2,1)S(1)}, bf16[144,128,128]{2,1,0:T(8,128)(2,1)}, u32[]{:S(2)}) %copy-start) | copy-done | bytes 4718616
  135.3 1.1 mix.1.own
  136.4 4.4 %collective-permute-start.8 = (bf16[256,512]{1,0:T(8,128)(2,1)S(1)}, bf16[256,512]{1,0:T(8,128)(2,1)S(1)}, u32[]{:S(2)}, u32[]{:S(2)}) collective-permute-start(bf16[256,512]{1,0:T(8,128)(2,1)S(1)} %mix.1.own), channel_id=1, source_target_pairs={{0,8},{8,0},{1,9},{9,1},{2,10},{10,2},{3,11},{11,3},{4,12},{12,4},... | collective-permute-start | bytes 786440 | tf_op jit(solution)/shard_map/ppermute | solution.py:24
  140.8 2.6 %collective-permute-start.9 = (bf16[256,512]{1,0:T(8,128)(2,1)S(1)}, bf16[256,512]{1,0:T(8,128)(2,1)S(1)}, u32[]{:S(2)}, u32[]{:S(2)}) collective-permute-start(bf16[256,512]{1,0:T(8,128)(2,1)S(1)} %mix.1.own), channel_id=1, source_target_pairs={{0,16},{16,0},{1,17},{17,1},{2,18},{18,2},{3,19},{19,3},{4,20},{20... | collective-permute-start | bytes 786440 | tf_op jit(solution)/shard_map/ppermute | solution.py:24
  143.4 3.9 %collective-permute-done.8.across = bf16[256,512]{1,0:T(8,128)(2,1)S(1)} collective-permute-done((bf16[256,512]{1,0:T(8,128)(2,1)S(1)}, bf16[256,512]{1,0:T(8,128)(2,1)S(1)}, u32[]{:S(2)}, u32[]{:S(2)}) %collective-permute-start.8) | collective-permute-done | bytes 262176 | tf_op jit(solution)/shard_map/ppermute | solution.py:24
  147.3 3.3 %collective-permute-start.10 = (bf16[256,512]{1,0:T(8,128)(2,1)S(1)}, bf16[256,512]{1,0:T(8,128)(2,1)S(1)}, u32[]{:S(2)}, u32[]{:S(2)}) collective-permute-start(bf16[256,512]{1,0:T(8,128)(2,1)S(1)} %collective-permute-done.8.across), channel_id=1, source_target_pairs={{0,16},{16,0},{1,17},{17,1},{2,18},{18,2},{3,19},{19,3},{4,20},{20... | collective-permute-start | bytes 786440 | tf_op jit(solution)/shard_map/ppermute | solution.py:24
  150.6 1.0 copy.16.gain
  153.0 7.2 %ff.1 = (f32[1024,256]{1,0:T(8,128)}, bf16[1024,256]{1,0:T(8,128)(2,1)}) custom-call(s32[2]{0:T(128)} %copy-done.8, bf16[256,512]{1,0:T(8,128)(2,1)} %copy-done.1, bf16[256,512]{1,0:T(8,128)(2,1)} %copy-done.11, bf16[256,512]{1,0:T(8,128)(2,1)} %copy-done.12, bf16[256,512]{1,0:T(8,128)(2,1)} %copy-done.13, bf16[8,18,128,128]{3,2,1,0:T(8,128)(2,1)} %bitcast.17, ...), custom_call_target="tpu_custom_call" | custom-call | tf_op jit(solution)/shard_map/ff/pallas_call | solution.py:347
  160.2 1.9 collective-permute-start.11
  162.2 2.1 %collective-permute-done.11 = bf16[1024,256]{1,0:T(8,128)(2,1)S(1)} collective-permute-done((bf16[1024,256]{1,0:T(8,128)(2,1)}, bf16[1024,256]{1,0:T(8,128)(2,1)S(1)}, u32[]{:S(2)}, u32[]{:S(2)}) %collective-permute-start.11) | collective-permute-done | bytes 524320 | tf_op jit(solution)/shard_map/ppermute | solution.py:24
  164.2 1.3 add_convert_fusion
  165.6 19.2 %all_to_all.21 = bf16[16,64,256]{2,1,0:T(8,128)(2,1)S(1)} all-to-all(bf16[16,64,256]{2,1,0:T(8,128)(2,1)S(1)} %bitcast.25), channel_id=1, replica_groups=mesh['xlo'=2,'y'=8,'core'=2,'xhi'=2,'z'=8] {'xhi','z'}, dimensions={0} | all-to-all | bytes 1048576 | tf_op jit(solution)/shard_map/all_to_all | solution.py:363
  (47 shorter events, 6.7 us)
Async XLA Ops:
  6.5 15.7 %copy-start.4 = (bf16[2048,64]{0,1:T(8,128)(2,1)S(1)}, bf16[2048,64]{0,1:T(8,128)(2,1)}, u32[]{:S(2)}) copy-start(bf16[2048,64]{0,1:T(8,128)(2,1)} %param.10) | copy-start | bytes 786436
  7.3 14.9 %collective-permute-start = (bf16[64,128]{1,0:T(8,128)(2,1)S(1)}, bf16[64,128]{1,0:T(8,128)(2,1)S(1)}, u32[]{:S(2)}, u32[]{:S(2)}) collective-permute-start(bf16[64,128]{1,0:T(8,128)(2,1)S(1)} %get-tuple-element.26), channel_id=1, source_target_pairs={{0,16},{16,32},{32,48},{48,64},{64,80},{80,96},{96,112},{112,128},... | collective-permute-start | bytes 49160 | tf_op jit(solution)/shard_map/ppermute | solution.py:271
  11.9 10.3 %collective-permute-start.1 = (bf16[64,128]{1,0:T(8,128)(2,1)S(1)}, bf16[64,128]{1,0:T(8,128)(2,1)S(1)}, u32[]{:S(2)}, u32[]{:S(2)}) collective-permute-start(bf16[64,128]{1,0:T(8,128)(2,1)S(1)} %get-tuple-element.25), channel_id=1, source_target_pairs={{16,0},{32,16},{48,32},{64,48},{80,64},{96,80},{112,96},{128,112},... | collective-permute-start | bytes 49160 | tf_op jit(solution)/shard_map/ppermute | solution.py:272
  17.5 115.5 %copy-start.8 = (s32[2]{0:T(128)}, s32[2]{0:T(128)S(1)}, u32[]{:S(2)}) copy-start(s32[2]{0:T(128)S(1)} %pad_add_fusion.place) | copy-start | bytes 28
  17.5 1.0 copy-start.5
  18.4 0.7 copy-start.7
  19.2 0.7 copy-start.9
  19.8 0.7 copy-start.10
  20.5 9.2 %copy-start.2 = (bf16[1024,256]{1,0:T(8,128)(2,1)S(1)}, bf16[1024,256]{1,0:T(8,128)(2,1)}, u32[]{:S(2)}) copy-start(bf16[1024,256]{1,0:T(8,128)(2,1)} %ff_in.1) | copy-start | bytes 1572868
  20.5 9.2 %copy-start.3 = (bf16[256,1024]{1,0:T(8,128)(2,1)S(1)}, bf16[256,1024]{1,0:T(8,128)(2,1)}, u32[]{:S(2)}) copy-start(bf16[256,1024]{1,0:T(8,128)(2,1)} %ff_out.1) | copy-start | bytes 1572868
  20.5 9.2 %copy-start.6 = (bf16[1024,64]{0,1:T(8,128)(2,1)S(1)}, bf16[1024,64]{0,1:T(8,128)(2,1)}, u32[]{:S(2)}) copy-start(bf16[1024,64]{0,1:T(8,128)(2,1)} %param.16) | copy-start | bytes 393220
  23.1 18.1 %all-to-all-start = ((bf16[8,144,128]{2,1,0:T(8,128)(2,1)}), bf16[8,144,128]{2,1,0:T(8,128)(2,1)S(1)}, u32[]{:S(2)}, u32[]{:S(2)}) async-start(bf16[8,144,128]{2,1,0:T(8,128)(2,1)} %pack.1), calls=%async_computation | async-start | bytes 589824 | tf_op jit(solution)/shard_map/all_to_all | solution.py:291
  29.6 103.4 %all-gather.3.cloned.1.call-start = ((), (), s32[]{:S(2)}) async-start(), calls=%async_computation.4 | async-start | bytes 5308416 | tf_op jit(solution)/shard_map/all_gather | solution.py:303
  41.2 17.4 %copy-start.14 = (f32[1024]{0:T(1024)S(1)}, f32[1024]{0:T(1024)}, u32[]{:S(2)}) copy-start(f32[1024]{0:T(1024)} %param.11) | copy-start | bytes 12292
  41.2 43.1 %all-to-all-start.1 = ((bf16[8,560,128]{2,1,0:T(8,128)(2,1)}), bf16[8,560,128]{2,1,0:T(8,128)(2,1)S(1)}, u32[]{:S(2)}, u32[]{:S(2)}) async-start(bf16[8,560,128]{2,1,0:T(8,128)(2,1)} %weights.1), calls=%async_computation.1 | async-start | bytes 2293760 | tf_op jit(solution)/shard_map/all_to_all | solution.py:292
  44.8 11.9 %collective-permute-start.2 = (bf16[8,144,128]{2,1,0:T(8,128)(2,1)S(1)}, bf16[8,144,128]{2,1,0:T(8,128)(2,1)S(1)}, u32[]{:S(2)}, u32[]{:S(2)}) collective-permute-start(bf16[8,144,128]{2,1,0:T(8,128)(2,1)S(1)} %all-to-all-done.own), channel_id=1, source_target_pairs={{0,8},{8,0},{1,9},{9,1},{2,10},{10,2},{3,11},{11,3},{4,12},{12,4},... | collective-permute-start | bytes 884744 | tf_op jit(solution)/shard_map/ppermute | solution.py:24
  49.5 9.4 %collective-permute-start.3 = (bf16[8,144,128]{2,1,0:T(8,128)(2,1)S(1)}, bf16[8,144,128]{2,1,0:T(8,128)(2,1)S(1)}, u32[]{:S(2)}, u32[]{:S(2)}) collective-permute-start(bf16[8,144,128]{2,1,0:T(8,128)(2,1)S(1)} %all-to-all-done.own), channel_id=1, source_target_pairs={{0,16},{16,0},{1,17},{17,1},{2,18},{18,2},{3,19},{19,3},{4,20},{20... | collective-permute-start | bytes 884744 | tf_op jit(solution)/shard_map/ppermute | solution.py:24
  56.7 3.5 %collective-permute-start.4 = (bf16[8,144,128]{2,1,0:T(8,128)(2,1)S(1)}, bf16[8,144,128]{2,1,0:T(8,128)(2,1)S(1)}, u32[]{:S(2)}, u32[]{:S(2)}) collective-permute-start(bf16[8,144,128]{2,1,0:T(8,128)(2,1)S(1)} %collective-permute-done.2.across), channel_id=1, source_target_pairs={{0,16},{16,0},{1,17},{17,1},{2,18},{18,2},{3,19},{19,3},{4,20},{20... | collective-permute-start | bytes 884744 | tf_op jit(solution)/shard_map/ppermute | solution.py:24
  117.1 9.7 %collective-permute-start.5 = (bf16[256,512]{1,0:T(8,128)(2,1)S(1)}, bf16[256,512]{1,0:T(8,128)(2,1)S(1)}, u32[]{:S(2)}, u32[]{:S(2)}) collective-permute-start(bf16[256,512]{1,0:T(8,128)(2,1)S(1)} %bn.1.own), channel_id=1, source_target_pairs={{0,8},{8,0},{1,9},{9,1},{2,10},{10,2},{3,11},{11,3},{4,12},{12,4},... | collective-permute-start | bytes 786440 | tf_op jit(solution)/shard_map/ppermute | solution.py:24
  121.5 10.3 %collective-permute-start.6 = (bf16[256,512]{1,0:T(8,128)(2,1)S(1)}, bf16[256,512]{1,0:T(8,128)(2,1)S(1)}, u32[]{:S(2)}, u32[]{:S(2)}) collective-permute-start(bf16[256,512]{1,0:T(8,128)(2,1)S(1)} %bn.1.own), channel_id=1, source_target_pairs={{0,16},{16,0},{1,17},{17,1},{2,18},{18,2},{3,19},{19,3},{4,20},{20... | collective-permute-start | bytes 786440 | tf_op jit(solution)/shard_map/ppermute | solution.py:24
  126.8 6.2 %collective-permute-start.7 = (bf16[256,512]{1,0:T(8,128)(2,1)S(1)}, bf16[256,512]{1,0:T(8,128)(2,1)S(1)}, u32[]{:S(2)}, u32[]{:S(2)}) collective-permute-start(bf16[256,512]{1,0:T(8,128)(2,1)S(1)} %collective-permute-done.5.across), channel_id=1, source_target_pairs={{0,16},{16,0},{1,17},{17,1},{2,18},{18,2},{3,19},{19,3},{4,20},{20... | collective-permute-start | bytes 786440 | tf_op jit(solution)/shard_map/ppermute | solution.py:24
  133.0 2.3 %copy-start = (bf16[144,128,128]{2,1,0:T(8,128)(2,1)S(1)}, bf16[144,128,128]{2,1,0:T(8,128)(2,1)}, u32[]{:S(2)}) copy-start(bf16[144,128,128]{2,1,0:T(8,128)(2,1)} %all-gather.3.cloned.1.call-done) | copy-start | bytes 14155780
  135.3 15.3 %copy-start.15 = (f32[1024]{0:T(1024)S(1)}, f32[1024]{0:T(1024)}, u32[]{:S(2)}) copy-start(f32[1024]{0:T(1024)} %param.17) | copy-start | bytes 12292
  136.4 15.3 %copy-start.1 = (bf16[256,512]{1,0:T(8,128)(2,1)}, bf16[256,512]{1,0:T(8,128)(2,1)S(1)}, u32[]{:S(2)}) copy-start(bf16[256,512]{1,0:T(8,128)(2,1)S(1)} %mix.1.own) | copy-start | bytes 786436
  136.4 10.9 %collective-permute-start.8 = (bf16[256,512]{1,0:T(8,128)(2,1)S(1)}, bf16[256,512]{1,0:T(8,128)(2,1)S(1)}, u32[]{:S(2)}, u32[]{:S(2)}) collective-permute-start(bf16[256,512]{1,0:T(8,128)(2,1)S(1)} %mix.1.own), channel_id=1, source_target_pairs={{0,8},{8,0},{1,9},{9,1},{2,10},{10,2},{3,11},{11,3},{4,12},{12,4},... | collective-permute-start | bytes 786440 | tf_op jit(solution)/shard_map/ppermute | solution.py:24
  140.8 10.8 %collective-permute-start.9 = (bf16[256,512]{1,0:T(8,128)(2,1)S(1)}, bf16[256,512]{1,0:T(8,128)(2,1)S(1)}, u32[]{:S(2)}, u32[]{:S(2)}) collective-permute-start(bf16[256,512]{1,0:T(8,128)(2,1)S(1)} %mix.1.own), channel_id=1, source_target_pairs={{0,16},{16,0},{1,17},{17,1},{2,18},{18,2},{3,19},{19,3},{4,20},{20... | collective-permute-start | bytes 786440 | tf_op jit(solution)/shard_map/ppermute | solution.py:24
  147.3 4.4 %copy-start.11 = (bf16[256,512]{1,0:T(8,128)(2,1)}, bf16[256,512]{1,0:T(8,128)(2,1)S(1)}, u32[]{:S(2)}) copy-start(bf16[256,512]{1,0:T(8,128)(2,1)S(1)} %collective-permute-done.8.across) | copy-start | bytes 786436
  147.3 4.3 %collective-permute-start.10 = (bf16[256,512]{1,0:T(8,128)(2,1)S(1)}, bf16[256,512]{1,0:T(8,128)(2,1)S(1)}, u32[]{:S(2)}, u32[]{:S(2)}) collective-permute-start(bf16[256,512]{1,0:T(8,128)(2,1)S(1)} %collective-permute-done.8.across), channel_id=1, source_target_pairs={{0,16},{16,0},{1,17},{17,1},{2,18},{18,2},{3,19},{19,3},{4,20},{20... | collective-permute-start | bytes 786440 | tf_op jit(solution)/shard_map/ppermute | solution.py:24
  151.7 0.7 copy-start.12
  152.3 0.7 copy-start.13
  160.2 4.0 %collective-permute-start.11 = (bf16[1024,256]{1,0:T(8,128)(2,1)}, bf16[1024,256]{1,0:T(8,128)(2,1)S(1)}, u32[]{:S(2)}, u32[]{:S(2)}) collective-permute-start(bf16[1024,256]{1,0:T(8,128)(2,1)} %get-tuple-element.24), channel_id=1, source_target_pairs={{0,16},{16,0},{1,17},{17,1},{2,18},{18,2},{3,19},{19,3},{4,20},{20... | collective-permute-start | bytes 1572872 | tf_op jit(solution)/shard_map/ppermute | solution.py:24
Sparse Core Ops, SparseCore 0:
  41.3 81.9 all-gather.2

commit v4 on v3

--- a/solution.py
+++ b/solution.py
@@ -12,7 +12,6 @@
 SPAN = 15
 VMEM = pl.BlockSpec(memory_space=pltpu.VMEM)
 SMEM = pl.BlockSpec(memory_space=pltpu.SMEM)
-ANY = pl.BlockSpec(memory_space=pl.ANY)
 PARAMS = pltpu.CompilerParams(vmem_limit_bytes=40 << 20)
 
 
@@ -41,7 +40,7 @@
     return pl.ds(pl.multiple_of(start, step), size)
 
 
-def weight_kernel(place, glu, depth, gain, shift, out, table):
+def weight_kernel(place, glu, conv_out, depth, gain, shift, out, table):
     core = place[0]
     lane = lax.broadcasted_iota(jnp.int32, table.shape, 1)
     table[...] = jnp.zeros_like(table)
@@ -56,24 +55,21 @@
         piece = rest.astype(BF).astype(F32)
         packed = packed + (piece if i == 0 else pltpu.roll(piece, 32 * i, 1))
         rest = rest - piece
-    nz = out.shape[0]
+    half = at(32 * core, 32, 32)
     for k in range(8):
+        tile = slice(LANES * k, LANES * (k + 1))
         for v in range(2):
-            tile = glu[v, at(32 * core, 32, 32), LANES * k : LANES * (k + 1)]
-            for z in range(nz):
-                out[z, 64 * k + 32 * v : 64 * k + 32 * v + 32] = tile
-    for z in range(nz):
-        out[z, 512:560] = packed.astype(BF)
-
-
-def block_kernel(place, ff_in, ff_out, conv_out, out):
+            out[64 * k + 32 * v : 64 * k + 32 * v + 32] = glu[v, half, tile]
+        out[512 + 32 * k : 512 + 32 * k + 32] = conv_out[half, tile]
+    out[768:816] = packed.astype(BF)
+
+
+def block_kernel(place, ff_in, ff_out, out):
     half = at(place[0] * LANES, LANES, LANES)
     for k in range(8):
         tile = slice(LANES * k, LANES * (k + 1))
         out[k] = ff_in[tile, half].astype(F32).T.astype(BF)
         out[8 + k] = ff_out[half, tile].astype(F32).T.astype(BF)
-        rows = slice(32 * (k % 4), 32 * (k % 4) + 32)
-        out[16 + k // 4, rows, :] = conv_out[at(place[0] * 32, 32, 32), tile]
 
 
 def pack_kernel(tok, left, right, out):
@@ -103,7 +99,7 @@
 
 
 def conv_kernel(
-    place, own, across, beside, far, glu, gain,
+    place, own, across, beside, far, glu, small, gain,
     conv, stats, par, res,
     tok, edge, win, weight,
 ):
@@ -132,7 +128,7 @@
     for h in range(2):
         total = jnp.zeros((48, LANES), F32)
         for i in range(4):
-            x = glu[4 * h + i, 512:560].astype(F32)
+            x = small[4 * h + i].astype(F32)
             x = x + (pltpu.roll(x, LANES - 32, 1) + pltpu.roll(x, LANES - 64, 1))
             x = jnp.where(lane < 32, x, 0.0)
             total = total + (x if i == 0 else pltpu.roll(x, 32 * i, 1))
@@ -210,25 +206,22 @@
     place_blocks(place, own, across, beside, far, whole)
     for z in range(8):
         for k in range(8):
-            rows = slice(32 * (k % 4), 32 * (k % 4) + 32)
-            weight[32 * z : 32 * z + 32, LANES * k : LANES * (k + 1)] = blocks[z, k // 4, rows, :]
+            tile = slice(LANES * k, LANES * (k + 1))
+            weight[32 * z : 32 * z + 32, tile] = blocks[z, 32 * k : 32 * k + 32]
     mixed = jnp.dot(weight[...], whole[...], preferred_element_type=F32)
     out[...] = (res[...].astype(F32) + mixed).astype(BF)
 
 
 def ff_kernel(
-    place, own, across, beside, far, weights, gain,
+    place, own, across, beside, far, w, gain,
     keep, give,
-    whole, normed, hidden, w, sem,
+    whole, normed, hidden,
 ):
-    copy = pltpu.make_async_copy(weights.at[:, 0:16], w, sem)
-    copy.start()
     place_blocks(place, own, across, beside, far, whole)
     half = 256
     for c in range(2):
         cols = slice(half * c, half * (c + 1))
         normed[:, cols] = norm_rows(whole[:, cols].astype(F32), gain[...])
-    copy.wait()
     for z in range(0, 8, 2):
         rows = [jnp.concatenate([w[z + i, k] for k in range(8)], axis=1) for i in range(2)]
         value = jnp.dot(
@@ -244,6 +237,13 @@
         mine = jnp.where(place[1] == k // 4, 1.0, 0.0)
         keep[rows, :] = 0.5 * value[:, :half] + mine * whole[rows, :half].astype(F32)
         give[rows, :] = (0.5 * value[:, half:]).astype(BF)
+
+
+def sum_kernel(parts, out):
+    nz, run = parts.shape[0] // 2, parts.shape[2]
+    for z in range(nz):
+        value = parts[z].astype(F32) + parts[nz + z].astype(F32)
+        out[:, run * z : run * (z + 1)] = value.astype(BF)
 
 
 def body(
@@ -265,20 +265,30 @@
     full = ln_conv_gain.shape[0]
     run = frames // nz
 
+    first = pl.pallas_call(
+        weight_kernel,
+        out_shape=shape((816, LANES), BF),
+        in_specs=[SMEM] + [VMEM] * 5,
+        out_specs=VMEM,
+        scratch_shapes=[pltpu.VMEM((48, LANES), F32)],
+        compiler_params=PARAMS,
+        name="weights",
+    )(
+        place,
+        glu_weight.transpose(1, 2, 0),
+        conv_out_weight.T,
+        depth_weight,
+        bn_gain[None],
+        bn_shift[None],
+    )
+    first, tokens = lax.optimization_barrier((first, tokens))
+    first = lax.all_gather(first, Z)
+
     tok = tokens.T
     tm = lax.axis_size((XLO, Y, CORE))
     up = [(i, i + 1) for i in range(tm - 1)]
     left = lax.ppermute(tok[:, frames - LANES :], (XLO, Y, CORE), up)
     right = lax.ppermute(tok[:, :LANES], (XLO, Y, CORE), [(j, i) for i, j in up])
-    glu = pl.pallas_call(
-        weight_kernel,
-        out_shape=shape((nz, 560, LANES), BF),
-        in_specs=[SMEM] + [VMEM] * 4,
-        out_specs=VMEM,
-        scratch_shapes=[pltpu.VMEM((48, LANES), F32)],
-        compiler_params=PARAMS,
-        name="weights",
-    )(place, glu_weight.transpose(1, 2, 0), depth_weight, bn_gain[None], bn_shift[None])
     parts = pl.pallas_call(
         pack_kernel,
         out_shape=shape((nz, 144, LANES), BF),
@@ -287,18 +297,16 @@
         compiler_params=PARAMS,
         name="pack",
     )(tok, left, right)
-    parts, glu = lax.optimization_barrier((parts, glu))
     parts = lax.all_to_all(parts, Z, 0, 0, tiled=True)
-    glu = lax.all_to_all(glu, Z, 0, 0, tiled=True)
 
     blocks = pl.pallas_call(
         block_kernel,
-        out_shape=shape((18, LANES, LANES), BF),
-        in_specs=[SMEM] + [VMEM] * 3,
+        out_shape=shape((16, LANES, LANES), BF),
+        in_specs=[SMEM] + [VMEM] * 2,
         out_specs=VMEM,
         compiler_params=PARAMS,
         name="blocks",
-    )(place, ff_in_weight, ff_out_weight, conv_out_weight.T)
+    )(place, ff_in_weight, ff_out_weight)
     blocks, parts = lax.optimization_barrier((blocks, parts))
     blocks = lax.all_gather(blocks, Z)
 
@@ -312,7 +320,14 @@
             shape((8, 256), F32),
             shape((256, 2 * run), BF),
         ),
-        in_specs=[SMEM] + [VMEM] * 6,
+        grid=(1,),
+        in_specs=[SMEM]
+        + [VMEM] * 4
+        + [
+            pl.BlockSpec((nz, 512, LANES), lambda i: (0, 0, 0)),
+            pl.BlockSpec((nz, 48, LANES), lambda i: (0, 16, 0)),
+            VMEM,
+        ],
         out_specs=(VMEM,) * 4,
         scratch_shapes=[
             pltpu.VMEM((full, 2 * run), BF),
@@ -322,7 +337,7 @@
         ],
         compiler_params=PARAMS,
         name="conv",
-    )(place, *whole, glu, ln_conv_gain[:, None])
+    )(place, *whole, first, first, ln_conv_gain[:, None])
     stats = lax.all_to_all(stats, (XLO, Y, Z), 0, 0, tiled=True)
     activated = pl.pallas_call(
         bn_kernel,
@@ -338,31 +353,36 @@
         grid=(1,),
         in_specs=[SMEM]
         + [VMEM] * 4
-        + [pl.BlockSpec((nz, 2, LANES, LANES), lambda i: (0, 8, 0, 0)), VMEM],
+        + [pl.BlockSpec((nz, 256, LANES), lambda i: (0, 2, 0)), VMEM],
         out_specs=VMEM,
         scratch_shapes=[pltpu.VMEM((full, 2 * run), BF), pltpu.VMEM((256, full), BF)],
         compiler_params=PARAMS,
         name="mix",
-    )(place, *group_gather(activated), blocks, res)
+    )(place, *group_gather(activated), first, res)
     keep, give = pl.pallas_call(
         ff_kernel,
         out_shape=(shape((full, run), F32), shape((full, run), BF)),
-        in_specs=[SMEM] + [VMEM] * 4 + [ANY, VMEM],
+        in_specs=[SMEM] + [VMEM] * 6,
         out_specs=(VMEM,) * 2,
         scratch_shapes=[
             pltpu.VMEM((full, 2 * run), BF),
             pltpu.VMEM((full, 2 * run), BF),
             pltpu.VMEM((full, 2 * run), BF),
-            pltpu.VMEM((8, 16, LANES, LANES), BF),
-            pltpu.SemaphoreType.DMA,
         ],
-        compiler_params=pltpu.CompilerParams(vmem_limit_bytes=58 << 20),
+        compiler_params=PARAMS,
         name="ff",
     )(place, *group_gather(block), blocks, ln_ff_gain[:, None])
     keep = (keep + swap(give, CORE).astype(F32)).astype(BF)
     keep = lax.all_to_all(keep.reshape(2 * nz, width, run), (XHI, Z), 0, 0, tiled=True)
-    out = (keep[:nz].astype(F32) + keep[nz:].astype(F32)).astype(BF)
-    return out.transpose(1, 0, 2).reshape(width, frames).T
+    out = pl.pallas_call(
+        sum_kernel,
+        out_shape=shape((width, frames), BF),
+        in_specs=[VMEM],
+        out_specs=VMEM,
+        compiler_params=PARAMS,
+        name="sum",
+    )(keep)
+    return out.T
 
 
 def solution(mesh):

time: 194 us -> 170 us (0.88)
  waiting for transfers between devices: 47.8 us -> 26.8 us
  Pallas kernels: 17.8 us -> 14.6 us
  local copies, waits for them, and re-layouts: 9.49 us -> 11.7 us
    all_to_all x1 -> x0, waiting for transfers between devices: 24.2 us -> none  [body(): glu = lax.all_to_all(glu, Z, 0, 0, tiled=True)]
    all_to_all x1, blocking collectives: 27.4 us -> 23.4 us  [body(): stats = lax.all_to_all(stats, (XLO, Y, Z), 0, 0, tiled=True)]
    unnamed x32 -> x26, local copies, waits for them, and re-layouts: 6.72 us -> 10.5 us
    pallas_call x1, Pallas kernels: 7.17 us -> 3.54 us  [body(): pl.pallas_call(ff_kernel, out_shape=(shape((full, run), F32), shape((full...]
    all_to_all x1 -> x0, starting transfers between devices: 3.57 us -> none  [body(): glu = lax.all_to_all(glu, Z, 0, 0, tiled=True)]
    all_to_all x1, starting transfers between devices: 6.47 us -> 8.79 us  [body(): parts = lax.all_to_all(parts, Z, 0, 0, tiled=True)]
    all_to_all x1, blocking collectives: 19.2 us -> 21.3 us  [body(): lax.all_to_all(keep.reshape(2 * nz, width, run), (XHI, Z), 0, 0, tiled=True)]
  transfers between devices with their start and end apart: 15 -> 15, of which waited for: 7 -> 9; matrix products, arithmetic and copies ran while one was open for 1% -> 1% of each run, Pallas kernels for 5% -> 5%
where the time goes in v4:
time: 170 us; the launch traced here: 167 us
  starting transfers between devices  55.8 us (33%)
  blocking collectives  44.7 us (26%)
  waiting for transfers between devices  26.8 us (16%)
  Pallas kernels  14.6 us (9%)
  between operations  13.6 us (8%)
  local copies, waits for them, and re-layouts  11.7 us (7%)
    ppermute x10, starting transfers between devices, swap(): return lax.ppermute(x, axis, [(0, 1), (1, 0)])  36.9 us
    all_to_all x1, blocking collectives, body(): stats = lax.all_to_all(stats, (XLO, Y, Z), 0, 0, tiled=True)  23.4 us
    all_to_all x1, blocking collectives, body(): lax.all_to_all(keep.reshape(2 * nz, width, run), (XHI, Z), 0, 0, tiled=True)  21.3 us
    ppermute x10, waiting for transfers between devices, swap(): return lax.ppermute(x, axis, [(0, 1), (1, 0)])  14.1 us
    all_to_all x1, waiting for transfers between devices, body(): parts = lax.all_to_all(parts, Z, 0, 0, tiled=True)  11.4 us
    unnamed x26, local copies, waits for them, and re-layouts  10.5 us
    all_to_all x1, starting transfers between devices, body(): parts = lax.all_to_all(parts, Z, 0, 0, tiled=True)  8.79 us
    ppermute x1, starting transfers between devices, body(): lax.ppermute(tok[:, :LANES], (XLO, Y, CORE), [(j, i) for i, j in up])  5.48 us
  transfers between devices with their start and end apart: 15, of which 9 were waited for; matrix products, arithmetic and copies ran while one was open for 1% of the time, Pallas kernels for 5%

profile of v4, /device:TPU:1, one launch (start us, length us, event | category | flops | bytes accessed | tf_op | source)
XLA Modules:
  0.0 167.4 jit_solution(1605960911370723810)
XLA Ops:
  6.6 0.9 copy-done.6
  10.5 1.4 weights.1
  12.6 4.6 %collective-permute-start = (bf16[64,128]{1,0:T(8,128)(2,1)S(1)}, bf16[64,128]{1,0:T(8,128)(2,1)S(1)}, u32[]{:S(2)}, u32[]{:S(2)}) collective-permute-start(bf16[64,128]{1,0:T(8,128)(2,1)S(1)} %get-tuple-element.26), channel_id=1, source_target_pairs={{0,16},{16,32},{32,48},{48,64},{64,80},{80,96},{96,112},{112,128},... | collective-permute-start | bytes 49160 | tf_op jit(solution)/shard_map/ppermute | solution.py:290
  17.2 5.5 %collective-permute-start.1 = (bf16[64,128]{1,0:T(8,128)(2,1)S(1)}, bf16[64,128]{1,0:T(8,128)(2,1)S(1)}, u32[]{:S(2)}, u32[]{:S(2)}) collective-permute-start(bf16[64,128]{1,0:T(8,128)(2,1)S(1)} %get-tuple-element.25), channel_id=1, source_target_pairs={{16,0},{32,16},{48,32},{64,48},{80,64},{96,80},{112,96},{128,112},... | collective-permute-start | bytes 49160 | tf_op jit(solution)/shard_map/ppermute | solution.py:291
  23.5 0.9 copy-done.5
  25.3 8.8 %all-to-all-start = ((bf16[8,144,128]{2,1,0:T(8,128)(2,1)}), bf16[8,144,128]{2,1,0:T(8,128)(2,1)S(1)}, u32[]{:S(2)}, u32[]{:S(2)}) async-start(bf16[8,144,128]{2,1,0:T(8,128)(2,1)} %pack.1), calls=%async_computation | async-start | bytes 589824 | tf_op jit(solution)/shard_map/all_to_all | solution.py:300
  34.2 1.0 copy-done.3
  35.2 1.0 copy-done.4
  36.3 1.6 blocks.1
  37.8 11.4 %all-to-all-done.own = bf16[8,144,128]{2,1,0:T(8,128)(2,1)S(1)} async-done(((bf16[8,144,128]{2,1,0:T(8,128)(2,1)}), bf16[8,144,128]{2,1,0:T(8,128)(2,1)S(1)}, u32[]{:S(2)}, u32[]{:S(2)}) %all-to-all-start) | async-done | bytes 294944 | tf_op jit(solution)/shard_map/all_to_all | solution.py:300
  49.3 4.7 %collective-permute-start.2 = (bf16[8,144,128]{2,1,0:T(8,128)(2,1)S(1)}, bf16[8,144,128]{2,1,0:T(8,128)(2,1)S(1)}, u32[]{:S(2)}, u32[]{:S(2)}) collective-permute-start(bf16[8,144,128]{2,1,0:T(8,128)(2,1)S(1)} %all-to-all-done.own), channel_id=1, source_target_pairs={{0,8},{8,0},{1,9},{9,1},{2,10},{10,2},{3,11},{11,3},{4,12},{12,4},... | collective-permute-start | bytes 884744 | tf_op jit(solution)/shard_map/ppermute | solution.py:23
  53.9 1.9 %collective-permute-start.3 = (bf16[8,144,128]{2,1,0:T(8,128)(2,1)S(1)}, bf16[8,144,128]{2,1,0:T(8,128)(2,1)S(1)}, u32[]{:S(2)}, u32[]{:S(2)}) collective-permute-start(bf16[8,144,128]{2,1,0:T(8,128)(2,1)S(1)} %all-to-all-done.own), channel_id=1, source_target_pairs={{0,16},{16,0},{1,17},{17,1},{2,18},{18,2},{3,19},{19,3},{4,20},{20... | collective-permute-start | bytes 884744 | tf_op jit(solution)/shard_map/ppermute | solution.py:23
  55.9 5.8 %collective-permute-done.2.across = bf16[8,144,128]{2,1,0:T(8,128)(2,1)S(1)} collective-permute-done((bf16[8,144,128]{2,1,0:T(8,128)(2,1)S(1)}, bf16[8,144,128]{2,1,0:T(8,128)(2,1)S(1)}, u32[]{:S(2)}, u32[]{:S(2)}) %collective-permute-start.2) | collective-permute-done | bytes 294944 | tf_op jit(solution)/shard_map/ppermute | solution.py:23
  61.6 2.3 %collective-permute-start.4 = (bf16[8,144,128]{2,1,0:T(8,128)(2,1)S(1)}, bf16[8,144,128]{2,1,0:T(8,128)(2,1)S(1)}, u32[]{:S(2)}, u32[]{:S(2)}) collective-permute-start(bf16[8,144,128]{2,1,0:T(8,128)(2,1)S(1)} %collective-permute-done.2.across), channel_id=1, source_target_pairs={{0,16},{16,0},{1,17},{17,1},{2,18},{18,2},{3,19},{19,3},{4,20},{20... | collective-permute-start | bytes 884744 | tf_op jit(solution)/shard_map/ppermute | solution.py:23
  64.2 0.9 collective-permute-done.4.far
  65.2 1.4 copy-done
  66.6 4.9 %conv.1 = (f32[512,256]{1,0:T(8,128)S(1)}, f32[128,4,128]{2,1,0:T(4,128)S(1)}, f32[8,256]{1,0:T(8,128)S(1)}, bf16[256,512]{1,0:T(8,128)(2,1)S(1)}) custom-call(s32[2]{0:T(128)S(1)} %pad_add_fusion.place, bf16[8,144,128]{2,1,0:T(8,128)(2,1)S(1)} %all-to-all-done.own, bf16[8,144,128]{2,1,0:T(8,128)(2,1)S(1)} %collective-permute-done.2.across, ...), custom_call_target="tpu_custom_call" | custom-call | tf_op jit(solution)/shard_map/conv/pallas_call | solution.py:315
  71.6 23.4 %all_to_all.15.stats = f32[128,4,128]{2,1,0:T(4,128)S(1)} all-to-all(f32[128,4,128]{2,1,0:T(4,128)S(1)} %get-tuple-element.19), channel_id=1, replica_groups=mesh['xlo'=2,'y'=8,'core'=2,'xhi'=2,'z'=8] {'xlo','y','z'}, dimensions={0} | all-to-all | bytes 524288 | tf_op jit(solution)/shard_map/all_to_all | solution.py:341
  95.5 4.3 %collective-permute-start.5 = (bf16[256,512]{1,0:T(8,128)(2,1)S(1)}, bf16[256,512]{1,0:T(8,128)(2,1)S(1)}, u32[]{:S(2)}, u32[]{:S(2)}) collective-permute-start(bf16[256,512]{1,0:T(8,128)(2,1)S(1)} %bn.1.own), channel_id=1, source_target_pairs={{0,8},{8,0},{1,9},{9,1},{2,10},{10,2},{3,11},{11,3},{4,12},{12,4},... | collective-permute-start | bytes 786440 | tf_op jit(solution)/shard_map/ppermute | solution.py:23
  99.8 5.8 %collective-permute-start.6 = (bf16[256,512]{1,0:T(8,128)(2,1)S(1)}, bf16[256,512]{1,0:T(8,128)(2,1)S(1)}, u32[]{:S(2)}, u32[]{:S(2)}) collective-permute-start(bf16[256,512]{1,0:T(8,128)(2,1)S(1)} %bn.1.own), channel_id=1, source_target_pairs={{0,16},{16,0},{1,17},{17,1},{2,18},{18,2},{3,19},{19,3},{4,20},{20... | collective-permute-start | bytes 786440 | tf_op jit(solution)/shard_map/ppermute | solution.py:23
  105.6 5.1 %collective-permute-start.7 = (bf16[256,512]{1,0:T(8,128)(2,1)S(1)}, bf16[256,512]{1,0:T(8,128)(2,1)S(1)}, u32[]{:S(2)}, u32[]{:S(2)}) collective-permute-start(bf16[256,512]{1,0:T(8,128)(2,1)S(1)} %collective-permute-done.5.across), channel_id=1, source_target_pairs={{0,16},{16,0},{1,17},{17,1},{2,18},{18,2},{3,19},{19,3},{4,20},{20... | collective-permute-start | bytes 786440 | tf_op jit(solution)/shard_map/ppermute | solution.py:23
  110.7 1.1 collective-permute-done.7.far
  111.9 1.1 mix.1.own
  112.9 4.3 %collective-permute-start.8 = (bf16[256,512]{1,0:T(8,128)(2,1)S(1)}, bf16[256,512]{1,0:T(8,128)(2,1)S(1)}, u32[]{:S(2)}, u32[]{:S(2)}) collective-permute-start(bf16[256,512]{1,0:T(8,128)(2,1)S(1)} %mix.1.own), channel_id=1, source_target_pairs={{0,8},{8,0},{1,9},{9,1},{2,10},{10,2},{3,11},{11,3},{4,12},{12,4},... | collective-permute-start | bytes 786440 | tf_op jit(solution)/shard_map/ppermute | solution.py:23
  117.3 2.6 %collective-permute-start.9 = (bf16[256,512]{1,0:T(8,128)(2,1)S(1)}, bf16[256,512]{1,0:T(8,128)(2,1)S(1)}, u32[]{:S(2)}, u32[]{:S(2)}) collective-permute-start(bf16[256,512]{1,0:T(8,128)(2,1)S(1)} %mix.1.own), channel_id=1, source_target_pairs={{0,16},{16,0},{1,17},{17,1},{2,18},{18,2},{3,19},{19,3},{4,20},{20... | collective-permute-start | bytes 786440 | tf_op jit(solution)/shard_map/ppermute | solution.py:23
  119.9 4.0 %collective-permute-done.8.across = bf16[256,512]{1,0:T(8,128)(2,1)S(1)} collective-permute-done((bf16[256,512]{1,0:T(8,128)(2,1)S(1)}, bf16[256,512]{1,0:T(8,128)(2,1)S(1)}, u32[]{:S(2)}, u32[]{:S(2)}) %collective-permute-start.8) | collective-permute-done | bytes 262176 | tf_op jit(solution)/shard_map/ppermute | solution.py:23
  123.9 3.3 %collective-permute-start.10 = (bf16[256,512]{1,0:T(8,128)(2,1)S(1)}, bf16[256,512]{1,0:T(8,128)(2,1)S(1)}, u32[]{:S(2)}, u32[]{:S(2)}) collective-permute-start(bf16[256,512]{1,0:T(8,128)(2,1)S(1)} %collective-permute-done.8.across), channel_id=1, source_target_pairs={{0,16},{16,0},{1,17},{17,1},{2,18},{18,2},{3,19},{19,3},{4,20},{20... | collective-permute-start | bytes 786440 | tf_op jit(solution)/shard_map/ppermute | solution.py:23
  128.6 2.2 %copy-done.2 = bf16[128,128,128]{2,1,0:T(8,128)(2,1)S(1)} copy-done((bf16[128,128,128]{2,1,0:T(8,128)(2,1)S(1)}, bf16[128,128,128]{2,1,0:T(8,128)(2,1)}, u32[]{:S(2)}) %copy-start.2) | copy-done | bytes 4194328
  130.8 3.5 %ff.1 = (f32[1024,256]{1,0:T(8,128)S(1)}, bf16[1024,256]{1,0:T(8,128)(2,1)S(1)}) custom-call(s32[2]{0:T(128)S(1)} %pad_add_fusion.place, bf16[256,512]{1,0:T(8,128)(2,1)S(1)} %mix.1.own, bf16[256,512]{1,0:T(8,128)(2,1)S(1)} %collective-permute-done.8.across, bf16[256,512]{1,0:T(8,128)(2,1)S(1)} %collective-permute-done.9.beside, ...), custom_call_target="tpu_custom_call" | custom-call | tf_op jit(solution)/shard_map/ff/pallas_call | solution.py:362
  134.3 2.6 %collective-permute-start.11 = (bf16[1024,256]{1,0:T(8,128)(2,1)S(1)}, bf16[1024,256]{1,0:T(8,128)(2,1)S(1)}, u32[]{:S(2)}, u32[]{:S(2)}) collective-permute-start(bf16[1024,256]{1,0:T(8,128)(2,1)S(1)} %get-tuple-element.24), channel_id=1, source_target_pairs={{0,16},{16,0},{1,17},{17,1},{2,18},{18,2},{3,19},{19,3},{4,20},{20... | collective-permute-start | bytes 1572872 | tf_op jit(solution)/shard_map/ppermute | solution.py:23
  136.9 1.5 collective-permute-done.11
  138.6 21.3 %all_to_all.16.parts = bf16[16,64,256]{2,1,0:T(8,128)(2,1)S(1)} all-to-all(bf16[16,64,256]{2,1,0:T(8,128)(2,1)S(1)} %bitcast.23), channel_id=1, replica_groups=mesh['xlo'=2,'y'=8,'core'=2,'xhi'=2,'z'=8] {'xhi','z'}, dimensions={0} | all-to-all | bytes 1048576 | tf_op jit(solution)/shard_map/all_to_all | solution.py:376
  (41 shorter events, 8.5 us)
Async XLA Ops:
  6.5 57.5 %copy-start.11 = (f32[1024]{0:T(1024)S(1)}, f32[1024]{0:T(1024)}, u32[]{:S(2)}) copy-start(f32[1024]{0:T(1024)} %param.11) | copy-start | bytes 12292
  6.5 58.6 %all-gather.5.cloned.1.call-start = ((), (), s32[]{:S(2)}) async-start(), calls=%async_computation.3 | async-start | bytes 1880064 | tf_op jit(solution)/shard_map/all_gather | solution.py:285
  6.6 0.9 copy-start.6
  7.6 0.9 copy-start.7
  8.5 0.7 copy-start.8
  9.2 0.7 copy-start.9
  9.8 0.7 copy-start.10
  12.6 10.1 %collective-permute-start = (bf16[64,128]{1,0:T(8,128)(2,1)S(1)}, bf16[64,128]{1,0:T(8,128)(2,1)S(1)}, u32[]{:S(2)}, u32[]{:S(2)}) collective-permute-start(bf16[64,128]{1,0:T(8,128)(2,1)S(1)} %get-tuple-element.26), channel_id=1, source_target_pairs={{0,16},{16,32},{32,48},{48,64},{64,80},{80,96},{96,112},{112,128},... | collective-permute-start | bytes 49160 | tf_op jit(solution)/shard_map/ppermute | solution.py:290
  17.2 6.3 %collective-permute-start.1 = (bf16[64,128]{1,0:T(8,128)(2,1)S(1)}, bf16[64,128]{1,0:T(8,128)(2,1)S(1)}, u32[]{:S(2)}, u32[]{:S(2)}) collective-permute-start(bf16[64,128]{1,0:T(8,128)(2,1)S(1)} %get-tuple-element.25), channel_id=1, source_target_pairs={{16,0},{32,16},{48,32},{64,48},{80,64},{96,80},{112,96},{128,112},... | collective-permute-start | bytes 49160 | tf_op jit(solution)/shard_map/ppermute | solution.py:291
  23.5 0.9 copy-start.5
  25.3 23.9 %all-to-all-start = ((bf16[8,144,128]{2,1,0:T(8,128)(2,1)}), bf16[8,144,128]{2,1,0:T(8,128)(2,1)S(1)}, u32[]{:S(2)}, u32[]{:S(2)}) async-start(bf16[8,144,128]{2,1,0:T(8,128)(2,1)} %pack.1), calls=%async_computation | async-start | bytes 589824 | tf_op jit(solution)/shard_map/all_to_all | solution.py:300
  34.1 94.4 %all-gather.7.cloned.1.call-start = ((), (), s32[]{:S(2)}) async-start(), calls=%async_computation.4 | async-start | bytes 4718592 | tf_op jit(solution)/shard_map/all_gather | solution.py:311
  34.2 1.0 copy-start.3
  35.2 1.0 copy-start.4
  49.3 12.4 %collective-permute-start.2 = (bf16[8,144,128]{2,1,0:T(8,128)(2,1)S(1)}, bf16[8,144,128]{2,1,0:T(8,128)(2,1)S(1)}, u32[]{:S(2)}, u32[]{:S(2)}) collective-permute-start(bf16[8,144,128]{2,1,0:T(8,128)(2,1)S(1)} %all-to-all-done.own), channel_id=1, source_target_pairs={{0,8},{8,0},{1,9},{9,1},{2,10},{10,2},{3,11},{11,3},{4,12},{12,4},... | collective-permute-start | bytes 884744 | tf_op jit(solution)/shard_map/ppermute | solution.py:23
  53.9 10.3 %collective-permute-start.3 = (bf16[8,144,128]{2,1,0:T(8,128)(2,1)S(1)}, bf16[8,144,128]{2,1,0:T(8,128)(2,1)S(1)}, u32[]{:S(2)}, u32[]{:S(2)}) collective-permute-start(bf16[8,144,128]{2,1,0:T(8,128)(2,1)S(1)} %all-to-all-done.own), channel_id=1, source_target_pairs={{0,16},{16,0},{1,17},{17,1},{2,18},{18,2},{3,19},{19,3},{4,20},{20... | collective-permute-start | bytes 884744 | tf_op jit(solution)/shard_map/ppermute | solution.py:23
  61.6 3.5 %collective-permute-start.4 = (bf16[8,144,128]{2,1,0:T(8,128)(2,1)S(1)}, bf16[8,144,128]{2,1,0:T(8,128)(2,1)S(1)}, u32[]{:S(2)}, u32[]{:S(2)}) collective-permute-start(bf16[8,144,128]{2,1,0:T(8,128)(2,1)S(1)} %collective-permute-done.2.across), channel_id=1, source_target_pairs={{0,16},{16,0},{1,17},{17,1},{2,18},{18,2},{3,19},{19,3},{4,20},{20... | collective-permute-start | bytes 884744 | tf_op jit(solution)/shard_map/ppermute | solution.py:23
  65.2 1.4 copy-start
  66.6 45.2 %copy-start.1 = (bf16[6528,128]{1,0:T(8,128)(2,1)S(1)}, bf16[6528,128]{1,0:T(8,128)(2,1)}, u32[]{:S(2)}) copy-start(bf16[6528,128]{1,0:T(8,128)(2,1)} %all-gather.5.cloned.1.call-done) | copy-start | bytes 5013508
  66.6 60.5 %copy-start.12 = (f32[1024]{0:T(1024)S(1)}, f32[1024]{0:T(1024)}, u32[]{:S(2)}) copy-start(f32[1024]{0:T(1024)} %param.17) | copy-start | bytes 12292
  95.5 10.1 %collective-permute-start.5 = (bf16[256,512]{1,0:T(8,128)(2,1)S(1)}, bf16[256,512]{1,0:T(8,128)(2,1)S(1)}, u32[]{:S(2)}, u32[]{:S(2)}) collective-permute-start(bf16[256,512]{1,0:T(8,128)(2,1)S(1)} %bn.1.own), channel_id=1, source_target_pairs={{0,8},{8,0},{1,9},{9,1},{2,10},{10,2},{3,11},{11,3},{4,12},{12,4},... | collective-permute-start | bytes 786440 | tf_op jit(solution)/shard_map/ppermute | solution.py:23
  99.8 10.9 %collective-permute-start.6 = (bf16[256,512]{1,0:T(8,128)(2,1)S(1)}, bf16[256,512]{1,0:T(8,128)(2,1)S(1)}, u32[]{:S(2)}, u32[]{:S(2)}) collective-permute-start(bf16[256,512]{1,0:T(8,128)(2,1)S(1)} %bn.1.own), channel_id=1, source_target_pairs={{0,16},{16,0},{1,17},{17,1},{2,18},{18,2},{3,19},{19,3},{4,20},{20... | collective-permute-start | bytes 786440 | tf_op jit(solution)/shard_map/ppermute | solution.py:23
  105.6 6.3 %collective-permute-start.7 = (bf16[256,512]{1,0:T(8,128)(2,1)S(1)}, bf16[256,512]{1,0:T(8,128)(2,1)S(1)}, u32[]{:S(2)}, u32[]{:S(2)}) collective-permute-start(bf16[256,512]{1,0:T(8,128)(2,1)S(1)} %collective-permute-done.5.across), channel_id=1, source_target_pairs={{0,16},{16,0},{1,17},{17,1},{2,18},{18,2},{3,19},{19,3},{4,20},{20... | collective-permute-start | bytes 786440 | tf_op jit(solution)/shard_map/ppermute | solution.py:23
  112.9 10.9 %collective-permute-start.8 = (bf16[256,512]{1,0:T(8,128)(2,1)S(1)}, bf16[256,512]{1,0:T(8,128)(2,1)S(1)}, u32[]{:S(2)}, u32[]{:S(2)}) collective-permute-start(bf16[256,512]{1,0:T(8,128)(2,1)S(1)} %mix.1.own), channel_id=1, source_target_pairs={{0,8},{8,0},{1,9},{9,1},{2,10},{10,2},{3,11},{11,3},{4,12},{12,4},... | collective-permute-start | bytes 786440 | tf_op jit(solution)/shard_map/ppermute | solution.py:23
  117.3 10.1 %collective-permute-start.9 = (bf16[256,512]{1,0:T(8,128)(2,1)S(1)}, bf16[256,512]{1,0:T(8,128)(2,1)S(1)}, u32[]{:S(2)}, u32[]{:S(2)}) collective-permute-start(bf16[256,512]{1,0:T(8,128)(2,1)S(1)} %mix.1.own), channel_id=1, source_target_pairs={{0,16},{16,0},{1,17},{17,1},{2,18},{18,2},{3,19},{19,3},{4,20},{20... | collective-permute-start | bytes 786440 | tf_op jit(solution)/shard_map/ppermute | solution.py:23
  123.9 4.2 %collective-permute-start.10 = (bf16[256,512]{1,0:T(8,128)(2,1)S(1)}, bf16[256,512]{1,0:T(8,128)(2,1)S(1)}, u32[]{:S(2)}, u32[]{:S(2)}) collective-permute-start(bf16[256,512]{1,0:T(8,128)(2,1)S(1)} %collective-permute-done.8.across), channel_id=1, source_target_pairs={{0,16},{16,0},{1,17},{17,1},{2,18},{18,2},{3,19},{19,3},{4,20},{20... | collective-permute-start | bytes 786440 | tf_op jit(solution)/shard_map/ppermute | solution.py:23
  128.6 2.2 %copy-start.2 = (bf16[128,128,128]{2,1,0:T(8,128)(2,1)S(1)}, bf16[128,128,128]{2,1,0:T(8,128)(2,1)}, u32[]{:S(2)}) copy-start(bf16[128,128,128]{2,1,0:T(8,128)(2,1)} %all-gather.7.cloned.1.call-done) | copy-start | bytes 12582916
  134.3 4.1 %collective-permute-start.11 = (bf16[1024,256]{1,0:T(8,128)(2,1)S(1)}, bf16[1024,256]{1,0:T(8,128)(2,1)S(1)}, u32[]{:S(2)}, u32[]{:S(2)}) collective-permute-start(bf16[1024,256]{1,0:T(8,128)(2,1)S(1)} %get-tuple-element.24), channel_id=1, source_target_pairs={{0,16},{16,0},{1,17},{17,1},{2,18},{18,2},{3,19},{19,3},{4,20},{20... | collective-permute-start | bytes 1572872 | tf_op jit(solution)/shard_map/ppermute | solution.py:23
Sparse Core Ops, SparseCore 0:
  12.0 49.4 all-gather.4
  63.6 64.9 all-gather.6

commit v5 on v4

--- a/solution.py
+++ b/solution.py
@@ -11,12 +11,16 @@
 LANES = 128
 SPAN = 15
 VMEM = pl.BlockSpec(memory_space=pltpu.VMEM)
-SMEM = pl.BlockSpec(memory_space=pltpu.SMEM)
+HBM = pl.BlockSpec(memory_space=pltpu.HBM)
 PARAMS = pltpu.CompilerParams(vmem_limit_bytes=40 << 20)
 
 
 def shape(dims, dtype):
     return jax.ShapeDtypeStruct(dims, dtype)
+
+
+def in_hbm(*arrays):
+    return [pltpu.with_memory_space_constraint(x, pltpu.HBM) for x in arrays]
 
 
 def swap(x, axis):
@@ -36,18 +40,52 @@
     return (centred * lax.rsqrt(spread + EPS) * gain).astype(BF)
 
 
+def place():
+    return lax.axis_index(CORE), lax.axis_index(XHI)
+
+
 def at(start, size, step):
     return pl.ds(pl.multiple_of(start, step), size)
 
 
-def weight_kernel(place, glu, conv_out, depth, gain, shift, out, table):
-    core = place[0]
+def weight_kernel(
+    glu, conv_out, depth, gain, shift, tok,
+    out, near, first, last,
+    table, parts, small, sems,
+):
+    core, _ = place()
+    half = at(32 * core, 32, 32)
+    taps, width = depth.shape
+    loads = [
+        pltpu.make_async_copy(depth, small.at[0:taps], sems.at[0]),
+        pltpu.make_async_copy(gain, small.at[32:33], sems.at[1]),
+        pltpu.make_async_copy(shift, small.at[40:41], sems.at[2]),
+    ]
+    stores = []
+    for k in range(8):
+        tile = slice(LANES * k, LANES * (k + 1))
+        for v in range(2):
+            stores.append((glu.at[v, half, tile], 64 * k + 32 * v))
+        stores.append((conv_out.at[half, tile], 512 + 32 * k))
+    stores = [
+        pltpu.make_async_copy(ref, out.at[row : row + 32], sems.at[4 + i])
+        for i, (ref, row) in enumerate(stores)
+    ]
+    frames = tok.shape[1]
+    stores += [
+        pltpu.make_async_copy(tok.at[:, 0:LANES], first, sems.at[28]),
+        pltpu.make_async_copy(tok.at[:, frames - LANES : frames], last, sems.at[29]),
+        pltpu.make_async_copy(tok, near, sems.at[30]),
+    ]
+    for copy in loads + stores:
+        copy.start()
+    table[...] = jnp.zeros_like(table)
+    for copy in loads:
+        copy.wait()
+    table[0:taps, 0:width] = small[0:taps]
+    table[taps : taps + 1, 0:width] = small[32:33]
+    table[taps + 1 : taps + 2, 0:width] = small[40:41]
     lane = lax.broadcasted_iota(jnp.int32, table.shape, 1)
-    table[...] = jnp.zeros_like(table)
-    width, taps = depth.shape[1], depth.shape[0]
-    table[0:taps, 0:width] = depth[...]
-    table[taps : taps + 1, 0:width] = gain[...]
-    table[taps + 1 : taps + 2, 0:width] = shift[...]
     rest = jnp.where(core == 0, table[...], pltpu.roll(table[...], LANES - 32, 1))
     rest = jnp.where(lane < 32, rest, 0.0)
     packed = jnp.zeros_like(rest)
@@ -55,17 +93,15 @@
         piece = rest.astype(BF).astype(F32)
         packed = packed + (piece if i == 0 else pltpu.roll(piece, 32 * i, 1))
         rest = rest - piece
-    half = at(32 * core, 32, 32)
-    for k in range(8):
-        tile = slice(LANES * k, LANES * (k + 1))
-        for v in range(2):
-            out[64 * k + 32 * v : 64 * k + 32 * v + 32] = glu[v, half, tile]
-        out[512 + 32 * k : 512 + 32 * k + 32] = conv_out[half, tile]
-    out[768:816] = packed.astype(BF)
-
-
-def block_kernel(place, ff_in, ff_out, out):
-    half = at(place[0] * LANES, LANES, LANES)
+    parts[...] = packed.astype(BF)
+    final = pltpu.make_async_copy(parts, out.at[768:816], sems.at[3])
+    final.start()
+    for copy in stores + [final]:
+        copy.wait()
+
+
+def block_kernel(ff_in, ff_out, out):
+    half = at(place()[0] * LANES, LANES, LANES)
     for k in range(8):
         tile = slice(LANES * k, LANES * (k + 1))
         out[k] = ff_in[tile, half].astype(F32).T.astype(BF)
@@ -99,11 +135,17 @@
 
 
 def conv_kernel(
-    place, own, across, beside, far, glu, small, gain,
+    own, across, beside, far, first, gain,
     conv, stats, par, res,
-    tok, edge, win, weight,
+    tok, edge, win, weight, glu, small, sems,
 ):
-    core, xhi = place[0], place[1]
+    loads = [
+        pltpu.make_async_copy(first.at[:, 0:512], glu, sems.at[0]),
+        pltpu.make_async_copy(first.at[:, 768:816], small, sems.at[1]),
+    ]
+    for copy in loads:
+        copy.start()
+    core, xhi = place()
     lane = lax.broadcasted_iota(jnp.int32, (16, LANES), 1)
     nz = glu.shape[0]
     for near, away, side in ((own, beside, xhi), (across, far, 1 - xhi)):
@@ -123,6 +165,8 @@
         row = xhi * (64 * nz) + 64 * z + 32 * core
         res[32 * z : 32 * z + 32, :] = tok[at(row, 32, 32), :]
 
+    for copy in loads:
+        copy.wait()
     table = []
     lane = lax.broadcasted_iota(jnp.int32, (48, LANES), 1)
     for h in range(2):
@@ -173,23 +217,33 @@
         stats[:, 2 + h : 3 + h, :] = jnp.broadcast_to(square[None], (n, 1, LANES))
 
 
+def merged(stats, count):
+    total = jnp.sum(stats, axis=0)
+    mean = total * (1.0 / stats.shape[0])
+    apart = stats - mean[None]
+    apart = jnp.sum(apart * apart, axis=0)
+    return mean[0:2], total[2:4] + count * apart[0:2]
+
+
+def merge_kernel(stats, out):
+    mean, square = merged(stats[...], 512)
+    out[:, 0:2] = jnp.broadcast_to(mean[None], (out.shape[0],) + mean.shape)
+    out[:, 2:4] = jnp.broadcast_to(square[None], (out.shape[0],) + square.shape)
+
+
 def bn_kernel(conv, stats, par, out):
-    n, frames = stats.shape[0], conv.shape[0]
-    s = stats[...]
-    total = jnp.sum(s, axis=0)
-    mean = total * (1.0 / n)
-    apart = s - mean[None]
-    apart = jnp.sum(apart * apart, axis=0)
+    frames = 8 * conv.shape[0]
+    mean, square = merged(stats[...], frames)
+    scale = lax.rsqrt(square * (1.0 / (frames * stats.shape[0])) + EPS)
     for h in range(2):
         cols = slice(LANES * h, LANES * (h + 1))
-        square = total[2 + h : 3 + h] + frames * apart[h : h + 1]
-        scale = lax.rsqrt(square * (1.0 / (n * frames)) + EPS) * par[0:1, cols]
-        value = (conv[:, cols] - mean[h : h + 1]) * scale + par[1:2, cols]
+        value = (conv[:, cols] - mean[h : h + 1]) * (scale[h : h + 1] * par[0:1, cols])
+        value = value + par[1:2, cols]
         out[cols, :] = (value * jax.nn.sigmoid(value)).T.astype(BF)
 
 
-def place_blocks(place, own, across, beside, far, whole):
-    core, xhi = place[0], place[1]
+def place_blocks(own, across, beside, far, whole):
+    core, xhi = place()
     nz, half = 8, 256
     for blk, c, x in ((own, core, xhi), (across, core, 1 - xhi)):
         for z in range(nz):
@@ -202,8 +256,8 @@
             whole[at(row, 32, 32), half:] = blk[32 * z : 32 * z + 32, :half]
 
 
-def mix_kernel(place, own, across, beside, far, blocks, res, out, whole, weight):
-    place_blocks(place, own, across, beside, far, whole)
+def mix_kernel(own, across, beside, far, blocks, res, out, whole, weight):
+    place_blocks(own, across, beside, far, whole)
     for z in range(8):
         for k in range(8):
             tile = slice(LANES * k, LANES * (k + 1))
@@ -213,28 +267,38 @@
 
 
 def ff_kernel(
-    place, own, across, beside, far, w, gain,
+    own, across, beside, far, blocks, gain,
     keep, give,
-    whole, normed, hidden,
+    whole, normed, hidden, w, sems,
 ):
-    place_blocks(place, own, across, beside, far, whole)
+    loads = [
+        pltpu.make_async_copy(blocks.at[2 * i : 2 * i + 2, 0:8], w.at[2 * i : 2 * i + 2, 0:8], sems.at[i])
+        for i in range(4)
+    ]
+    loads.append(pltpu.make_async_copy(blocks.at[:, 8:16], w.at[:, 8:16], sems.at[4]))
+    for copy in loads:
+        copy.start()
+    xhi = place()[1]
+    place_blocks(own, across, beside, far, whole)
     half = 256
     for c in range(2):
         cols = slice(half * c, half * (c + 1))
         normed[:, cols] = norm_rows(whole[:, cols].astype(F32), gain[...])
     for z in range(0, 8, 2):
+        loads[z // 2].wait()
         rows = [jnp.concatenate([w[z + i, k] for k in range(8)], axis=1) for i in range(2)]
         value = jnp.dot(
             jnp.concatenate(rows, axis=0), normed[...], preferred_element_type=F32
         )
         hidden[LANES * z : LANES * (z + 2), :] = (value * jax.nn.sigmoid(value)).astype(BF)
+    loads[4].wait()
     for k in range(0, 8, 2):
         rows = [jnp.concatenate([w[z, 8 + k + i] for z in range(8)], axis=1) for i in range(2)]
         value = jnp.dot(
             jnp.concatenate(rows, axis=0), hidden[...], preferred_element_type=F32
         )
         rows = slice(LANES * k, LANES * (k + 2))
-        mine = jnp.where(place[1] == k // 4, 1.0, 0.0)
+        mine = jnp.where(xhi == k // 4, 1.0, 0.0)
         keep[rows, :] = 0.5 * value[:, :half] + mine * whole[rows, :half].astype(F32)
         give[rows, :] = (0.5 * value[:, half:]).astype(BF)
 
@@ -258,37 +322,45 @@
     ff_in_weight,
     ff_out_weight,
 ):
-    core, xhi = (lax.axis_index(CORE), lax.axis_index(XHI))
-    place = jnp.stack([core, xhi]).astype(jnp.int32)
     nz = lax.axis_size(Z)
     frames, width = tokens.shape
     full = ln_conv_gain.shape[0]
     run = frames // nz
 
-    first = pl.pallas_call(
+    first, tok, head, tail = pl.pallas_call(
         weight_kernel,
-        out_shape=shape((816, LANES), BF),
-        in_specs=[SMEM] + [VMEM] * 5,
-        out_specs=VMEM,
-        scratch_shapes=[pltpu.VMEM((48, LANES), F32)],
+        out_shape=(
+            shape((816, LANES), BF),
+            shape((width, frames), BF),
+            shape((width, LANES), BF),
+            shape((width, LANES), BF),
+        ),
+        in_specs=[HBM] * 6,
+        out_specs=(HBM, VMEM, VMEM, VMEM),
+        scratch_shapes=[
+            pltpu.VMEM((48, LANES), F32),
+            pltpu.VMEM((48, LANES), BF),
+            pltpu.VMEM((48, width), F32),
+            pltpu.SemaphoreType.DMA((31,)),
+        ],
         compiler_params=PARAMS,
         name="weights",
     )(
-        place,
-        glu_weight.transpose(1, 2, 0),
-        conv_out_weight.T,
-        depth_weight,
-        bn_gain[None],
-        bn_shift[None],
+        *in_hbm(
+            glu_weight.transpose(1, 2, 0),
+            conv_out_weight.T,
+            depth_weight,
+            bn_gain[None],
+            bn_shift[None],
+            tokens.T,
+        )
     )
-    first, tokens = lax.optimization_barrier((first, tokens))
     first = lax.all_gather(first, Z)
 
-    tok = tokens.T
     tm = lax.axis_size((XLO, Y, CORE))
     up = [(i, i + 1) for i in range(tm - 1)]
-    left = lax.ppermute(tok[:, frames - LANES :], (XLO, Y, CORE), up)
-    right = lax.ppermute(tok[:, :LANES], (XLO, Y, CORE), [(j, i) for i, j in up])
+    left = lax.ppermute(tail, (XLO, Y, CORE), up)
+    right = lax.ppermute(head, (XLO, Y, CORE), [(j, i) for i, j in up])
     parts = pl.pallas_call(
         pack_kernel,
         out_shape=shape((nz, 144, LANES), BF),
@@ -302,43 +374,47 @@
     blocks = pl.pallas_call(
         block_kernel,
         out_shape=shape((16, LANES, LANES), BF),
-        in_specs=[SMEM] + [VMEM] * 2,
+        in_specs=[VMEM] * 2,
         out_specs=VMEM,
         compiler_params=PARAMS,
         name="blocks",
-    )(place, ff_in_weight, ff_out_weight)
+    )(ff_in_weight, ff_out_weight)
     blocks, parts = lax.optimization_barrier((blocks, parts))
     blocks = lax.all_gather(blocks, Z)
 
     whole = group_gather(parts)
-    peers = lax.axis_size((XLO, Y, Z))
     conv, stats, par, res = pl.pallas_call(
         conv_kernel,
         out_shape=(
             shape((2 * run, 256), F32),
-            shape((peers, 4, LANES), F32),
+            shape((nz, 4, LANES), F32),
             shape((8, 256), F32),
             shape((256, 2 * run), BF),
         ),
-        grid=(1,),
-        in_specs=[SMEM]
-        + [VMEM] * 4
-        + [
-            pl.BlockSpec((nz, 512, LANES), lambda i: (0, 0, 0)),
-            pl.BlockSpec((nz, 48, LANES), lambda i: (0, 16, 0)),
-            VMEM,
-        ],
+        in_specs=[VMEM] * 4 + [HBM, VMEM],
         out_specs=(VMEM,) * 4,
         scratch_shapes=[
             pltpu.VMEM((full, 2 * run), BF),
             pltpu.VMEM((full, LANES), F32),
             pltpu.VMEM((2, run + 40, 256), F32),
             pltpu.VMEM((512, full), BF),
+            pltpu.VMEM((nz, 512, LANES), BF),
+            pltpu.VMEM((nz, 48, LANES), BF),
+            pltpu.SemaphoreType.DMA((2,)),
         ],
         compiler_params=PARAMS,
         name="conv",
-    )(place, *whole, first, first, ln_conv_gain[:, None])
-    stats = lax.all_to_all(stats, (XLO, Y, Z), 0, 0, tiled=True)
+    )(*whole, *in_hbm(first), ln_conv_gain[:, None])
+    stats = lax.all_to_all(stats, Z, 0, 0, tiled=True)
+    stats = pl.pallas_call(
+        merge_kernel,
+        out_shape=shape((lax.axis_size((XLO, Y)), 4, LANES), F32),
+        in_specs=[VMEM],
+        out_specs=VMEM,
+        compiler_params=PARAMS,
+        name="merge",
+    )(stats)
+    stats = lax.all_to_all(stats, (XLO, Y), 0, 0, tiled=True)
     activated = pl.pallas_call(
         bn_kernel,
         out_shape=shape((256, 2 * run), BF),
@@ -351,27 +427,31 @@
         mix_kernel,
         out_shape=shape((256, 2 * run), BF),
         grid=(1,),
-        in_specs=[SMEM]
-        + [VMEM] * 4
-        + [pl.BlockSpec((nz, 256, LANES), lambda i: (0, 2, 0)), VMEM],
+        in_specs=[VMEM] * 4
+        + [
+            pl.BlockSpec((nz, 256, LANES), lambda i: (0, 2, 0)),
+            VMEM,
+        ],
         out_specs=VMEM,
         scratch_shapes=[pltpu.VMEM((full, 2 * run), BF), pltpu.VMEM((256, full), BF)],
         compiler_params=PARAMS,
         name="mix",
-    )(place, *group_gather(activated), first, res)
+    )(*group_gather(activated), first, res)
     keep, give = pl.pallas_call(
         ff_kernel,
         out_shape=(shape((full, run), F32), shape((full, run), BF)),
-        in_specs=[SMEM] + [VMEM] * 6,
+        in_specs=[VMEM] * 4 + [HBM, VMEM],
         out_specs=(VMEM,) * 2,
         scratch_shapes=[
             pltpu.VMEM((full, 2 * run), BF),
             pltpu.VMEM((full, 2 * run), BF),
             pltpu.VMEM((full, 2 * run), BF),
+            pltpu.VMEM((nz, 16, LANES, LANES), BF),
+            pltpu.SemaphoreType.DMA((5,)),
         ],
         compiler_params=PARAMS,
         name="ff",
-    )(place, *group_gather(block), blocks, ln_ff_gain[:, None])
+    )(*group_gather(block), *in_hbm(blocks), ln_ff_gain[:, None])
     keep = (keep + swap(give, CORE).astype(F32)).astype(BF)
     keep = lax.all_to_all(keep.reshape(2 * nz, width, run), (XHI, Z), 0, 0, tiled=True)
     out = pl.pallas_call(

time: 170 us -> 166 us (0.976); the launches traced: 167 us -> 165 us
  local copies, waits for them, and re-layouts: 11.7 us -> 3.21 us
  Pallas kernels: 14.6 us -> 21.1 us
  starting transfers between devices: 55.8 us -> 59.2 us
  blocking collectives: 44.7 us -> 42.5 us
    unnamed x26 -> x8, local copies, waits for them, and re-layouts: 10.5 us -> 2.09 us
    pallas_call x1 -> x2, Pallas kernels: 1.38 us -> 7.37 us  [the longest x1 7.35 us: body(): pl.pallas_call(weight_kernel, out_shape=(shape((816, LANES), BF), shape((...]
    ppermute x10, starting transfers between devices: 36.9 us -> 40.3 us  [swap(): return lax.ppermute(x, axis, [(0, 1), (1, 0)])]
    all_to_all x1, blocking collectives: 21.3 us -> 18.9 us  [body(): lax.all_to_all(keep.reshape(2 * nz, width, run), (XHI, Z), 0, 0, tiled=True)]
    all_to_all x1 -> x2, blocking collectives: 23.4 us -> 23.7 us  [the longest x1 14 us: body(): stats = lax.all_to_all(stats, (XLO, Y), 0, 0, tiled=True)]
  transfers between devices with their start and end apart: 15 -> 15, of which waited for: 9 -> 8; matrix products, arithmetic and copies ran while one was open for 1% -> 1% of each run, Pallas kernels for 5% -> 5%
where the time goes in v5:
time: 166 us; the launch traced here: 165 us
  starting transfers between devices  59.2 us (36%)
  blocking collectives  42.5 us (26%)
  waiting for transfers between devices  25.6 us (15%)
  Pallas kernels  21.1 us (13%)
  between operations  13.6 us (8%)
  local copies, waits for them, and re-layouts  3.21 us (2%)
    ppermute x10, starting transfers between devices, swap(): return lax.ppermute(x, axis, [(0, 1), (1, 0)])  40.3 us
    all_to_all x1, blocking collectives, body(): lax.all_to_all(keep.reshape(2 * nz, width, run), (XHI, Z), 0, 0, tiled=True)  18.9 us
    all_to_all x1, blocking collectives, body(): stats = lax.all_to_all(stats, (XLO, Y), 0, 0, tiled=True)  14 us
    ppermute x10, waiting for transfers between devices, swap(): return lax.ppermute(x, axis, [(0, 1), (1, 0)])  13 us
    all_to_all x1, waiting for transfers between devices, body(): parts = lax.all_to_all(parts, Z, 0, 0, tiled=True)  11.7 us
    all_to_all x1, blocking collectives, body(): stats = lax.all_to_all(stats, Z, 0, 0, tiled=True)  9.68 us
    all_to_all x1, starting transfers between devices, body(): parts = lax.all_to_all(parts, Z, 0, 0, tiled=True)  8.79 us
    pallas_call x1, Pallas kernels, body(): pl.pallas_call(weight_kernel, out_shape=(shape((816, LANES), BF), shape((...  7.35 us
  transfers between devices with their start and end apart: 15, of which 8 were waited for; matrix products, arithmetic and copies ran while one was open for 1% of the time, Pallas kernels for 5%

profile of v5, /device:TPU:1, one launch (start us, length us, event | category | flops | bytes accessed | tf_op | source)
XLA Modules:
  0.0 165.3 jit_solution(11505980180735622882)
XLA Ops:
  6.5 7.3 %weights.1 = (bf16[816,128]{1,0:T(8,128)(2,1)}, bf16[64,2048]{1,0:T(8,128)(2,1)S(1)}, bf16[64,128]{1,0:T(8,128)(2,1)S(1)}, bf16[64,128]{1,0:T(8,128)(2,1)S(1)}) custom-call(bf16[2,64,1024]{2,1,0:T(8,128)(2,1)} %bitcast.15, bf16[64,1024]{1,0:T(8,128)(2,1)} %bitcast.17, f32[31,64]{1,0:T(8,128)} %depth.1, f32[1,64]{1,0:T(1,128)} %bitcast.20, f32[1,64]{1,0:T(1,128)} %bitcast.21, ...), custom_call_target="tpu_custom_call" | custom-call | tf_op jit(solution)/shard_map/weights/pallas_call | solution.py:330
  13.9 4.6 %collective-permute-start = (bf16[64,128]{1,0:T(8,128)(2,1)S(1)}, bf16[64,128]{1,0:T(8,128)(2,1)S(1)}, u32[]{:S(2)}, u32[]{:S(2)}) collective-permute-start(bf16[64,128]{1,0:T(8,128)(2,1)S(1)} %get-tuple-element.18), channel_id=1, source_target_pairs={{0,16},{16,32},{32,48},{48,64},{64,80},{80,96},{96,112},{112,128},... | collective-permute-start | bytes 49160 | tf_op jit(solution)/shard_map/ppermute | solution.py:362
  18.5 5.5 %collective-permute-start.1 = (bf16[64,128]{1,0:T(8,128)(2,1)S(1)}, bf16[64,128]{1,0:T(8,128)(2,1)S(1)}, u32[]{:S(2)}, u32[]{:S(2)}) collective-permute-start(bf16[64,128]{1,0:T(8,128)(2,1)S(1)} %get-tuple-element.19), channel_id=1, source_target_pairs={{16,0},{32,16},{48,32},{64,48},{80,64},{96,80},{112,96},{128,112},... | collective-permute-start | bytes 49160 | tf_op jit(solution)/shard_map/ppermute | solution.py:363
  24.0 0.8 collective-permute-done.1.right
  24.8 0.8 pack.1
  25.7 8.8 %all-to-all-start = ((bf16[8,144,128]{2,1,0:T(8,128)(2,1)}), bf16[8,144,128]{2,1,0:T(8,128)(2,1)S(1)}, u32[]{:S(2)}, u32[]{:S(2)}) async-start(bf16[8,144,128]{2,1,0:T(8,128)(2,1)} %pack.1), calls=%async_computation | async-start | bytes 589824 | tf_op jit(solution)/shard_map/all_to_all | solution.py:372
  34.5 1.0 copy-done.1
  35.6 1.0 copy-done.2
  36.6 1.0 blocks.1
  37.6 11.7 %all-to-all-done.own = bf16[8,144,128]{2,1,0:T(8,128)(2,1)S(1)} async-done(((bf16[8,144,128]{2,1,0:T(8,128)(2,1)}), bf16[8,144,128]{2,1,0:T(8,128)(2,1)S(1)}, u32[]{:S(2)}, u32[]{:S(2)}) %all-to-all-start) | async-done | bytes 294944 | tf_op jit(solution)/shard_map/all_to_all | solution.py:372
  49.4 4.7 %collective-permute-start.2 = (bf16[8,144,128]{2,1,0:T(8,128)(2,1)S(1)}, bf16[8,144,128]{2,1,0:T(8,128)(2,1)S(1)}, u32[]{:S(2)}, u32[]{:S(2)}) collective-permute-start(bf16[8,144,128]{2,1,0:T(8,128)(2,1)S(1)} %all-to-all-done.own), channel_id=1, source_target_pairs={{0,8},{8,0},{1,9},{9,1},{2,10},{10,2},{3,11},{11,3},{4,12},{12,4},... | collective-permute-start | bytes 884744 | tf_op jit(solution)/shard_map/ppermute | solution.py:27
  54.1 2.1 %collective-permute-start.3 = (bf16[8,144,128]{2,1,0:T(8,128)(2,1)S(1)}, bf16[8,144,128]{2,1,0:T(8,128)(2,1)S(1)}, u32[]{:S(2)}, u32[]{:S(2)}) collective-permute-start(bf16[8,144,128]{2,1,0:T(8,128)(2,1)S(1)} %all-to-all-done.own), channel_id=1, source_target_pairs={{0,16},{16,0},{1,17},{17,1},{2,18},{18,2},{3,19},{19,3},{4,20},{20... | collective-permute-start | bytes 884744 | tf_op jit(solution)/shard_map/ppermute | solution.py:27
  56.2 5.2 %collective-permute-done.2.across = bf16[8,144,128]{2,1,0:T(8,128)(2,1)S(1)} collective-permute-done((bf16[8,144,128]{2,1,0:T(8,128)(2,1)S(1)}, bf16[8,144,128]{2,1,0:T(8,128)(2,1)S(1)}, u32[]{:S(2)}, u32[]{:S(2)}) %collective-permute-start.2) | collective-permute-done | bytes 294944 | tf_op jit(solution)/shard_map/ppermute | solution.py:27
  61.3 2.8 %collective-permute-start.4 = (bf16[8,144,128]{2,1,0:T(8,128)(2,1)S(1)}, bf16[8,144,128]{2,1,0:T(8,128)(2,1)S(1)}, u32[]{:S(2)}, u32[]{:S(2)}) collective-permute-start(bf16[8,144,128]{2,1,0:T(8,128)(2,1)S(1)} %collective-permute-done.2.across), channel_id=1, source_target_pairs={{0,16},{16,0},{1,17},{17,1},{2,18},{18,2},{3,19},{19,3},{4,20},{20... | collective-permute-start | bytes 884744 | tf_op jit(solution)/shard_map/ppermute | solution.py:27
  64.1 0.9 copy.13.gain
  65.3 5.6 %conv.1 = (f32[512,256]{1,0:T(8,128)S(1)}, f32[8,4,128]{2,1,0:T(4,128)S(1)}, f32[8,256]{1,0:T(8,128)S(1)}, bf16[256,512]{1,0:T(8,128)(2,1)S(1)}) custom-call(bf16[8,144,128]{2,1,0:T(8,128)(2,1)S(1)} %all-to-all-done.own, bf16[8,144,128]{2,1,0:T(8,128)(2,1)S(1)} %collective-permute-done.2.across, bf16[8,144,128]{2,1,0:T(8,128)(2,1)S(1)} %collective-permute-done.3.beside, ...), custom_call_target="tpu_custom_call" | custom-call | tf_op jit(solution)/shard_map/conv/pallas_call | solution.py:386
  70.9 9.7 %all_to_all.20.stats = f32[8,4,128]{2,1,0:T(4,128)S(1)} all-to-all(f32[8,4,128]{2,1,0:T(4,128)S(1)} %get-tuple-element.23), channel_id=1, replica_groups=mesh['xlo'=2,'y'=8,'core'=2,'xhi'=2,'z'=8] {'z'}, dimensions={0} | all-to-all | bytes 32768 | tf_op jit(solution)/shard_map/all_to_all | solution.py:408
  80.6 14.0 %all_to_all.21.stats = f32[16,4,128]{2,1,0:T(4,128)S(1)} all-to-all(f32[16,4,128]{2,1,0:T(4,128)S(1)} %merge.1), channel_id=1, replica_groups=mesh['xlo'=2,'y'=8,'core'=2,'xhi'=2,'z'=8] {'xlo','y'}, dimensions={0} | all-to-all | bytes 65536 | tf_op jit(solution)/shard_map/all_to_all | solution.py:417
  94.8 4.3 %collective-permute-start.5 = (bf16[256,512]{1,0:T(8,128)(2,1)S(1)}, bf16[256,512]{1,0:T(8,128)(2,1)S(1)}, u32[]{:S(2)}, u32[]{:S(2)}) collective-permute-start(bf16[256,512]{1,0:T(8,128)(2,1)S(1)} %bn.1.own), channel_id=1, source_target_pairs={{0,8},{8,0},{1,9},{9,1},{2,10},{10,2},{3,11},{11,3},{4,12},{12,4},... | collective-permute-start | bytes 786440 | tf_op jit(solution)/shard_map/ppermute | solution.py:27
  99.1 9.1 %collective-permute-start.6 = (bf16[256,512]{1,0:T(8,128)(2,1)S(1)}, bf16[256,512]{1,0:T(8,128)(2,1)S(1)}, u32[]{:S(2)}, u32[]{:S(2)}) collective-permute-start(bf16[256,512]{1,0:T(8,128)(2,1)S(1)} %bn.1.own), channel_id=1, source_target_pairs={{0,16},{16,0},{1,17},{17,1},{2,18},{18,2},{3,19},{19,3},{4,20},{20... | collective-permute-start | bytes 786440 | tf_op jit(solution)/shard_map/ppermute | solution.py:27
  108.2 5.1 %collective-permute-start.7 = (bf16[256,512]{1,0:T(8,128)(2,1)S(1)}, bf16[256,512]{1,0:T(8,128)(2,1)S(1)}, u32[]{:S(2)}, u32[]{:S(2)}) collective-permute-start(bf16[256,512]{1,0:T(8,128)(2,1)S(1)} %collective-permute-done.5.across), channel_id=1, source_target_pairs={{0,16},{16,0},{1,17},{17,1},{2,18},{18,2},{3,19},{19,3},{4,20},{20... | collective-permute-start | bytes 786440 | tf_op jit(solution)/shard_map/ppermute | solution.py:27
  113.3 1.1 collective-permute-done.7.far
  115.0 4.3 %collective-permute-start.8 = (bf16[256,512]{1,0:T(8,128)(2,1)S(1)}, bf16[256,512]{1,0:T(8,128)(2,1)S(1)}, u32[]{:S(2)}, u32[]{:S(2)}) collective-permute-start(bf16[256,512]{1,0:T(8,128)(2,1)S(1)} %mix.1.own), channel_id=1, source_target_pairs={{0,8},{8,0},{1,9},{9,1},{2,10},{10,2},{3,11},{11,3},{4,12},{12,4},... | collective-permute-start | bytes 786440 | tf_op jit(solution)/shard_map/ppermute | solution.py:27
  119.4 2.6 %collective-permute-start.9 = (bf16[256,512]{1,0:T(8,128)(2,1)S(1)}, bf16[256,512]{1,0:T(8,128)(2,1)S(1)}, u32[]{:S(2)}, u32[]{:S(2)}) collective-permute-start(bf16[256,512]{1,0:T(8,128)(2,1)S(1)} %mix.1.own), channel_id=1, source_target_pairs={{0,16},{16,0},{1,17},{17,1},{2,18},{18,2},{3,19},{19,3},{4,20},{20... | collective-permute-start | bytes 786440 | tf_op jit(solution)/shard_map/ppermute | solution.py:27
  121.9 4.0 %collective-permute-done.8.across = bf16[256,512]{1,0:T(8,128)(2,1)S(1)} collective-permute-done((bf16[256,512]{1,0:T(8,128)(2,1)S(1)}, bf16[256,512]{1,0:T(8,128)(2,1)S(1)}, u32[]{:S(2)}, u32[]{:S(2)}) %collective-permute-start.8) | collective-permute-done | bytes 262176 | tf_op jit(solution)/shard_map/ppermute | solution.py:27
  125.9 3.1 %collective-permute-start.10 = (bf16[256,512]{1,0:T(8,128)(2,1)S(1)}, bf16[256,512]{1,0:T(8,128)(2,1)S(1)}, u32[]{:S(2)}, u32[]{:S(2)}) collective-permute-start(bf16[256,512]{1,0:T(8,128)(2,1)S(1)} %collective-permute-done.8.across), channel_id=1, source_target_pairs={{0,16},{16,0},{1,17},{17,1},{2,18},{18,2},{3,19},{19,3},{4,20},{20... | collective-permute-start | bytes 786440 | tf_op jit(solution)/shard_map/ppermute | solution.py:27
  129.3 0.9 collective-permute-done.10.far
  130.2 4.7 %ff.1 = (f32[1024,256]{1,0:T(8,128)S(1)}, bf16[1024,256]{1,0:T(8,128)(2,1)S(1)}) custom-call(bf16[256,512]{1,0:T(8,128)(2,1)S(1)} %mix.1.own, bf16[256,512]{1,0:T(8,128)(2,1)S(1)} %collective-permute-done.8.across, bf16[256,512]{1,0:T(8,128)(2,1)S(1)} %collective-permute-done.9.beside, bf16[256,512]{1,0:T(8,128)(2,1)S(1)} %collective-permute-done.10.far, ...), custom_call_target="tpu_custom_call" | custom-call | tf_op jit(solution)/shard_map/ff/pallas_call | solution.py:440
  134.9 2.3 %collective-permute-start.11 = (bf16[1024,256]{1,0:T(8,128)(2,1)S(1)}, bf16[1024,256]{1,0:T(8,128)(2,1)S(1)}, u32[]{:S(2)}, u32[]{:S(2)}) collective-permute-start(bf16[1024,256]{1,0:T(8,128)(2,1)S(1)} %get-tuple-element.28), channel_id=1, source_target_pairs={{0,16},{16,0},{1,17},{17,1},{2,18},{18,2},{3,19},{19,3},{4,20},{20... | collective-permute-start | bytes 1572872 | tf_op jit(solution)/shard_map/ppermute | solution.py:27
  137.2 1.5 collective-permute-done.11
  138.8 18.9 %all_to_all.22.parts = bf16[16,64,256]{2,1,0:T(8,128)(2,1)S(1)} all-to-all(bf16[16,64,256]{2,1,0:T(8,128)(2,1)S(1)} %bitcast.14), channel_id=1, replica_groups=mesh['xlo'=2,'y'=8,'core'=2,'xhi'=2,'z'=8] {'xhi','z'}, dimensions={0} | all-to-all | bytes 1048576 | tf_op jit(solution)/shard_map/all_to_all | solution.py:456
  157.7 0.8 sum.1
  (23 shorter events, 1.5 us)
Async XLA Ops:
  6.5 58.7 %all-gather.5.cloned.1.call-start = ((), (), s32[]{:S(2)}) async-start(), calls=%async_computation.4 | async-start | bytes 1880064 | tf_op jit(solution)/shard_map/all_gather | solution.py:358
  13.9 10.1 %collective-permute-start = (bf16[64,128]{1,0:T(8,128)(2,1)S(1)}, bf16[64,128]{1,0:T(8,128)(2,1)S(1)}, u32[]{:S(2)}, u32[]{:S(2)}) collective-permute-start(bf16[64,128]{1,0:T(8,128)(2,1)S(1)} %get-tuple-element.18), channel_id=1, source_target_pairs={{0,16},{16,32},{32,48},{48,64},{64,80},{80,96},{96,112},{112,128},... | collective-permute-start | bytes 49160 | tf_op jit(solution)/shard_map/ppermute | solution.py:362
  18.5 6.3 %collective-permute-start.1 = (bf16[64,128]{1,0:T(8,128)(2,1)S(1)}, bf16[64,128]{1,0:T(8,128)(2,1)S(1)}, u32[]{:S(2)}, u32[]{:S(2)}) collective-permute-start(bf16[64,128]{1,0:T(8,128)(2,1)S(1)} %get-tuple-element.19), channel_id=1, source_target_pairs={{16,0},{32,16},{48,32},{64,48},{80,64},{96,80},{112,96},{128,112},... | collective-permute-start | bytes 49160 | tf_op jit(solution)/shard_map/ppermute | solution.py:363
  25.7 23.7 %all-to-all-start = ((bf16[8,144,128]{2,1,0:T(8,128)(2,1)}), bf16[8,144,128]{2,1,0:T(8,128)(2,1)S(1)}, u32[]{:S(2)}, u32[]{:S(2)}) async-start(bf16[8,144,128]{2,1,0:T(8,128)(2,1)} %pack.1), calls=%async_computation | async-start | bytes 589824 | tf_op jit(solution)/shard_map/all_to_all | solution.py:372
  34.5 95.7 %all-gather.7.cloned.1.call-start = ((), (), s32[]{:S(2)}) async-start(), calls=%async_computation.5 | async-start | bytes 4718592 | tf_op jit(solution)/shard_map/all_gather | solution.py:383
  34.5 1.0 copy-start.1
  35.6 1.0 copy-start.2
  49.4 79.7 %copy-start.3 = (f32[1024]{0:T(1024)S(1)}, f32[1024]{0:T(1024)}, u32[]{:S(2)}) copy-start(f32[1024]{0:T(1024)} %param.17) | copy-start | bytes 12292
  49.4 12.0 %collective-permute-start.2 = (bf16[8,144,128]{2,1,0:T(8,128)(2,1)S(1)}, bf16[8,144,128]{2,1,0:T(8,128)(2,1)S(1)}, u32[]{:S(2)}, u32[]{:S(2)}) collective-permute-start(bf16[8,144,128]{2,1,0:T(8,128)(2,1)S(1)} %all-to-all-done.own), channel_id=1, source_target_pairs={{0,8},{8,0},{1,9},{9,1},{2,10},{10,2},{3,11},{11,3},{4,12},{12,4},... | collective-permute-start | bytes 884744 | tf_op jit(solution)/shard_map/ppermute | solution.py:27
  54.1 11.0 %collective-permute-start.3 = (bf16[8,144,128]{2,1,0:T(8,128)(2,1)S(1)}, bf16[8,144,128]{2,1,0:T(8,128)(2,1)S(1)}, u32[]{:S(2)}, u32[]{:S(2)}) collective-permute-start(bf16[8,144,128]{2,1,0:T(8,128)(2,1)S(1)} %all-to-all-done.own), channel_id=1, source_target_pairs={{0,16},{16,0},{1,17},{17,1},{2,18},{18,2},{3,19},{19,3},{4,20},{20... | collective-permute-start | bytes 884744 | tf_op jit(solution)/shard_map/ppermute | solution.py:27
  61.3 4.0 %collective-permute-start.4 = (bf16[8,144,128]{2,1,0:T(8,128)(2,1)S(1)}, bf16[8,144,128]{2,1,0:T(8,128)(2,1)S(1)}, u32[]{:S(2)}, u32[]{:S(2)}) collective-permute-start(bf16[8,144,128]{2,1,0:T(8,128)(2,1)S(1)} %collective-permute-done.2.across), channel_id=1, source_target_pairs={{0,16},{16,0},{1,17},{17,1},{2,18},{18,2},{3,19},{19,3},{4,20},{20... | collective-permute-start | bytes 884744 | tf_op jit(solution)/shard_map/ppermute | solution.py:27
  65.3 49.2 %copy-start = (bf16[6528,128]{1,0:T(8,128)(2,1)S(1)}, bf16[6528,128]{1,0:T(8,128)(2,1)}, u32[]{:S(2)}) copy-start(bf16[6528,128]{1,0:T(8,128)(2,1)} %all-gather.5.cloned.1.call-done) | copy-start | bytes 5013508
  94.8 13.3 %collective-permute-start.5 = (bf16[256,512]{1,0:T(8,128)(2,1)S(1)}, bf16[256,512]{1,0:T(8,128)(2,1)S(1)}, u32[]{:S(2)}, u32[]{:S(2)}) collective-permute-start(bf16[256,512]{1,0:T(8,128)(2,1)S(1)} %bn.1.own), channel_id=1, source_target_pairs={{0,8},{8,0},{1,9},{9,1},{2,10},{10,2},{3,11},{11,3},{4,12},{12,4},... | collective-permute-start | bytes 786440 | tf_op jit(solution)/shard_map/ppermute | solution.py:27
  99.1 14.2 %collective-permute-start.6 = (bf16[256,512]{1,0:T(8,128)(2,1)S(1)}, bf16[256,512]{1,0:T(8,128)(2,1)S(1)}, u32[]{:S(2)}, u32[]{:S(2)}) collective-permute-start(bf16[256,512]{1,0:T(8,128)(2,1)S(1)} %bn.1.own), channel_id=1, source_target_pairs={{0,16},{16,0},{1,17},{17,1},{2,18},{18,2},{3,19},{19,3},{4,20},{20... | collective-permute-start | bytes 786440 | tf_op jit(solution)/shard_map/ppermute | solution.py:27
  108.2 6.3 %collective-permute-start.7 = (bf16[256,512]{1,0:T(8,128)(2,1)S(1)}, bf16[256,512]{1,0:T(8,128)(2,1)S(1)}, u32[]{:S(2)}, u32[]{:S(2)}) collective-permute-start(bf16[256,512]{1,0:T(8,128)(2,1)S(1)} %collective-permute-done.5.across), channel_id=1, source_target_pairs={{0,16},{16,0},{1,17},{17,1},{2,18},{18,2},{3,19},{19,3},{4,20},{20... | collective-permute-start | bytes 786440 | tf_op jit(solution)/shard_map/ppermute | solution.py:27
  115.0 10.9 %collective-permute-start.8 = (bf16[256,512]{1,0:T(8,128)(2,1)S(1)}, bf16[256,512]{1,0:T(8,128)(2,1)S(1)}, u32[]{:S(2)}, u32[]{:S(2)}) collective-permute-start(bf16[256,512]{1,0:T(8,128)(2,1)S(1)} %mix.1.own), channel_id=1, source_target_pairs={{0,8},{8,0},{1,9},{9,1},{2,10},{10,2},{3,11},{11,3},{4,12},{12,4},... | collective-permute-start | bytes 786440 | tf_op jit(solution)/shard_map/ppermute | solution.py:27
  119.4 9.9 %collective-permute-start.9 = (bf16[256,512]{1,0:T(8,128)(2,1)S(1)}, bf16[256,512]{1,0:T(8,128)(2,1)S(1)}, u32[]{:S(2)}, u32[]{:S(2)}) collective-permute-start(bf16[256,512]{1,0:T(8,128)(2,1)S(1)} %mix.1.own), channel_id=1, source_target_pairs={{0,16},{16,0},{1,17},{17,1},{2,18},{18,2},{3,19},{19,3},{4,20},{20... | collective-permute-start | bytes 786440 | tf_op jit(solution)/shard_map/ppermute | solution.py:27
  125.9 4.2 %collective-permute-start.10 = (bf16[256,512]{1,0:T(8,128)(2,1)S(1)}, bf16[256,512]{1,0:T(8,128)(2,1)S(1)}, u32[]{:S(2)}, u32[]{:S(2)}) collective-permute-start(bf16[256,512]{1,0:T(8,128)(2,1)S(1)} %collective-permute-done.8.across), channel_id=1, source_target_pairs={{0,16},{16,0},{1,17},{17,1},{2,18},{18,2},{3,19},{19,3},{4,20},{20... | collective-permute-start | bytes 786440 | tf_op jit(solution)/shard_map/ppermute | solution.py:27
  134.9 3.8 %collective-permute-start.11 = (bf16[1024,256]{1,0:T(8,128)(2,1)S(1)}, bf16[1024,256]{1,0:T(8,128)(2,1)S(1)}, u32[]{:S(2)}, u32[]{:S(2)}) collective-permute-start(bf16[1024,256]{1,0:T(8,128)(2,1)S(1)} %get-tuple-element.28), channel_id=1, source_target_pairs={{0,16},{16,0},{1,17},{17,1},{2,18},{18,2},{3,19},{19,3},{4,20},{20... | collective-permute-start | bytes 1572872 | tf_op jit(solution)/shard_map/ppermute | solution.py:27
Sparse Core Ops, SparseCore 0:
  14.0 50.2 all-gather.4
  66.4 59.2 all-gather.6

commit v6 on v5

--- a/solution.py
+++ b/solution.py
@@ -56,31 +56,23 @@
     core, _ = place()
     half = at(32 * core, 32, 32)
     taps, width = depth.shape
-    loads = [
-        pltpu.make_async_copy(depth, small.at[0:taps], sems.at[0]),
-        pltpu.make_async_copy(gain, small.at[32:33], sems.at[1]),
-        pltpu.make_async_copy(shift, small.at[40:41], sems.at[2]),
+    frames = tok.shape[1]
+    pairs = [
+        (depth, small.at[0:taps]),
+        (gain, small.at[32:33]),
+        (shift, small.at[40:41]),
+        (glu.at[0, half], parts.at[0:32]),
+        (glu.at[1, half], parts.at[32:64]),
+        (conv_out.at[half], parts.at[64:96]),
+        (tok.at[:, 0:LANES], first),
+        (tok.at[:, frames - LANES : frames], last),
+        (tok, near),
     ]
-    stores = []
-    for k in range(8):
-        tile = slice(LANES * k, LANES * (k + 1))
-        for v in range(2):
-            stores.append((glu.at[v, half, tile], 64 * k + 32 * v))
-        stores.append((conv_out.at[half, tile], 512 + 32 * k))
-    stores = [
-        pltpu.make_async_copy(ref, out.at[row : row + 32], sems.at[4 + i])
-        for i, (ref, row) in enumerate(stores)
-    ]
-    frames = tok.shape[1]
-    stores += [
-        pltpu.make_async_copy(tok.at[:, 0:LANES], first, sems.at[28]),
-        pltpu.make_async_copy(tok.at[:, frames - LANES : frames], last, sems.at[29]),
-        pltpu.make_async_copy(tok, near, sems.at[30]),
-    ]
-    for copy in loads + stores:
+    loads = [pltpu.make_async_copy(a, b, sems.at[i]) for i, (a, b) in enumerate(pairs)]
+    for copy in loads:
         copy.start()
     table[...] = jnp.zeros_like(table)
-    for copy in loads:
+    for copy in loads[:3]:
         copy.wait()
     table[0:taps, 0:width] = small[0:taps]
     table[taps : taps + 1, 0:width] = small[32:33]
@@ -93,10 +85,14 @@
         piece = rest.astype(BF).astype(F32)
         packed = packed + (piece if i == 0 else pltpu.roll(piece, 32 * i, 1))
         rest = rest - piece
-    parts[...] = packed.astype(BF)
-    final = pltpu.make_async_copy(parts, out.at[768:816], sems.at[3])
+    parts[96:112] = jnp.zeros((16, parts.shape[1]), BF)
+    for i in range(3):
+        parts[96:112, LANES * i : LANES * (i + 1)] = packed[16 * i : 16 * i + 16].astype(BF)
+    for copy in loads[3:6]:
+        copy.wait()
+    final = pltpu.make_async_copy(parts, out, sems.at[9])
     final.start()
-    for copy in stores + [final]:
+    for copy in loads[6:] + [final]:
         copy.wait()
 
 
@@ -137,17 +133,17 @@
 def conv_kernel(
     own, across, beside, far, first, gain,
     conv, stats, par, res,
-    tok, edge, win, weight, glu, small, sems,
+    tok, edge, win, weight, small, sems,
 ):
     loads = [
-        pltpu.make_async_copy(first.at[:, 0:512], glu, sems.at[0]),
-        pltpu.make_async_copy(first.at[:, 768:816], small, sems.at[1]),
+        pltpu.make_async_copy(first.at[:, 0:64], weight, sems.at[0]),
+        pltpu.make_async_copy(first.at[:, 96:112, 0:384], small, sems.at[1]),
     ]
     for copy in loads:
         copy.start()
     core, xhi = place()
     lane = lax.broadcasted_iota(jnp.int32, (16, LANES), 1)
-    nz = glu.shape[0]
+    nz = small.shape[0]
     for near, away, side in ((own, beside, xhi), (across, far, 1 - xhi)):
         for z in range(nz):
             row = side * (64 * nz) + 64 * z
@@ -172,20 +168,18 @@
     for h in range(2):
         total = jnp.zeros((48, LANES), F32)
         for i in range(4):
-            x = small[4 * h + i].astype(F32)
+            x = [small[4 * h + i, :, LANES * k : LANES * (k + 1)] for k in range(3)]
+            x = jnp.concatenate(x, axis=0).astype(F32)
             x = x + (pltpu.roll(x, LANES - 32, 1) + pltpu.roll(x, LANES - 64, 1))
             x = jnp.where(lane < 32, x, 0.0)
             total = total + (x if i == 0 else pltpu.roll(x, 32 * i, 1))
         par[:, LANES * h : LANES * (h + 1)] = total[31:39]
         table.append(total)
-    for z in range(nz):
-        for k in range(8):
-            weight[64 * z : 64 * z + 64, LANES * k : LANES * (k + 1)] = glu[z, 64 * k : 64 * k + 64]
-
+    glu = weight[...].reshape(64 * nz, weight.shape[2])
     scale = gain[...]
     for c in range(3):
         x = edge[...] if c == 2 else tok[:, 256 * c : 256 * (c + 1)].astype(F32)
-        paired = jnp.dot(weight[...], norm_rows(x, scale), preferred_element_type=F32)
+        paired = jnp.dot(glu, norm_rows(x, scale), preferred_element_type=F32)
         cols = x.shape[1]
         paired = paired.reshape(nz, 2, 32, cols)
         gated = (paired[:, 0] * jax.nn.sigmoid(paired[:, 1])).astype(BF).astype(F32)
@@ -226,15 +220,13 @@
 
 
 def merge_kernel(stats, out):
-    mean, square = merged(stats[...], 512)
-    out[:, 0:2] = jnp.broadcast_to(mean[None], (out.shape[0],) + mean.shape)
-    out[:, 2:4] = jnp.broadcast_to(square[None], (out.shape[0],) + square.shape)
-
-
-def bn_kernel(conv, stats, par, out):
-    frames = 8 * conv.shape[0]
-    mean, square = merged(stats[...], frames)
-    scale = lax.rsqrt(square * (1.0 / (frames * stats.shape[0])) + EPS)
+    out[0:2], out[2:4] = merged(stats[...], 512)
+
+
+def bn_kernel(conv, near, away, par, out):
+    frames = 64 * conv.shape[0]
+    mean, square = merged(jnp.stack([near[...], away[...]]), frames)
+    scale = lax.rsqrt(square * (1.0 / (2 * frames)) + EPS)
     for h in range(2):
         cols = slice(LANES * h, LANES * (h + 1))
         value = (conv[:, cols] - mean[h : h + 1]) * (scale[h : h + 1] * par[0:1, cols])
@@ -256,13 +248,10 @@
             whole[at(row, 32, 32), half:] = blk[32 * z : 32 * z + 32, :half]
 
 
-def mix_kernel(own, across, beside, far, blocks, res, out, whole, weight):
+def mix_kernel(own, across, beside, far, blocks, res, out, whole):
     place_blocks(own, across, beside, far, whole)
-    for z in range(8):
-        for k in range(8):
-            tile = slice(LANES * k, LANES * (k + 1))
-            weight[32 * z : 32 * z + 32, tile] = blocks[z, 32 * k : 32 * k + 32]
-    mixed = jnp.dot(weight[...], whole[...], preferred_element_type=F32)
+    weight = blocks[...].reshape(256, blocks.shape[2])
+    mixed = jnp.dot(weight, whole[...], preferred_element_type=F32)
     out[...] = (res[...].astype(F32) + mixed).astype(BF)
 
 
@@ -330,7 +319,7 @@
     first, tok, head, tail = pl.pallas_call(
         weight_kernel,
         out_shape=(
-            shape((816, LANES), BF),
+            shape((112, full), BF),
             shape((width, frames), BF),
             shape((width, LANES), BF),
             shape((width, LANES), BF),
@@ -339,9 +328,9 @@
         out_specs=(HBM, VMEM, VMEM, VMEM),
         scratch_shapes=[
             pltpu.VMEM((48, LANES), F32),
-            pltpu.VMEM((48, LANES), BF),
+            pltpu.VMEM((112, full), BF),
             pltpu.VMEM((48, width), F32),
-            pltpu.SemaphoreType.DMA((31,)),
+            pltpu.SemaphoreType.DMA((10,)),
         ],
         compiler_params=PARAMS,
         name="weights",
@@ -387,7 +376,7 @@
         conv_kernel,
         out_shape=(
             shape((2 * run, 256), F32),
-            shape((nz, 4, LANES), F32),
+            shape((lax.axis_size((Y, Z)), 4, LANES), F32),
             shape((8, 256), F32),
             shape((256, 2 * run), BF),
         ),
@@ -397,43 +386,41 @@
             pltpu.VMEM((full, 2 * run), BF),
             pltpu.VMEM((full, LANES), F32),
             pltpu.VMEM((2, run + 40, 256), F32),
-            pltpu.VMEM((512, full), BF),
-            pltpu.VMEM((nz, 512, LANES), BF),
-            pltpu.VMEM((nz, 48, LANES), BF),
+            pltpu.VMEM((nz, 64, full), BF),
+            pltpu.VMEM((nz, 16, 3 * LANES), BF),
             pltpu.SemaphoreType.DMA((2,)),
         ],
         compiler_params=PARAMS,
         name="conv",
     )(*whole, *in_hbm(first), ln_conv_gain[:, None])
-    stats = lax.all_to_all(stats, Z, 0, 0, tiled=True)
+    stats = lax.all_to_all(stats, (Y, Z), 0, 0, tiled=True)
     stats = pl.pallas_call(
         merge_kernel,
-        out_shape=shape((lax.axis_size((XLO, Y)), 4, LANES), F32),
+        out_shape=shape((4, LANES), F32),
         in_specs=[VMEM],
         out_specs=VMEM,
         compiler_params=PARAMS,
         name="merge",
     )(stats)
-    stats = lax.all_to_all(stats, (XLO, Y), 0, 0, tiled=True)
     activated = pl.pallas_call(
         bn_kernel,
         out_shape=shape((256, 2 * run), BF),
-        in_specs=[VMEM] * 3,
+        in_specs=[VMEM] * 4,
         out_specs=VMEM,
         compiler_params=PARAMS,
         name="bn",
-    )(conv, stats, par)
+    )(conv, stats, swap(stats, XLO), par)
     block = pl.pallas_call(
         mix_kernel,
         out_shape=shape((256, 2 * run), BF),
         grid=(1,),
         in_specs=[VMEM] * 4
         + [
-            pl.BlockSpec((nz, 256, LANES), lambda i: (0, 2, 0)),
+            pl.BlockSpec((nz, 32, full), lambda i: (0, 2, 0)),
             VMEM,
         ],
         out_specs=VMEM,
-        scratch_shapes=[pltpu.VMEM((full, 2 * run), BF), pltpu.VMEM((256, full), BF)],
+        scratch_shapes=[pltpu.VMEM((full, 2 * run), BF)],
         compiler_params=PARAMS,
         name="mix",
     )(*group_gather(activated), first, res)

time: 166 us -> 164 us (0.988)
  Pallas kernels: 21.1 us -> 15.1 us
  waiting for transfers between devices: 25.6 us -> 28.2 us
  starting transfers between devices: 59.2 us -> 61.2 us
    pallas_call x2, Pallas kernels: 7.37 us -> 1.88 us  [the longest x1 1.74 us: body(): pl.pallas_call(weight_kernel, out_shape=(shape((112, full), BF), shape((w...]
    ppermute x10 -> x11, starting transfers between devices: 40.3 us -> 42.3 us  [swap(): return lax.ppermute(x, axis, [(0, 1), (1, 0)])]
    all_to_all x2 -> x1, blocking collectives: 23.7 us -> 21.9 us  [body(): stats = lax.all_to_all(stats, (Y, Z), 0, 0, tiled=True)]
    ppermute x10 -> x11, waiting for transfers between devices: 13 us -> 14.6 us  [swap(): return lax.ppermute(x, axis, [(0, 1), (1, 0)])]
  transfers between devices with their start and end apart: 15 -> 16, of which waited for: 8 -> 10; matrix products, arithmetic and copies ran while one was open for 1% -> 0% of each run, Pallas kernels for 5% -> 5%
where the time goes in v6:
time: 164 us; the launch traced here: 162 us
  starting transfers between devices  61.2 us (37%)
  blocking collectives  41.7 us (25%)
  waiting for transfers between devices  28.2 us (17%)
  Pallas kernels  15.1 us (9%)
  between operations  13.6 us (8%)
  local copies, waits for them, and re-layouts  2.53 us (2%)
    ppermute x11, starting transfers between devices, swap(): return lax.ppermute(x, axis, [(0, 1), (1, 0)])  42.3 us
    all_to_all x1, blocking collectives, body(): stats = lax.all_to_all(stats, (Y, Z), 0, 0, tiled=True)  21.9 us
    all_to_all x1, blocking collectives, body(): lax.all_to_all(keep.reshape(2 * nz, width, run), (XHI, Z), 0, 0, tiled=True)  19.7 us
    ppermute x11, waiting for transfers between devices, swap(): return lax.ppermute(x, axis, [(0, 1), (1, 0)])  14.6 us
    all_to_all x1, waiting for transfers between devices, body(): parts = lax.all_to_all(parts, Z, 0, 0, tiled=True)  11.6 us
    all_to_all x1, starting transfers between devices, body(): parts = lax.all_to_all(parts, Z, 0, 0, tiled=True)  8.79 us
    ppermute x1, starting transfers between devices, body(): right = lax.ppermute(head, (XLO, Y, CORE), [(j, i) for i, j in up])  5.48 us
    pallas_call x1, Pallas kernels, body(): pl.pallas_call(conv_kernel, out_shape=(shape((2 * run, 256), F32), shape(...  5.16 us
  transfers between devices with their start and end apart: 16, of which 10 were waited for; matrix products, arithmetic and copies ran while one was open for 0% of the time, Pallas kernels for 5%

profile of v6, /device:TPU:1, one launch (start us, length us, event | category | flops | bytes accessed | tf_op | source)
XLA Modules:
  0.0 162.5 jit_solution(11534650887212736785)
XLA Ops:
  6.5 1.7 %weights.1 = (bf16[112,1024]{1,0:T(8,128)(2,1)}, bf16[64,2048]{1,0:T(8,128)(2,1)S(1)}, bf16[64,128]{1,0:T(8,128)(2,1)S(1)}, bf16[64,128]{1,0:T(8,128)(2,1)S(1)}) custom-call(bf16[2,64,1024]{2,1,0:T(8,128)(2,1)} %bitcast.15, bf16[64,1024]{1,0:T(8,128)(2,1)} %bitcast.17, f32[31,64]{1,0:T(8,128)} %depth.1, f32[1,64]{1,0:T(1,128)} %bitcast.20, ...), custom_call_target="tpu_custom_call" | custom-call | tf_op jit(solution)/shard_map/weights/pallas_call | solution.py:319
  8.3 4.6 %collective-permute-start = (bf16[64,128]{1,0:T(8,128)(2,1)S(1)}, bf16[64,128]{1,0:T(8,128)(2,1)S(1)}, u32[]{:S(2)}, u32[]{:S(2)}) collective-permute-start(bf16[64,128]{1,0:T(8,128)(2,1)S(1)} %get-tuple-element.18), channel_id=1, source_target_pairs={{0,16},{16,32},{32,48},{48,64},{64,80},{80,96},{96,112},{112,128},... | collective-permute-start | bytes 49160 | tf_op jit(solution)/shard_map/ppermute | solution.py:351
  12.9 5.5 %collective-permute-start.1 = (bf16[64,128]{1,0:T(8,128)(2,1)S(1)}, bf16[64,128]{1,0:T(8,128)(2,1)S(1)}, u32[]{:S(2)}, u32[]{:S(2)}) collective-permute-start(bf16[64,128]{1,0:T(8,128)(2,1)S(1)} %get-tuple-element.19), channel_id=1, source_target_pairs={{16,0},{32,16},{48,32},{64,48},{80,64},{96,80},{112,96},{128,112},... | collective-permute-start | bytes 49160 | tf_op jit(solution)/shard_map/ppermute | solution.py:352
  19.2 0.9 pack.1
  20.1 8.8 %all-to-all-start = ((bf16[8,144,128]{2,1,0:T(8,128)(2,1)}), bf16[8,144,128]{2,1,0:T(8,128)(2,1)S(1)}, u32[]{:S(2)}, u32[]{:S(2)}) async-start(bf16[8,144,128]{2,1,0:T(8,128)(2,1)} %pack.1), calls=%async_computation | async-start | bytes 589824 | tf_op jit(solution)/shard_map/all_to_all | solution.py:361
  28.9 1.0 copy-done.1
  30.0 1.0 copy-done.2
  31.0 1.0 blocks.1
  32.0 11.6 %all-to-all-done.own = bf16[8,144,128]{2,1,0:T(8,128)(2,1)S(1)} async-done(((bf16[8,144,128]{2,1,0:T(8,128)(2,1)}), bf16[8,144,128]{2,1,0:T(8,128)(2,1)S(1)}, u32[]{:S(2)}, u32[]{:S(2)}) %all-to-all-start) | async-done | bytes 294944 | tf_op jit(solution)/shard_map/all_to_all | solution.py:361
  43.7 4.7 %collective-permute-start.2 = (bf16[8,144,128]{2,1,0:T(8,128)(2,1)S(1)}, bf16[8,144,128]{2,1,0:T(8,128)(2,1)S(1)}, u32[]{:S(2)}, u32[]{:S(2)}) collective-permute-start(bf16[8,144,128]{2,1,0:T(8,128)(2,1)S(1)} %all-to-all-done.own), channel_id=1, source_target_pairs={{0,8},{8,0},{1,9},{9,1},{2,10},{10,2},{3,11},{11,3},{4,12},{12,4},... | collective-permute-start | bytes 884744 | tf_op jit(solution)/shard_map/ppermute | solution.py:27
  48.3 1.9 %collective-permute-start.3 = (bf16[8,144,128]{2,1,0:T(8,128)(2,1)S(1)}, bf16[8,144,128]{2,1,0:T(8,128)(2,1)S(1)}, u32[]{:S(2)}, u32[]{:S(2)}) collective-permute-start(bf16[8,144,128]{2,1,0:T(8,128)(2,1)S(1)} %all-to-all-done.own), channel_id=1, source_target_pairs={{0,16},{16,0},{1,17},{17,1},{2,18},{18,2},{3,19},{19,3},{4,20},{20... | collective-permute-start | bytes 884744 | tf_op jit(solution)/shard_map/ppermute | solution.py:27
  50.3 4.6 %collective-permute-done.2.across = bf16[8,144,128]{2,1,0:T(8,128)(2,1)S(1)} collective-permute-done((bf16[8,144,128]{2,1,0:T(8,128)(2,1)S(1)}, bf16[8,144,128]{2,1,0:T(8,128)(2,1)S(1)}, u32[]{:S(2)}, u32[]{:S(2)}) %collective-permute-start.2) | collective-permute-done | bytes 294944 | tf_op jit(solution)/shard_map/ppermute | solution.py:27
  54.9 1.9 %collective-permute-start.4 = (bf16[8,144,128]{2,1,0:T(8,128)(2,1)S(1)}, bf16[8,144,128]{2,1,0:T(8,128)(2,1)S(1)}, u32[]{:S(2)}, u32[]{:S(2)}) collective-permute-start(bf16[8,144,128]{2,1,0:T(8,128)(2,1)S(1)} %collective-permute-done.2.across), channel_id=1, source_target_pairs={{0,16},{16,0},{1,17},{17,1},{2,18},{18,2},{3,19},{19,3},{4,20},{20... | collective-permute-start | bytes 884744 | tf_op jit(solution)/shard_map/ppermute | solution.py:27
  57.1 1.3 collective-permute-done.4.far
  58.4 1.1 all-gather.5.cloned.1.call-done
  59.5 5.2 %conv.1 = (f32[512,256]{1,0:T(8,128)S(1)}, f32[64,4,128]{2,1,0:T(4,128)S(1)}, f32[8,256]{1,0:T(8,128)S(1)}, bf16[256,512]{1,0:T(8,128)(2,1)S(1)}) custom-call(bf16[8,144,128]{2,1,0:T(8,128)(2,1)S(1)} %all-to-all-done.own, bf16[8,144,128]{2,1,0:T(8,128)(2,1)S(1)} %collective-permute-done.2.across, bf16[8,144,128]{2,1,0:T(8,128)(2,1)S(1)} %collective-permute-done.3.beside, ...), custom_call_target="tpu_custom_call" | custom-call | tf_op jit(solution)/shard_map/conv/pallas_call | solution.py:375
  64.7 21.9 %all_to_all.15.stats = f32[64,4,128]{2,1,0:T(4,128)S(1)} all-to-all(f32[64,4,128]{2,1,0:T(4,128)S(1)} %get-tuple-element.23), channel_id=1, replica_groups=mesh['xlo'=2,'y'=8,'core'=2,'xhi'=2,'z'=8] {'y','z'}, dimensions={0} | all-to-all | bytes 262144 | tf_op jit(solution)/shard_map/all_to_all | solution.py:396
  86.7 3.1 %collective-permute-start.5 = (f32[4,128]{1,0:T(4,128)S(1)}, f32[4,128]{1,0:T(4,128)S(1)}, u32[]{:S(2)}, u32[]{:S(2)}) collective-permute-start(f32[4,128]{1,0:T(4,128)S(1)} %merge.1.near), channel_id=1, source_target_pairs={{0,256},{256,0},{1,257},{257,1},{2,258},{258,2},{3,259},{259,3},{4... | collective-permute-start | bytes 6152 | tf_op jit(solution)/shard_map/ppermute | solution.py:27
  89.9 1.6 collective-permute-done.5.away
  91.7 4.6 %collective-permute-start.6 = (bf16[256,512]{1,0:T(8,128)(2,1)S(1)}, bf16[256,512]{1,0:T(8,128)(2,1)S(1)}, u32[]{:S(2)}, u32[]{:S(2)}) collective-permute-start(bf16[256,512]{1,0:T(8,128)(2,1)S(1)} %bn.1.own), channel_id=1, source_target_pairs={{0,8},{8,0},{1,9},{9,1},{2,10},{10,2},{3,11},{11,3},{4,12},{12,4},... | collective-permute-start | bytes 786440 | tf_op jit(solution)/shard_map/ppermute | solution.py:27
  96.3 8.7 %collective-permute-start.7 = (bf16[256,512]{1,0:T(8,128)(2,1)S(1)}, bf16[256,512]{1,0:T(8,128)(2,1)S(1)}, u32[]{:S(2)}, u32[]{:S(2)}) collective-permute-start(bf16[256,512]{1,0:T(8,128)(2,1)S(1)} %bn.1.own), channel_id=1, source_target_pairs={{0,16},{16,0},{1,17},{17,1},{2,18},{18,2},{3,19},{19,3},{4,20},{20... | collective-permute-start | bytes 786440 | tf_op jit(solution)/shard_map/ppermute | solution.py:27
  105.1 4.5 %collective-permute-start.8 = (bf16[256,512]{1,0:T(8,128)(2,1)S(1)}, bf16[256,512]{1,0:T(8,128)(2,1)S(1)}, u32[]{:S(2)}, u32[]{:S(2)}) collective-permute-start(bf16[256,512]{1,0:T(8,128)(2,1)S(1)} %collective-permute-done.6.across), channel_id=1, source_target_pairs={{0,16},{16,0},{1,17},{17,1},{2,18},{18,2},{3,19},{19,3},{4,20},{20... | collective-permute-start | bytes 786440 | tf_op jit(solution)/shard_map/ppermute | solution.py:27
  109.6 1.1 collective-permute-done.8.far
  111.3 4.9 %collective-permute-start.9 = (bf16[256,512]{1,0:T(8,128)(2,1)S(1)}, bf16[256,512]{1,0:T(8,128)(2,1)S(1)}, u32[]{:S(2)}, u32[]{:S(2)}) collective-permute-start(bf16[256,512]{1,0:T(8,128)(2,1)S(1)} %mix.1.own), channel_id=1, source_target_pairs={{0,8},{8,0},{1,9},{9,1},{2,10},{10,2},{3,11},{11,3},{4,12},{12,4},... | collective-permute-start | bytes 786440 | tf_op jit(solution)/shard_map/ppermute | solution.py:27
  116.2 2.6 %collective-permute-start.10 = (bf16[256,512]{1,0:T(8,128)(2,1)S(1)}, bf16[256,512]{1,0:T(8,128)(2,1)S(1)}, u32[]{:S(2)}, u32[]{:S(2)}) collective-permute-start(bf16[256,512]{1,0:T(8,128)(2,1)S(1)} %mix.1.own), channel_id=1, source_target_pairs={{0,16},{16,0},{1,17},{17,1},{2,18},{18,2},{3,19},{19,3},{4,20},{20... | collective-permute-start | bytes 786440 | tf_op jit(solution)/shard_map/ppermute | solution.py:27
  118.8 3.5 %collective-permute-done.9.across = bf16[256,512]{1,0:T(8,128)(2,1)S(1)} collective-permute-done((bf16[256,512]{1,0:T(8,128)(2,1)S(1)}, bf16[256,512]{1,0:T(8,128)(2,1)S(1)}, u32[]{:S(2)}, u32[]{:S(2)}) %collective-permute-start.9) | collective-permute-done | bytes 262176 | tf_op jit(solution)/shard_map/ppermute | solution.py:27
  122.3 3.0 %collective-permute-start.11 = (bf16[256,512]{1,0:T(8,128)(2,1)S(1)}, bf16[256,512]{1,0:T(8,128)(2,1)S(1)}, u32[]{:S(2)}, u32[]{:S(2)}) collective-permute-start(bf16[256,512]{1,0:T(8,128)(2,1)S(1)} %collective-permute-done.9.across), channel_id=1, source_target_pairs={{0,16},{16,0},{1,17},{17,1},{2,18},{18,2},{3,19},{19,3},{4,20},{20... | collective-permute-start | bytes 786440 | tf_op jit(solution)/shard_map/ppermute | solution.py:27
  125.6 0.9 collective-permute-done.11.far
  126.5 4.7 %ff.1 = (f32[1024,256]{1,0:T(8,128)S(1)}, bf16[1024,256]{1,0:T(8,128)(2,1)S(1)}) custom-call(bf16[256,512]{1,0:T(8,128)(2,1)S(1)} %mix.1.own, bf16[256,512]{1,0:T(8,128)(2,1)S(1)} %collective-permute-done.9.across, bf16[256,512]{1,0:T(8,128)(2,1)S(1)} %collective-permute-done.10.beside, bf16[256,512]{1,0:T(8,128)(2,1)S(1)} %collective-permute-done.11.far, ...), custom_call_target="tpu_custom_call" | custom-call | tf_op jit(solution)/shard_map/ff/pallas_call | solution.py:427
  131.2 2.3 %collective-permute-start.12 = (bf16[1024,256]{1,0:T(8,128)(2,1)S(1)}, bf16[1024,256]{1,0:T(8,128)(2,1)S(1)}, u32[]{:S(2)}, u32[]{:S(2)}) collective-permute-start(bf16[1024,256]{1,0:T(8,128)(2,1)S(1)} %get-tuple-element.28), channel_id=1, source_target_pairs={{0,16},{16,0},{1,17},{17,1},{2,18},{18,2},{3,19},{19,3},{4,20},{20... | collective-permute-start | bytes 1572872 | tf_op jit(solution)/shard_map/ppermute | solution.py:27
  133.5 1.5 collective-permute-done.12
  135.1 19.7 %all_to_all.16.parts = bf16[16,64,256]{2,1,0:T(8,128)(2,1)S(1)} all-to-all(bf16[16,64,256]{2,1,0:T(8,128)(2,1)S(1)} %bitcast.14), channel_id=1, replica_groups=mesh['xlo'=2,'y'=8,'core'=2,'xhi'=2,'z'=8] {'xhi','z'}, dimensions={0} | all-to-all | bytes 1048576 | tf_op jit(solution)/shard_map/all_to_all | solution.py:443
  (26 shorter events, 3.1 us)
Async XLA Ops:
  6.5 50.3 %copy-start.3 = (f32[1024]{0:T(1024)S(1)}, f32[1024]{0:T(1024)}, u32[]{:S(2)}) copy-start(f32[1024]{0:T(1024)} %param.11) | copy-start | bytes 12292
  6.5 53.0 %all-gather.5.cloned.1.call-start = ((), (), s32[]{:S(2)}) async-start(), calls=%async_computation.3 | async-start | bytes 2064384 | tf_op jit(solution)/shard_map/all_gather | solution.py:347
  8.3 10.1 %collective-permute-start = (bf16[64,128]{1,0:T(8,128)(2,1)S(1)}, bf16[64,128]{1,0:T(8,128)(2,1)S(1)}, u32[]{:S(2)}, u32[]{:S(2)}) collective-permute-start(bf16[64,128]{1,0:T(8,128)(2,1)S(1)} %get-tuple-element.18), channel_id=1, source_target_pairs={{0,16},{16,32},{32,48},{48,64},{64,80},{80,96},{96,112},{112,128},... | collective-permute-start | bytes 49160 | tf_op jit(solution)/shard_map/ppermute | solution.py:351
  12.9 6.3 %collective-permute-start.1 = (bf16[64,128]{1,0:T(8,128)(2,1)S(1)}, bf16[64,128]{1,0:T(8,128)(2,1)S(1)}, u32[]{:S(2)}, u32[]{:S(2)}) collective-permute-start(bf16[64,128]{1,0:T(8,128)(2,1)S(1)} %get-tuple-element.19), channel_id=1, source_target_pairs={{16,0},{32,16},{48,32},{64,48},{80,64},{96,80},{112,96},{128,112},... | collective-permute-start | bytes 49160 | tf_op jit(solution)/shard_map/ppermute | solution.py:352
  20.1 23.6 %all-to-all-start = ((bf16[8,144,128]{2,1,0:T(8,128)(2,1)}), bf16[8,144,128]{2,1,0:T(8,128)(2,1)S(1)}, u32[]{:S(2)}, u32[]{:S(2)}) async-start(bf16[8,144,128]{2,1,0:T(8,128)(2,1)} %pack.1), calls=%async_computation | async-start | bytes 589824 | tf_op jit(solution)/shard_map/all_to_all | solution.py:361
  28.9 97.6 %all-gather.7.cloned.1.call-start = ((), (), s32[]{:S(2)}) async-start(), calls=%async_computation.4 | async-start | bytes 4718592 | tf_op jit(solution)/shard_map/all_gather | solution.py:372
  28.9 1.0 copy-start.1
  30.0 1.0 copy-start.2
  43.7 11.2 %collective-permute-start.2 = (bf16[8,144,128]{2,1,0:T(8,128)(2,1)S(1)}, bf16[8,144,128]{2,1,0:T(8,128)(2,1)S(1)}, u32[]{:S(2)}, u32[]{:S(2)}) collective-permute-start(bf16[8,144,128]{2,1,0:T(8,128)(2,1)S(1)} %all-to-all-done.own), channel_id=1, source_target_pairs={{0,8},{8,0},{1,9},{9,1},{2,10},{10,2},{3,11},{11,3},{4,12},{12,4},... | collective-permute-start | bytes 884744 | tf_op jit(solution)/shard_map/ppermute | solution.py:27
  48.3 8.7 %collective-permute-start.3 = (bf16[8,144,128]{2,1,0:T(8,128)(2,1)S(1)}, bf16[8,144,128]{2,1,0:T(8,128)(2,1)S(1)}, u32[]{:S(2)}, u32[]{:S(2)}) collective-permute-start(bf16[8,144,128]{2,1,0:T(8,128)(2,1)S(1)} %all-to-all-done.own), channel_id=1, source_target_pairs={{0,16},{16,0},{1,17},{17,1},{2,18},{18,2},{3,19},{19,3},{4,20},{20... | collective-permute-start | bytes 884744 | tf_op jit(solution)/shard_map/ppermute | solution.py:27
  54.9 3.5 %collective-permute-start.4 = (bf16[8,144,128]{2,1,0:T(8,128)(2,1)S(1)}, bf16[8,144,128]{2,1,0:T(8,128)(2,1)S(1)}, u32[]{:S(2)}, u32[]{:S(2)}) collective-permute-start(bf16[8,144,128]{2,1,0:T(8,128)(2,1)S(1)} %collective-permute-done.2.across), channel_id=1, source_target_pairs={{0,16},{16,0},{1,17},{17,1},{2,18},{18,2},{3,19},{19,3},{4,20},{20... | collective-permute-start | bytes 884744 | tf_op jit(solution)/shard_map/ppermute | solution.py:27
  57.0 68.3 %copy-start.4 = (f32[1024]{0:T(1024)S(1)}, f32[1024]{0:T(1024)}, u32[]{:S(2)}) copy-start(f32[1024]{0:T(1024)} %param.17) | copy-start | bytes 12292
  59.5 51.2 %copy-start = (bf16[896,1024]{1,0:T(8,128)(2,1)S(1)}, bf16[896,1024]{1,0:T(8,128)(2,1)}, u32[]{:S(2)}) copy-start(bf16[896,1024]{1,0:T(8,128)(2,1)} %all-gather.5.cloned.1.call-done) | copy-start | bytes 5505028
  86.7 4.7 %collective-permute-start.5 = (f32[4,128]{1,0:T(4,128)S(1)}, f32[4,128]{1,0:T(4,128)S(1)}, u32[]{:S(2)}, u32[]{:S(2)}) collective-permute-start(f32[4,128]{1,0:T(4,128)S(1)} %merge.1.near), channel_id=1, source_target_pairs={{0,256},{256,0},{1,257},{257,1},{2,258},{258,2},{3,259},{259,3},{4... | collective-permute-start | bytes 6152 | tf_op jit(solution)/shard_map/ppermute | solution.py:27
  91.7 13.4 %collective-permute-start.6 = (bf16[256,512]{1,0:T(8,128)(2,1)S(1)}, bf16[256,512]{1,0:T(8,128)(2,1)S(1)}, u32[]{:S(2)}, u32[]{:S(2)}) collective-permute-start(bf16[256,512]{1,0:T(8,128)(2,1)S(1)} %bn.1.own), channel_id=1, source_target_pairs={{0,8},{8,0},{1,9},{9,1},{2,10},{10,2},{3,11},{11,3},{4,12},{12,4},... | collective-permute-start | bytes 786440 | tf_op jit(solution)/shard_map/ppermute | solution.py:27
  96.3 13.3 %collective-permute-start.7 = (bf16[256,512]{1,0:T(8,128)(2,1)S(1)}, bf16[256,512]{1,0:T(8,128)(2,1)S(1)}, u32[]{:S(2)}, u32[]{:S(2)}) collective-permute-start(bf16[256,512]{1,0:T(8,128)(2,1)S(1)} %bn.1.own), channel_id=1, source_target_pairs={{0,16},{16,0},{1,17},{17,1},{2,18},{18,2},{3,19},{19,3},{4,20},{20... | collective-permute-start | bytes 786440 | tf_op jit(solution)/shard_map/ppermute | solution.py:27
  105.1 5.7 %collective-permute-start.8 = (bf16[256,512]{1,0:T(8,128)(2,1)S(1)}, bf16[256,512]{1,0:T(8,128)(2,1)S(1)}, u32[]{:S(2)}, u32[]{:S(2)}) collective-permute-start(bf16[256,512]{1,0:T(8,128)(2,1)S(1)} %collective-permute-done.6.across), channel_id=1, source_target_pairs={{0,16},{16,0},{1,17},{17,1},{2,18},{18,2},{3,19},{19,3},{4,20},{20... | collective-permute-start | bytes 786440 | tf_op jit(solution)/shard_map/ppermute | solution.py:27
  111.3 11.0 %collective-permute-start.9 = (bf16[256,512]{1,0:T(8,128)(2,1)S(1)}, bf16[256,512]{1,0:T(8,128)(2,1)S(1)}, u32[]{:S(2)}, u32[]{:S(2)}) collective-permute-start(bf16[256,512]{1,0:T(8,128)(2,1)S(1)} %mix.1.own), channel_id=1, source_target_pairs={{0,8},{8,0},{1,9},{9,1},{2,10},{10,2},{3,11},{11,3},{4,12},{12,4},... | collective-permute-start | bytes 786440 | tf_op jit(solution)/shard_map/ppermute | solution.py:27
  116.2 9.4 %collective-permute-start.10 = (bf16[256,512]{1,0:T(8,128)(2,1)S(1)}, bf16[256,512]{1,0:T(8,128)(2,1)S(1)}, u32[]{:S(2)}, u32[]{:S(2)}) collective-permute-start(bf16[256,512]{1,0:T(8,128)(2,1)S(1)} %mix.1.own), channel_id=1, source_target_pairs={{0,16},{16,0},{1,17},{17,1},{2,18},{18,2},{3,19},{19,3},{4,20},{20... | collective-permute-start | bytes 786440 | tf_op jit(solution)/shard_map/ppermute | solution.py:27
  122.3 4.2 %collective-permute-start.11 = (bf16[256,512]{1,0:T(8,128)(2,1)S(1)}, bf16[256,512]{1,0:T(8,128)(2,1)S(1)}, u32[]{:S(2)}, u32[]{:S(2)}) collective-permute-start(bf16[256,512]{1,0:T(8,128)(2,1)S(1)} %collective-permute-done.9.across), channel_id=1, source_target_pairs={{0,16},{16,0},{1,17},{17,1},{2,18},{18,2},{3,19},{19,3},{4,20},{20... | collective-permute-start | bytes 786440 | tf_op jit(solution)/shard_map/ppermute | solution.py:27
  131.2 3.8 %collective-permute-start.12 = (bf16[1024,256]{1,0:T(8,128)(2,1)S(1)}, bf16[1024,256]{1,0:T(8,128)(2,1)S(1)}, u32[]{:S(2)}, u32[]{:S(2)}) collective-permute-start(bf16[1024,256]{1,0:T(8,128)(2,1)S(1)} %get-tuple-element.28), channel_id=1, source_target_pairs={{0,16},{16,0},{1,17},{17,1},{2,18},{18,2},{3,19},{19,3},{4,20},{20... | collective-permute-start | bytes 1572872 | tf_op jit(solution)/shard_map/ppermute | solution.py:27
Sparse Core Ops, SparseCore 0:
  9.4 50.0 all-gather.4
  61.6 62.8 all-gather.6

commit v7 on v6

--- a/solution.py
+++ b/solution.py
@@ -211,22 +211,15 @@
         stats[:, 2 + h : 3 + h, :] = jnp.broadcast_to(square[None], (n, 1, LANES))
 
 
-def merged(stats, count):
-    total = jnp.sum(stats, axis=0)
-    mean = total * (1.0 / stats.shape[0])
-    apart = stats - mean[None]
+def bn_kernel(conv, stats, par, out):
+    n, frames = stats.shape[0], conv.shape[0]
+    s = stats[...]
+    total = jnp.sum(s, axis=0)
+    mean = total * (1.0 / n)
+    apart = s - mean[None]
     apart = jnp.sum(apart * apart, axis=0)
-    return mean[0:2], total[2:4] + count * apart[0:2]
-
-
-def merge_kernel(stats, out):
-    out[0:2], out[2:4] = merged(stats[...], 512)
-
-
-def bn_kernel(conv, near, away, par, out):
-    frames = 64 * conv.shape[0]
-    mean, square = merged(jnp.stack([near[...], away[...]]), frames)
-    scale = lax.rsqrt(square * (1.0 / (2 * frames)) + EPS)
+    square = total[2:4] + frames * apart[0:2]
+    scale = lax.rsqrt(square * (1.0 / (n * frames)) + EPS)
     for h in range(2):
         cols = slice(LANES * h, LANES * (h + 1))
         value = (conv[:, cols] - mean[h : h + 1]) * (scale[h : h + 1] * par[0:1, cols])
@@ -255,24 +248,27 @@
     out[...] = (res[...].astype(F32) + mixed).astype(BF)
 
 
-def ff_kernel(
-    own, across, beside, far, blocks, gain,
-    keep, give,
-    whole, normed, hidden, w, sems,
-):
+def norm_kernel(own, across, beside, far, gain, near, normed, whole):
+    place_blocks(own, across, beside, far, whole)
+    half = normed.shape[1] // 2
+    near[...] = whole[:, :half]
+    for c in range(2):
+        cols = slice(half * c, half * (c + 1))
+        normed[:, cols] = norm_rows(whole[:, cols].astype(F32), gain[...])
+
+
+def ff_kernel(near, normed, blocks, keep, give, hidden, w, sems):
     loads = [
-        pltpu.make_async_copy(blocks.at[2 * i : 2 * i + 2, 0:8], w.at[2 * i : 2 * i + 2, 0:8], sems.at[i])
+        pltpu.make_async_copy(
+            blocks.at[2 * i : 2 * i + 2, 0:8], w.at[2 * i : 2 * i + 2, 0:8], sems.at[i]
+        )
         for i in range(4)
     ]
     loads.append(pltpu.make_async_copy(blocks.at[:, 8:16], w.at[:, 8:16], sems.at[4]))
     for copy in loads:
         copy.start()
     xhi = place()[1]
-    place_blocks(own, across, beside, far, whole)
-    half = 256
-    for c in range(2):
-        cols = slice(half * c, half * (c + 1))
-        normed[:, cols] = norm_rows(whole[:, cols].astype(F32), gain[...])
+    half = normed.shape[1] // 2
     for z in range(0, 8, 2):
         loads[z // 2].wait()
         rows = [jnp.concatenate([w[z + i, k] for k in range(8)], axis=1) for i in range(2)]
@@ -288,7 +284,7 @@
         )
         rows = slice(LANES * k, LANES * (k + 2))
         mine = jnp.where(xhi == k // 4, 1.0, 0.0)
-        keep[rows, :] = 0.5 * value[:, :half] + mine * whole[rows, :half].astype(F32)
+        keep[rows, :] = 0.5 * value[:, :half] + mine * near[rows, :].astype(F32)
         give[rows, :] = (0.5 * value[:, half:]).astype(BF)
 
 
@@ -376,7 +372,7 @@
         conv_kernel,
         out_shape=(
             shape((2 * run, 256), F32),
-            shape((lax.axis_size((Y, Z)), 4, LANES), F32),
+            shape((lax.axis_size((XLO, Y, Z)), 4, LANES), F32),
             shape((8, 256), F32),
             shape((256, 2 * run), BF),
         ),
@@ -393,23 +389,15 @@
         compiler_params=PARAMS,
         name="conv",
     )(*whole, *in_hbm(first), ln_conv_gain[:, None])
-    stats = lax.all_to_all(stats, (Y, Z), 0, 0, tiled=True)
-    stats = pl.pallas_call(
-        merge_kernel,
-        out_shape=shape((4, LANES), F32),
-        in_specs=[VMEM],
-        out_specs=VMEM,
-        compiler_params=PARAMS,
-        name="merge",
-    )(stats)
+    stats = lax.all_to_all(stats, (XLO, Y, Z), 0, 0, tiled=True)
     activated = pl.pallas_call(
         bn_kernel,
         out_shape=shape((256, 2 * run), BF),
-        in_specs=[VMEM] * 4,
+        in_specs=[VMEM] * 3,
         out_specs=VMEM,
         compiler_params=PARAMS,
         name="bn",
-    )(conv, stats, swap(stats, XLO), par)
+    )(conv, stats, par)
     block = pl.pallas_call(
         mix_kernel,
         out_shape=shape((256, 2 * run), BF),
@@ -424,21 +412,28 @@
         compiler_params=PARAMS,
         name="mix",
     )(*group_gather(activated), first, res)
+    near, normed = pl.pallas_call(
+        norm_kernel,
+        out_shape=(shape((full, run), BF), shape((full, 2 * run), BF)),
+        in_specs=[VMEM] * 5,
+        out_specs=(VMEM,) * 2,
+        scratch_shapes=[pltpu.VMEM((full, 2 * run), BF)],
+        compiler_params=PARAMS,
+        name="norm",
+    )(*group_gather(block), ln_ff_gain[:, None])
     keep, give = pl.pallas_call(
         ff_kernel,
         out_shape=(shape((full, run), F32), shape((full, run), BF)),
-        in_specs=[VMEM] * 4 + [HBM, VMEM],
+        in_specs=[VMEM] * 2 + [HBM],
         out_specs=(VMEM,) * 2,
         scratch_shapes=[
-            pltpu.VMEM((full, 2 * run), BF),
-            pltpu.VMEM((full, 2 * run), BF),
             pltpu.VMEM((full, 2 * run), BF),
             pltpu.VMEM((nz, 16, LANES, LANES), BF),
             pltpu.SemaphoreType.DMA((5,)),
         ],
         compiler_params=PARAMS,
         name="ff",
-    )(*group_gather(block), *in_hbm(blocks), ln_ff_gain[:, None])
+    )(near, normed, *in_hbm(blocks))
     keep = (keep + swap(give, CORE).astype(F32)).astype(BF)
     keep = lax.all_to_all(keep.reshape(2 * nz, width, run), (XHI, Z), 0, 0, tiled=True)
     out = pl.pallas_call(

time: 164 us -> 166 us (1.012)
  blocking collectives: 41.7 us -> 47.1 us
  starting transfers between devices: 61.2 us -> 56.9 us
    all_to_all x1, blocking collectives: 21.9 us -> 26.2 us  [body(): stats = lax.all_to_all(stats, (XLO, Y, Z), 0, 0, tiled=True)]
    ppermute x11 -> x10, starting transfers between devices: 42.3 us -> 38 us  [swap(): return lax.ppermute(x, axis, [(0, 1), (1, 0)])]
    ppermute x11 -> x10, waiting for transfers between devices: 14.6 us -> 13.5 us  [swap(): return lax.ppermute(x, axis, [(0, 1), (1, 0)])]
  transfers between devices with their start and end apart: 16 -> 15, of which waited for: 10 -> 10; matrix products, arithmetic and copies ran while one was open for 0% -> 0% of each run, Pallas kernels for 5% -> 5%
where the time goes in v7:
time: 166 us; the launch traced here: 164 us
  starting transfers between devices  56.9 us (34%)
  blocking collectives  47.1 us (28%)
  waiting for transfers between devices  28.4 us (17%)
  Pallas kernels  15.5 us (9%)
  between operations  13.6 us (8%)
  local copies, waits for them, and re-layouts  2.53 us (2%)
    ppermute x10, starting transfers between devices, swap(): return lax.ppermute(x, axis, [(0, 1), (1, 0)])  38 us
    all_to_all x1, blocking collectives, body(): stats = lax.all_to_all(stats, (XLO, Y, Z), 0, 0, tiled=True)  26.2 us
    all_to_all x1, blocking collectives, body(): lax.all_to_all(keep.reshape(2 * nz, width, run), (XHI, Z), 0, 0, tiled=True)  20.8 us
    ppermute x10, waiting for transfers between devices, swap(): return lax.ppermute(x, axis, [(0, 1), (1, 0)])  13.5 us
    all_to_all x1, waiting for transfers between devices, body(): parts = lax.all_to_all(parts, Z, 0, 0, tiled=True)  11.6 us
    all_to_all x1, starting transfers between devices, body(): parts = lax.all_to_all(parts, Z, 0, 0, tiled=True)  8.79 us
    ppermute x1, starting transfers between devices, body(): right = lax.ppermute(head, (XLO, Y, CORE), [(j, i) for i, j in up])  5.48 us
    pallas_call x1, Pallas kernels, body(): pl.pallas_call(conv_kernel, out_shape=(shape((2 * run, 256), F32), shape(...  5.22 us
  transfers between devices with their start and end apart: 15, of which 10 were waited for; matrix products, arithmetic and copies ran while one was open for 0% of the time, Pallas kernels for 5%

profile of v7, /device:TPU:1, one launch (start us, length us, event | category | flops | bytes accessed | tf_op | source)
XLA Modules:
  0.0 164.2 jit_solution(3310149021887493624)
XLA Ops:
  6.5 1.7 %weights.1 = (bf16[112,1024]{1,0:T(8,128)(2,1)}, bf16[64,2048]{1,0:T(8,128)(2,1)S(1)}, bf16[64,128]{1,0:T(8,128)(2,1)S(1)}, bf16[64,128]{1,0:T(8,128)(2,1)S(1)}) custom-call(bf16[2,64,1024]{2,1,0:T(8,128)(2,1)} %bitcast.15, bf16[64,1024]{1,0:T(8,128)(2,1)} %bitcast.17, f32[31,64]{1,0:T(8,128)} %depth.1, f32[1,64]{1,0:T(1,128)} %bitcast.20, ...), custom_call_target="tpu_custom_call" | custom-call | tf_op jit(solution)/shard_map/weights/pallas_call | solution.py:315
  8.3 4.6 %collective-permute-start = (bf16[64,128]{1,0:T(8,128)(2,1)S(1)}, bf16[64,128]{1,0:T(8,128)(2,1)S(1)}, u32[]{:S(2)}, u32[]{:S(2)}) collective-permute-start(bf16[64,128]{1,0:T(8,128)(2,1)S(1)} %get-tuple-element.20), channel_id=1, source_target_pairs={{0,16},{16,32},{32,48},{48,64},{64,80},{80,96},{96,112},{112,128},... | collective-permute-start | bytes 49160 | tf_op jit(solution)/shard_map/ppermute | solution.py:347
  12.9 5.5 %collective-permute-start.1 = (bf16[64,128]{1,0:T(8,128)(2,1)S(1)}, bf16[64,128]{1,0:T(8,128)(2,1)S(1)}, u32[]{:S(2)}, u32[]{:S(2)}) collective-permute-start(bf16[64,128]{1,0:T(8,128)(2,1)S(1)} %get-tuple-element.21), channel_id=1, source_target_pairs={{16,0},{32,16},{48,32},{64,48},{80,64},{96,80},{112,96},{128,112},... | collective-permute-start | bytes 49160 | tf_op jit(solution)/shard_map/ppermute | solution.py:348
  18.4 0.8 collective-permute-done.1.right
  19.2 0.9 pack.1
  20.1 8.8 %all-to-all-start = ((bf16[8,144,128]{2,1,0:T(8,128)(2,1)}), bf16[8,144,128]{2,1,0:T(8,128)(2,1)S(1)}, u32[]{:S(2)}, u32[]{:S(2)}) async-start(bf16[8,144,128]{2,1,0:T(8,128)(2,1)} %pack.1), calls=%async_computation | async-start | bytes 589824 | tf_op jit(solution)/shard_map/all_to_all | solution.py:357
  28.9 1.0 copy-done.1
  30.0 1.0 copy-done.2
  31.0 1.0 blocks.1
  32.0 11.6 %all-to-all-done.own = bf16[8,144,128]{2,1,0:T(8,128)(2,1)S(1)} async-done(((bf16[8,144,128]{2,1,0:T(8,128)(2,1)}), bf16[8,144,128]{2,1,0:T(8,128)(2,1)S(1)}, u32[]{:S(2)}, u32[]{:S(2)}) %all-to-all-start) | async-done | bytes 294944 | tf_op jit(solution)/shard_map/all_to_all | solution.py:357
  43.7 4.7 %collective-permute-start.2 = (bf16[8,144,128]{2,1,0:T(8,128)(2,1)S(1)}, bf16[8,144,128]{2,1,0:T(8,128)(2,1)S(1)}, u32[]{:S(2)}, u32[]{:S(2)}) collective-permute-start(bf16[8,144,128]{2,1,0:T(8,128)(2,1)S(1)} %all-to-all-done.own), channel_id=1, source_target_pairs={{0,8},{8,0},{1,9},{9,1},{2,10},{10,2},{3,11},{11,3},{4,12},{12,4},... | collective-permute-start | bytes 884744 | tf_op jit(solution)/shard_map/ppermute | solution.py:27
  48.3 1.9 %collective-permute-start.3 = (bf16[8,144,128]{2,1,0:T(8,128)(2,1)S(1)}, bf16[8,144,128]{2,1,0:T(8,128)(2,1)S(1)}, u32[]{:S(2)}, u32[]{:S(2)}) collective-permute-start(bf16[8,144,128]{2,1,0:T(8,128)(2,1)S(1)} %all-to-all-done.own), channel_id=1, source_target_pairs={{0,16},{16,0},{1,17},{17,1},{2,18},{18,2},{3,19},{19,3},{4,20},{20... | collective-permute-start | bytes 884744 | tf_op jit(solution)/shard_map/ppermute | solution.py:27
  50.3 4.6 %collective-permute-done.2.across = bf16[8,144,128]{2,1,0:T(8,128)(2,1)S(1)} collective-permute-done((bf16[8,144,128]{2,1,0:T(8,128)(2,1)S(1)}, bf16[8,144,128]{2,1,0:T(8,128)(2,1)S(1)}, u32[]{:S(2)}, u32[]{:S(2)}) %collective-permute-start.2) | collective-permute-done | bytes 294944 | tf_op jit(solution)/shard_map/ppermute | solution.py:27
  54.9 1.9 %collective-permute-start.4 = (bf16[8,144,128]{2,1,0:T(8,128)(2,1)S(1)}, bf16[8,144,128]{2,1,0:T(8,128)(2,1)S(1)}, u32[]{:S(2)}, u32[]{:S(2)}) collective-permute-start(bf16[8,144,128]{2,1,0:T(8,128)(2,1)S(1)} %collective-permute-done.2.across), channel_id=1, source_target_pairs={{0,16},{16,0},{1,17},{17,1},{2,18},{18,2},{3,19},{19,3},{4,20},{20... | collective-permute-start | bytes 884744 | tf_op jit(solution)/shard_map/ppermute | solution.py:27
  57.1 1.3 collective-permute-done.4.far
  58.4 1.1 all-gather.5.cloned.1.call-done
  59.5 5.2 %conv.1 = (f32[512,256]{1,0:T(8,128)S(1)}, f32[128,4,128]{2,1,0:T(4,128)S(1)}, f32[8,256]{1,0:T(8,128)S(1)}, bf16[256,512]{1,0:T(8,128)(2,1)S(1)}) custom-call(bf16[8,144,128]{2,1,0:T(8,128)(2,1)S(1)} %all-to-all-done.own, bf16[8,144,128]{2,1,0:T(8,128)(2,1)S(1)} %collective-permute-done.2.across, bf16[8,144,128]{2,1,0:T(8,128)(2,1)S(1)} %collective-permute-done.3.beside, ...), custom_call_target="tpu_custom_call" | custom-call | tf_op jit(solution)/shard_map/conv/pallas_call | solution.py:371
  64.7 26.2 %all_to_all.15.stats = f32[128,4,128]{2,1,0:T(4,128)S(1)} all-to-all(f32[128,4,128]{2,1,0:T(4,128)S(1)} %get-tuple-element.25), channel_id=1, replica_groups=mesh['xlo'=2,'y'=8,'core'=2,'xhi'=2,'z'=8] {'xlo','y','z'}, dimensions={0} | all-to-all | bytes 524288 | tf_op jit(solution)/shard_map/all_to_all | solution.py:392
  91.5 4.4 %collective-permute-start.5 = (bf16[256,512]{1,0:T(8,128)(2,1)S(1)}, bf16[256,512]{1,0:T(8,128)(2,1)S(1)}, u32[]{:S(2)}, u32[]{:S(2)}) collective-permute-start(bf16[256,512]{1,0:T(8,128)(2,1)S(1)} %bn.1.own), channel_id=1, source_target_pairs={{0,8},{8,0},{1,9},{9,1},{2,10},{10,2},{3,11},{11,3},{4,12},{12,4},... | collective-permute-start | bytes 786440 | tf_op jit(solution)/shard_map/ppermute | solution.py:27
  95.8 7.6 %collective-permute-start.6 = (bf16[256,512]{1,0:T(8,128)(2,1)S(1)}, bf16[256,512]{1,0:T(8,128)(2,1)S(1)}, u32[]{:S(2)}, u32[]{:S(2)}) collective-permute-start(bf16[256,512]{1,0:T(8,128)(2,1)S(1)} %bn.1.own), channel_id=1, source_target_pairs={{0,16},{16,0},{1,17},{17,1},{2,18},{18,2},{3,19},{19,3},{4,20},{20... | collective-permute-start | bytes 786440 | tf_op jit(solution)/shard_map/ppermute | solution.py:27
  103.5 5.1 %collective-permute-start.7 = (bf16[256,512]{1,0:T(8,128)(2,1)S(1)}, bf16[256,512]{1,0:T(8,128)(2,1)S(1)}, u32[]{:S(2)}, u32[]{:S(2)}) collective-permute-start(bf16[256,512]{1,0:T(8,128)(2,1)S(1)} %collective-permute-done.5.across), channel_id=1, source_target_pairs={{0,16},{16,0},{1,17},{17,1},{2,18},{18,2},{3,19},{19,3},{4,20},{20... | collective-permute-start | bytes 786440 | tf_op jit(solution)/shard_map/ppermute | solution.py:27
  108.6 1.1 collective-permute-done.7.far
  110.3 4.3 %collective-permute-start.8 = (bf16[256,512]{1,0:T(8,128)(2,1)S(1)}, bf16[256,512]{1,0:T(8,128)(2,1)S(1)}, u32[]{:S(2)}, u32[]{:S(2)}) collective-permute-start(bf16[256,512]{1,0:T(8,128)(2,1)S(1)} %mix.1.own), channel_id=1, source_target_pairs={{0,8},{8,0},{1,9},{9,1},{2,10},{10,2},{3,11},{11,3},{4,12},{12,4},... | collective-permute-start | bytes 786440 | tf_op jit(solution)/shard_map/ppermute | solution.py:27
  114.6 2.6 %collective-permute-start.9 = (bf16[256,512]{1,0:T(8,128)(2,1)S(1)}, bf16[256,512]{1,0:T(8,128)(2,1)S(1)}, u32[]{:S(2)}, u32[]{:S(2)}) collective-permute-start(bf16[256,512]{1,0:T(8,128)(2,1)S(1)} %mix.1.own), channel_id=1, source_target_pairs={{0,16},{16,0},{1,17},{17,1},{2,18},{18,2},{3,19},{19,3},{4,20},{20... | collective-permute-start | bytes 786440 | tf_op jit(solution)/shard_map/ppermute | solution.py:27
  117.2 4.0 %collective-permute-done.8.across = bf16[256,512]{1,0:T(8,128)(2,1)S(1)} collective-permute-done((bf16[256,512]{1,0:T(8,128)(2,1)S(1)}, bf16[256,512]{1,0:T(8,128)(2,1)S(1)}, u32[]{:S(2)}, u32[]{:S(2)}) %collective-permute-start.8) | collective-permute-done | bytes 262176 | tf_op jit(solution)/shard_map/ppermute | solution.py:27
  121.2 3.1 %collective-permute-start.10 = (bf16[256,512]{1,0:T(8,128)(2,1)S(1)}, bf16[256,512]{1,0:T(8,128)(2,1)S(1)}, u32[]{:S(2)}, u32[]{:S(2)}) collective-permute-start(bf16[256,512]{1,0:T(8,128)(2,1)S(1)} %collective-permute-done.8.across), channel_id=1, source_target_pairs={{0,16},{16,0},{1,17},{17,1},{2,18},{18,2},{3,19},{19,3},{4,20},{20... | collective-permute-start | bytes 786440 | tf_op jit(solution)/shard_map/ppermute | solution.py:27
  124.5 0.9 collective-permute-done.10.far
  126.2 1.3 all-gather.7.cloned.1.call-done
  127.6 4.1 %ff.1 = (f32[1024,256]{1,0:T(8,128)S(1)}, bf16[1024,256]{1,0:T(8,128)(2,1)S(1)}) custom-call(bf16[1024,256]{1,0:T(8,128)(2,1)S(1)} %get-tuple-element.28.near, bf16[1024,512]{1,0:T(8,128)(2,1)S(1)} %get-tuple-element.29.normed, bf16[8,16,128,128]{3,2,1,0:T(8,128)(2,1)} %bitcast.13), custom_call_target="tpu_custom_call" | custom-call | tf_op jit(solution)/shard_map/ff/pallas_call | solution.py:424
  131.7 2.4 %collective-permute-start.11 = (bf16[1024,256]{1,0:T(8,128)(2,1)S(1)}, bf16[1024,256]{1,0:T(8,128)(2,1)S(1)}, u32[]{:S(2)}, u32[]{:S(2)}) collective-permute-start(bf16[1024,256]{1,0:T(8,128)(2,1)S(1)} %get-tuple-element.32), channel_id=1, source_target_pairs={{0,16},{16,0},{1,17},{17,1},{2,18},{18,2},{3,19},{19,3},{4,20},{20... | collective-permute-start | bytes 1572872 | tf_op jit(solution)/shard_map/ppermute | solution.py:27
  134.1 1.5 collective-permute-done.11
  135.7 20.8 %all_to_all.16.parts = bf16[16,64,256]{2,1,0:T(8,128)(2,1)S(1)} all-to-all(bf16[16,64,256]{2,1,0:T(8,128)(2,1)S(1)} %bitcast.14), channel_id=1, replica_groups=mesh['xlo'=2,'y'=8,'core'=2,'xhi'=2,'z'=8] {'xhi','z'}, dimensions={0} | all-to-all | bytes 1048576 | tf_op jit(solution)/shard_map/all_to_all | solution.py:438
  (24 shorter events, 3.2 us)
Async XLA Ops:
  6.5 50.3 %copy-start.3 = (f32[1024]{0:T(1024)S(1)}, f32[1024]{0:T(1024)}, u32[]{:S(2)}) copy-start(f32[1024]{0:T(1024)} %param.11) | copy-start | bytes 12292
  6.5 53.0 %all-gather.5.cloned.1.call-start = ((), (), s32[]{:S(2)}) async-start(), calls=%async_computation.3 | async-start | bytes 2064384 | tf_op jit(solution)/shard_map/all_gather | solution.py:343
  8.3 10.1 %collective-permute-start = (bf16[64,128]{1,0:T(8,128)(2,1)S(1)}, bf16[64,128]{1,0:T(8,128)(2,1)S(1)}, u32[]{:S(2)}, u32[]{:S(2)}) collective-permute-start(bf16[64,128]{1,0:T(8,128)(2,1)S(1)} %get-tuple-element.20), channel_id=1, source_target_pairs={{0,16},{16,32},{32,48},{48,64},{64,80},{80,96},{96,112},{112,128},... | collective-permute-start | bytes 49160 | tf_op jit(solution)/shard_map/ppermute | solution.py:347
  12.9 6.3 %collective-permute-start.1 = (bf16[64,128]{1,0:T(8,128)(2,1)S(1)}, bf16[64,128]{1,0:T(8,128)(2,1)S(1)}, u32[]{:S(2)}, u32[]{:S(2)}) collective-permute-start(bf16[64,128]{1,0:T(8,128)(2,1)S(1)} %get-tuple-element.21), channel_id=1, source_target_pairs={{16,0},{32,16},{48,32},{64,48},{80,64},{96,80},{112,96},{128,112},... | collective-permute-start | bytes 49160 | tf_op jit(solution)/shard_map/ppermute | solution.py:348
  20.1 23.6 %all-to-all-start = ((bf16[8,144,128]{2,1,0:T(8,128)(2,1)}), bf16[8,144,128]{2,1,0:T(8,128)(2,1)S(1)}, u32[]{:S(2)}, u32[]{:S(2)}) async-start(bf16[8,144,128]{2,1,0:T(8,128)(2,1)} %pack.1), calls=%async_computation | async-start | bytes 589824 | tf_op jit(solution)/shard_map/all_to_all | solution.py:357
  28.9 98.7 %all-gather.7.cloned.1.call-start = ((), (), s32[]{:S(2)}) async-start(), calls=%async_computation.4 | async-start | bytes 4718592 | tf_op jit(solution)/shard_map/all_gather | solution.py:368
  28.9 1.0 copy-start.1
  30.0 1.0 copy-start.2
  43.7 11.2 %collective-permute-start.2 = (bf16[8,144,128]{2,1,0:T(8,128)(2,1)S(1)}, bf16[8,144,128]{2,1,0:T(8,128)(2,1)S(1)}, u32[]{:S(2)}, u32[]{:S(2)}) collective-permute-start(bf16[8,144,128]{2,1,0:T(8,128)(2,1)S(1)} %all-to-all-done.own), channel_id=1, source_target_pairs={{0,8},{8,0},{1,9},{9,1},{2,10},{10,2},{3,11},{11,3},{4,12},{12,4},... | collective-permute-start | bytes 884744 | tf_op jit(solution)/shard_map/ppermute | solution.py:27
  48.3 8.7 %collective-permute-start.3 = (bf16[8,144,128]{2,1,0:T(8,128)(2,1)S(1)}, bf16[8,144,128]{2,1,0:T(8,128)(2,1)S(1)}, u32[]{:S(2)}, u32[]{:S(2)}) collective-permute-start(bf16[8,144,128]{2,1,0:T(8,128)(2,1)S(1)} %all-to-all-done.own), channel_id=1, source_target_pairs={{0,16},{16,0},{1,17},{17,1},{2,18},{18,2},{3,19},{19,3},{4,20},{20... | collective-permute-start | bytes 884744 | tf_op jit(solution)/shard_map/ppermute | solution.py:27
  54.9 3.5 %collective-permute-start.4 = (bf16[8,144,128]{2,1,0:T(8,128)(2,1)S(1)}, bf16[8,144,128]{2,1,0:T(8,128)(2,1)S(1)}, u32[]{:S(2)}, u32[]{:S(2)}) collective-permute-start(bf16[8,144,128]{2,1,0:T(8,128)(2,1)S(1)} %collective-permute-done.2.across), channel_id=1, source_target_pairs={{0,16},{16,0},{1,17},{17,1},{2,18},{18,2},{3,19},{19,3},{4,20},{20... | collective-permute-start | bytes 884744 | tf_op jit(solution)/shard_map/ppermute | solution.py:27
  59.5 50.3 %copy-start = (bf16[896,1024]{1,0:T(8,128)(2,1)S(1)}, bf16[896,1024]{1,0:T(8,128)(2,1)}, u32[]{:S(2)}) copy-start(bf16[896,1024]{1,0:T(8,128)(2,1)} %all-gather.5.cloned.1.call-done) | copy-start | bytes 5505028
  59.5 64.8 %copy-start.4 = (f32[1024]{0:T(1024)S(1)}, f32[1024]{0:T(1024)}, u32[]{:S(2)}) copy-start(f32[1024]{0:T(1024)} %param.17) | copy-start | bytes 12292
  91.5 12.0 %collective-permute-start.5 = (bf16[256,512]{1,0:T(8,128)(2,1)S(1)}, bf16[256,512]{1,0:T(8,128)(2,1)S(1)}, u32[]{:S(2)}, u32[]{:S(2)}) collective-permute-start(bf16[256,512]{1,0:T(8,128)(2,1)S(1)} %bn.1.own), channel_id=1, source_target_pairs={{0,8},{8,0},{1,9},{9,1},{2,10},{10,2},{3,11},{11,3},{4,12},{12,4},... | collective-permute-start | bytes 786440 | tf_op jit(solution)/shard_map/ppermute | solution.py:27
  95.8 12.8 %collective-permute-start.6 = (bf16[256,512]{1,0:T(8,128)(2,1)S(1)}, bf16[256,512]{1,0:T(8,128)(2,1)S(1)}, u32[]{:S(2)}, u32[]{:S(2)}) collective-permute-start(bf16[256,512]{1,0:T(8,128)(2,1)S(1)} %bn.1.own), channel_id=1, source_target_pairs={{0,16},{16,0},{1,17},{17,1},{2,18},{18,2},{3,19},{19,3},{4,20},{20... | collective-permute-start | bytes 786440 | tf_op jit(solution)/shard_map/ppermute | solution.py:27
  103.5 6.3 %collective-permute-start.7 = (bf16[256,512]{1,0:T(8,128)(2,1)S(1)}, bf16[256,512]{1,0:T(8,128)(2,1)S(1)}, u32[]{:S(2)}, u32[]{:S(2)}) collective-permute-start(bf16[256,512]{1,0:T(8,128)(2,1)S(1)} %collective-permute-done.5.across), channel_id=1, source_target_pairs={{0,16},{16,0},{1,17},{17,1},{2,18},{18,2},{3,19},{19,3},{4,20},{20... | collective-permute-start | bytes 786440 | tf_op jit(solution)/shard_map/ppermute | solution.py:27
  110.3 10.9 %collective-permute-start.8 = (bf16[256,512]{1,0:T(8,128)(2,1)S(1)}, bf16[256,512]{1,0:T(8,128)(2,1)S(1)}, u32[]{:S(2)}, u32[]{:S(2)}) collective-permute-start(bf16[256,512]{1,0:T(8,128)(2,1)S(1)} %mix.1.own), channel_id=1, source_target_pairs={{0,8},{8,0},{1,9},{9,1},{2,10},{10,2},{3,11},{11,3},{4,12},{12,4},... | collective-permute-start | bytes 786440 | tf_op jit(solution)/shard_map/ppermute | solution.py:27
  114.6 9.9 %collective-permute-start.9 = (bf16[256,512]{1,0:T(8,128)(2,1)S(1)}, bf16[256,512]{1,0:T(8,128)(2,1)S(1)}, u32[]{:S(2)}, u32[]{:S(2)}) collective-permute-start(bf16[256,512]{1,0:T(8,128)(2,1)S(1)} %mix.1.own), channel_id=1, source_target_pairs={{0,16},{16,0},{1,17},{17,1},{2,18},{18,2},{3,19},{19,3},{4,20},{20... | collective-permute-start | bytes 786440 | tf_op jit(solution)/shard_map/ppermute | solution.py:27
  121.2 4.2 %collective-permute-start.10 = (bf16[256,512]{1,0:T(8,128)(2,1)S(1)}, bf16[256,512]{1,0:T(8,128)(2,1)S(1)}, u32[]{:S(2)}, u32[]{:S(2)}) collective-permute-start(bf16[256,512]{1,0:T(8,128)(2,1)S(1)} %collective-permute-done.8.across), channel_id=1, source_target_pairs={{0,16},{16,0},{1,17},{17,1},{2,18},{18,2},{3,19},{19,3},{4,20},{20... | collective-permute-start | bytes 786440 | tf_op jit(solution)/shard_map/ppermute | solution.py:27
  131.7 3.9 %collective-permute-start.11 = (bf16[1024,256]{1,0:T(8,128)(2,1)S(1)}, bf16[1024,256]{1,0:T(8,128)(2,1)S(1)}, u32[]{:S(2)}, u32[]{:S(2)}) collective-permute-start(bf16[1024,256]{1,0:T(8,128)(2,1)S(1)} %get-tuple-element.32), channel_id=1, source_target_pairs={{0,16},{16,0},{1,17},{17,1},{2,18},{18,2},{3,19},{19,3},{4,20},{20... | collective-permute-start | bytes 1572872 | tf_op jit(solution)/shard_map/ppermute | solution.py:27
Sparse Core Ops, SparseCore 0:
  9.4 50.0 all-gather.4
  61.6 65.9 all-gather.6

commit v8 on v7

--- a/solution.py
+++ b/solution.py
@@ -211,15 +211,24 @@
         stats[:, 2 + h : 3 + h, :] = jnp.broadcast_to(square[None], (n, 1, LANES))
 
 
+def merged(stats, count):
+    total = jnp.sum(stats, axis=0)
+    mean = total * (1.0 / stats.shape[0])
+    apart = stats - mean[None]
+    apart = jnp.sum(apart * apart, axis=0)
+    return mean[0:2], total[2:4] + count * apart[0:2]
+
+
+def merge_kernel(stats, out):
+    mean, square = merged(stats[...], 512)
+    out[:, 0:2] = jnp.broadcast_to(mean[None], (out.shape[0],) + mean.shape)
+    out[:, 2:4] = jnp.broadcast_to(square[None], (out.shape[0],) + square.shape)
+
+
 def bn_kernel(conv, stats, par, out):
-    n, frames = stats.shape[0], conv.shape[0]
-    s = stats[...]
-    total = jnp.sum(s, axis=0)
-    mean = total * (1.0 / n)
-    apart = s - mean[None]
-    apart = jnp.sum(apart * apart, axis=0)
-    square = total[2:4] + frames * apart[0:2]
-    scale = lax.rsqrt(square * (1.0 / (n * frames)) + EPS)
+    frames = 8 * conv.shape[0]
+    mean, square = merged(stats[...], frames)
+    scale = lax.rsqrt(square * (1.0 / (frames * stats.shape[0])) + EPS)
     for h in range(2):
         cols = slice(LANES * h, LANES * (h + 1))
         value = (conv[:, cols] - mean[h : h + 1]) * (scale[h : h + 1] * par[0:1, cols])
@@ -372,7 +381,7 @@
         conv_kernel,
         out_shape=(
             shape((2 * run, 256), F32),
-            shape((lax.axis_size((XLO, Y, Z)), 4, LANES), F32),
+            shape((nz, 4, LANES), F32),
             shape((8, 256), F32),
             shape((256, 2 * run), BF),
         ),
@@ -389,7 +398,16 @@
         compiler_params=PARAMS,
         name="conv",
     )(*whole, *in_hbm(first), ln_conv_gain[:, None])
-    stats = lax.all_to_all(stats, (XLO, Y, Z), 0, 0, tiled=True)
+    stats = lax.all_to_all(stats, Z, 0, 0, tiled=True)
+    stats = pl.pallas_call(
+        merge_kernel,
+        out_shape=shape((lax.axis_size((XLO, Y)), 4, LANES), F32),
+        in_specs=[VMEM],
+        out_specs=VMEM,
+        compiler_params=PARAMS,
+        name="merge",
+    )(stats)
+    stats = lax.all_to_all(stats, (XLO, Y), 0, 0, tiled=True)
     activated = pl.pallas_call(
         bn_kernel,
         out_shape=shape((256, 2 * run), BF),

time: 166 us -> 163 us (0.982)
  blocking collectives: 47.1 us -> 44.5 us
    all_to_all x1, blocking collectives: 20.8 us -> 18.8 us  [body(): lax.all_to_all(keep.reshape(2 * nz, width, run), (XHI, Z), 0, 0, tiled=True)]
    all_to_all x1 -> x2, blocking collectives: 26.2 us -> 25.8 us  [the longest x1 15.3 us: body(): stats = lax.all_to_all(stats, (XLO, Y), 0, 0, tiled=True)]
  transfers between devices with their start and end apart: 15 -> 15, of which waited for: 10 -> 9; matrix products, arithmetic and copies ran while one was open for 0% -> 0% of each run, Pallas kernels for 5% -> 5%
where the time goes in v8:
time: 163 us; the launch traced here: 161 us
  starting transfers between devices  58.3 us (36%)
  blocking collectives  44.5 us (27%)
  waiting for transfers between devices  27.1 us (17%)
  Pallas kernels  15.2 us (9%)
  between operations  13.6 us (8%)
  local copies, waits for them, and re-layouts  2.53 us (2%)
    ppermute x10, starting transfers between devices, swap(): return lax.ppermute(x, axis, [(0, 1), (1, 0)])  39.4 us
    all_to_all x1, blocking collectives, body(): lax.all_to_all(keep.reshape(2 * nz, width, run), (XHI, Z), 0, 0, tiled=True)  18.8 us
    all_to_all x1, blocking collectives, body(): stats = lax.all_to_all(stats, (XLO, Y), 0, 0, tiled=True)  15.3 us
    ppermute x10, waiting for transfers between devices, swap(): return lax.ppermute(x, axis, [(0, 1), (1, 0)])  13.5 us
    all_to_all x1, waiting for transfers between devices, body(): parts = lax.all_to_all(parts, Z, 0, 0, tiled=True)  11.6 us
    all_to_all x1, blocking collectives, body(): stats = lax.all_to_all(stats, Z, 0, 0, tiled=True)  10.4 us
    all_to_all x1, starting transfers between devices, body(): parts = lax.all_to_all(parts, Z, 0, 0, tiled=True)  8.79 us
    ppermute x1, starting transfers between devices, body(): right = lax.ppermute(head, (XLO, Y, CORE), [(j, i) for i, j in up])  5.48 us
  transfers between devices with their start and end apart: 15, of which 9 were waited for; matrix products, arithmetic and copies ran while one was open for 0% of the time, Pallas kernels for 5%

profile of v8, /device:TPU:1, one launch (start us, length us, event | category | flops | bytes accessed | tf_op | source)
XLA Modules:
  0.0 161.5 jit_solution(1685525421620971436)
XLA Ops:
  6.5 1.7 %weights.1 = (bf16[112,1024]{1,0:T(8,128)(2,1)}, bf16[64,2048]{1,0:T(8,128)(2,1)S(1)}, bf16[64,128]{1,0:T(8,128)(2,1)S(1)}, bf16[64,128]{1,0:T(8,128)(2,1)S(1)}) custom-call(bf16[2,64,1024]{2,1,0:T(8,128)(2,1)} %bitcast.15, bf16[64,1024]{1,0:T(8,128)(2,1)} %bitcast.17, f32[31,64]{1,0:T(8,128)} %depth.1, f32[1,64]{1,0:T(1,128)} %bitcast.20, ...), custom_call_target="tpu_custom_call" | custom-call | tf_op jit(solution)/shard_map/weights/pallas_call | solution.py:324
  8.3 4.6 %collective-permute-start = (bf16[64,128]{1,0:T(8,128)(2,1)S(1)}, bf16[64,128]{1,0:T(8,128)(2,1)S(1)}, u32[]{:S(2)}, u32[]{:S(2)}) collective-permute-start(bf16[64,128]{1,0:T(8,128)(2,1)S(1)} %get-tuple-element.20), channel_id=1, source_target_pairs={{0,16},{16,32},{32,48},{48,64},{64,80},{80,96},{96,112},{112,128},... | collective-permute-start | bytes 49160 | tf_op jit(solution)/shard_map/ppermute | solution.py:356
  12.9 5.5 %collective-permute-start.1 = (bf16[64,128]{1,0:T(8,128)(2,1)S(1)}, bf16[64,128]{1,0:T(8,128)(2,1)S(1)}, u32[]{:S(2)}, u32[]{:S(2)}) collective-permute-start(bf16[64,128]{1,0:T(8,128)(2,1)S(1)} %get-tuple-element.21), channel_id=1, source_target_pairs={{16,0},{32,16},{48,32},{64,48},{80,64},{96,80},{112,96},{128,112},... | collective-permute-start | bytes 49160 | tf_op jit(solution)/shard_map/ppermute | solution.py:357
  18.4 0.8 collective-permute-done.1.right
  19.2 0.9 pack.1
  20.1 8.8 %all-to-all-start = ((bf16[8,144,128]{2,1,0:T(8,128)(2,1)}), bf16[8,144,128]{2,1,0:T(8,128)(2,1)S(1)}, u32[]{:S(2)}, u32[]{:S(2)}) async-start(bf16[8,144,128]{2,1,0:T(8,128)(2,1)} %pack.1), calls=%async_computation | async-start | bytes 589824 | tf_op jit(solution)/shard_map/all_to_all | solution.py:366
  28.9 1.0 copy-done.1
  30.0 1.0 copy-done.2
  31.0 1.0 blocks.1
  32.0 11.6 %all-to-all-done.own = bf16[8,144,128]{2,1,0:T(8,128)(2,1)S(1)} async-done(((bf16[8,144,128]{2,1,0:T(8,128)(2,1)}), bf16[8,144,128]{2,1,0:T(8,128)(2,1)S(1)}, u32[]{:S(2)}, u32[]{:S(2)}) %all-to-all-start) | async-done | bytes 294944 | tf_op jit(solution)/shard_map/all_to_all | solution.py:366
  43.7 4.7 %collective-permute-start.2 = (bf16[8,144,128]{2,1,0:T(8,128)(2,1)S(1)}, bf16[8,144,128]{2,1,0:T(8,128)(2,1)S(1)}, u32[]{:S(2)}, u32[]{:S(2)}) collective-permute-start(bf16[8,144,128]{2,1,0:T(8,128)(2,1)S(1)} %all-to-all-done.own), channel_id=1, source_target_pairs={{0,8},{8,0},{1,9},{9,1},{2,10},{10,2},{3,11},{11,3},{4,12},{12,4},... | collective-permute-start | bytes 884744 | tf_op jit(solution)/shard_map/ppermute | solution.py:27
  48.3 1.9 %collective-permute-start.3 = (bf16[8,144,128]{2,1,0:T(8,128)(2,1)S(1)}, bf16[8,144,128]{2,1,0:T(8,128)(2,1)S(1)}, u32[]{:S(2)}, u32[]{:S(2)}) collective-permute-start(bf16[8,144,128]{2,1,0:T(8,128)(2,1)S(1)} %all-to-all-done.own), channel_id=1, source_target_pairs={{0,16},{16,0},{1,17},{17,1},{2,18},{18,2},{3,19},{19,3},{4,20},{20... | collective-permute-start | bytes 884744 | tf_op jit(solution)/shard_map/ppermute | solution.py:27
  50.3 4.6 %collective-permute-done.2.across = bf16[8,144,128]{2,1,0:T(8,128)(2,1)S(1)} collective-permute-done((bf16[8,144,128]{2,1,0:T(8,128)(2,1)S(1)}, bf16[8,144,128]{2,1,0:T(8,128)(2,1)S(1)}, u32[]{:S(2)}, u32[]{:S(2)}) %collective-permute-start.2) | collective-permute-done | bytes 294944 | tf_op jit(solution)/shard_map/ppermute | solution.py:27
  54.9 1.9 %collective-permute-start.4 = (bf16[8,144,128]{2,1,0:T(8,128)(2,1)S(1)}, bf16[8,144,128]{2,1,0:T(8,128)(2,1)S(1)}, u32[]{:S(2)}, u32[]{:S(2)}) collective-permute-start(bf16[8,144,128]{2,1,0:T(8,128)(2,1)S(1)} %collective-permute-done.2.across), channel_id=1, source_target_pairs={{0,16},{16,0},{1,17},{17,1},{2,18},{18,2},{3,19},{19,3},{4,20},{20... | collective-permute-start | bytes 884744 | tf_op jit(solution)/shard_map/ppermute | solution.py:27
  57.1 1.3 collective-permute-done.4.far
  58.4 1.1 all-gather.5.cloned.1.call-done
  59.5 5.1 %conv.1 = (f32[512,256]{1,0:T(8,128)S(1)}, f32[8,4,128]{2,1,0:T(4,128)S(1)}, f32[8,256]{1,0:T(8,128)S(1)}, bf16[256,512]{1,0:T(8,128)(2,1)S(1)}) custom-call(bf16[8,144,128]{2,1,0:T(8,128)(2,1)S(1)} %all-to-all-done.own, bf16[8,144,128]{2,1,0:T(8,128)(2,1)S(1)} %collective-permute-done.2.across, bf16[8,144,128]{2,1,0:T(8,128)(2,1)S(1)} %collective-permute-done.3.beside, ...), custom_call_target="tpu_custom_call" | custom-call | tf_op jit(solution)/shard_map/conv/pallas_call | solution.py:380
  64.6 10.4 %all_to_all.20.stats = f32[8,4,128]{2,1,0:T(4,128)S(1)} all-to-all(f32[8,4,128]{2,1,0:T(4,128)S(1)} %get-tuple-element.25), channel_id=1, replica_groups=mesh['xlo'=2,'y'=8,'core'=2,'xhi'=2,'z'=8] {'z'}, dimensions={0} | all-to-all | bytes 32768 | tf_op jit(solution)/shard_map/all_to_all | solution.py:401
  75.1 15.3 %all_to_all.21.stats = f32[16,4,128]{2,1,0:T(4,128)S(1)} all-to-all(f32[16,4,128]{2,1,0:T(4,128)S(1)} %merge.1), channel_id=1, replica_groups=mesh['xlo'=2,'y'=8,'core'=2,'xhi'=2,'z'=8] {'xlo','y'}, dimensions={0} | all-to-all | bytes 65536 | tf_op jit(solution)/shard_map/all_to_all | solution.py:410
  90.7 4.4 %collective-permute-start.5 = (bf16[256,512]{1,0:T(8,128)(2,1)S(1)}, bf16[256,512]{1,0:T(8,128)(2,1)S(1)}, u32[]{:S(2)}, u32[]{:S(2)}) collective-permute-start(bf16[256,512]{1,0:T(8,128)(2,1)S(1)} %bn.1.own), channel_id=1, source_target_pairs={{0,8},{8,0},{1,9},{9,1},{2,10},{10,2},{3,11},{11,3},{4,12},{12,4},... | collective-permute-start | bytes 786440 | tf_op jit(solution)/shard_map/ppermute | solution.py:27
  95.1 9.2 %collective-permute-start.6 = (bf16[256,512]{1,0:T(8,128)(2,1)S(1)}, bf16[256,512]{1,0:T(8,128)(2,1)S(1)}, u32[]{:S(2)}, u32[]{:S(2)}) collective-permute-start(bf16[256,512]{1,0:T(8,128)(2,1)S(1)} %bn.1.own), channel_id=1, source_target_pairs={{0,16},{16,0},{1,17},{17,1},{2,18},{18,2},{3,19},{19,3},{4,20},{20... | collective-permute-start | bytes 786440 | tf_op jit(solution)/shard_map/ppermute | solution.py:27
  104.2 5.1 %collective-permute-start.7 = (bf16[256,512]{1,0:T(8,128)(2,1)S(1)}, bf16[256,512]{1,0:T(8,128)(2,1)S(1)}, u32[]{:S(2)}, u32[]{:S(2)}) collective-permute-start(bf16[256,512]{1,0:T(8,128)(2,1)S(1)} %collective-permute-done.5.across), channel_id=1, source_target_pairs={{0,16},{16,0},{1,17},{17,1},{2,18},{18,2},{3,19},{19,3},{4,20},{20... | collective-permute-start | bytes 786440 | tf_op jit(solution)/shard_map/ppermute | solution.py:27
  109.4 1.1 collective-permute-done.7.far
  111.0 4.3 %collective-permute-start.8 = (bf16[256,512]{1,0:T(8,128)(2,1)S(1)}, bf16[256,512]{1,0:T(8,128)(2,1)S(1)}, u32[]{:S(2)}, u32[]{:S(2)}) collective-permute-start(bf16[256,512]{1,0:T(8,128)(2,1)S(1)} %mix.1.own), channel_id=1, source_target_pairs={{0,8},{8,0},{1,9},{9,1},{2,10},{10,2},{3,11},{11,3},{4,12},{12,4},... | collective-permute-start | bytes 786440 | tf_op jit(solution)/shard_map/ppermute | solution.py:27
  115.4 2.6 %collective-permute-start.9 = (bf16[256,512]{1,0:T(8,128)(2,1)S(1)}, bf16[256,512]{1,0:T(8,128)(2,1)S(1)}, u32[]{:S(2)}, u32[]{:S(2)}) collective-permute-start(bf16[256,512]{1,0:T(8,128)(2,1)S(1)} %mix.1.own), channel_id=1, source_target_pairs={{0,16},{16,0},{1,17},{17,1},{2,18},{18,2},{3,19},{19,3},{4,20},{20... | collective-permute-start | bytes 786440 | tf_op jit(solution)/shard_map/ppermute | solution.py:27
  117.9 4.0 %collective-permute-done.8.across = bf16[256,512]{1,0:T(8,128)(2,1)S(1)} collective-permute-done((bf16[256,512]{1,0:T(8,128)(2,1)S(1)}, bf16[256,512]{1,0:T(8,128)(2,1)S(1)}, u32[]{:S(2)}, u32[]{:S(2)}) %collective-permute-start.8) | collective-permute-done | bytes 262176 | tf_op jit(solution)/shard_map/ppermute | solution.py:27
  121.9 3.1 %collective-permute-start.10 = (bf16[256,512]{1,0:T(8,128)(2,1)S(1)}, bf16[256,512]{1,0:T(8,128)(2,1)S(1)}, u32[]{:S(2)}, u32[]{:S(2)}) collective-permute-start(bf16[256,512]{1,0:T(8,128)(2,1)S(1)} %collective-permute-done.8.across), channel_id=1, source_target_pairs={{0,16},{16,0},{1,17},{17,1},{2,18},{18,2},{3,19},{19,3},{4,20},{20... | collective-permute-start | bytes 786440 | tf_op jit(solution)/shard_map/ppermute | solution.py:27
  125.3 0.9 collective-permute-done.10.far
  127.0 4.1 %ff.1 = (f32[1024,256]{1,0:T(8,128)S(1)}, bf16[1024,256]{1,0:T(8,128)(2,1)S(1)}) custom-call(bf16[1024,256]{1,0:T(8,128)(2,1)S(1)} %get-tuple-element.28.near, bf16[1024,512]{1,0:T(8,128)(2,1)S(1)} %get-tuple-element.29.normed, bf16[8,16,128,128]{3,2,1,0:T(8,128)(2,1)} %bitcast.13), custom_call_target="tpu_custom_call" | custom-call | tf_op jit(solution)/shard_map/ff/pallas_call | solution.py:442
  131.2 2.3 %collective-permute-start.11 = (bf16[1024,256]{1,0:T(8,128)(2,1)S(1)}, bf16[1024,256]{1,0:T(8,128)(2,1)S(1)}, u32[]{:S(2)}, u32[]{:S(2)}) collective-permute-start(bf16[1024,256]{1,0:T(8,128)(2,1)S(1)} %get-tuple-element.32), channel_id=1, source_target_pairs={{0,16},{16,0},{1,17},{17,1},{2,18},{18,2},{3,19},{19,3},{4,20},{20... | collective-permute-start | bytes 1572872 | tf_op jit(solution)/shard_map/ppermute | solution.py:27
  133.5 1.5 collective-permute-done.11
  135.1 18.8 %all_to_all.22.parts = bf16[16,64,256]{2,1,0:T(8,128)(2,1)S(1)} all-to-all(bf16[16,64,256]{2,1,0:T(8,128)(2,1)S(1)} %bitcast.14), channel_id=1, replica_groups=mesh['xlo'=2,'y'=8,'core'=2,'xhi'=2,'z'=8] {'xhi','z'}, dimensions={0} | all-to-all | bytes 1048576 | tf_op jit(solution)/shard_map/all_to_all | solution.py:456
  (26 shorter events, 3.0 us)
Async XLA Ops:
  6.5 50.3 %copy-start.3 = (f32[1024]{0:T(1024)S(1)}, f32[1024]{0:T(1024)}, u32[]{:S(2)}) copy-start(f32[1024]{0:T(1024)} %param.11) | copy-start | bytes 12292
  6.5 53.0 %all-gather.5.cloned.1.call-start = ((), (), s32[]{:S(2)}) async-start(), calls=%async_computation.4 | async-start | bytes 2064384 | tf_op jit(solution)/shard_map/all_gather | solution.py:352
  8.3 10.1 %collective-permute-start = (bf16[64,128]{1,0:T(8,128)(2,1)S(1)}, bf16[64,128]{1,0:T(8,128)(2,1)S(1)}, u32[]{:S(2)}, u32[]{:S(2)}) collective-permute-start(bf16[64,128]{1,0:T(8,128)(2,1)S(1)} %get-tuple-element.20), channel_id=1, source_target_pairs={{0,16},{16,32},{32,48},{48,64},{64,80},{80,96},{96,112},{112,128},... | collective-permute-start | bytes 49160 | tf_op jit(solution)/shard_map/ppermute | solution.py:356
  12.9 6.3 %collective-permute-start.1 = (bf16[64,128]{1,0:T(8,128)(2,1)S(1)}, bf16[64,128]{1,0:T(8,128)(2,1)S(1)}, u32[]{:S(2)}, u32[]{:S(2)}) collective-permute-start(bf16[64,128]{1,0:T(8,128)(2,1)S(1)} %get-tuple-element.21), channel_id=1, source_target_pairs={{16,0},{32,16},{48,32},{64,48},{80,64},{96,80},{112,96},{128,112},... | collective-permute-start | bytes 49160 | tf_op jit(solution)/shard_map/ppermute | solution.py:357
  20.1 23.6 %all-to-all-start = ((bf16[8,144,128]{2,1,0:T(8,128)(2,1)}), bf16[8,144,128]{2,1,0:T(8,128)(2,1)S(1)}, u32[]{:S(2)}, u32[]{:S(2)}) async-start(bf16[8,144,128]{2,1,0:T(8,128)(2,1)} %pack.1), calls=%async_computation | async-start | bytes 589824 | tf_op jit(solution)/shard_map/all_to_all | solution.py:366
  28.9 98.1 %all-gather.7.cloned.1.call-start = ((), (), s32[]{:S(2)}) async-start(), calls=%async_computation.5 | async-start | bytes 4718592 | tf_op jit(solution)/shard_map/all_gather | solution.py:377
  28.9 1.0 copy-start.1
  30.0 1.0 copy-start.2
  43.7 11.2 %collective-permute-start.2 = (bf16[8,144,128]{2,1,0:T(8,128)(2,1)S(1)}, bf16[8,144,128]{2,1,0:T(8,128)(2,1)S(1)}, u32[]{:S(2)}, u32[]{:S(2)}) collective-permute-start(bf16[8,144,128]{2,1,0:T(8,128)(2,1)S(1)} %all-to-all-done.own), channel_id=1, source_target_pairs={{0,8},{8,0},{1,9},{9,1},{2,10},{10,2},{3,11},{11,3},{4,12},{12,4},... | collective-permute-start | bytes 884744 | tf_op jit(solution)/shard_map/ppermute | solution.py:27
  48.3 8.7 %collective-permute-start.3 = (bf16[8,144,128]{2,1,0:T(8,128)(2,1)S(1)}, bf16[8,144,128]{2,1,0:T(8,128)(2,1)S(1)}, u32[]{:S(2)}, u32[]{:S(2)}) collective-permute-start(bf16[8,144,128]{2,1,0:T(8,128)(2,1)S(1)} %all-to-all-done.own), channel_id=1, source_target_pairs={{0,16},{16,0},{1,17},{17,1},{2,18},{18,2},{3,19},{19,3},{4,20},{20... | collective-permute-start | bytes 884744 | tf_op jit(solution)/shard_map/ppermute | solution.py:27
  54.9 3.5 %collective-permute-start.4 = (bf16[8,144,128]{2,1,0:T(8,128)(2,1)S(1)}, bf16[8,144,128]{2,1,0:T(8,128)(2,1)S(1)}, u32[]{:S(2)}, u32[]{:S(2)}) collective-permute-start(bf16[8,144,128]{2,1,0:T(8,128)(2,1)S(1)} %collective-permute-done.2.across), channel_id=1, source_target_pairs={{0,16},{16,0},{1,17},{17,1},{2,18},{18,2},{3,19},{19,3},{4,20},{20... | collective-permute-start | bytes 884744 | tf_op jit(solution)/shard_map/ppermute | solution.py:27
  56.8 68.2 %copy-start.4 = (f32[1024]{0:T(1024)S(1)}, f32[1024]{0:T(1024)}, u32[]{:S(2)}) copy-start(f32[1024]{0:T(1024)} %param.17) | copy-start | bytes 12292
  59.5 51.0 %copy-start = (bf16[896,1024]{1,0:T(8,128)(2,1)S(1)}, bf16[896,1024]{1,0:T(8,128)(2,1)}, u32[]{:S(2)}) copy-start(bf16[896,1024]{1,0:T(8,128)(2,1)} %all-gather.5.cloned.1.call-done) | copy-start | bytes 5505028
  90.7 13.6 %collective-permute-start.5 = (bf16[256,512]{1,0:T(8,128)(2,1)S(1)}, bf16[256,512]{1,0:T(8,128)(2,1)S(1)}, u32[]{:S(2)}, u32[]{:S(2)}) collective-permute-start(bf16[256,512]{1,0:T(8,128)(2,1)S(1)} %bn.1.own), channel_id=1, source_target_pairs={{0,8},{8,0},{1,9},{9,1},{2,10},{10,2},{3,11},{11,3},{4,12},{12,4},... | collective-permute-start | bytes 786440 | tf_op jit(solution)/shard_map/ppermute | solution.py:27
  95.1 14.3 %collective-permute-start.6 = (bf16[256,512]{1,0:T(8,128)(2,1)S(1)}, bf16[256,512]{1,0:T(8,128)(2,1)S(1)}, u32[]{:S(2)}, u32[]{:S(2)}) collective-permute-start(bf16[256,512]{1,0:T(8,128)(2,1)S(1)} %bn.1.own), channel_id=1, source_target_pairs={{0,16},{16,0},{1,17},{17,1},{2,18},{18,2},{3,19},{19,3},{4,20},{20... | collective-permute-start | bytes 786440 | tf_op jit(solution)/shard_map/ppermute | solution.py:27
  104.2 6.3 %collective-permute-start.7 = (bf16[256,512]{1,0:T(8,128)(2,1)S(1)}, bf16[256,512]{1,0:T(8,128)(2,1)S(1)}, u32[]{:S(2)}, u32[]{:S(2)}) collective-permute-start(bf16[256,512]{1,0:T(8,128)(2,1)S(1)} %collective-permute-done.5.across), channel_id=1, source_target_pairs={{0,16},{16,0},{1,17},{17,1},{2,18},{18,2},{3,19},{19,3},{4,20},{20... | collective-permute-start | bytes 786440 | tf_op jit(solution)/shard_map/ppermute | solution.py:27
  111.0 10.9 %collective-permute-start.8 = (bf16[256,512]{1,0:T(8,128)(2,1)S(1)}, bf16[256,512]{1,0:T(8,128)(2,1)S(1)}, u32[]{:S(2)}, u32[]{:S(2)}) collective-permute-start(bf16[256,512]{1,0:T(8,128)(2,1)S(1)} %mix.1.own), channel_id=1, source_target_pairs={{0,8},{8,0},{1,9},{9,1},{2,10},{10,2},{3,11},{11,3},{4,12},{12,4},... | collective-permute-start | bytes 786440 | tf_op jit(solution)/shard_map/ppermute | solution.py:27
  115.4 9.9 %collective-permute-start.9 = (bf16[256,512]{1,0:T(8,128)(2,1)S(1)}, bf16[256,512]{1,0:T(8,128)(2,1)S(1)}, u32[]{:S(2)}, u32[]{:S(2)}) collective-permute-start(bf16[256,512]{1,0:T(8,128)(2,1)S(1)} %mix.1.own), channel_id=1, source_target_pairs={{0,16},{16,0},{1,17},{17,1},{2,18},{18,2},{3,19},{19,3},{4,20},{20... | collective-permute-start | bytes 786440 | tf_op jit(solution)/shard_map/ppermute | solution.py:27
  121.9 4.2 %collective-permute-start.10 = (bf16[256,512]{1,0:T(8,128)(2,1)S(1)}, bf16[256,512]{1,0:T(8,128)(2,1)S(1)}, u32[]{:S(2)}, u32[]{:S(2)}) collective-permute-start(bf16[256,512]{1,0:T(8,128)(2,1)S(1)} %collective-permute-done.8.across), channel_id=1, source_target_pairs={{0,16},{16,0},{1,17},{17,1},{2,18},{18,2},{3,19},{19,3},{4,20},{20... | collective-permute-start | bytes 786440 | tf_op jit(solution)/shard_map/ppermute | solution.py:27
  131.2 3.8 %collective-permute-start.11 = (bf16[1024,256]{1,0:T(8,128)(2,1)S(1)}, bf16[1024,256]{1,0:T(8,128)(2,1)S(1)}, u32[]{:S(2)}, u32[]{:S(2)}) collective-permute-start(bf16[1024,256]{1,0:T(8,128)(2,1)S(1)} %get-tuple-element.32), channel_id=1, source_target_pairs={{0,16},{16,0},{1,17},{17,1},{2,18},{18,2},{3,19},{19,3},{4,20},{20... | collective-permute-start | bytes 1572872 | tf_op jit(solution)/shard_map/ppermute | solution.py:27
Sparse Core Ops, SparseCore 0:
  9.4 50.0 all-gather.4
  61.6 60.8 all-gather.6

commit v9 on v8

--- a/solution.py
+++ b/solution.py
@@ -63,7 +63,7 @@
         (shift, small.at[40:41]),
         (glu.at[0, half], parts.at[0:32]),
         (glu.at[1, half], parts.at[32:64]),
-        (conv_out.at[half], parts.at[64:96]),
+        (conv_out, parts.at[64:128]),
         (tok.at[:, 0:LANES], first),
         (tok.at[:, frames - LANES : frames], last),
         (tok, near),
@@ -85,9 +85,9 @@
         piece = rest.astype(BF).astype(F32)
         packed = packed + (piece if i == 0 else pltpu.roll(piece, 32 * i, 1))
         rest = rest - piece
-    parts[96:112] = jnp.zeros((16, parts.shape[1]), BF)
+    parts[128:144] = jnp.zeros((16, parts.shape[1]), BF)
     for i in range(3):
-        parts[96:112, LANES * i : LANES * (i + 1)] = packed[16 * i : 16 * i + 16].astype(BF)
+        parts[128:144, LANES * i : LANES * (i + 1)] = packed[16 * i : 16 * i + 16].astype(BF)
     for copy in loads[3:6]:
         copy.wait()
     final = pltpu.make_async_copy(parts, out, sems.at[9])
@@ -137,7 +137,7 @@
 ):
     loads = [
         pltpu.make_async_copy(first.at[:, 0:64], weight, sems.at[0]),
-        pltpu.make_async_copy(first.at[:, 96:112, 0:384], small, sems.at[1]),
+        pltpu.make_async_copy(first.at[:, 128:144, 0:384], small, sems.at[1]),
     ]
     for copy in loads:
         copy.start()
@@ -157,9 +157,7 @@
                 high = pltpu.roll(two, (LANES + 32 - 32 * i) % LANES, 1)
                 part = jnp.where(lane < 32, low, jnp.where(lane < 64, high, 0.0))
                 edge[at(row + 16 * i, 16, 16), :] = part
-    for z in range(nz):
-        row = xhi * (64 * nz) + 64 * z + 32 * core
-        res[32 * z : 32 * z + 32, :] = tok[at(row, 32, 32), :]
+    res[...] = tok[at(xhi * (64 * nz), 64 * nz, 64 * nz), 0:256]
 
     for copy in loads:
         copy.wait()
@@ -225,7 +223,7 @@
     out[:, 2:4] = jnp.broadcast_to(square[None], (out.shape[0],) + square.shape)
 
 
-def bn_kernel(conv, stats, par, out):
+def bn_kernel(conv, stats, par, near, away):
     frames = 8 * conv.shape[0]
     mean, square = merged(stats[...], frames)
     scale = lax.rsqrt(square * (1.0 / (frames * stats.shape[0])) + EPS)
@@ -233,33 +231,35 @@
         cols = slice(LANES * h, LANES * (h + 1))
         value = (conv[:, cols] - mean[h : h + 1]) * (scale[h : h + 1] * par[0:1, cols])
         value = value + par[1:2, cols]
-        out[cols, :] = (value * jax.nn.sigmoid(value)).T.astype(BF)
-
-
-def place_blocks(own, across, beside, far, whole):
+        value = (value * jax.nn.sigmoid(value)).T.astype(BF)
+        half = near.shape[1]
+        near[cols, :] = value[:, :half]
+        away[cols, :] = value[:, half:]
+
+
+def mix_kernel(own, across, beside, far, weight, res, out, whole):
     core, xhi = place()
-    nz, half = 8, 256
-    for blk, c, x in ((own, core, xhi), (across, core, 1 - xhi)):
-        for z in range(nz):
+    for blk, c, x in (
+        (own, core, xhi),
+        (across, core, 1 - xhi),
+        (beside, 1 - core, xhi),
+        (far, 1 - core, 1 - xhi),
+    ):
+        for z in range(8):
             row = x * 512 + 64 * z + 32 * c
             whole[at(row, 32, 32), :] = blk[32 * z : 32 * z + 32, :]
-    for blk, c, x in ((beside, 1 - core, xhi), (far, 1 - core, 1 - xhi)):
-        for z in range(nz):
-            row = x * 512 + 64 * z + 32 * c
-            whole[at(row, 32, 32), :half] = blk[32 * z : 32 * z + 32, half:]
-            whole[at(row, 32, 32), half:] = blk[32 * z : 32 * z + 32, :half]
-
-
-def mix_kernel(own, across, beside, far, blocks, res, out, whole):
-    place_blocks(own, across, beside, far, whole)
-    weight = blocks[...].reshape(256, blocks.shape[2])
-    mixed = jnp.dot(weight, whole[...], preferred_element_type=F32)
+    w = weight[...].reshape(512, weight.shape[2])
+    mixed = jnp.dot(w, whole[...], preferred_element_type=F32)
     out[...] = (res[...].astype(F32) + mixed).astype(BF)
 
 
 def norm_kernel(own, across, beside, far, gain, near, normed, whole):
-    place_blocks(own, across, beside, far, whole)
-    half = normed.shape[1] // 2
+    xhi = place()[1]
+    size, half = own.shape
+    whole[at(xhi * size, size, size), :half] = own[...]
+    whole[at((1 - xhi) * size, size, size), :half] = across[...]
+    whole[at(xhi * size, size, size), half:] = beside[...]
+    whole[at((1 - xhi) * size, size, size), half:] = far[...]
     near[...] = whole[:, :half]
     for c in range(2):
         cols = slice(half * c, half * (c + 1))
@@ -324,7 +324,7 @@
     first, tok, head, tail = pl.pallas_call(
         weight_kernel,
         out_shape=(
-            shape((112, full), BF),
+            shape((144, full), BF),
             shape((width, frames), BF),
             shape((width, LANES), BF),
             shape((width, LANES), BF),
@@ -333,7 +333,7 @@
         out_specs=(HBM, VMEM, VMEM, VMEM),
         scratch_shapes=[
             pltpu.VMEM((48, LANES), F32),
-            pltpu.VMEM((112, full), BF),
+            pltpu.VMEM((144, full), BF),
             pltpu.VMEM((48, width), F32),
             pltpu.SemaphoreType.DMA((10,)),
         ],
@@ -383,7 +383,7 @@
             shape((2 * run, 256), F32),
             shape((nz, 4, LANES), F32),
             shape((8, 256), F32),
-            shape((256, 2 * run), BF),
+            shape((full // 2, run), BF),
         ),
         in_specs=[VMEM] * 4 + [HBM, VMEM],
         out_specs=(VMEM,) * 4,
@@ -408,28 +408,31 @@
         name="merge",
     )(stats)
     stats = lax.all_to_all(stats, (XLO, Y), 0, 0, tiled=True)
-    activated = pl.pallas_call(
+    own, other = pl.pallas_call(
         bn_kernel,
-        out_shape=shape((256, 2 * run), BF),
+        out_shape=(shape((256, run), BF),) * 2,
         in_specs=[VMEM] * 3,
-        out_specs=VMEM,
+        out_specs=(VMEM,) * 2,
         compiler_params=PARAMS,
         name="bn",
     )(conv, stats, par)
+    across = swap(own, XHI)
+    far = lax.ppermute(other, (CORE, XHI), [(i, 3 - i) for i in range(4)])
+    beside = swap(other, CORE)
     block = pl.pallas_call(
         mix_kernel,
-        out_shape=shape((256, 2 * run), BF),
+        out_shape=shape((full // 2, run), BF),
         grid=(1,),
         in_specs=[VMEM] * 4
         + [
-            pl.BlockSpec((nz, 32, full), lambda i: (0, 2, 0)),
+            pl.BlockSpec((nz, 64, full), lambda i: (0, 1, 0)),
             VMEM,
         ],
         out_specs=VMEM,
-        scratch_shapes=[pltpu.VMEM((full, 2 * run), BF)],
+        scratch_shapes=[pltpu.VMEM((full, run), BF)],
         compiler_params=PARAMS,
         name="mix",
-    )(*group_gather(activated), first, res)
+    )(own, across, beside, far, first, res)
     near, normed = pl.pallas_call(
         norm_kernel,
         out_shape=(shape((full, run), BF), shape((full, 2 * run), BF)),

time: 163 us -> 166 us (1.018)
  waiting for transfers between devices: 27.1 us -> 37.2 us
  starting transfers between devices: 58.3 us -> 51.8 us
    ppermute x10 -> x9, starting transfers between devices: 39.4 us -> 30.9 us  [swap(): return lax.ppermute(x, axis, [(0, 1), (1, 0)])]
    ppermute x0 -> x1, waiting for transfers between devices: none -> 6.54 us  [body(): far = lax.ppermute(other, (CORE, XHI), [(i, 3 - i) for i in range(4)])]
    ppermute x0 -> x1, starting transfers between devices: none -> 1.99 us  [body(): far = lax.ppermute(other, (CORE, XHI), [(i, 3 - i) for i in range(4)])]
    ppermute x10 -> x9, waiting for transfers between devices: 13.5 us -> 15.3 us  [swap(): return lax.ppermute(x, axis, [(0, 1), (1, 0)])]
    all_gather x1, waiting for transfers between devices: 1.14 us -> 2.81 us  [body(): first = lax.all_gather(first, Z)]
where the time goes in v9:
time: 166 us; the launch traced here: 165 us
  starting transfers between devices  51.8 us (31%)
  blocking collectives  44.7 us (27%)
  waiting for transfers between devices  37.2 us (22%)
  Pallas kernels  15.3 us (9%)
  between operations  13.6 us (8%)
  local copies, waits for them, and re-layouts  2.53 us (2%)
    ppermute x9, starting transfers between devices, swap(): return lax.ppermute(x, axis, [(0, 1), (1, 0)])  30.9 us
    all_to_all x1, blocking collectives, body(): lax.all_to_all(keep.reshape(2 * nz, width, run), (XHI, Z), 0, 0, tiled=True)  18.6 us
    ppermute x9, waiting for transfers between devices, swap(): return lax.ppermute(x, axis, [(0, 1), (1, 0)])  15.3 us
    all_to_all x1, blocking collectives, body(): stats = lax.all_to_all(stats, (XLO, Y), 0, 0, tiled=True)  15.2 us
    all_to_all x1, waiting for transfers between devices, body(): parts = lax.all_to_all(parts, Z, 0, 0, tiled=True)  11.7 us
    all_to_all x1, blocking collectives, body(): stats = lax.all_to_all(stats, Z, 0, 0, tiled=True)  10.9 us
    all_to_all x1, starting transfers between devices, body(): parts = lax.all_to_all(parts, Z, 0, 0, tiled=True)  8.79 us
    ppermute x1, waiting for transfers between devices, body(): far = lax.ppermute(other, (CORE, XHI), [(i, 3 - i) for i in range(4)])  6.54 us
  transfers between devices with their start and end apart: 15, of which 9 were waited for; matrix products, arithmetic and copies ran while one was open for 0% of the time, Pallas kernels for 5%

profile of v9, /device:TPU:1, one launch (start us, length us, event | category | flops | bytes accessed | tf_op | source)
XLA Modules:
  0.0 165.4 jit_solution(17471899192119764100)
XLA Ops:
  6.5 1.8 %weights.1 = (bf16[144,1024]{1,0:T(8,128)(2,1)}, bf16[64,2048]{1,0:T(8,128)(2,1)S(1)}, bf16[64,128]{1,0:T(8,128)(2,1)S(1)}, bf16[64,128]{1,0:T(8,128)(2,1)S(1)}) custom-call(bf16[2,64,1024]{2,1,0:T(8,128)(2,1)} %bitcast.15, bf16[64,1024]{1,0:T(8,128)(2,1)} %bitcast.17, f32[31,64]{1,0:T(8,128)} %depth.1, f32[1,64]{1,0:T(1,128)} %bitcast.20, ...), custom_call_target="tpu_custom_call" | custom-call | tf_op jit(solution)/shard_map/weights/pallas_call | solution.py:324
  8.4 4.6 %collective-permute-start = (bf16[64,128]{1,0:T(8,128)(2,1)S(1)}, bf16[64,128]{1,0:T(8,128)(2,1)S(1)}, u32[]{:S(2)}, u32[]{:S(2)}) collective-permute-start(bf16[64,128]{1,0:T(8,128)(2,1)S(1)} %get-tuple-element.22), channel_id=1, source_target_pairs={{0,16},{16,32},{32,48},{48,64},{64,80},{80,96},{96,112},{112,128},... | collective-permute-start | bytes 49160 | tf_op jit(solution)/shard_map/ppermute | solution.py:356
  13.0 5.5 %collective-permute-start.1 = (bf16[64,128]{1,0:T(8,128)(2,1)S(1)}, bf16[64,128]{1,0:T(8,128)(2,1)S(1)}, u32[]{:S(2)}, u32[]{:S(2)}) collective-permute-start(bf16[64,128]{1,0:T(8,128)(2,1)S(1)} %get-tuple-element.23), channel_id=1, source_target_pairs={{16,0},{32,16},{48,32},{64,48},{80,64},{96,80},{112,96},{128,112},... | collective-permute-start | bytes 49160 | tf_op jit(solution)/shard_map/ppermute | solution.py:357
  19.3 0.9 pack.1
  20.2 8.8 %all-to-all-start = ((bf16[8,144,128]{2,1,0:T(8,128)(2,1)}), bf16[8,144,128]{2,1,0:T(8,128)(2,1)S(1)}, u32[]{:S(2)}, u32[]{:S(2)}) async-start(bf16[8,144,128]{2,1,0:T(8,128)(2,1)} %pack.1), calls=%async_computation | async-start | bytes 589824 | tf_op jit(solution)/shard_map/all_to_all | solution.py:366
  29.0 1.0 copy-done.1
  30.0 1.0 copy-done.2
  31.1 1.0 blocks.1
  32.1 11.7 %all-to-all-done.own = bf16[8,144,128]{2,1,0:T(8,128)(2,1)S(1)} async-done(((bf16[8,144,128]{2,1,0:T(8,128)(2,1)}), bf16[8,144,128]{2,1,0:T(8,128)(2,1)S(1)}, u32[]{:S(2)}, u32[]{:S(2)}) %all-to-all-start) | async-done | bytes 294944 | tf_op jit(solution)/shard_map/all_to_all | solution.py:366
  43.7 4.7 %collective-permute-start.2 = (bf16[8,144,128]{2,1,0:T(8,128)(2,1)S(1)}, bf16[8,144,128]{2,1,0:T(8,128)(2,1)S(1)}, u32[]{:S(2)}, u32[]{:S(2)}) collective-permute-start(bf16[8,144,128]{2,1,0:T(8,128)(2,1)S(1)} %all-to-all-done.own), channel_id=1, source_target_pairs={{0,8},{8,0},{1,9},{9,1},{2,10},{10,2},{3,11},{11,3},{4,12},{12,4},... | collective-permute-start | bytes 884744 | tf_op jit(solution)/shard_map/ppermute | solution.py:27
  48.4 1.9 %collective-permute-start.3 = (bf16[8,144,128]{2,1,0:T(8,128)(2,1)S(1)}, bf16[8,144,128]{2,1,0:T(8,128)(2,1)S(1)}, u32[]{:S(2)}, u32[]{:S(2)}) collective-permute-start(bf16[8,144,128]{2,1,0:T(8,128)(2,1)S(1)} %all-to-all-done.own), channel_id=1, source_target_pairs={{0,16},{16,0},{1,17},{17,1},{2,18},{18,2},{3,19},{19,3},{4,20},{20... | collective-permute-start | bytes 884744 | tf_op jit(solution)/shard_map/ppermute | solution.py:27
  50.3 4.7 %collective-permute-done.2.across = bf16[8,144,128]{2,1,0:T(8,128)(2,1)S(1)} collective-permute-done((bf16[8,144,128]{2,1,0:T(8,128)(2,1)S(1)}, bf16[8,144,128]{2,1,0:T(8,128)(2,1)S(1)}, u32[]{:S(2)}, u32[]{:S(2)}) %collective-permute-start.2) | collective-permute-done | bytes 294944 | tf_op jit(solution)/shard_map/ppermute | solution.py:27
  55.0 1.9 %collective-permute-start.4 = (bf16[8,144,128]{2,1,0:T(8,128)(2,1)S(1)}, bf16[8,144,128]{2,1,0:T(8,128)(2,1)S(1)}, u32[]{:S(2)}, u32[]{:S(2)}) collective-permute-start(bf16[8,144,128]{2,1,0:T(8,128)(2,1)S(1)} %collective-permute-done.2.across), channel_id=1, source_target_pairs={{0,16},{16,0},{1,17},{17,1},{2,18},{18,2},{3,19},{19,3},{4,20},{20... | collective-permute-start | bytes 884744 | tf_op jit(solution)/shard_map/ppermute | solution.py:27
  57.2 1.3 collective-permute-done.4.far
  58.5 2.8 %all-gather.5.cloned.1.call-done = bf16[1152,1024]{1,0:T(8,128)(2,1)} async-done(((bf16[144,1024]{1,0:T(8,128)(2,1)}), bf16[1152,1024]{1,0:T(8,128)(2,1)}) %all-gather.5.cloned.1.call-update) | async-done | bytes 2359312 | tf_op jit(solution)/shard_map/all_gather | solution.py:352
  61.3 5.2 %conv.1 = (f32[512,256]{1,0:T(8,128)S(1)}, f32[8,4,128]{2,1,0:T(4,128)S(1)}, f32[8,256]{1,0:T(8,128)S(1)}, bf16[512,256]{1,0:T(8,128)(2,1)S(1)}) custom-call(bf16[8,144,128]{2,1,0:T(8,128)(2,1)S(1)} %all-to-all-done.own, bf16[8,144,128]{2,1,0:T(8,128)(2,1)S(1)} %collective-permute-done.2.across, bf16[8,144,128]{2,1,0:T(8,128)(2,1)S(1)} %collective-permute-done.3.beside, ...), custom_call_target="tpu_custom_call" | custom-call | tf_op jit(solution)/shard_map/conv/pallas_call | solution.py:380
  66.5 10.9 %all_to_all.20.stats = f32[8,4,128]{2,1,0:T(4,128)S(1)} all-to-all(f32[8,4,128]{2,1,0:T(4,128)S(1)} %get-tuple-element.27), channel_id=1, replica_groups=mesh['xlo'=2,'y'=8,'core'=2,'xhi'=2,'z'=8] {'z'}, dimensions={0} | all-to-all | bytes 32768 | tf_op jit(solution)/shard_map/all_to_all | solution.py:401
  77.4 15.2 %all_to_all.21.stats = f32[16,4,128]{2,1,0:T(4,128)S(1)} all-to-all(f32[16,4,128]{2,1,0:T(4,128)S(1)} %merge.1), channel_id=1, replica_groups=mesh['xlo'=2,'y'=8,'core'=2,'xhi'=2,'z'=8] {'xlo','y'}, dimensions={0} | all-to-all | bytes 65536 | tf_op jit(solution)/shard_map/all_to_all | solution.py:410
  92.9 4.4 %collective-permute-start.5 = (bf16[256,256]{1,0:T(8,128)(2,1)S(1)}, bf16[256,256]{1,0:T(8,128)(2,1)S(1)}, u32[]{:S(2)}, u32[]{:S(2)}) collective-permute-start(bf16[256,256]{1,0:T(8,128)(2,1)S(1)} %get-tuple-element.29.own), channel_id=1, source_target_pairs={{0,8},{8,0},{1,9},{9,1},{2,10},{10,2},{3,11},{11,3},{4,12},{12,4},... | collective-permute-start | bytes 393224 | tf_op jit(solution)/shard_map/ppermute | solution.py:27
  97.3 8.8 %collective-permute-start.6 = (bf16[256,256]{1,0:T(8,128)(2,1)S(1)}, bf16[256,256]{1,0:T(8,128)(2,1)S(1)}, u32[]{:S(2)}, u32[]{:S(2)}) collective-permute-start(bf16[256,256]{1,0:T(8,128)(2,1)S(1)} %get-tuple-element.30), channel_id=1, source_target_pairs={{0,16},{16,0},{1,17},{17,1},{2,18},{18,2},{3,19},{19,3},{4,20},{20... | collective-permute-start | bytes 393224 | tf_op jit(solution)/shard_map/ppermute | solution.py:27
  106.0 2.0 %collective-permute-start.7 = (bf16[256,256]{1,0:T(8,128)(2,1)S(1)}, bf16[256,256]{1,0:T(8,128)(2,1)S(1)}, u32[]{:S(2)}, u32[]{:S(2)}) collective-permute-start(bf16[256,256]{1,0:T(8,128)(2,1)S(1)} %get-tuple-element.30), channel_id=1, source_target_pairs={{0,24},{8,16},{16,8},{24,0},{1,25},{9,17},{17,9},{25,1},{2,26},{10... | collective-permute-start | bytes 393224 | tf_op jit(solution)/shard_map/ppermute | solution.py:420
  108.0 6.5 %collective-permute-done.7.far = bf16[256,256]{1,0:T(8,128)(2,1)S(1)} collective-permute-done((bf16[256,256]{1,0:T(8,128)(2,1)S(1)}, bf16[256,256]{1,0:T(8,128)(2,1)S(1)}, u32[]{:S(2)}, u32[]{:S(2)}) %collective-permute-start.7) | collective-permute-done | bytes 131104 | tf_op jit(solution)/shard_map/ppermute | solution.py:420
  115.1 2.5 %collective-permute-start.8 = (bf16[512,256]{1,0:T(8,128)(2,1)S(1)}, bf16[512,256]{1,0:T(8,128)(2,1)S(1)}, u32[]{:S(2)}, u32[]{:S(2)}) collective-permute-start(bf16[512,256]{1,0:T(8,128)(2,1)S(1)} %mix.1.own), channel_id=1, source_target_pairs={{0,8},{8,0},{1,9},{9,1},{2,10},{10,2},{3,11},{11,3},{4,12},{12,4},... | collective-permute-start | bytes 786440 | tf_op jit(solution)/shard_map/ppermute | solution.py:27
  117.5 1.9 %collective-permute-start.9 = (bf16[512,256]{1,0:T(8,128)(2,1)S(1)}, bf16[512,256]{1,0:T(8,128)(2,1)S(1)}, u32[]{:S(2)}, u32[]{:S(2)}) collective-permute-start(bf16[512,256]{1,0:T(8,128)(2,1)S(1)} %mix.1.own), channel_id=1, source_target_pairs={{0,16},{16,0},{1,17},{17,1},{2,18},{18,2},{3,19},{19,3},{4,20},{20... | collective-permute-start | bytes 786440 | tf_op jit(solution)/shard_map/ppermute | solution.py:27
  119.5 6.9 %collective-permute-done.8.across = bf16[512,256]{1,0:T(8,128)(2,1)S(1)} collective-permute-done((bf16[512,256]{1,0:T(8,128)(2,1)S(1)}, bf16[512,256]{1,0:T(8,128)(2,1)S(1)}, u32[]{:S(2)}, u32[]{:S(2)}) %collective-permute-start.8) | collective-permute-done | bytes 262176 | tf_op jit(solution)/shard_map/ppermute | solution.py:27
  126.4 2.7 %collective-permute-start.10 = (bf16[512,256]{1,0:T(8,128)(2,1)S(1)}, bf16[512,256]{1,0:T(8,128)(2,1)S(1)}, u32[]{:S(2)}, u32[]{:S(2)}) collective-permute-start(bf16[512,256]{1,0:T(8,128)(2,1)S(1)} %collective-permute-done.8.across), channel_id=1, source_target_pairs={{0,16},{16,0},{1,17},{17,1},{2,18},{18,2},{3,19},{19,3},{4,20},{20... | collective-permute-start | bytes 786440 | tf_op jit(solution)/shard_map/ppermute | solution.py:27
  129.4 0.9 collective-permute-done.10.far
  130.2 0.9 norm.1
  131.1 4.1 %ff.1 = (f32[1024,256]{1,0:T(8,128)S(1)}, bf16[1024,256]{1,0:T(8,128)(2,1)S(1)}) custom-call(bf16[1024,256]{1,0:T(8,128)(2,1)S(1)} %get-tuple-element.32.near, bf16[1024,512]{1,0:T(8,128)(2,1)S(1)} %get-tuple-element.33.normed, bf16[8,16,128,128]{3,2,1,0:T(8,128)(2,1)} %bitcast.13), custom_call_target="tpu_custom_call" | custom-call | tf_op jit(solution)/shard_map/ff/pallas_call | solution.py:445
  135.3 2.3 %collective-permute-start.11 = (bf16[1024,256]{1,0:T(8,128)(2,1)S(1)}, bf16[1024,256]{1,0:T(8,128)(2,1)S(1)}, u32[]{:S(2)}, u32[]{:S(2)}) collective-permute-start(bf16[1024,256]{1,0:T(8,128)(2,1)S(1)} %get-tuple-element.36), channel_id=1, source_target_pairs={{0,16},{16,0},{1,17},{17,1},{2,18},{18,2},{3,19},{19,3},{4,20},{20... | collective-permute-start | bytes 1572872 | tf_op jit(solution)/shard_map/ppermute | solution.py:27
  137.6 1.5 collective-permute-done.11
  139.2 18.6 %all_to_all.22.parts = bf16[16,64,256]{2,1,0:T(8,128)(2,1)S(1)} all-to-all(bf16[16,64,256]{2,1,0:T(8,128)(2,1)S(1)} %bitcast.14), channel_id=1, replica_groups=mesh['xlo'=2,'y'=8,'core'=2,'xhi'=2,'z'=8] {'xhi','z'}, dimensions={0} | all-to-all | bytes 1048576 | tf_op jit(solution)/shard_map/all_to_all | solution.py:459
  (26 shorter events, 3.0 us)
Async XLA Ops:
  6.5 50.4 %copy-start.3 = (f32[1024]{0:T(1024)S(1)}, f32[1024]{0:T(1024)}, u32[]{:S(2)}) copy-start(f32[1024]{0:T(1024)} %param.11) | copy-start | bytes 12292
  6.5 54.8 %all-gather.5.cloned.1.call-start = ((), (), s32[]{:S(2)}) async-start(), calls=%async_computation.4 | async-start | bytes 2654208 | tf_op jit(solution)/shard_map/all_gather | solution.py:352
  8.4 10.1 %collective-permute-start = (bf16[64,128]{1,0:T(8,128)(2,1)S(1)}, bf16[64,128]{1,0:T(8,128)(2,1)S(1)}, u32[]{:S(2)}, u32[]{:S(2)}) collective-permute-start(bf16[64,128]{1,0:T(8,128)(2,1)S(1)} %get-tuple-element.22), channel_id=1, source_target_pairs={{0,16},{16,32},{32,48},{48,64},{64,80},{80,96},{96,112},{112,128},... | collective-permute-start | bytes 49160 | tf_op jit(solution)/shard_map/ppermute | solution.py:356
  13.0 6.3 %collective-permute-start.1 = (bf16[64,128]{1,0:T(8,128)(2,1)S(1)}, bf16[64,128]{1,0:T(8,128)(2,1)S(1)}, u32[]{:S(2)}, u32[]{:S(2)}) collective-permute-start(bf16[64,128]{1,0:T(8,128)(2,1)S(1)} %get-tuple-element.23), channel_id=1, source_target_pairs={{16,0},{32,16},{48,32},{64,48},{80,64},{96,80},{112,96},{128,112},... | collective-permute-start | bytes 49160 | tf_op jit(solution)/shard_map/ppermute | solution.py:357
  20.2 23.6 %all-to-all-start = ((bf16[8,144,128]{2,1,0:T(8,128)(2,1)}), bf16[8,144,128]{2,1,0:T(8,128)(2,1)S(1)}, u32[]{:S(2)}, u32[]{:S(2)}) async-start(bf16[8,144,128]{2,1,0:T(8,128)(2,1)} %pack.1), calls=%async_computation | async-start | bytes 589824 | tf_op jit(solution)/shard_map/all_to_all | solution.py:366
  28.9 102.2 %all-gather.7.cloned.1.call-start = ((), (), s32[]{:S(2)}) async-start(), calls=%async_computation.5 | async-start | bytes 4718592 | tf_op jit(solution)/shard_map/all_gather | solution.py:377
  29.0 1.0 copy-start.1
  30.0 1.0 copy-start.2
  43.7 11.3 %collective-permute-start.2 = (bf16[8,144,128]{2,1,0:T(8,128)(2,1)S(1)}, bf16[8,144,128]{2,1,0:T(8,128)(2,1)S(1)}, u32[]{:S(2)}, u32[]{:S(2)}) collective-permute-start(bf16[8,144,128]{2,1,0:T(8,128)(2,1)S(1)} %all-to-all-done.own), channel_id=1, source_target_pairs={{0,8},{8,0},{1,9},{9,1},{2,10},{10,2},{3,11},{11,3},{4,12},{12,4},... | collective-permute-start | bytes 884744 | tf_op jit(solution)/shard_map/ppermute | solution.py:27
  48.4 8.8 %collective-permute-start.3 = (bf16[8,144,128]{2,1,0:T(8,128)(2,1)S(1)}, bf16[8,144,128]{2,1,0:T(8,128)(2,1)S(1)}, u32[]{:S(2)}, u32[]{:S(2)}) collective-permute-start(bf16[8,144,128]{2,1,0:T(8,128)(2,1)S(1)} %all-to-all-done.own), channel_id=1, source_target_pairs={{0,16},{16,0},{1,17},{17,1},{2,18},{18,2},{3,19},{19,3},{4,20},{20... | collective-permute-start | bytes 884744 | tf_op jit(solution)/shard_map/ppermute | solution.py:27
  55.0 3.5 %collective-permute-start.4 = (bf16[8,144,128]{2,1,0:T(8,128)(2,1)S(1)}, bf16[8,144,128]{2,1,0:T(8,128)(2,1)S(1)}, u32[]{:S(2)}, u32[]{:S(2)}) collective-permute-start(bf16[8,144,128]{2,1,0:T(8,128)(2,1)S(1)} %collective-permute-done.2.across), channel_id=1, source_target_pairs={{0,16},{16,0},{1,17},{17,1},{2,18},{18,2},{3,19},{19,3},{4,20},{20... | collective-permute-start | bytes 884744 | tf_op jit(solution)/shard_map/ppermute | solution.py:27
  57.2 71.9 %copy-start.4 = (f32[1024]{0:T(1024)S(1)}, f32[1024]{0:T(1024)}, u32[]{:S(2)}) copy-start(f32[1024]{0:T(1024)} %param.17) | copy-start | bytes 12292
  61.3 53.3 %copy-start = (bf16[1152,1024]{1,0:T(8,128)(2,1)S(1)}, bf16[1152,1024]{1,0:T(8,128)(2,1)}, u32[]{:S(2)}) copy-start(bf16[1152,1024]{1,0:T(8,128)(2,1)} %all-gather.5.cloned.1.call-done) | copy-start | bytes 7077892
  92.9 15.1 %collective-permute-start.5 = (bf16[256,256]{1,0:T(8,128)(2,1)S(1)}, bf16[256,256]{1,0:T(8,128)(2,1)S(1)}, u32[]{:S(2)}, u32[]{:S(2)}) collective-permute-start(bf16[256,256]{1,0:T(8,128)(2,1)S(1)} %get-tuple-element.29.own), channel_id=1, source_target_pairs={{0,8},{8,0},{1,9},{9,1},{2,10},{10,2},{3,11},{11,3},{4,12},{12,4},... | collective-permute-start | bytes 393224 | tf_op jit(solution)/shard_map/ppermute | solution.py:27
  97.3 10.8 %collective-permute-start.6 = (bf16[256,256]{1,0:T(8,128)(2,1)S(1)}, bf16[256,256]{1,0:T(8,128)(2,1)S(1)}, u32[]{:S(2)}, u32[]{:S(2)}) collective-permute-start(bf16[256,256]{1,0:T(8,128)(2,1)S(1)} %get-tuple-element.30), channel_id=1, source_target_pairs={{0,16},{16,0},{1,17},{17,1},{2,18},{18,2},{3,19},{19,3},{4,20},{20... | collective-permute-start | bytes 393224 | tf_op jit(solution)/shard_map/ppermute | solution.py:27
  106.0 8.6 %collective-permute-start.7 = (bf16[256,256]{1,0:T(8,128)(2,1)S(1)}, bf16[256,256]{1,0:T(8,128)(2,1)S(1)}, u32[]{:S(2)}, u32[]{:S(2)}) collective-permute-start(bf16[256,256]{1,0:T(8,128)(2,1)S(1)} %get-tuple-element.30), channel_id=1, source_target_pairs={{0,24},{8,16},{16,8},{24,0},{1,25},{9,17},{17,9},{25,1},{2,26},{10... | collective-permute-start | bytes 393224 | tf_op jit(solution)/shard_map/ppermute | solution.py:420
  115.1 11.3 %collective-permute-start.8 = (bf16[512,256]{1,0:T(8,128)(2,1)S(1)}, bf16[512,256]{1,0:T(8,128)(2,1)S(1)}, u32[]{:S(2)}, u32[]{:S(2)}) collective-permute-start(bf16[512,256]{1,0:T(8,128)(2,1)S(1)} %mix.1.own), channel_id=1, source_target_pairs={{0,8},{8,0},{1,9},{9,1},{2,10},{10,2},{3,11},{11,3},{4,12},{12,4},... | collective-permute-start | bytes 786440 | tf_op jit(solution)/shard_map/ppermute | solution.py:27
  117.5 11.8 %collective-permute-start.9 = (bf16[512,256]{1,0:T(8,128)(2,1)S(1)}, bf16[512,256]{1,0:T(8,128)(2,1)S(1)}, u32[]{:S(2)}, u32[]{:S(2)}) collective-permute-start(bf16[512,256]{1,0:T(8,128)(2,1)S(1)} %mix.1.own), channel_id=1, source_target_pairs={{0,16},{16,0},{1,17},{17,1},{2,18},{18,2},{3,19},{19,3},{4,20},{20... | collective-permute-start | bytes 786440 | tf_op jit(solution)/shard_map/ppermute | solution.py:27
  126.4 3.8 %collective-permute-start.10 = (bf16[512,256]{1,0:T(8,128)(2,1)S(1)}, bf16[512,256]{1,0:T(8,128)(2,1)S(1)}, u32[]{:S(2)}, u32[]{:S(2)}) collective-permute-start(bf16[512,256]{1,0:T(8,128)(2,1)S(1)} %collective-permute-done.8.across), channel_id=1, source_target_pairs={{0,16},{16,0},{1,17},{17,1},{2,18},{18,2},{3,19},{19,3},{4,20},{20... | collective-permute-start | bytes 786440 | tf_op jit(solution)/shard_map/ppermute | solution.py:27
  135.3 3.8 %collective-permute-start.11 = (bf16[1024,256]{1,0:T(8,128)(2,1)S(1)}, bf16[1024,256]{1,0:T(8,128)(2,1)S(1)}, u32[]{:S(2)}, u32[]{:S(2)}) collective-permute-start(bf16[1024,256]{1,0:T(8,128)(2,1)S(1)} %get-tuple-element.36), channel_id=1, source_target_pairs={{0,16},{16,0},{1,17},{17,1},{2,18},{18,2},{3,19},{19,3},{4,20},{20... | collective-permute-start | bytes 1572872 | tf_op jit(solution)/shard_map/ppermute | solution.py:27
Sparse Core Ops, SparseCore 0:
  9.4 51.8 all-gather.4
  63.4 60.5 all-gather.6

commit v10 on v8

--- a/solution.py
+++ b/solution.py
@@ -130,20 +130,10 @@
         out[z, 128:144] = packed.astype(BF)
 
 
-def conv_kernel(
-    own, across, beside, far, first, gain,
-    conv, stats, par, res,
-    tok, edge, win, weight, small, sems,
-):
-    loads = [
-        pltpu.make_async_copy(first.at[:, 0:64], weight, sems.at[0]),
-        pltpu.make_async_copy(first.at[:, 96:112, 0:384], small, sems.at[1]),
-    ]
-    for copy in loads:
-        copy.start()
+def gather_kernel(own, across, beside, far, gain, normed, res, tok, edge):
     core, xhi = place()
     lane = lax.broadcasted_iota(jnp.int32, (16, LANES), 1)
-    nz = small.shape[0]
+    nz = own.shape[0]
     for near, away, side in ((own, beside, xhi), (across, far, 1 - xhi)):
         for z in range(nz):
             row = side * (64 * nz) + 64 * z
@@ -161,8 +151,22 @@
         row = xhi * (64 * nz) + 64 * z + 32 * core
         res[32 * z : 32 * z + 32, :] = tok[at(row, 32, 32), :]
 
+    scale = gain[...]
+    for c in range(2):
+        cols = slice(256 * c, 256 * (c + 1))
+        normed[:, cols] = norm_rows(tok[:, cols].astype(F32), scale)
+    normed[:, 512:640] = norm_rows(edge[...], scale)
+
+
+def conv_kernel(normed, first, conv, stats, par, win, weight, small, sems):
+    loads = [
+        pltpu.make_async_copy(first.at[:, 96:112, 0:384], small, sems.at[1]),
+        pltpu.make_async_copy(first.at[:, 0:64], weight, sems.at[0]),
+    ]
     for copy in loads:
-        copy.wait()
+        copy.start()
+    nz = small.shape[0]
+    loads[0].wait()
     table = []
     lane = lax.broadcasted_iota(jnp.int32, (48, LANES), 1)
     for h in range(2):
@@ -175,11 +179,11 @@
             total = total + (x if i == 0 else pltpu.roll(x, 32 * i, 1))
         par[:, LANES * h : LANES * (h + 1)] = total[31:39]
         table.append(total)
+    loads[1].wait()
     glu = weight[...].reshape(64 * nz, weight.shape[2])
-    scale = gain[...]
     for c in range(3):
-        x = edge[...] if c == 2 else tok[:, 256 * c : 256 * (c + 1)].astype(F32)
-        paired = jnp.dot(glu, norm_rows(x, scale), preferred_element_type=F32)
+        x = normed[:, 512:640] if c == 2 else normed[:, 256 * c : 256 * (c + 1)]
+        paired = jnp.dot(glu, x, preferred_element_type=F32)
         cols = x.shape[1]
         paired = paired.reshape(nz, 2, 32, cols)
         gated = (paired[:, 0] * jax.nn.sigmoid(paired[:, 1])).astype(BF).astype(F32)
@@ -377,19 +381,25 @@
     blocks = lax.all_gather(blocks, Z)
 
     whole = group_gather(parts)
-    conv, stats, par, res = pl.pallas_call(
+    normed, res = pl.pallas_call(
+        gather_kernel,
+        out_shape=(shape((full, 2 * run + LANES), BF), shape((256, 2 * run), BF)),
+        in_specs=[VMEM] * 5,
+        out_specs=(VMEM,) * 2,
+        scratch_shapes=[pltpu.VMEM((full, 2 * run), BF), pltpu.VMEM((full, LANES), F32)],
+        compiler_params=PARAMS,
+        name="gather",
+    )(*whole, ln_conv_gain[:, None])
+    conv, stats, par = pl.pallas_call(
         conv_kernel,
         out_shape=(
             shape((2 * run, 256), F32),
             shape((nz, 4, LANES), F32),
             shape((8, 256), F32),
-            shape((256, 2 * run), BF),
         ),
-        in_specs=[VMEM] * 4 + [HBM, VMEM],
-        out_specs=(VMEM,) * 4,
+        in_specs=[VMEM, HBM],
+        out_specs=(VMEM,) * 3,
         scratch_shapes=[
-            pltpu.VMEM((full, 2 * run), BF),
-            pltpu.VMEM((full, LANES), F32),
             pltpu.VMEM((2, run + 40, 256), F32),
             pltpu.VMEM((nz, 64, full), BF),
             pltpu.VMEM((nz, 16, 3 * LANES), BF),
@@ -397,7 +407,7 @@
         ],
         compiler_params=PARAMS,
         name="conv",
-    )(*whole, *in_hbm(first), ln_conv_gain[:, None])
+    )(normed, *in_hbm(first))
     stats = lax.all_to_all(stats, Z, 0, 0, tiled=True)
     stats = pl.pallas_call(
         merge_kernel,

time: 163 us -> 162 us (level)
  local copies, waits for them, and re-layouts: 2.53 us -> 0.46 us
    unnamed x10, local copies, waits for them, and re-layouts: 2.09 us -> 0.02 us
    all_to_all x1, waiting for transfers between devices: 11.6 us -> 13.7 us  [body(): parts = lax.all_to_all(parts, Z, 0, 0, tiled=True)]
  transfers between devices with their start and end apart: 15 -> 15, of which waited for: 9 -> 9; matrix products, arithmetic and copies ran while one was open for 0% -> 0% of each run, Pallas kernels for 5% -> 6%
where the time goes in v10:
time: 162 us; the launch traced here: 161 us
  starting transfers between devices  58.2 us (36%)
  blocking collectives  44.5 us (27%)
  waiting for transfers between devices  28.2 us (17%)
  Pallas kernels  16.1 us (10%)
  between operations  13.7 us (8%)
    ppermute x10, starting transfers between devices, swap(): return lax.ppermute(x, axis, [(0, 1), (1, 0)])  39.3 us
    all_to_all x1, blocking collectives, body(): lax.all_to_all(keep.reshape(2 * nz, width, run), (XHI, Z), 0, 0, tiled=True)  18.7 us
    all_to_all x1, blocking collectives, body(): stats = lax.all_to_all(stats, (XLO, Y), 0, 0, tiled=True)  15.4 us
    all_to_all x1, waiting for transfers between devices, body(): parts = lax.all_to_all(parts, Z, 0, 0, tiled=True)  13.7 us
    ppermute x10, waiting for transfers between devices, swap(): return lax.ppermute(x, axis, [(0, 1), (1, 0)])  13.6 us
    all_to_all x1, blocking collectives, body(): stats = lax.all_to_all(stats, Z, 0, 0, tiled=True)  10.4 us
    all_to_all x1, starting transfers between devices, body(): parts = lax.all_to_all(parts, Z, 0, 0, tiled=True)  8.79 us
    ppermute x1, starting transfers between devices, body(): right = lax.ppermute(head, (XLO, Y, CORE), [(j, i) for i, j in up])  5.48 us
  transfers between devices with their start and end apart: 15, of which 9 were waited for; matrix products, arithmetic and copies ran while one was open for 0% of the time, Pallas kernels for 6%

profile of v10, /device:TPU:1, one launch (start us, length us, event | category | flops | bytes accessed | tf_op | source)
XLA Modules:
  0.0 161.3 jit_solution(16813845236191266469)
XLA Ops:
  6.5 1.8 %weights.1 = (bf16[112,1024]{1,0:T(8,128)(2,1)}, bf16[64,2048]{1,0:T(8,128)(2,1)S(1)}, bf16[64,128]{1,0:T(8,128)(2,1)S(1)}, bf16[64,128]{1,0:T(8,128)(2,1)S(1)}) custom-call(bf16[2,64,1024]{2,1,0:T(8,128)(2,1)} %bitcast.15, bf16[64,1024]{1,0:T(8,128)(2,1)} %bitcast.17, f32[31,64]{1,0:T(8,128)} %depth.1, f32[1,64]{1,0:T(1,128)} %bitcast.20, ...), custom_call_target="tpu_custom_call" | custom-call | tf_op jit(solution)/shard_map/weights/pallas_call | solution.py:328
  8.4 4.6 %collective-permute-start = (bf16[64,128]{1,0:T(8,128)(2,1)S(1)}, bf16[64,128]{1,0:T(8,128)(2,1)S(1)}, u32[]{:S(2)}, u32[]{:S(2)}) collective-permute-start(bf16[64,128]{1,0:T(8,128)(2,1)S(1)} %get-tuple-element.21), channel_id=1, source_target_pairs={{0,16},{16,32},{32,48},{48,64},{64,80},{80,96},{96,112},{112,128},... | collective-permute-start | bytes 49160 | tf_op jit(solution)/shard_map/ppermute | solution.py:360
  13.0 5.5 %collective-permute-start.1 = (bf16[64,128]{1,0:T(8,128)(2,1)S(1)}, bf16[64,128]{1,0:T(8,128)(2,1)S(1)}, u32[]{:S(2)}, u32[]{:S(2)}) collective-permute-start(bf16[64,128]{1,0:T(8,128)(2,1)S(1)} %get-tuple-element.22), channel_id=1, source_target_pairs={{16,0},{32,16},{48,32},{64,48},{80,64},{96,80},{112,96},{128,112},... | collective-permute-start | bytes 49160 | tf_op jit(solution)/shard_map/ppermute | solution.py:361
  18.5 0.8 collective-permute-done.1.right
  19.3 0.9 pack.1
  20.2 8.8 %all-to-all-start = ((bf16[8,144,128]{2,1,0:T(8,128)(2,1)}), bf16[8,144,128]{2,1,0:T(8,128)(2,1)S(1)}, u32[]{:S(2)}, u32[]{:S(2)}) async-start(bf16[8,144,128]{2,1,0:T(8,128)(2,1)} %pack.1), calls=%async_computation | async-start | bytes 589824 | tf_op jit(solution)/shard_map/all_to_all | solution.py:370
  29.0 1.0 blocks.1
  30.0 13.7 %all-to-all-done.own = bf16[8,144,128]{2,1,0:T(8,128)(2,1)S(1)} async-done(((bf16[8,144,128]{2,1,0:T(8,128)(2,1)}), bf16[8,144,128]{2,1,0:T(8,128)(2,1)S(1)}, u32[]{:S(2)}, u32[]{:S(2)}) %all-to-all-start) | async-done | bytes 294944 | tf_op jit(solution)/shard_map/all_to_all | solution.py:370
  43.8 4.7 %collective-permute-start.2 = (bf16[8,144,128]{2,1,0:T(8,128)(2,1)S(1)}, bf16[8,144,128]{2,1,0:T(8,128)(2,1)S(1)}, u32[]{:S(2)}, u32[]{:S(2)}) collective-permute-start(bf16[8,144,128]{2,1,0:T(8,128)(2,1)S(1)} %all-to-all-done.own), channel_id=1, source_target_pairs={{0,8},{8,0},{1,9},{9,1},{2,10},{10,2},{3,11},{11,3},{4,12},{12,4},... | collective-permute-start | bytes 884744 | tf_op jit(solution)/shard_map/ppermute | solution.py:27
  48.4 1.9 %collective-permute-start.3 = (bf16[8,144,128]{2,1,0:T(8,128)(2,1)S(1)}, bf16[8,144,128]{2,1,0:T(8,128)(2,1)S(1)}, u32[]{:S(2)}, u32[]{:S(2)}) collective-permute-start(bf16[8,144,128]{2,1,0:T(8,128)(2,1)S(1)} %all-to-all-done.own), channel_id=1, source_target_pairs={{0,16},{16,0},{1,17},{17,1},{2,18},{18,2},{3,19},{19,3},{4,20},{20... | collective-permute-start | bytes 884744 | tf_op jit(solution)/shard_map/ppermute | solution.py:27
  50.3 4.7 %collective-permute-done.2.across = bf16[8,144,128]{2,1,0:T(8,128)(2,1)S(1)} collective-permute-done((bf16[8,144,128]{2,1,0:T(8,128)(2,1)S(1)}, bf16[8,144,128]{2,1,0:T(8,128)(2,1)S(1)}, u32[]{:S(2)}, u32[]{:S(2)}) %collective-permute-start.2) | collective-permute-done | bytes 294944 | tf_op jit(solution)/shard_map/ppermute | solution.py:27
  55.0 1.9 %collective-permute-start.4 = (bf16[8,144,128]{2,1,0:T(8,128)(2,1)S(1)}, bf16[8,144,128]{2,1,0:T(8,128)(2,1)S(1)}, u32[]{:S(2)}, u32[]{:S(2)}) collective-permute-start(bf16[8,144,128]{2,1,0:T(8,128)(2,1)S(1)} %collective-permute-done.2.across), channel_id=1, source_target_pairs={{0,16},{16,0},{1,17},{17,1},{2,18},{18,2},{3,19},{19,3},{4,20},{20... | collective-permute-start | bytes 884744 | tf_op jit(solution)/shard_map/ppermute | solution.py:27
  57.2 1.3 collective-permute-done.4.far
  58.5 1.0 gather.1
  59.6 5.0 %conv.1 = (f32[512,256]{1,0:T(8,128)S(1)}, f32[8,4,128]{2,1,0:T(4,128)S(1)}, f32[8,256]{1,0:T(8,128)S(1)}) custom-call(bf16[1024,640]{1,0:T(8,128)(2,1)S(1)} %get-tuple-element.24.normed, bf16[8,112,1024]{2,1,0:T(8,128)(2,1)} %bitcast.11), custom_call_target="tpu_custom_call" | custom-call | tf_op jit(solution)/shard_map/conv/pallas_call | solution.py:393
  64.5 10.4 %all_to_all.20.stats = f32[8,4,128]{2,1,0:T(4,128)S(1)} all-to-all(f32[8,4,128]{2,1,0:T(4,128)S(1)} %get-tuple-element.27), channel_id=1, replica_groups=mesh['xlo'=2,'y'=8,'core'=2,'xhi'=2,'z'=8] {'z'}, dimensions={0} | all-to-all | bytes 32768 | tf_op jit(solution)/shard_map/all_to_all | solution.py:411
  75.0 15.4 %all_to_all.21.stats = f32[16,4,128]{2,1,0:T(4,128)S(1)} all-to-all(f32[16,4,128]{2,1,0:T(4,128)S(1)} %merge.1), channel_id=1, replica_groups=mesh['xlo'=2,'y'=8,'core'=2,'xhi'=2,'z'=8] {'xlo','y'}, dimensions={0} | all-to-all | bytes 65536 | tf_op jit(solution)/shard_map/all_to_all | solution.py:420
  90.6 4.3 %collective-permute-start.5 = (bf16[256,512]{1,0:T(8,128)(2,1)S(1)}, bf16[256,512]{1,0:T(8,128)(2,1)S(1)}, u32[]{:S(2)}, u32[]{:S(2)}) collective-permute-start(bf16[256,512]{1,0:T(8,128)(2,1)S(1)} %bn.1.own), channel_id=1, source_target_pairs={{0,8},{8,0},{1,9},{9,1},{2,10},{10,2},{3,11},{11,3},{4,12},{12,4},... | collective-permute-start | bytes 786440 | tf_op jit(solution)/shard_map/ppermute | solution.py:27
  95.0 9.1 %collective-permute-start.6 = (bf16[256,512]{1,0:T(8,128)(2,1)S(1)}, bf16[256,512]{1,0:T(8,128)(2,1)S(1)}, u32[]{:S(2)}, u32[]{:S(2)}) collective-permute-start(bf16[256,512]{1,0:T(8,128)(2,1)S(1)} %bn.1.own), channel_id=1, source_target_pairs={{0,16},{16,0},{1,17},{17,1},{2,18},{18,2},{3,19},{19,3},{4,20},{20... | collective-permute-start | bytes 786440 | tf_op jit(solution)/shard_map/ppermute | solution.py:27
  104.0 5.2 %collective-permute-start.7 = (bf16[256,512]{1,0:T(8,128)(2,1)S(1)}, bf16[256,512]{1,0:T(8,128)(2,1)S(1)}, u32[]{:S(2)}, u32[]{:S(2)}) collective-permute-start(bf16[256,512]{1,0:T(8,128)(2,1)S(1)} %collective-permute-done.5.across), channel_id=1, source_target_pairs={{0,16},{16,0},{1,17},{17,1},{2,18},{18,2},{3,19},{19,3},{4,20},{20... | collective-permute-start | bytes 786440 | tf_op jit(solution)/shard_map/ppermute | solution.py:27
  109.2 1.1 collective-permute-done.7.far
  110.9 4.3 %collective-permute-start.8 = (bf16[256,512]{1,0:T(8,128)(2,1)S(1)}, bf16[256,512]{1,0:T(8,128)(2,1)S(1)}, u32[]{:S(2)}, u32[]{:S(2)}) collective-permute-start(bf16[256,512]{1,0:T(8,128)(2,1)S(1)} %mix.1.own), channel_id=1, source_target_pairs={{0,8},{8,0},{1,9},{9,1},{2,10},{10,2},{3,11},{11,3},{4,12},{12,4},... | collective-permute-start | bytes 786440 | tf_op jit(solution)/shard_map/ppermute | solution.py:27
  115.2 2.6 %collective-permute-start.9 = (bf16[256,512]{1,0:T(8,128)(2,1)S(1)}, bf16[256,512]{1,0:T(8,128)(2,1)S(1)}, u32[]{:S(2)}, u32[]{:S(2)}) collective-permute-start(bf16[256,512]{1,0:T(8,128)(2,1)S(1)} %mix.1.own), channel_id=1, source_target_pairs={{0,16},{16,0},{1,17},{17,1},{2,18},{18,2},{3,19},{19,3},{4,20},{20... | collective-permute-start | bytes 786440 | tf_op jit(solution)/shard_map/ppermute | solution.py:27
  117.7 4.1 %collective-permute-done.8.across = bf16[256,512]{1,0:T(8,128)(2,1)S(1)} collective-permute-done((bf16[256,512]{1,0:T(8,128)(2,1)S(1)}, bf16[256,512]{1,0:T(8,128)(2,1)S(1)}, u32[]{:S(2)}, u32[]{:S(2)}) %collective-permute-start.8) | collective-permute-done | bytes 262176 | tf_op jit(solution)/shard_map/ppermute | solution.py:27
  121.8 3.1 %collective-permute-start.10 = (bf16[256,512]{1,0:T(8,128)(2,1)S(1)}, bf16[256,512]{1,0:T(8,128)(2,1)S(1)}, u32[]{:S(2)}, u32[]{:S(2)}) collective-permute-start(bf16[256,512]{1,0:T(8,128)(2,1)S(1)} %collective-permute-done.8.across), channel_id=1, source_target_pairs={{0,16},{16,0},{1,17},{17,1},{2,18},{18,2},{3,19},{19,3},{4,20},{20... | collective-permute-start | bytes 786440 | tf_op jit(solution)/shard_map/ppermute | solution.py:27
  125.2 0.9 collective-permute-done.10.far
  126.1 0.8 norm.1
  126.9 4.1 %ff.1 = (f32[1024,256]{1,0:T(8,128)S(1)}, bf16[1024,256]{1,0:T(8,128)(2,1)S(1)}) custom-call(bf16[1024,256]{1,0:T(8,128)(2,1)S(1)} %get-tuple-element.30.near, bf16[1024,512]{1,0:T(8,128)(2,1)S(1)} %get-tuple-element.31.normed, bf16[8,16,128,128]{3,2,1,0:T(8,128)(2,1)} %bitcast.13), custom_call_target="tpu_custom_call" | custom-call | tf_op jit(solution)/shard_map/ff/pallas_call | solution.py:452
  131.0 2.3 %collective-permute-start.11 = (bf16[1024,256]{1,0:T(8,128)(2,1)S(1)}, bf16[1024,256]{1,0:T(8,128)(2,1)S(1)}, u32[]{:S(2)}, u32[]{:S(2)}) collective-permute-start(bf16[1024,256]{1,0:T(8,128)(2,1)S(1)} %get-tuple-element.34), channel_id=1, source_target_pairs={{0,16},{16,0},{1,17},{17,1},{2,18},{18,2},{3,19},{19,3},{4,20},{20... | collective-permute-start | bytes 1572872 | tf_op jit(solution)/shard_map/ppermute | solution.py:27
  133.3 1.5 collective-permute-done.11
  135.0 18.7 %all_to_all.22.parts = bf16[16,64,256]{2,1,0:T(8,128)(2,1)S(1)} all-to-all(bf16[16,64,256]{2,1,0:T(8,128)(2,1)S(1)} %bitcast.14), channel_id=1, replica_groups=mesh['xlo'=2,'y'=8,'core'=2,'xhi'=2,'z'=8] {'xhi','z'}, dimensions={0} | all-to-all | bytes 1048576 | tf_op jit(solution)/shard_map/all_to_all | solution.py:466
  153.7 0.8 sum.1
  (27 shorter events, 1.5 us)
Async XLA Ops:
  6.5 22.5 %copy-start.1 = (bf16[1024,256]{1,0:T(8,128)(2,1)S(1)}, bf16[1024,256]{1,0:T(8,128)(2,1)}, u32[]{:S(2)}) copy-start(bf16[1024,256]{1,0:T(8,128)(2,1)} %ff_in.1) | copy-start | bytes 1572868
  6.5 22.5 %copy-start.2 = (bf16[256,1024]{1,0:T(8,128)(2,1)S(1)}, bf16[256,1024]{1,0:T(8,128)(2,1)}, u32[]{:S(2)}) copy-start(bf16[256,1024]{1,0:T(8,128)(2,1)} %ff_out.1) | copy-start | bytes 1572868
  6.5 53.0 %all-gather.5.cloned.1.call-start = ((), (), s32[]{:S(2)}) async-start(), calls=%async_computation.4 | async-start | bytes 2064384 | tf_op jit(solution)/shard_map/all_gather | solution.py:356
  8.4 48.6 %copy-start.3 = (f32[1024]{0:T(1024)S(1)}, f32[1024]{0:T(1024)}, u32[]{:S(2)}) copy-start(f32[1024]{0:T(1024)} %param.11) | copy-start | bytes 12292
  8.4 10.1 %collective-permute-start = (bf16[64,128]{1,0:T(8,128)(2,1)S(1)}, bf16[64,128]{1,0:T(8,128)(2,1)S(1)}, u32[]{:S(2)}, u32[]{:S(2)}) collective-permute-start(bf16[64,128]{1,0:T(8,128)(2,1)S(1)} %get-tuple-element.21), channel_id=1, source_target_pairs={{0,16},{16,32},{32,48},{48,64},{64,80},{80,96},{96,112},{112,128},... | collective-permute-start | bytes 49160 | tf_op jit(solution)/shard_map/ppermute | solution.py:360
  13.0 6.3 %collective-permute-start.1 = (bf16[64,128]{1,0:T(8,128)(2,1)S(1)}, bf16[64,128]{1,0:T(8,128)(2,1)S(1)}, u32[]{:S(2)}, u32[]{:S(2)}) collective-permute-start(bf16[64,128]{1,0:T(8,128)(2,1)S(1)} %get-tuple-element.22), channel_id=1, source_target_pairs={{16,0},{32,16},{48,32},{64,48},{80,64},{96,80},{112,96},{128,112},... | collective-permute-start | bytes 49160 | tf_op jit(solution)/shard_map/ppermute | solution.py:361
  20.2 23.6 %all-to-all-start = ((bf16[8,144,128]{2,1,0:T(8,128)(2,1)}), bf16[8,144,128]{2,1,0:T(8,128)(2,1)S(1)}, u32[]{:S(2)}, u32[]{:S(2)}) async-start(bf16[8,144,128]{2,1,0:T(8,128)(2,1)} %pack.1), calls=%async_computation | async-start | bytes 589824 | tf_op jit(solution)/shard_map/all_to_all | solution.py:370
  29.0 97.9 %all-gather.7.cloned.1.call-start = ((), (), s32[]{:S(2)}) async-start(), calls=%async_computation.5 | async-start | bytes 4718592 | tf_op jit(solution)/shard_map/all_gather | solution.py:381
  43.8 11.3 %collective-permute-start.2 = (bf16[8,144,128]{2,1,0:T(8,128)(2,1)S(1)}, bf16[8,144,128]{2,1,0:T(8,128)(2,1)S(1)}, u32[]{:S(2)}, u32[]{:S(2)}) collective-permute-start(bf16[8,144,128]{2,1,0:T(8,128)(2,1)S(1)} %all-to-all-done.own), channel_id=1, source_target_pairs={{0,8},{8,0},{1,9},{9,1},{2,10},{10,2},{3,11},{11,3},{4,12},{12,4},... | collective-permute-start | bytes 884744 | tf_op jit(solution)/shard_map/ppermute | solution.py:27
  48.4 8.7 %collective-permute-start.3 = (bf16[8,144,128]{2,1,0:T(8,128)(2,1)S(1)}, bf16[8,144,128]{2,1,0:T(8,128)(2,1)S(1)}, u32[]{:S(2)}, u32[]{:S(2)}) collective-permute-start(bf16[8,144,128]{2,1,0:T(8,128)(2,1)S(1)} %all-to-all-done.own), channel_id=1, source_target_pairs={{0,16},{16,0},{1,17},{17,1},{2,18},{18,2},{3,19},{19,3},{4,20},{20... | collective-permute-start | bytes 884744 | tf_op jit(solution)/shard_map/ppermute | solution.py:27
  55.0 3.5 %collective-permute-start.4 = (bf16[8,144,128]{2,1,0:T(8,128)(2,1)S(1)}, bf16[8,144,128]{2,1,0:T(8,128)(2,1)S(1)}, u32[]{:S(2)}, u32[]{:S(2)}) collective-permute-start(bf16[8,144,128]{2,1,0:T(8,128)(2,1)S(1)} %collective-permute-done.2.across), channel_id=1, source_target_pairs={{0,16},{16,0},{1,17},{17,1},{2,18},{18,2},{3,19},{19,3},{4,20},{20... | collective-permute-start | bytes 884744 | tf_op jit(solution)/shard_map/ppermute | solution.py:27
  59.5 50.8 %copy-start = (bf16[896,1024]{1,0:T(8,128)(2,1)S(1)}, bf16[896,1024]{1,0:T(8,128)(2,1)}, u32[]{:S(2)}) copy-start(bf16[896,1024]{1,0:T(8,128)(2,1)} %all-gather.5.cloned.1.call-done) | copy-start | bytes 5505028
  90.6 34.3 %copy-start.4 = (f32[1024]{0:T(1024)S(1)}, f32[1024]{0:T(1024)}, u32[]{:S(2)}) copy-start(f32[1024]{0:T(1024)} %param.17) | copy-start | bytes 12292
  90.6 13.4 %collective-permute-start.5 = (bf16[256,512]{1,0:T(8,128)(2,1)S(1)}, bf16[256,512]{1,0:T(8,128)(2,1)S(1)}, u32[]{:S(2)}, u32[]{:S(2)}) collective-permute-start(bf16[256,512]{1,0:T(8,128)(2,1)S(1)} %bn.1.own), channel_id=1, source_target_pairs={{0,8},{8,0},{1,9},{9,1},{2,10},{10,2},{3,11},{11,3},{4,12},{12,4},... | collective-permute-start | bytes 786440 | tf_op jit(solution)/shard_map/ppermute | solution.py:27
  95.0 14.3 %collective-permute-start.6 = (bf16[256,512]{1,0:T(8,128)(2,1)S(1)}, bf16[256,512]{1,0:T(8,128)(2,1)S(1)}, u32[]{:S(2)}, u32[]{:S(2)}) collective-permute-start(bf16[256,512]{1,0:T(8,128)(2,1)S(1)} %bn.1.own), channel_id=1, source_target_pairs={{0,16},{16,0},{1,17},{17,1},{2,18},{18,2},{3,19},{19,3},{4,20},{20... | collective-permute-start | bytes 786440 | tf_op jit(solution)/shard_map/ppermute | solution.py:27
  104.0 6.3 %collective-permute-start.7 = (bf16[256,512]{1,0:T(8,128)(2,1)S(1)}, bf16[256,512]{1,0:T(8,128)(2,1)S(1)}, u32[]{:S(2)}, u32[]{:S(2)}) collective-permute-start(bf16[256,512]{1,0:T(8,128)(2,1)S(1)} %collective-permute-done.5.across), channel_id=1, source_target_pairs={{0,16},{16,0},{1,17},{17,1},{2,18},{18,2},{3,19},{19,3},{4,20},{20... | collective-permute-start | bytes 786440 | tf_op jit(solution)/shard_map/ppermute | solution.py:27
  110.9 10.9 %collective-permute-start.8 = (bf16[256,512]{1,0:T(8,128)(2,1)S(1)}, bf16[256,512]{1,0:T(8,128)(2,1)S(1)}, u32[]{:S(2)}, u32[]{:S(2)}) collective-permute-start(bf16[256,512]{1,0:T(8,128)(2,1)S(1)} %mix.1.own), channel_id=1, source_target_pairs={{0,8},{8,0},{1,9},{9,1},{2,10},{10,2},{3,11},{11,3},{4,12},{12,4},... | collective-permute-start | bytes 786440 | tf_op jit(solution)/shard_map/ppermute | solution.py:27
  115.2 10.0 %collective-permute-start.9 = (bf16[256,512]{1,0:T(8,128)(2,1)S(1)}, bf16[256,512]{1,0:T(8,128)(2,1)S(1)}, u32[]{:S(2)}, u32[]{:S(2)}) collective-permute-start(bf16[256,512]{1,0:T(8,128)(2,1)S(1)} %mix.1.own), channel_id=1, source_target_pairs={{0,16},{16,0},{1,17},{17,1},{2,18},{18,2},{3,19},{19,3},{4,20},{20... | collective-permute-start | bytes 786440 | tf_op jit(solution)/shard_map/ppermute | solution.py:27
  121.8 4.3 %collective-permute-start.10 = (bf16[256,512]{1,0:T(8,128)(2,1)S(1)}, bf16[256,512]{1,0:T(8,128)(2,1)S(1)}, u32[]{:S(2)}, u32[]{:S(2)}) collective-permute-start(bf16[256,512]{1,0:T(8,128)(2,1)S(1)} %collective-permute-done.8.across), channel_id=1, source_target_pairs={{0,16},{16,0},{1,17},{17,1},{2,18},{18,2},{3,19},{19,3},{4,20},{20... | collective-permute-start | bytes 786440 | tf_op jit(solution)/shard_map/ppermute | solution.py:27
  131.0 3.8 %collective-permute-start.11 = (bf16[1024,256]{1,0:T(8,128)(2,1)S(1)}, bf16[1024,256]{1,0:T(8,128)(2,1)S(1)}, u32[]{:S(2)}, u32[]{:S(2)}) collective-permute-start(bf16[1024,256]{1,0:T(8,128)(2,1)S(1)} %get-tuple-element.34), channel_id=1, source_target_pairs={{0,16},{16,0},{1,17},{17,1},{2,18},{18,2},{3,19},{19,3},{4,20},{20... | collective-permute-start | bytes 1572872 | tf_op jit(solution)/shard_map/ppermute | solution.py:27
Sparse Core Ops, SparseCore 0:
  9.4 50.0 all-gather.4
  61.6 60.5 all-gather.6

commit v11 on v10

--- a/solution.py
+++ b/solution.py
@@ -261,16 +261,33 @@
     out[...] = (res[...].astype(F32) + mixed).astype(BF)
 
 
-def norm_kernel(own, across, beside, far, gain, near, normed, whole):
+def norm_kernel(own, across, beside, far, gain, near, here, there, whole):
     place_blocks(own, across, beside, far, whole)
-    half = normed.shape[1] // 2
+    half = here.shape[1]
     near[...] = whole[:, :half]
-    for c in range(2):
+    for c, normed in ((0, here), (1, there)):
         cols = slice(half * c, half * (c + 1))
-        normed[:, cols] = norm_rows(whole[:, cols].astype(F32), gain[...])
-
-
-def ff_kernel(near, normed, blocks, keep, give, hidden, w, sems):
+        normed[...] = norm_rows(whole[:, cols].astype(F32), gain[...])
+
+
+def feed_forward(normed, w, hidden, ready):
+    for z in range(0, 8, 2):
+        ready(z // 2)
+        rows = [jnp.concatenate([w[z + i, k] for k in range(8)], axis=1) for i in range(2)]
+        value = jnp.dot(
+            jnp.concatenate(rows, axis=0), normed[...], preferred_element_type=F32
+        )
+        hidden[LANES * z : LANES * (z + 2), :] = (value * jax.nn.sigmoid(value)).astype(BF)
+    ready(4)
+    for k in range(0, 8, 2):
+        rows = [jnp.concatenate([w[z, 8 + k + i] for z in range(8)], axis=1) for i in range(2)]
+        value = jnp.dot(
+            jnp.concatenate(rows, axis=0), hidden[...], preferred_element_type=F32
+        )
+        yield k, slice(LANES * k, LANES * (k + 2)), 0.5 * value
+
+
+def give_kernel(normed, blocks, give, w, hidden, sems):
     loads = [
         pltpu.make_async_copy(
             blocks.at[2 * i : 2 * i + 2, 0:8], w.at[2 * i : 2 * i + 2, 0:8], sems.at[i]
@@ -280,25 +297,15 @@
     loads.append(pltpu.make_async_copy(blocks.at[:, 8:16], w.at[:, 8:16], sems.at[4]))
     for copy in loads:
         copy.start()
+    for _, rows, value in feed_forward(normed, w, hidden, lambda i: loads[i].wait()):
+        give[rows, :] = value.astype(BF)
+
+
+def keep_kernel(near, normed, w, keep, hidden):
     xhi = place()[1]
-    half = normed.shape[1] // 2
-    for z in range(0, 8, 2):
-        loads[z // 2].wait()
-        rows = [jnp.concatenate([w[z + i, k] for k in range(8)], axis=1) for i in range(2)]
-        value = jnp.dot(
-            jnp.concatenate(rows, axis=0), normed[...], preferred_element_type=F32
-        )
-        hidden[LANES * z : LANES * (z + 2), :] = (value * jax.nn.sigmoid(value)).astype(BF)
-    loads[4].wait()
-    for k in range(0, 8, 2):
-        rows = [jnp.concatenate([w[z, 8 + k + i] for z in range(8)], axis=1) for i in range(2)]
-        value = jnp.dot(
-            jnp.concatenate(rows, axis=0), hidden[...], preferred_element_type=F32
-        )
-        rows = slice(LANES * k, LANES * (k + 2))
+    for k, rows, value in feed_forward(normed, w, hidden, lambda i: None):
         mine = jnp.where(xhi == k // 4, 1.0, 0.0)
-        keep[rows, :] = 0.5 * value[:, :half] + mine * near[rows, :].astype(F32)
-        give[rows, :] = (0.5 * value[:, half:]).astype(BF)
+        keep[rows, :] = value + mine * near[rows, :].astype(F32)
 
 
 def sum_kernel(parts, out):
@@ -440,28 +447,36 @@
         compiler_params=PARAMS,
         name="mix",
     )(*group_gather(activated), first, res)
-    near, normed = pl.pallas_call(
+    near, here, there = pl.pallas_call(
         norm_kernel,
-        out_shape=(shape((full, run), BF), shape((full, 2 * run), BF)),
+        out_shape=(shape((full, run), BF),) * 3,
         in_specs=[VMEM] * 5,
-        out_specs=(VMEM,) * 2,
+        out_specs=(VMEM,) * 3,
         scratch_shapes=[pltpu.VMEM((full, 2 * run), BF)],
         compiler_params=PARAMS,
         name="norm",
     )(*group_gather(block), ln_ff_gain[:, None])
-    keep, give = pl.pallas_call(
-        ff_kernel,
-        out_shape=(shape((full, run), F32), shape((full, run), BF)),
-        in_specs=[VMEM] * 2 + [HBM],
+    give, blocks = pl.pallas_call(
+        give_kernel,
+        out_shape=(shape((full, run), BF), shape((nz, 16, LANES, LANES), BF)),
+        in_specs=[VMEM, HBM],
         out_specs=(VMEM,) * 2,
-        scratch_shapes=[
-            pltpu.VMEM((full, 2 * run), BF),
-            pltpu.VMEM((nz, 16, LANES, LANES), BF),
-            pltpu.SemaphoreType.DMA((5,)),
-        ],
-        compiler_params=PARAMS,
-        name="ff",
-    )(near, normed, *in_hbm(blocks))
+        scratch_shapes=[pltpu.VMEM((full, run), BF), pltpu.SemaphoreType.DMA((5,))],
+        compiler_params=PARAMS,
+        name="give",
+    )(there, *in_hbm(blocks))
+    keep = pl.pallas_call(
+        keep_kernel,
+        out_shape=shape((full, run), F32),
+        in_specs=[VMEM] * 3,
+        out_specs=VMEM,
+        scratch_shapes=[pltpu.VMEM((full, run), BF)],
+        compiler_params=PARAMS,
+        cost_estimate=pl.CostEstimate(
+            flops=4 * full * full * run, bytes_accessed=6 << 20, transcendentals=full * run
+        ),
+        name="keep",
+    )(near, here, blocks)
     keep = (keep + swap(give, CORE).astype(F32)).astype(BF)
     keep = lax.all_to_all(keep.reshape(2 * nz, width, run), (XHI, Z), 0, 0, tiled=True)
     out = pl.pallas_call(

time: 162 us -> 162 us (level)
  waiting for transfers between devices: 28.2 us -> 24.9 us
  local copies, waits for them, and re-layouts: 0.46 us -> 2.53 us
    unnamed x10, local copies, waits for them, and re-layouts: 0.02 us -> 2.09 us
    all_to_all x1, waiting for transfers between devices: 13.7 us -> 11.6 us  [body(): parts = lax.all_to_all(parts, Z, 0, 0, tiled=True)]
    pallas_call x2 -> x3, Pallas kernels: 4.93 us -> 5.55 us  [the longest x1 3.51 us: body(): pl.pallas_call(give_kernel, out_shape=(shape((full, run), BF), shape((nz,...]
  transfers between devices with their start and end apart: 15 -> 15, of which waited for: 9 -> 9; matrix products, arithmetic and copies ran while one was open for 0% -> 0% of each run, Pallas kernels for 6% -> 7%
where the time goes in v11:
time: 162 us; the launch traced here: 161 us
  starting transfers between devices  58.3 us (36%)
  blocking collectives  44.5 us (27%)
  waiting for transfers between devices  24.9 us (15%)
  Pallas kernels  16.6 us (10%)
  between operations  13.7 us (8%)
  local copies, waits for them, and re-layouts  2.53 us (2%)
    ppermute x10, starting transfers between devices, swap(): return lax.ppermute(x, axis, [(0, 1), (1, 0)])  39.4 us
    all_to_all x1, blocking collectives, body(): lax.all_to_all(keep.reshape(2 * nz, width, run), (XHI, Z), 0, 0, tiled=True)  18.8 us
    all_to_all x1, blocking collectives, body(): stats = lax.all_to_all(stats, (XLO, Y), 0, 0, tiled=True)  15.3 us
    ppermute x10, waiting for transfers between devices, swap(): return lax.ppermute(x, axis, [(0, 1), (1, 0)])  12.3 us
    all_to_all x1, waiting for transfers between devices, body(): parts = lax.all_to_all(parts, Z, 0, 0, tiled=True)  11.6 us
    all_to_all x1, blocking collectives, body(): stats = lax.all_to_all(stats, Z, 0, 0, tiled=True)  10.4 us
    all_to_all x1, starting transfers between devices, body(): parts = lax.all_to_all(parts, Z, 0, 0, tiled=True)  8.79 us
    ppermute x1, starting transfers between devices, body(): right = lax.ppermute(head, (XLO, Y, CORE), [(j, i) for i, j in up])  5.48 us
  transfers between devices with their start and end apart: 15, of which 9 were waited for; matrix products, arithmetic and copies ran while one was open for 0% of the time, Pallas kernels for 7%

profile of v11, /device:TPU:1, one launch (start us, length us, event | category | flops | bytes accessed | tf_op | source)
XLA Modules:
  0.0 160.7 jit_solution(18219827460657180693)
XLA Ops:
  6.5 1.7 %weights.1 = (bf16[112,1024]{1,0:T(8,128)(2,1)}, bf16[64,2048]{1,0:T(8,128)(2,1)S(1)}, bf16[64,128]{1,0:T(8,128)(2,1)S(1)}, bf16[64,128]{1,0:T(8,128)(2,1)S(1)}) custom-call(bf16[2,64,1024]{2,1,0:T(8,128)(2,1)} %bitcast.15, bf16[64,1024]{1,0:T(8,128)(2,1)} %bitcast.17, f32[31,64]{1,0:T(8,128)} %depth.1, f32[1,64]{1,0:T(1,128)} %bitcast.20, ...), custom_call_target="tpu_custom_call" | custom-call | tf_op jit(solution)/shard_map/weights/pallas_call | solution.py:335
  8.3 4.6 %collective-permute-start = (bf16[64,128]{1,0:T(8,128)(2,1)S(1)}, bf16[64,128]{1,0:T(8,128)(2,1)S(1)}, u32[]{:S(2)}, u32[]{:S(2)}) collective-permute-start(bf16[64,128]{1,0:T(8,128)(2,1)S(1)} %get-tuple-element.22), channel_id=1, source_target_pairs={{0,16},{16,32},{32,48},{48,64},{64,80},{80,96},{96,112},{112,128},... | collective-permute-start | bytes 49160 | tf_op jit(solution)/shard_map/ppermute | solution.py:367
  12.9 5.5 %collective-permute-start.1 = (bf16[64,128]{1,0:T(8,128)(2,1)S(1)}, bf16[64,128]{1,0:T(8,128)(2,1)S(1)}, u32[]{:S(2)}, u32[]{:S(2)}) collective-permute-start(bf16[64,128]{1,0:T(8,128)(2,1)S(1)} %get-tuple-element.23), channel_id=1, source_target_pairs={{16,0},{32,16},{48,32},{64,48},{80,64},{96,80},{112,96},{128,112},... | collective-permute-start | bytes 49160 | tf_op jit(solution)/shard_map/ppermute | solution.py:368
  18.4 0.8 collective-permute-done.1.right
  19.2 0.9 pack.1
  20.1 8.8 %all-to-all-start = ((bf16[8,144,128]{2,1,0:T(8,128)(2,1)}), bf16[8,144,128]{2,1,0:T(8,128)(2,1)S(1)}, u32[]{:S(2)}, u32[]{:S(2)}) async-start(bf16[8,144,128]{2,1,0:T(8,128)(2,1)} %pack.1), calls=%async_computation | async-start | bytes 589824 | tf_op jit(solution)/shard_map/all_to_all | solution.py:377
  28.9 1.0 copy-done.1
  30.0 1.0 copy-done.2
  31.0 1.0 blocks.1
  32.0 11.6 %all-to-all-done.own = bf16[8,144,128]{2,1,0:T(8,128)(2,1)S(1)} async-done(((bf16[8,144,128]{2,1,0:T(8,128)(2,1)}), bf16[8,144,128]{2,1,0:T(8,128)(2,1)S(1)}, u32[]{:S(2)}, u32[]{:S(2)}) %all-to-all-start) | async-done | bytes 294944 | tf_op jit(solution)/shard_map/all_to_all | solution.py:377
  43.7 4.6 %collective-permute-start.2 = (bf16[8,144,128]{2,1,0:T(8,128)(2,1)S(1)}, bf16[8,144,128]{2,1,0:T(8,128)(2,1)S(1)}, u32[]{:S(2)}, u32[]{:S(2)}) collective-permute-start(bf16[8,144,128]{2,1,0:T(8,128)(2,1)S(1)} %all-to-all-done.own), channel_id=1, source_target_pairs={{0,8},{8,0},{1,9},{9,1},{2,10},{10,2},{3,11},{11,3},{4,12},{12,4},... | collective-permute-start | bytes 884744 | tf_op jit(solution)/shard_map/ppermute | solution.py:27
  48.3 1.9 %collective-permute-start.3 = (bf16[8,144,128]{2,1,0:T(8,128)(2,1)S(1)}, bf16[8,144,128]{2,1,0:T(8,128)(2,1)S(1)}, u32[]{:S(2)}, u32[]{:S(2)}) collective-permute-start(bf16[8,144,128]{2,1,0:T(8,128)(2,1)S(1)} %all-to-all-done.own), channel_id=1, source_target_pairs={{0,16},{16,0},{1,17},{17,1},{2,18},{18,2},{3,19},{19,3},{4,20},{20... | collective-permute-start | bytes 884744 | tf_op jit(solution)/shard_map/ppermute | solution.py:27
  50.2 4.7 %collective-permute-done.2.across = bf16[8,144,128]{2,1,0:T(8,128)(2,1)S(1)} collective-permute-done((bf16[8,144,128]{2,1,0:T(8,128)(2,1)S(1)}, bf16[8,144,128]{2,1,0:T(8,128)(2,1)S(1)}, u32[]{:S(2)}, u32[]{:S(2)}) %collective-permute-start.2) | collective-permute-done | bytes 294944 | tf_op jit(solution)/shard_map/ppermute | solution.py:27
  54.9 1.9 %collective-permute-start.4 = (bf16[8,144,128]{2,1,0:T(8,128)(2,1)S(1)}, bf16[8,144,128]{2,1,0:T(8,128)(2,1)S(1)}, u32[]{:S(2)}, u32[]{:S(2)}) collective-permute-start(bf16[8,144,128]{2,1,0:T(8,128)(2,1)S(1)} %collective-permute-done.2.across), channel_id=1, source_target_pairs={{0,16},{16,0},{1,17},{17,1},{2,18},{18,2},{3,19},{19,3},{4,20},{20... | collective-permute-start | bytes 884744 | tf_op jit(solution)/shard_map/ppermute | solution.py:27
  57.1 1.3 collective-permute-done.4.far
  58.4 1.0 gather.1
  59.5 5.0 %conv.1 = (f32[512,256]{1,0:T(8,128)S(1)}, f32[8,4,128]{2,1,0:T(4,128)S(1)}, f32[8,256]{1,0:T(8,128)S(1)}) custom-call(bf16[1024,640]{1,0:T(8,128)(2,1)S(1)} %get-tuple-element.25.normed, bf16[8,112,1024]{2,1,0:T(8,128)(2,1)} %bitcast.11), custom_call_target="tpu_custom_call" | custom-call | tf_op jit(solution)/shard_map/conv/pallas_call | solution.py:400
  64.5 10.4 %all_to_all.20.stats = f32[8,4,128]{2,1,0:T(4,128)S(1)} all-to-all(f32[8,4,128]{2,1,0:T(4,128)S(1)} %get-tuple-element.28), channel_id=1, replica_groups=mesh['xlo'=2,'y'=8,'core'=2,'xhi'=2,'z'=8] {'z'}, dimensions={0} | all-to-all | bytes 32768 | tf_op jit(solution)/shard_map/all_to_all | solution.py:418
  74.9 15.3 %all_to_all.21.stats = f32[16,4,128]{2,1,0:T(4,128)S(1)} all-to-all(f32[16,4,128]{2,1,0:T(4,128)S(1)} %merge.1), channel_id=1, replica_groups=mesh['xlo'=2,'y'=8,'core'=2,'xhi'=2,'z'=8] {'xlo','y'}, dimensions={0} | all-to-all | bytes 65536 | tf_op jit(solution)/shard_map/all_to_all | solution.py:427
  90.5 4.4 %collective-permute-start.5 = (bf16[256,512]{1,0:T(8,128)(2,1)S(1)}, bf16[256,512]{1,0:T(8,128)(2,1)S(1)}, u32[]{:S(2)}, u32[]{:S(2)}) collective-permute-start(bf16[256,512]{1,0:T(8,128)(2,1)S(1)} %bn.1.own), channel_id=1, source_target_pairs={{0,8},{8,0},{1,9},{9,1},{2,10},{10,2},{3,11},{11,3},{4,12},{12,4},... | collective-permute-start | bytes 786440 | tf_op jit(solution)/shard_map/ppermute | solution.py:27
  94.9 9.2 %collective-permute-start.6 = (bf16[256,512]{1,0:T(8,128)(2,1)S(1)}, bf16[256,512]{1,0:T(8,128)(2,1)S(1)}, u32[]{:S(2)}, u32[]{:S(2)}) collective-permute-start(bf16[256,512]{1,0:T(8,128)(2,1)S(1)} %bn.1.own), channel_id=1, source_target_pairs={{0,16},{16,0},{1,17},{17,1},{2,18},{18,2},{3,19},{19,3},{4,20},{20... | collective-permute-start | bytes 786440 | tf_op jit(solution)/shard_map/ppermute | solution.py:27
  104.0 5.1 %collective-permute-start.7 = (bf16[256,512]{1,0:T(8,128)(2,1)S(1)}, bf16[256,512]{1,0:T(8,128)(2,1)S(1)}, u32[]{:S(2)}, u32[]{:S(2)}) collective-permute-start(bf16[256,512]{1,0:T(8,128)(2,1)S(1)} %collective-permute-done.5.across), channel_id=1, source_target_pairs={{0,16},{16,0},{1,17},{17,1},{2,18},{18,2},{3,19},{19,3},{4,20},{20... | collective-permute-start | bytes 786440 | tf_op jit(solution)/shard_map/ppermute | solution.py:27
  109.2 1.1 collective-permute-done.7.far
  110.8 4.3 %collective-permute-start.8 = (bf16[256,512]{1,0:T(8,128)(2,1)S(1)}, bf16[256,512]{1,0:T(8,128)(2,1)S(1)}, u32[]{:S(2)}, u32[]{:S(2)}) collective-permute-start(bf16[256,512]{1,0:T(8,128)(2,1)S(1)} %mix.1.own), channel_id=1, source_target_pairs={{0,8},{8,0},{1,9},{9,1},{2,10},{10,2},{3,11},{11,3},{4,12},{12,4},... | collective-permute-start | bytes 786440 | tf_op jit(solution)/shard_map/ppermute | solution.py:27
  115.2 2.6 %collective-permute-start.9 = (bf16[256,512]{1,0:T(8,128)(2,1)S(1)}, bf16[256,512]{1,0:T(8,128)(2,1)S(1)}, u32[]{:S(2)}, u32[]{:S(2)}) collective-permute-start(bf16[256,512]{1,0:T(8,128)(2,1)S(1)} %mix.1.own), channel_id=1, source_target_pairs={{0,16},{16,0},{1,17},{17,1},{2,18},{18,2},{3,19},{19,3},{4,20},{20... | collective-permute-start | bytes 786440 | tf_op jit(solution)/shard_map/ppermute | solution.py:27
  117.7 4.0 %collective-permute-done.8.across = bf16[256,512]{1,0:T(8,128)(2,1)S(1)} collective-permute-done((bf16[256,512]{1,0:T(8,128)(2,1)S(1)}, bf16[256,512]{1,0:T(8,128)(2,1)S(1)}, u32[]{:S(2)}, u32[]{:S(2)}) %collective-permute-start.8) | collective-permute-done | bytes 262176 | tf_op jit(solution)/shard_map/ppermute | solution.py:27
  121.8 3.1 %collective-permute-start.10 = (bf16[256,512]{1,0:T(8,128)(2,1)S(1)}, bf16[256,512]{1,0:T(8,128)(2,1)S(1)}, u32[]{:S(2)}, u32[]{:S(2)}) collective-permute-start(bf16[256,512]{1,0:T(8,128)(2,1)S(1)} %collective-permute-done.8.across), channel_id=1, source_target_pairs={{0,16},{16,0},{1,17},{17,1},{2,18},{18,2},{3,19},{19,3},{4,20},{20... | collective-permute-start | bytes 786440 | tf_op jit(solution)/shard_map/ppermute | solution.py:27
  125.1 0.9 collective-permute-done.10.far
  126.8 3.5 %give.1 = (bf16[1024,256]{1,0:T(8,128)(2,1)S(1)}, bf16[8,16,128,128]{3,2,1,0:T(8,128)(2,1)S(1)}) custom-call(bf16[1024,256]{1,0:T(8,128)(2,1)S(1)} %get-tuple-element.33.normed, bf16[8,16,128,128]{3,2,1,0:T(8,128)(2,1)} %bitcast.13), custom_call_target="tpu_custom_call" | custom-call | tf_op jit(solution)/shard_map/give/pallas_call | solution.py:459
  130.3 2.3 %collective-permute-start.11 = (bf16[1024,256]{1,0:T(8,128)(2,1)S(1)}, bf16[1024,256]{1,0:T(8,128)(2,1)S(1)}, u32[]{:S(2)}, u32[]{:S(2)}) collective-permute-start(bf16[1024,256]{1,0:T(8,128)(2,1)S(1)} %get-tuple-element.36), channel_id=1, source_target_pairs={{0,16},{16,0},{1,17},{17,1},{2,18},{18,2},{3,19},{19,3},{4,20},{20... | collective-permute-start | bytes 1572872 | tf_op jit(solution)/shard_map/ppermute | solution.py:27
  132.6 1.3 keep.1
  134.3 18.8 %all_to_all.22.parts = bf16[16,64,256]{2,1,0:T(8,128)(2,1)S(1)} all-to-all(bf16[16,64,256]{2,1,0:T(8,128)(2,1)S(1)} %bitcast.14), channel_id=1, replica_groups=mesh['xlo'=2,'y'=8,'core'=2,'xhi'=2,'z'=8] {'xhi','z'}, dimensions={0} | all-to-all | bytes 1048576 | tf_op jit(solution)/shard_map/all_to_all | solution.py:481
  (28 shorter events, 3.4 us)
Async XLA Ops:
  6.5 50.3 %copy-start.3 = (f32[1024]{0:T(1024)S(1)}, f32[1024]{0:T(1024)}, u32[]{:S(2)}) copy-start(f32[1024]{0:T(1024)} %param.11) | copy-start | bytes 12292
  6.5 53.0 %all-gather.5.cloned.1.call-start = ((), (), s32[]{:S(2)}) async-start(), calls=%async_computation.4 | async-start | bytes 2064384 | tf_op jit(solution)/shard_map/all_gather | solution.py:363
  8.3 10.1 %collective-permute-start = (bf16[64,128]{1,0:T(8,128)(2,1)S(1)}, bf16[64,128]{1,0:T(8,128)(2,1)S(1)}, u32[]{:S(2)}, u32[]{:S(2)}) collective-permute-start(bf16[64,128]{1,0:T(8,128)(2,1)S(1)} %get-tuple-element.22), channel_id=1, source_target_pairs={{0,16},{16,32},{32,48},{48,64},{64,80},{80,96},{96,112},{112,128},... | collective-permute-start | bytes 49160 | tf_op jit(solution)/shard_map/ppermute | solution.py:367
  12.9 6.3 %collective-permute-start.1 = (bf16[64,128]{1,0:T(8,128)(2,1)S(1)}, bf16[64,128]{1,0:T(8,128)(2,1)S(1)}, u32[]{:S(2)}, u32[]{:S(2)}) collective-permute-start(bf16[64,128]{1,0:T(8,128)(2,1)S(1)} %get-tuple-element.23), channel_id=1, source_target_pairs={{16,0},{32,16},{48,32},{64,48},{80,64},{96,80},{112,96},{128,112},... | collective-permute-start | bytes 49160 | tf_op jit(solution)/shard_map/ppermute | solution.py:368
  20.1 23.6 %all-to-all-start = ((bf16[8,144,128]{2,1,0:T(8,128)(2,1)}), bf16[8,144,128]{2,1,0:T(8,128)(2,1)S(1)}, u32[]{:S(2)}, u32[]{:S(2)}) async-start(bf16[8,144,128]{2,1,0:T(8,128)(2,1)} %pack.1), calls=%async_computation | async-start | bytes 589824 | tf_op jit(solution)/shard_map/all_to_all | solution.py:377
  28.9 98.0 %all-gather.7.cloned.1.call-start = ((), (), s32[]{:S(2)}) async-start(), calls=%async_computation.5 | async-start | bytes 4718592 | tf_op jit(solution)/shard_map/all_gather | solution.py:388
  28.9 1.0 copy-start.1
  30.0 1.0 copy-start.2
  43.7 11.2 %collective-permute-start.2 = (bf16[8,144,128]{2,1,0:T(8,128)(2,1)S(1)}, bf16[8,144,128]{2,1,0:T(8,128)(2,1)S(1)}, u32[]{:S(2)}, u32[]{:S(2)}) collective-permute-start(bf16[8,144,128]{2,1,0:T(8,128)(2,1)S(1)} %all-to-all-done.own), channel_id=1, source_target_pairs={{0,8},{8,0},{1,9},{9,1},{2,10},{10,2},{3,11},{11,3},{4,12},{12,4},... | collective-permute-start | bytes 884744 | tf_op jit(solution)/shard_map/ppermute | solution.py:27
  48.3 8.7 %collective-permute-start.3 = (bf16[8,144,128]{2,1,0:T(8,128)(2,1)S(1)}, bf16[8,144,128]{2,1,0:T(8,128)(2,1)S(1)}, u32[]{:S(2)}, u32[]{:S(2)}) collective-permute-start(bf16[8,144,128]{2,1,0:T(8,128)(2,1)S(1)} %all-to-all-done.own), channel_id=1, source_target_pairs={{0,16},{16,0},{1,17},{17,1},{2,18},{18,2},{3,19},{19,3},{4,20},{20... | collective-permute-start | bytes 884744 | tf_op jit(solution)/shard_map/ppermute | solution.py:27
  54.9 3.5 %collective-permute-start.4 = (bf16[8,144,128]{2,1,0:T(8,128)(2,1)S(1)}, bf16[8,144,128]{2,1,0:T(8,128)(2,1)S(1)}, u32[]{:S(2)}, u32[]{:S(2)}) collective-permute-start(bf16[8,144,128]{2,1,0:T(8,128)(2,1)S(1)} %collective-permute-done.2.across), channel_id=1, source_target_pairs={{0,16},{16,0},{1,17},{17,1},{2,18},{18,2},{3,19},{19,3},{4,20},{20... | collective-permute-start | bytes 884744 | tf_op jit(solution)/shard_map/ppermute | solution.py:27
  59.4 65.5 %copy-start.4 = (f32[1024]{0:T(1024)S(1)}, f32[1024]{0:T(1024)}, u32[]{:S(2)}) copy-start(f32[1024]{0:T(1024)} %param.17) | copy-start | bytes 12292
  59.5 50.8 %copy-start = (bf16[896,1024]{1,0:T(8,128)(2,1)S(1)}, bf16[896,1024]{1,0:T(8,128)(2,1)}, u32[]{:S(2)}) copy-start(bf16[896,1024]{1,0:T(8,128)(2,1)} %all-gather.5.cloned.1.call-done) | copy-start | bytes 5505028
  90.5 13.6 %collective-permute-start.5 = (bf16[256,512]{1,0:T(8,128)(2,1)S(1)}, bf16[256,512]{1,0:T(8,128)(2,1)S(1)}, u32[]{:S(2)}, u32[]{:S(2)}) collective-permute-start(bf16[256,512]{1,0:T(8,128)(2,1)S(1)} %bn.1.own), channel_id=1, source_target_pairs={{0,8},{8,0},{1,9},{9,1},{2,10},{10,2},{3,11},{11,3},{4,12},{12,4},... | collective-permute-start | bytes 786440 | tf_op jit(solution)/shard_map/ppermute | solution.py:27
  94.9 14.3 %collective-permute-start.6 = (bf16[256,512]{1,0:T(8,128)(2,1)S(1)}, bf16[256,512]{1,0:T(8,128)(2,1)S(1)}, u32[]{:S(2)}, u32[]{:S(2)}) collective-permute-start(bf16[256,512]{1,0:T(8,128)(2,1)S(1)} %bn.1.own), channel_id=1, source_target_pairs={{0,16},{16,0},{1,17},{17,1},{2,18},{18,2},{3,19},{19,3},{4,20},{20... | collective-permute-start | bytes 786440 | tf_op jit(solution)/shard_map/ppermute | solution.py:27
  104.0 6.3 %collective-permute-start.7 = (bf16[256,512]{1,0:T(8,128)(2,1)S(1)}, bf16[256,512]{1,0:T(8,128)(2,1)S(1)}, u32[]{:S(2)}, u32[]{:S(2)}) collective-permute-start(bf16[256,512]{1,0:T(8,128)(2,1)S(1)} %collective-permute-done.5.across), channel_id=1, source_target_pairs={{0,16},{16,0},{1,17},{17,1},{2,18},{18,2},{3,19},{19,3},{4,20},{20... | collective-permute-start | bytes 786440 | tf_op jit(solution)/shard_map/ppermute | solution.py:27
  110.8 10.9 %collective-permute-start.8 = (bf16[256,512]{1,0:T(8,128)(2,1)S(1)}, bf16[256,512]{1,0:T(8,128)(2,1)S(1)}, u32[]{:S(2)}, u32[]{:S(2)}) collective-permute-start(bf16[256,512]{1,0:T(8,128)(2,1)S(1)} %mix.1.own), channel_id=1, source_target_pairs={{0,8},{8,0},{1,9},{9,1},{2,10},{10,2},{3,11},{11,3},{4,12},{12,4},... | collective-permute-start | bytes 786440 | tf_op jit(solution)/shard_map/ppermute | solution.py:27
  115.2 9.9 %collective-permute-start.9 = (bf16[256,512]{1,0:T(8,128)(2,1)S(1)}, bf16[256,512]{1,0:T(8,128)(2,1)S(1)}, u32[]{:S(2)}, u32[]{:S(2)}) collective-permute-start(bf16[256,512]{1,0:T(8,128)(2,1)S(1)} %mix.1.own), channel_id=1, source_target_pairs={{0,16},{16,0},{1,17},{17,1},{2,18},{18,2},{3,19},{19,3},{4,20},{20... | collective-permute-start | bytes 786440 | tf_op jit(solution)/shard_map/ppermute | solution.py:27
  121.8 4.2 %collective-permute-start.10 = (bf16[256,512]{1,0:T(8,128)(2,1)S(1)}, bf16[256,512]{1,0:T(8,128)(2,1)S(1)}, u32[]{:S(2)}, u32[]{:S(2)}) collective-permute-start(bf16[256,512]{1,0:T(8,128)(2,1)S(1)} %collective-permute-done.8.across), channel_id=1, source_target_pairs={{0,16},{16,0},{1,17},{17,1},{2,18},{18,2},{3,19},{19,3},{4,20},{20... | collective-permute-start | bytes 786440 | tf_op jit(solution)/shard_map/ppermute | solution.py:27
  130.3 3.8 %collective-permute-start.11 = (bf16[1024,256]{1,0:T(8,128)(2,1)S(1)}, bf16[1024,256]{1,0:T(8,128)(2,1)S(1)}, u32[]{:S(2)}, u32[]{:S(2)}) collective-permute-start(bf16[1024,256]{1,0:T(8,128)(2,1)S(1)} %get-tuple-element.36), channel_id=1, source_target_pairs={{0,16},{16,0},{1,17},{17,1},{2,18},{18,2},{3,19},{19,3},{4,20},{20... | collective-permute-start | bytes 1572872 | tf_op jit(solution)/shard_map/ppermute | solution.py:27
Sparse Core Ops, SparseCore 0:
  9.4 50.0 all-gather.4
  61.6 60.8 all-gather.6

commit v12 on v11

--- a/solution.py
+++ b/solution.py
@@ -159,9 +159,9 @@
 
 
 def conv_kernel(normed, first, conv, stats, par, win, weight, small, sems):
-    loads = [
-        pltpu.make_async_copy(first.at[:, 96:112, 0:384], small, sems.at[1]),
-        pltpu.make_async_copy(first.at[:, 0:64], weight, sems.at[0]),
+    loads = [pltpu.make_async_copy(first.at[:, 96:112, 0:384], small, sems.at[8])]
+    loads += [
+        pltpu.make_async_copy(first.at[z, 0:64], weight.at[z], sems.at[z]) for z in range(8)
     ]
     for copy in loads:
         copy.start()
@@ -179,7 +179,8 @@
             total = total + (x if i == 0 else pltpu.roll(x, 32 * i, 1))
         par[:, LANES * h : LANES * (h + 1)] = total[31:39]
         table.append(total)
-    loads[1].wait()
+    for copy in loads[1:]:
+        copy.wait()
     glu = weight[...].reshape(64 * nz, weight.shape[2])
     for c in range(3):
         x = normed[:, 512:640] if c == 2 else normed[:, 256 * c : 256 * (c + 1)]
@@ -290,14 +291,19 @@
 def give_kernel(normed, blocks, give, w, hidden, sems):
     loads = [
         pltpu.make_async_copy(
-            blocks.at[2 * i : 2 * i + 2, 0:8], w.at[2 * i : 2 * i + 2, 0:8], sems.at[i]
+            blocks.at[z, 8 * i : 8 * i + 8], w.at[z, 8 * i : 8 * i + 8], sems.at[8 * i + z]
         )
-        for i in range(4)
+        for i in range(2)
+        for z in range(8)
     ]
-    loads.append(pltpu.make_async_copy(blocks.at[:, 8:16], w.at[:, 8:16], sems.at[4]))
     for copy in loads:
         copy.start()
-    for _, rows, value in feed_forward(normed, w, hidden, lambda i: loads[i].wait()):
+
+    def ready(step):
+        for copy in loads[8:] if step == 4 else loads[2 * step : 2 * step + 2]:
+            copy.wait()
+
+    for _, rows, value in feed_forward(normed, w, hidden, ready):
         give[rows, :] = value.astype(BF)
 
 
@@ -410,7 +416,7 @@
             pltpu.VMEM((2, run + 40, 256), F32),
             pltpu.VMEM((nz, 64, full), BF),
             pltpu.VMEM((nz, 16, 3 * LANES), BF),
-            pltpu.SemaphoreType.DMA((2,)),
+            pltpu.SemaphoreType.DMA((9,)),
         ],
         compiler_params=PARAMS,
         name="conv",
@@ -461,7 +467,7 @@
         out_shape=(shape((full, run), BF), shape((nz, 16, LANES, LANES), BF)),
         in_specs=[VMEM, HBM],
         out_specs=(VMEM,) * 2,
-        scratch_shapes=[pltpu.VMEM((full, run), BF), pltpu.SemaphoreType.DMA((5,))],
+        scratch_shapes=[pltpu.VMEM((full, run), BF), pltpu.SemaphoreType.DMA((16,))],
         compiler_params=PARAMS,
         name="give",
     )(there, *in_hbm(blocks))

time: 162 us -> 162 us (level)
  no operation moved by 1% of the time
where the time goes in v12:
time: 162 us; the launch traced here: 161 us
  starting transfers between devices  58.3 us (36%)
  blocking collectives  44.5 us (27%)
  waiting for transfers between devices  24.9 us (15%)
  Pallas kernels  16.8 us (10%)
  between operations  13.7 us (8%)
  local copies, waits for them, and re-layouts  2.53 us (2%)
    ppermute x10, starting transfers between devices, swap(): return lax.ppermute(x, axis, [(0, 1), (1, 0)])  39.4 us
    all_to_all x1, blocking collectives, body(): lax.all_to_all(keep.reshape(2 * nz, width, run), (XHI, Z), 0, 0, tiled=True)  18.8 us
    all_to_all x1, blocking collectives, body(): stats = lax.all_to_all(stats, (XLO, Y), 0, 0, tiled=True)  15.3 us
    ppermute x10, waiting for transfers between devices, swap(): return lax.ppermute(x, axis, [(0, 1), (1, 0)])  12.3 us
    all_to_all x1, waiting for transfers between devices, body(): parts = lax.all_to_all(parts, Z, 0, 0, tiled=True)  11.6 us
    all_to_all x1, blocking collectives, body(): stats = lax.all_to_all(stats, Z, 0, 0, tiled=True)  10.4 us
    all_to_all x1, starting transfers between devices, body(): parts = lax.all_to_all(parts, Z, 0, 0, tiled=True)  8.79 us
    ppermute x1, starting transfers between devices, body(): right = lax.ppermute(head, (XLO, Y, CORE), [(j, i) for i, j in up])  5.48 us
  transfers between devices with their start and end apart: 15, of which 9 were waited for; matrix products, arithmetic and copies ran while one was open for 0% of the time, Pallas kernels for 7%

profile of v12, /device:TPU:1, one launch (start us, length us, event | category | flops | bytes accessed | tf_op | source)
XLA Modules:
  0.0 160.9 jit_solution(11975596801085589912)
XLA Ops:
  6.5 1.7 %weights.1 = (bf16[112,1024]{1,0:T(8,128)(2,1)}, bf16[64,2048]{1,0:T(8,128)(2,1)S(1)}, bf16[64,128]{1,0:T(8,128)(2,1)S(1)}, bf16[64,128]{1,0:T(8,128)(2,1)S(1)}) custom-call(bf16[2,64,1024]{2,1,0:T(8,128)(2,1)} %bitcast.15, bf16[64,1024]{1,0:T(8,128)(2,1)} %bitcast.17, f32[31,64]{1,0:T(8,128)} %depth.1, f32[1,64]{1,0:T(1,128)} %bitcast.20, ...), custom_call_target="tpu_custom_call" | custom-call | tf_op jit(solution)/shard_map/weights/pallas_call | solution.py:341
  8.3 4.6 %collective-permute-start = (bf16[64,128]{1,0:T(8,128)(2,1)S(1)}, bf16[64,128]{1,0:T(8,128)(2,1)S(1)}, u32[]{:S(2)}, u32[]{:S(2)}) collective-permute-start(bf16[64,128]{1,0:T(8,128)(2,1)S(1)} %get-tuple-element.22), channel_id=1, source_target_pairs={{0,16},{16,32},{32,48},{48,64},{64,80},{80,96},{96,112},{112,128},... | collective-permute-start | bytes 49160 | tf_op jit(solution)/shard_map/ppermute | solution.py:373
  12.9 5.5 %collective-permute-start.1 = (bf16[64,128]{1,0:T(8,128)(2,1)S(1)}, bf16[64,128]{1,0:T(8,128)(2,1)S(1)}, u32[]{:S(2)}, u32[]{:S(2)}) collective-permute-start(bf16[64,128]{1,0:T(8,128)(2,1)S(1)} %get-tuple-element.23), channel_id=1, source_target_pairs={{16,0},{32,16},{48,32},{64,48},{80,64},{96,80},{112,96},{128,112},... | collective-permute-start | bytes 49160 | tf_op jit(solution)/shard_map/ppermute | solution.py:374
  18.4 0.8 collective-permute-done.1.right
  19.2 0.9 pack.1
  20.1 8.8 %all-to-all-start = ((bf16[8,144,128]{2,1,0:T(8,128)(2,1)}), bf16[8,144,128]{2,1,0:T(8,128)(2,1)S(1)}, u32[]{:S(2)}, u32[]{:S(2)}) async-start(bf16[8,144,128]{2,1,0:T(8,128)(2,1)} %pack.1), calls=%async_computation | async-start | bytes 589824 | tf_op jit(solution)/shard_map/all_to_all | solution.py:383
  28.9 1.0 copy-done.1
  30.0 1.0 copy-done.2
  31.0 1.0 blocks.1
  32.0 11.6 %all-to-all-done.own = bf16[8,144,128]{2,1,0:T(8,128)(2,1)S(1)} async-done(((bf16[8,144,128]{2,1,0:T(8,128)(2,1)}), bf16[8,144,128]{2,1,0:T(8,128)(2,1)S(1)}, u32[]{:S(2)}, u32[]{:S(2)}) %all-to-all-start) | async-done | bytes 294944 | tf_op jit(solution)/shard_map/all_to_all | solution.py:383
  43.7 4.6 %collective-permute-start.2 = (bf16[8,144,128]{2,1,0:T(8,128)(2,1)S(1)}, bf16[8,144,128]{2,1,0:T(8,128)(2,1)S(1)}, u32[]{:S(2)}, u32[]{:S(2)}) collective-permute-start(bf16[8,144,128]{2,1,0:T(8,128)(2,1)S(1)} %all-to-all-done.own), channel_id=1, source_target_pairs={{0,8},{8,0},{1,9},{9,1},{2,10},{10,2},{3,11},{11,3},{4,12},{12,4},... | collective-permute-start | bytes 884744 | tf_op jit(solution)/shard_map/ppermute | solution.py:27
  48.3 1.9 %collective-permute-start.3 = (bf16[8,144,128]{2,1,0:T(8,128)(2,1)S(1)}, bf16[8,144,128]{2,1,0:T(8,128)(2,1)S(1)}, u32[]{:S(2)}, u32[]{:S(2)}) collective-permute-start(bf16[8,144,128]{2,1,0:T(8,128)(2,1)S(1)} %all-to-all-done.own), channel_id=1, source_target_pairs={{0,16},{16,0},{1,17},{17,1},{2,18},{18,2},{3,19},{19,3},{4,20},{20... | collective-permute-start | bytes 884744 | tf_op jit(solution)/shard_map/ppermute | solution.py:27
  50.2 4.7 %collective-permute-done.2.across = bf16[8,144,128]{2,1,0:T(8,128)(2,1)S(1)} collective-permute-done((bf16[8,144,128]{2,1,0:T(8,128)(2,1)S(1)}, bf16[8,144,128]{2,1,0:T(8,128)(2,1)S(1)}, u32[]{:S(2)}, u32[]{:S(2)}) %collective-permute-start.2) | collective-permute-done | bytes 294944 | tf_op jit(solution)/shard_map/ppermute | solution.py:27
  54.9 1.9 %collective-permute-start.4 = (bf16[8,144,128]{2,1,0:T(8,128)(2,1)S(1)}, bf16[8,144,128]{2,1,0:T(8,128)(2,1)S(1)}, u32[]{:S(2)}, u32[]{:S(2)}) collective-permute-start(bf16[8,144,128]{2,1,0:T(8,128)(2,1)S(1)} %collective-permute-done.2.across), channel_id=1, source_target_pairs={{0,16},{16,0},{1,17},{17,1},{2,18},{18,2},{3,19},{19,3},{4,20},{20... | collective-permute-start | bytes 884744 | tf_op jit(solution)/shard_map/ppermute | solution.py:27
  57.1 1.3 collective-permute-done.4.far
  58.4 1.0 gather.1
  59.5 5.1 %conv.1 = (f32[512,256]{1,0:T(8,128)S(1)}, f32[8,4,128]{2,1,0:T(4,128)S(1)}, f32[8,256]{1,0:T(8,128)S(1)}) custom-call(bf16[1024,640]{1,0:T(8,128)(2,1)S(1)} %get-tuple-element.25.normed, bf16[8,112,1024]{2,1,0:T(8,128)(2,1)} %bitcast.11), custom_call_target="tpu_custom_call" | custom-call | tf_op jit(solution)/shard_map/conv/pallas_call | solution.py:406
  64.6 10.4 %all_to_all.20.stats = f32[8,4,128]{2,1,0:T(4,128)S(1)} all-to-all(f32[8,4,128]{2,1,0:T(4,128)S(1)} %get-tuple-element.28), channel_id=1, replica_groups=mesh['xlo'=2,'y'=8,'core'=2,'xhi'=2,'z'=8] {'z'}, dimensions={0} | all-to-all | bytes 32768 | tf_op jit(solution)/shard_map/all_to_all | solution.py:424
  75.0 15.3 %all_to_all.21.stats = f32[16,4,128]{2,1,0:T(4,128)S(1)} all-to-all(f32[16,4,128]{2,1,0:T(4,128)S(1)} %merge.1), channel_id=1, replica_groups=mesh['xlo'=2,'y'=8,'core'=2,'xhi'=2,'z'=8] {'xlo','y'}, dimensions={0} | all-to-all | bytes 65536 | tf_op jit(solution)/shard_map/all_to_all | solution.py:433
  90.6 4.4 %collective-permute-start.5 = (bf16[256,512]{1,0:T(8,128)(2,1)S(1)}, bf16[256,512]{1,0:T(8,128)(2,1)S(1)}, u32[]{:S(2)}, u32[]{:S(2)}) collective-permute-start(bf16[256,512]{1,0:T(8,128)(2,1)S(1)} %bn.1.own), channel_id=1, source_target_pairs={{0,8},{8,0},{1,9},{9,1},{2,10},{10,2},{3,11},{11,3},{4,12},{12,4},... | collective-permute-start | bytes 786440 | tf_op jit(solution)/shard_map/ppermute | solution.py:27
  95.0 9.2 %collective-permute-start.6 = (bf16[256,512]{1,0:T(8,128)(2,1)S(1)}, bf16[256,512]{1,0:T(8,128)(2,1)S(1)}, u32[]{:S(2)}, u32[]{:S(2)}) collective-permute-start(bf16[256,512]{1,0:T(8,128)(2,1)S(1)} %bn.1.own), channel_id=1, source_target_pairs={{0,16},{16,0},{1,17},{17,1},{2,18},{18,2},{3,19},{19,3},{4,20},{20... | collective-permute-start | bytes 786440 | tf_op jit(solution)/shard_map/ppermute | solution.py:27
  104.2 5.1 %collective-permute-start.7 = (bf16[256,512]{1,0:T(8,128)(2,1)S(1)}, bf16[256,512]{1,0:T(8,128)(2,1)S(1)}, u32[]{:S(2)}, u32[]{:S(2)}) collective-permute-start(bf16[256,512]{1,0:T(8,128)(2,1)S(1)} %collective-permute-done.5.across), channel_id=1, source_target_pairs={{0,16},{16,0},{1,17},{17,1},{2,18},{18,2},{3,19},{19,3},{4,20},{20... | collective-permute-start | bytes 786440 | tf_op jit(solution)/shard_map/ppermute | solution.py:27
  109.3 1.1 collective-permute-done.7.far
  110.9 4.3 %collective-permute-start.8 = (bf16[256,512]{1,0:T(8,128)(2,1)S(1)}, bf16[256,512]{1,0:T(8,128)(2,1)S(1)}, u32[]{:S(2)}, u32[]{:S(2)}) collective-permute-start(bf16[256,512]{1,0:T(8,128)(2,1)S(1)} %mix.1.own), channel_id=1, source_target_pairs={{0,8},{8,0},{1,9},{9,1},{2,10},{10,2},{3,11},{11,3},{4,12},{12,4},... | collective-permute-start | bytes 786440 | tf_op jit(solution)/shard_map/ppermute | solution.py:27
  115.3 2.6 %collective-permute-start.9 = (bf16[256,512]{1,0:T(8,128)(2,1)S(1)}, bf16[256,512]{1,0:T(8,128)(2,1)S(1)}, u32[]{:S(2)}, u32[]{:S(2)}) collective-permute-start(bf16[256,512]{1,0:T(8,128)(2,1)S(1)} %mix.1.own), channel_id=1, source_target_pairs={{0,16},{16,0},{1,17},{17,1},{2,18},{18,2},{3,19},{19,3},{4,20},{20... | collective-permute-start | bytes 786440 | tf_op jit(solution)/shard_map/ppermute | solution.py:27
  117.9 4.0 %collective-permute-done.8.across = bf16[256,512]{1,0:T(8,128)(2,1)S(1)} collective-permute-done((bf16[256,512]{1,0:T(8,128)(2,1)S(1)}, bf16[256,512]{1,0:T(8,128)(2,1)S(1)}, u32[]{:S(2)}, u32[]{:S(2)}) %collective-permute-start.8) | collective-permute-done | bytes 262176 | tf_op jit(solution)/shard_map/ppermute | solution.py:27
  121.9 3.1 %collective-permute-start.10 = (bf16[256,512]{1,0:T(8,128)(2,1)S(1)}, bf16[256,512]{1,0:T(8,128)(2,1)S(1)}, u32[]{:S(2)}, u32[]{:S(2)}) collective-permute-start(bf16[256,512]{1,0:T(8,128)(2,1)S(1)} %collective-permute-done.8.across), channel_id=1, source_target_pairs={{0,16},{16,0},{1,17},{17,1},{2,18},{18,2},{3,19},{19,3},{4,20},{20... | collective-permute-start | bytes 786440 | tf_op jit(solution)/shard_map/ppermute | solution.py:27
  125.2 0.9 collective-permute-done.10.far
  126.9 3.6 %give.1 = (bf16[1024,256]{1,0:T(8,128)(2,1)S(1)}, bf16[8,16,128,128]{3,2,1,0:T(8,128)(2,1)S(1)}) custom-call(bf16[1024,256]{1,0:T(8,128)(2,1)S(1)} %get-tuple-element.33.normed, bf16[8,16,128,128]{3,2,1,0:T(8,128)(2,1)} %bitcast.13), custom_call_target="tpu_custom_call" | custom-call | tf_op jit(solution)/shard_map/give/pallas_call | solution.py:465
  130.6 2.3 %collective-permute-start.11 = (bf16[1024,256]{1,0:T(8,128)(2,1)S(1)}, bf16[1024,256]{1,0:T(8,128)(2,1)S(1)}, u32[]{:S(2)}, u32[]{:S(2)}) collective-permute-start(bf16[1024,256]{1,0:T(8,128)(2,1)S(1)} %get-tuple-element.36), channel_id=1, source_target_pairs={{0,16},{16,0},{1,17},{17,1},{2,18},{18,2},{3,19},{19,3},{4,20},{20... | collective-permute-start | bytes 1572872 | tf_op jit(solution)/shard_map/ppermute | solution.py:27
  132.8 1.2 keep.1
  134.5 18.8 %all_to_all.22.parts = bf16[16,64,256]{2,1,0:T(8,128)(2,1)S(1)} all-to-all(bf16[16,64,256]{2,1,0:T(8,128)(2,1)S(1)} %bitcast.14), channel_id=1, replica_groups=mesh['xlo'=2,'y'=8,'core'=2,'xhi'=2,'z'=8] {'xhi','z'}, dimensions={0} | all-to-all | bytes 1048576 | tf_op jit(solution)/shard_map/all_to_all | solution.py:487
  (28 shorter events, 3.4 us)
Async XLA Ops:
  6.5 50.3 %copy-start.3 = (f32[1024]{0:T(1024)S(1)}, f32[1024]{0:T(1024)}, u32[]{:S(2)}) copy-start(f32[1024]{0:T(1024)} %param.11) | copy-start | bytes 12292
  6.5 53.0 %all-gather.5.cloned.1.call-start = ((), (), s32[]{:S(2)}) async-start(), calls=%async_computation.4 | async-start | bytes 2064384 | tf_op jit(solution)/shard_map/all_gather | solution.py:369
  8.3 10.1 %collective-permute-start = (bf16[64,128]{1,0:T(8,128)(2,1)S(1)}, bf16[64,128]{1,0:T(8,128)(2,1)S(1)}, u32[]{:S(2)}, u32[]{:S(2)}) collective-permute-start(bf16[64,128]{1,0:T(8,128)(2,1)S(1)} %get-tuple-element.22), channel_id=1, source_target_pairs={{0,16},{16,32},{32,48},{48,64},{64,80},{80,96},{96,112},{112,128},... | collective-permute-start | bytes 49160 | tf_op jit(solution)/shard_map/ppermute | solution.py:373
  12.9 6.3 %collective-permute-start.1 = (bf16[64,128]{1,0:T(8,128)(2,1)S(1)}, bf16[64,128]{1,0:T(8,128)(2,1)S(1)}, u32[]{:S(2)}, u32[]{:S(2)}) collective-permute-start(bf16[64,128]{1,0:T(8,128)(2,1)S(1)} %get-tuple-element.23), channel_id=1, source_target_pairs={{16,0},{32,16},{48,32},{64,48},{80,64},{96,80},{112,96},{128,112},... | collective-permute-start | bytes 49160 | tf_op jit(solution)/shard_map/ppermute | solution.py:374
  20.1 23.6 %all-to-all-start = ((bf16[8,144,128]{2,1,0:T(8,128)(2,1)}), bf16[8,144,128]{2,1,0:T(8,128)(2,1)S(1)}, u32[]{:S(2)}, u32[]{:S(2)}) async-start(bf16[8,144,128]{2,1,0:T(8,128)(2,1)} %pack.1), calls=%async_computation | async-start | bytes 589824 | tf_op jit(solution)/shard_map/all_to_all | solution.py:383
  28.9 98.1 %all-gather.7.cloned.1.call-start = ((), (), s32[]{:S(2)}) async-start(), calls=%async_computation.5 | async-start | bytes 4718592 | tf_op jit(solution)/shard_map/all_gather | solution.py:394
  28.9 1.0 copy-start.1
  30.0 1.0 copy-start.2
  43.7 11.2 %collective-permute-start.2 = (bf16[8,144,128]{2,1,0:T(8,128)(2,1)S(1)}, bf16[8,144,128]{2,1,0:T(8,128)(2,1)S(1)}, u32[]{:S(2)}, u32[]{:S(2)}) collective-permute-start(bf16[8,144,128]{2,1,0:T(8,128)(2,1)S(1)} %all-to-all-done.own), channel_id=1, source_target_pairs={{0,8},{8,0},{1,9},{9,1},{2,10},{10,2},{3,11},{11,3},{4,12},{12,4},... | collective-permute-start | bytes 884744 | tf_op jit(solution)/shard_map/ppermute | solution.py:27
  48.3 8.7 %collective-permute-start.3 = (bf16[8,144,128]{2,1,0:T(8,128)(2,1)S(1)}, bf16[8,144,128]{2,1,0:T(8,128)(2,1)S(1)}, u32[]{:S(2)}, u32[]{:S(2)}) collective-permute-start(bf16[8,144,128]{2,1,0:T(8,128)(2,1)S(1)} %all-to-all-done.own), channel_id=1, source_target_pairs={{0,16},{16,0},{1,17},{17,1},{2,18},{18,2},{3,19},{19,3},{4,20},{20... | collective-permute-start | bytes 884744 | tf_op jit(solution)/shard_map/ppermute | solution.py:27
  54.9 3.5 %collective-permute-start.4 = (bf16[8,144,128]{2,1,0:T(8,128)(2,1)S(1)}, bf16[8,144,128]{2,1,0:T(8,128)(2,1)S(1)}, u32[]{:S(2)}, u32[]{:S(2)}) collective-permute-start(bf16[8,144,128]{2,1,0:T(8,128)(2,1)S(1)} %collective-permute-done.2.across), channel_id=1, source_target_pairs={{0,16},{16,0},{1,17},{17,1},{2,18},{18,2},{3,19},{19,3},{4,20},{20... | collective-permute-start | bytes 884744 | tf_op jit(solution)/shard_map/ppermute | solution.py:27
  59.4 65.6 %copy-start.4 = (f32[1024]{0:T(1024)S(1)}, f32[1024]{0:T(1024)}, u32[]{:S(2)}) copy-start(f32[1024]{0:T(1024)} %param.17) | copy-start | bytes 12292
  59.5 50.9 %copy-start = (bf16[896,1024]{1,0:T(8,128)(2,1)S(1)}, bf16[896,1024]{1,0:T(8,128)(2,1)}, u32[]{:S(2)}) copy-start(bf16[896,1024]{1,0:T(8,128)(2,1)} %all-gather.5.cloned.1.call-done) | copy-start | bytes 5505028
  90.6 13.6 %collective-permute-start.5 = (bf16[256,512]{1,0:T(8,128)(2,1)S(1)}, bf16[256,512]{1,0:T(8,128)(2,1)S(1)}, u32[]{:S(2)}, u32[]{:S(2)}) collective-permute-start(bf16[256,512]{1,0:T(8,128)(2,1)S(1)} %bn.1.own), channel_id=1, source_target_pairs={{0,8},{8,0},{1,9},{9,1},{2,10},{10,2},{3,11},{11,3},{4,12},{12,4},... | collective-permute-start | bytes 786440 | tf_op jit(solution)/shard_map/ppermute | solution.py:27
  95.0 14.3 %collective-permute-start.6 = (bf16[256,512]{1,0:T(8,128)(2,1)S(1)}, bf16[256,512]{1,0:T(8,128)(2,1)S(1)}, u32[]{:S(2)}, u32[]{:S(2)}) collective-permute-start(bf16[256,512]{1,0:T(8,128)(2,1)S(1)} %bn.1.own), channel_id=1, source_target_pairs={{0,16},{16,0},{1,17},{17,1},{2,18},{18,2},{3,19},{19,3},{4,20},{20... | collective-permute-start | bytes 786440 | tf_op jit(solution)/shard_map/ppermute | solution.py:27
  104.2 6.3 %collective-permute-start.7 = (bf16[256,512]{1,0:T(8,128)(2,1)S(1)}, bf16[256,512]{1,0:T(8,128)(2,1)S(1)}, u32[]{:S(2)}, u32[]{:S(2)}) collective-permute-start(bf16[256,512]{1,0:T(8,128)(2,1)S(1)} %collective-permute-done.5.across), channel_id=1, source_target_pairs={{0,16},{16,0},{1,17},{17,1},{2,18},{18,2},{3,19},{19,3},{4,20},{20... | collective-permute-start | bytes 786440 | tf_op jit(solution)/shard_map/ppermute | solution.py:27
  110.9 10.9 %collective-permute-start.8 = (bf16[256,512]{1,0:T(8,128)(2,1)S(1)}, bf16[256,512]{1,0:T(8,128)(2,1)S(1)}, u32[]{:S(2)}, u32[]{:S(2)}) collective-permute-start(bf16[256,512]{1,0:T(8,128)(2,1)S(1)} %mix.1.own), channel_id=1, source_target_pairs={{0,8},{8,0},{1,9},{9,1},{2,10},{10,2},{3,11},{11,3},{4,12},{12,4},... | collective-permute-start | bytes 786440 | tf_op jit(solution)/shard_map/ppermute | solution.py:27
  115.3 9.9 %collective-permute-start.9 = (bf16[256,512]{1,0:T(8,128)(2,1)S(1)}, bf16[256,512]{1,0:T(8,128)(2,1)S(1)}, u32[]{:S(2)}, u32[]{:S(2)}) collective-permute-start(bf16[256,512]{1,0:T(8,128)(2,1)S(1)} %mix.1.own), channel_id=1, source_target_pairs={{0,16},{16,0},{1,17},{17,1},{2,18},{18,2},{3,19},{19,3},{4,20},{20... | collective-permute-start | bytes 786440 | tf_op jit(solution)/shard_map/ppermute | solution.py:27
  121.9 4.2 %collective-permute-start.10 = (bf16[256,512]{1,0:T(8,128)(2,1)S(1)}, bf16[256,512]{1,0:T(8,128)(2,1)S(1)}, u32[]{:S(2)}, u32[]{:S(2)}) collective-permute-start(bf16[256,512]{1,0:T(8,128)(2,1)S(1)} %collective-permute-done.8.across), channel_id=1, source_target_pairs={{0,16},{16,0},{1,17},{17,1},{2,18},{18,2},{3,19},{19,3},{4,20},{20... | collective-permute-start | bytes 786440 | tf_op jit(solution)/shard_map/ppermute | solution.py:27
  130.6 3.8 %collective-permute-start.11 = (bf16[1024,256]{1,0:T(8,128)(2,1)S(1)}, bf16[1024,256]{1,0:T(8,128)(2,1)S(1)}, u32[]{:S(2)}, u32[]{:S(2)}) collective-permute-start(bf16[1024,256]{1,0:T(8,128)(2,1)S(1)} %get-tuple-element.36), channel_id=1, source_target_pairs={{0,16},{16,0},{1,17},{17,1},{2,18},{18,2},{3,19},{19,3},{4,20},{20... | collective-permute-start | bytes 1572872 | tf_op jit(solution)/shard_map/ppermute | solution.py:27
Sparse Core Ops, SparseCore 0:
  9.4 50.0 all-gather.4
  61.6 60.8 all-gather.6

commit v13 on v11

--- a/solution.py
+++ b/solution.py
@@ -230,7 +230,7 @@
 
 
 def bn_kernel(conv, stats, par, out):
-    frames = 8 * conv.shape[0]
+    frames = 16 * conv.shape[0]
     mean, square = merged(stats[...], frames)
     scale = lax.rsqrt(square * (1.0 / (frames * stats.shape[0])) + EPS)
     for h in range(2):
@@ -401,7 +401,7 @@
         conv_kernel,
         out_shape=(
             shape((2 * run, 256), F32),
-            shape((nz, 4, LANES), F32),
+            shape((lax.axis_size((XLO, Y)), 4, LANES), F32),
             shape((8, 256), F32),
         ),
         in_specs=[VMEM, HBM],
@@ -415,16 +415,16 @@
         compiler_params=PARAMS,
         name="conv",
     )(normed, *in_hbm(first))
-    stats = lax.all_to_all(stats, Z, 0, 0, tiled=True)
+    stats = lax.all_to_all(stats, (XLO, Y), 0, 0, tiled=True)
     stats = pl.pallas_call(
         merge_kernel,
-        out_shape=shape((lax.axis_size((XLO, Y)), 4, LANES), F32),
+        out_shape=shape((nz, 4, LANES), F32),
         in_specs=[VMEM],
         out_specs=VMEM,
         compiler_params=PARAMS,
         name="merge",
     )(stats)
-    stats = lax.all_to_all(stats, (XLO, Y), 0, 0, tiled=True)
+    stats = lax.all_to_all(stats, Z, 0, 0, tiled=True)
     activated = pl.pallas_call(
         bn_kernel,
         out_shape=shape((256, 2 * run), BF),

time: 162 us -> 162 us (level)
  no operation moved by 1% of the time
where the time goes in v13:
time: 162 us; the launch traced here: 161 us
  starting transfers between devices  58.2 us (36%)
  blocking collectives  44.8 us (28%)
  waiting for transfers between devices  24.8 us (15%)
  Pallas kernels  16.6 us (10%)
  between operations  13.7 us (8%)
  local copies, waits for them, and re-layouts  2.53 us (2%)
    ppermute x10, starting transfers between devices, swap(): return lax.ppermute(x, axis, [(0, 1), (1, 0)])  39.3 us
    all_to_all x1, blocking collectives, body(): lax.all_to_all(keep.reshape(2 * nz, width, run), (XHI, Z), 0, 0, tiled=True)  18.8 us
    all_to_all x1, blocking collectives, body(): stats = lax.all_to_all(stats, (XLO, Y), 0, 0, tiled=True)  15.5 us
    ppermute x10, waiting for transfers between devices, swap(): return lax.ppermute(x, axis, [(0, 1), (1, 0)])  12.2 us
    all_to_all x1, waiting for transfers between devices, body(): parts = lax.all_to_all(parts, Z, 0, 0, tiled=True)  11.6 us
    all_to_all x1, blocking collectives, body(): stats = lax.all_to_all(stats, Z, 0, 0, tiled=True)  10.4 us
    all_to_all x1, starting transfers between devices, body(): parts = lax.all_to_all(parts, Z, 0, 0, tiled=True)  8.79 us
    ppermute x1, starting transfers between devices, body(): right = lax.ppermute(head, (XLO, Y, CORE), [(j, i) for i, j in up])  5.48 us
  transfers between devices with their start and end apart: 15, of which 9 were waited for; matrix products, arithmetic and copies ran while one was open for 0% of the time, Pallas kernels for 7%

profile of v13, /device:TPU:1, one launch (start us, length us, event | category | flops | bytes accessed | tf_op | source)
XLA Modules:
  0.0 160.8 jit_solution(10626859022382800850)
XLA Ops:
  6.5 1.7 %weights.1 = (bf16[112,1024]{1,0:T(8,128)(2,1)}, bf16[64,2048]{1,0:T(8,128)(2,1)S(1)}, bf16[64,128]{1,0:T(8,128)(2,1)S(1)}, bf16[64,128]{1,0:T(8,128)(2,1)S(1)}) custom-call(bf16[2,64,1024]{2,1,0:T(8,128)(2,1)} %bitcast.15, bf16[64,1024]{1,0:T(8,128)(2,1)} %bitcast.17, f32[31,64]{1,0:T(8,128)} %depth.1, f32[1,64]{1,0:T(1,128)} %bitcast.20, ...), custom_call_target="tpu_custom_call" | custom-call | tf_op jit(solution)/shard_map/weights/pallas_call | solution.py:335
  8.3 4.6 %collective-permute-start = (bf16[64,128]{1,0:T(8,128)(2,1)S(1)}, bf16[64,128]{1,0:T(8,128)(2,1)S(1)}, u32[]{:S(2)}, u32[]{:S(2)}) collective-permute-start(bf16[64,128]{1,0:T(8,128)(2,1)S(1)} %get-tuple-element.22), channel_id=1, source_target_pairs={{0,16},{16,32},{32,48},{48,64},{64,80},{80,96},{96,112},{112,128},... | collective-permute-start | bytes 49160 | tf_op jit(solution)/shard_map/ppermute | solution.py:367
  12.9 5.5 %collective-permute-start.1 = (bf16[64,128]{1,0:T(8,128)(2,1)S(1)}, bf16[64,128]{1,0:T(8,128)(2,1)S(1)}, u32[]{:S(2)}, u32[]{:S(2)}) collective-permute-start(bf16[64,128]{1,0:T(8,128)(2,1)S(1)} %get-tuple-element.23), channel_id=1, source_target_pairs={{16,0},{32,16},{48,32},{64,48},{80,64},{96,80},{112,96},{128,112},... | collective-permute-start | bytes 49160 | tf_op jit(solution)/shard_map/ppermute | solution.py:368
  18.4 0.8 collective-permute-done.1.right
  19.2 0.9 pack.1
  20.1 8.8 %all-to-all-start = ((bf16[8,144,128]{2,1,0:T(8,128)(2,1)}), bf16[8,144,128]{2,1,0:T(8,128)(2,1)S(1)}, u32[]{:S(2)}, u32[]{:S(2)}) async-start(bf16[8,144,128]{2,1,0:T(8,128)(2,1)} %pack.1), calls=%async_computation | async-start | bytes 589824 | tf_op jit(solution)/shard_map/all_to_all | solution.py:377
  28.9 1.0 copy-done.1
  30.0 1.0 copy-done.2
  31.0 1.0 blocks.1
  32.0 11.6 %all-to-all-done.own = bf16[8,144,128]{2,1,0:T(8,128)(2,1)S(1)} async-done(((bf16[8,144,128]{2,1,0:T(8,128)(2,1)}), bf16[8,144,128]{2,1,0:T(8,128)(2,1)S(1)}, u32[]{:S(2)}, u32[]{:S(2)}) %all-to-all-start) | async-done | bytes 294944 | tf_op jit(solution)/shard_map/all_to_all | solution.py:377
  43.7 4.6 %collective-permute-start.2 = (bf16[8,144,128]{2,1,0:T(8,128)(2,1)S(1)}, bf16[8,144,128]{2,1,0:T(8,128)(2,1)S(1)}, u32[]{:S(2)}, u32[]{:S(2)}) collective-permute-start(bf16[8,144,128]{2,1,0:T(8,128)(2,1)S(1)} %all-to-all-done.own), channel_id=1, source_target_pairs={{0,8},{8,0},{1,9},{9,1},{2,10},{10,2},{3,11},{11,3},{4,12},{12,4},... | collective-permute-start | bytes 884744 | tf_op jit(solution)/shard_map/ppermute | solution.py:27
  48.3 1.9 %collective-permute-start.3 = (bf16[8,144,128]{2,1,0:T(8,128)(2,1)S(1)}, bf16[8,144,128]{2,1,0:T(8,128)(2,1)S(1)}, u32[]{:S(2)}, u32[]{:S(2)}) collective-permute-start(bf16[8,144,128]{2,1,0:T(8,128)(2,1)S(1)} %all-to-all-done.own), channel_id=1, source_target_pairs={{0,16},{16,0},{1,17},{17,1},{2,18},{18,2},{3,19},{19,3},{4,20},{20... | collective-permute-start | bytes 884744 | tf_op jit(solution)/shard_map/ppermute | solution.py:27
  50.2 4.7 %collective-permute-done.2.across = bf16[8,144,128]{2,1,0:T(8,128)(2,1)S(1)} collective-permute-done((bf16[8,144,128]{2,1,0:T(8,128)(2,1)S(1)}, bf16[8,144,128]{2,1,0:T(8,128)(2,1)S(1)}, u32[]{:S(2)}, u32[]{:S(2)}) %collective-permute-start.2) | collective-permute-done | bytes 294944 | tf_op jit(solution)/shard_map/ppermute | solution.py:27
  54.9 1.9 %collective-permute-start.4 = (bf16[8,144,128]{2,1,0:T(8,128)(2,1)S(1)}, bf16[8,144,128]{2,1,0:T(8,128)(2,1)S(1)}, u32[]{:S(2)}, u32[]{:S(2)}) collective-permute-start(bf16[8,144,128]{2,1,0:T(8,128)(2,1)S(1)} %collective-permute-done.2.across), channel_id=1, source_target_pairs={{0,16},{16,0},{1,17},{17,1},{2,18},{18,2},{3,19},{19,3},{4,20},{20... | collective-permute-start | bytes 884744 | tf_op jit(solution)/shard_map/ppermute | solution.py:27
  57.1 1.3 collective-permute-done.4.far
  58.4 1.0 gather.1
  59.5 5.0 %conv.1 = (f32[512,256]{1,0:T(8,128)S(1)}, f32[16,4,128]{2,1,0:T(4,128)S(1)}, f32[8,256]{1,0:T(8,128)S(1)}) custom-call(bf16[1024,640]{1,0:T(8,128)(2,1)S(1)} %get-tuple-element.25.normed, bf16[8,112,1024]{2,1,0:T(8,128)(2,1)} %bitcast.11), custom_call_target="tpu_custom_call" | custom-call | tf_op jit(solution)/shard_map/conv/pallas_call | solution.py:400
  64.5 15.5 %all_to_all.20.stats = f32[16,4,128]{2,1,0:T(4,128)S(1)} all-to-all(f32[16,4,128]{2,1,0:T(4,128)S(1)} %get-tuple-element.28), channel_id=1, replica_groups=mesh['xlo'=2,'y'=8,'core'=2,'xhi'=2,'z'=8] {'xlo','y'}, dimensions={0} | all-to-all | bytes 65536 | tf_op jit(solution)/shard_map/all_to_all | solution.py:418
  80.0 10.4 %all_to_all.21.stats = f32[8,4,128]{2,1,0:T(4,128)S(1)} all-to-all(f32[8,4,128]{2,1,0:T(4,128)S(1)} %merge.1), channel_id=1, replica_groups=mesh['xlo'=2,'y'=8,'core'=2,'xhi'=2,'z'=8] {'z'}, dimensions={0} | all-to-all | bytes 32768 | tf_op jit(solution)/shard_map/all_to_all | solution.py:427
  90.7 4.4 %collective-permute-start.5 = (bf16[256,512]{1,0:T(8,128)(2,1)S(1)}, bf16[256,512]{1,0:T(8,128)(2,1)S(1)}, u32[]{:S(2)}, u32[]{:S(2)}) collective-permute-start(bf16[256,512]{1,0:T(8,128)(2,1)S(1)} %bn.1.own), channel_id=1, source_target_pairs={{0,8},{8,0},{1,9},{9,1},{2,10},{10,2},{3,11},{11,3},{4,12},{12,4},... | collective-permute-start | bytes 786440 | tf_op jit(solution)/shard_map/ppermute | solution.py:27
  95.1 9.1 %collective-permute-start.6 = (bf16[256,512]{1,0:T(8,128)(2,1)S(1)}, bf16[256,512]{1,0:T(8,128)(2,1)S(1)}, u32[]{:S(2)}, u32[]{:S(2)}) collective-permute-start(bf16[256,512]{1,0:T(8,128)(2,1)S(1)} %bn.1.own), channel_id=1, source_target_pairs={{0,16},{16,0},{1,17},{17,1},{2,18},{18,2},{3,19},{19,3},{4,20},{20... | collective-permute-start | bytes 786440 | tf_op jit(solution)/shard_map/ppermute | solution.py:27
  104.2 5.1 %collective-permute-start.7 = (bf16[256,512]{1,0:T(8,128)(2,1)S(1)}, bf16[256,512]{1,0:T(8,128)(2,1)S(1)}, u32[]{:S(2)}, u32[]{:S(2)}) collective-permute-start(bf16[256,512]{1,0:T(8,128)(2,1)S(1)} %collective-permute-done.5.across), channel_id=1, source_target_pairs={{0,16},{16,0},{1,17},{17,1},{2,18},{18,2},{3,19},{19,3},{4,20},{20... | collective-permute-start | bytes 786440 | tf_op jit(solution)/shard_map/ppermute | solution.py:27
  109.3 1.1 collective-permute-done.7.far
  111.0 4.3 %collective-permute-start.8 = (bf16[256,512]{1,0:T(8,128)(2,1)S(1)}, bf16[256,512]{1,0:T(8,128)(2,1)S(1)}, u32[]{:S(2)}, u32[]{:S(2)}) collective-permute-start(bf16[256,512]{1,0:T(8,128)(2,1)S(1)} %mix.1.own), channel_id=1, source_target_pairs={{0,8},{8,0},{1,9},{9,1},{2,10},{10,2},{3,11},{11,3},{4,12},{12,4},... | collective-permute-start | bytes 786440 | tf_op jit(solution)/shard_map/ppermute | solution.py:27
  115.3 2.6 %collective-permute-start.9 = (bf16[256,512]{1,0:T(8,128)(2,1)S(1)}, bf16[256,512]{1,0:T(8,128)(2,1)S(1)}, u32[]{:S(2)}, u32[]{:S(2)}) collective-permute-start(bf16[256,512]{1,0:T(8,128)(2,1)S(1)} %mix.1.own), channel_id=1, source_target_pairs={{0,16},{16,0},{1,17},{17,1},{2,18},{18,2},{3,19},{19,3},{4,20},{20... | collective-permute-start | bytes 786440 | tf_op jit(solution)/shard_map/ppermute | solution.py:27
  117.9 4.0 %collective-permute-done.8.across = bf16[256,512]{1,0:T(8,128)(2,1)S(1)} collective-permute-done((bf16[256,512]{1,0:T(8,128)(2,1)S(1)}, bf16[256,512]{1,0:T(8,128)(2,1)S(1)}, u32[]{:S(2)}, u32[]{:S(2)}) %collective-permute-start.8) | collective-permute-done | bytes 262176 | tf_op jit(solution)/shard_map/ppermute | solution.py:27
  121.9 3.1 %collective-permute-start.10 = (bf16[256,512]{1,0:T(8,128)(2,1)S(1)}, bf16[256,512]{1,0:T(8,128)(2,1)S(1)}, u32[]{:S(2)}, u32[]{:S(2)}) collective-permute-start(bf16[256,512]{1,0:T(8,128)(2,1)S(1)} %collective-permute-done.8.across), channel_id=1, source_target_pairs={{0,16},{16,0},{1,17},{17,1},{2,18},{18,2},{3,19},{19,3},{4,20},{20... | collective-permute-start | bytes 786440 | tf_op jit(solution)/shard_map/ppermute | solution.py:27
  125.2 0.9 collective-permute-done.10.far
  127.0 3.5 %give.1 = (bf16[1024,256]{1,0:T(8,128)(2,1)S(1)}, bf16[8,16,128,128]{3,2,1,0:T(8,128)(2,1)S(1)}) custom-call(bf16[1024,256]{1,0:T(8,128)(2,1)S(1)} %get-tuple-element.33.normed, bf16[8,16,128,128]{3,2,1,0:T(8,128)(2,1)} %bitcast.13), custom_call_target="tpu_custom_call" | custom-call | tf_op jit(solution)/shard_map/give/pallas_call | solution.py:459
  130.5 2.3 %collective-permute-start.11 = (bf16[1024,256]{1,0:T(8,128)(2,1)S(1)}, bf16[1024,256]{1,0:T(8,128)(2,1)S(1)}, u32[]{:S(2)}, u32[]{:S(2)}) collective-permute-start(bf16[1024,256]{1,0:T(8,128)(2,1)S(1)} %get-tuple-element.36), channel_id=1, source_target_pairs={{0,16},{16,0},{1,17},{17,1},{2,18},{18,2},{3,19},{19,3},{4,20},{20... | collective-permute-start | bytes 1572872 | tf_op jit(solution)/shard_map/ppermute | solution.py:27
  132.8 1.3 keep.1
  134.4 18.8 %all_to_all.22.parts = bf16[16,64,256]{2,1,0:T(8,128)(2,1)S(1)} all-to-all(bf16[16,64,256]{2,1,0:T(8,128)(2,1)S(1)} %bitcast.14), channel_id=1, replica_groups=mesh['xlo'=2,'y'=8,'core'=2,'xhi'=2,'z'=8] {'xhi','z'}, dimensions={0} | all-to-all | bytes 1048576 | tf_op jit(solution)/shard_map/all_to_all | solution.py:481
  (28 shorter events, 3.4 us)
Async XLA Ops:
  6.5 50.3 %copy-start.3 = (f32[1024]{0:T(1024)S(1)}, f32[1024]{0:T(1024)}, u32[]{:S(2)}) copy-start(f32[1024]{0:T(1024)} %param.11) | copy-start | bytes 12292
  6.5 53.0 %all-gather.5.cloned.1.call-start = ((), (), s32[]{:S(2)}) async-start(), calls=%async_computation.4 | async-start | bytes 2064384 | tf_op jit(solution)/shard_map/all_gather | solution.py:363
  8.3 10.1 %collective-permute-start = (bf16[64,128]{1,0:T(8,128)(2,1)S(1)}, bf16[64,128]{1,0:T(8,128)(2,1)S(1)}, u32[]{:S(2)}, u32[]{:S(2)}) collective-permute-start(bf16[64,128]{1,0:T(8,128)(2,1)S(1)} %get-tuple-element.22), channel_id=1, source_target_pairs={{0,16},{16,32},{32,48},{48,64},{64,80},{80,96},{96,112},{112,128},... | collective-permute-start | bytes 49160 | tf_op jit(solution)/shard_map/ppermute | solution.py:367
  12.9 6.3 %collective-permute-start.1 = (bf16[64,128]{1,0:T(8,128)(2,1)S(1)}, bf16[64,128]{1,0:T(8,128)(2,1)S(1)}, u32[]{:S(2)}, u32[]{:S(2)}) collective-permute-start(bf16[64,128]{1,0:T(8,128)(2,1)S(1)} %get-tuple-element.23), channel_id=1, source_target_pairs={{16,0},{32,16},{48,32},{64,48},{80,64},{96,80},{112,96},{128,112},... | collective-permute-start | bytes 49160 | tf_op jit(solution)/shard_map/ppermute | solution.py:368
  20.1 23.6 %all-to-all-start = ((bf16[8,144,128]{2,1,0:T(8,128)(2,1)}), bf16[8,144,128]{2,1,0:T(8,128)(2,1)S(1)}, u32[]{:S(2)}, u32[]{:S(2)}) async-start(bf16[8,144,128]{2,1,0:T(8,128)(2,1)} %pack.1), calls=%async_computation | async-start | bytes 589824 | tf_op jit(solution)/shard_map/all_to_all | solution.py:377
  28.9 98.1 %all-gather.7.cloned.1.call-start = ((), (), s32[]{:S(2)}) async-start(), calls=%async_computation.5 | async-start | bytes 4718592 | tf_op jit(solution)/shard_map/all_gather | solution.py:388
  28.9 1.0 copy-start.1
  30.0 1.0 copy-start.2
  43.7 11.2 %collective-permute-start.2 = (bf16[8,144,128]{2,1,0:T(8,128)(2,1)S(1)}, bf16[8,144,128]{2,1,0:T(8,128)(2,1)S(1)}, u32[]{:S(2)}, u32[]{:S(2)}) collective-permute-start(bf16[8,144,128]{2,1,0:T(8,128)(2,1)S(1)} %all-to-all-done.own), channel_id=1, source_target_pairs={{0,8},{8,0},{1,9},{9,1},{2,10},{10,2},{3,11},{11,3},{4,12},{12,4},... | collective-permute-start | bytes 884744 | tf_op jit(solution)/shard_map/ppermute | solution.py:27
  48.3 8.8 %collective-permute-start.3 = (bf16[8,144,128]{2,1,0:T(8,128)(2,1)S(1)}, bf16[8,144,128]{2,1,0:T(8,128)(2,1)S(1)}, u32[]{:S(2)}, u32[]{:S(2)}) collective-permute-start(bf16[8,144,128]{2,1,0:T(8,128)(2,1)S(1)} %all-to-all-done.own), channel_id=1, source_target_pairs={{0,16},{16,0},{1,17},{17,1},{2,18},{18,2},{3,19},{19,3},{4,20},{20... | collective-permute-start | bytes 884744 | tf_op jit(solution)/shard_map/ppermute | solution.py:27
  54.9 3.5 %collective-permute-start.4 = (bf16[8,144,128]{2,1,0:T(8,128)(2,1)S(1)}, bf16[8,144,128]{2,1,0:T(8,128)(2,1)S(1)}, u32[]{:S(2)}, u32[]{:S(2)}) collective-permute-start(bf16[8,144,128]{2,1,0:T(8,128)(2,1)S(1)} %collective-permute-done.2.across), channel_id=1, source_target_pairs={{0,16},{16,0},{1,17},{17,1},{2,18},{18,2},{3,19},{19,3},{4,20},{20... | collective-permute-start | bytes 884744 | tf_op jit(solution)/shard_map/ppermute | solution.py:27
  57.1 67.9 %copy-start.4 = (f32[1024]{0:T(1024)S(1)}, f32[1024]{0:T(1024)}, u32[]{:S(2)}) copy-start(f32[1024]{0:T(1024)} %param.17) | copy-start | bytes 12292
  59.5 51.0 %copy-start = (bf16[896,1024]{1,0:T(8,128)(2,1)S(1)}, bf16[896,1024]{1,0:T(8,128)(2,1)}, u32[]{:S(2)}) copy-start(bf16[896,1024]{1,0:T(8,128)(2,1)} %all-gather.5.cloned.1.call-done) | copy-start | bytes 5505028
  90.7 13.5 %collective-permute-start.5 = (bf16[256,512]{1,0:T(8,128)(2,1)S(1)}, bf16[256,512]{1,0:T(8,128)(2,1)S(1)}, u32[]{:S(2)}, u32[]{:S(2)}) collective-permute-start(bf16[256,512]{1,0:T(8,128)(2,1)S(1)} %bn.1.own), channel_id=1, source_target_pairs={{0,8},{8,0},{1,9},{9,1},{2,10},{10,2},{3,11},{11,3},{4,12},{12,4},... | collective-permute-start | bytes 786440 | tf_op jit(solution)/shard_map/ppermute | solution.py:27
  95.1 14.2 %collective-permute-start.6 = (bf16[256,512]{1,0:T(8,128)(2,1)S(1)}, bf16[256,512]{1,0:T(8,128)(2,1)S(1)}, u32[]{:S(2)}, u32[]{:S(2)}) collective-permute-start(bf16[256,512]{1,0:T(8,128)(2,1)S(1)} %bn.1.own), channel_id=1, source_target_pairs={{0,16},{16,0},{1,17},{17,1},{2,18},{18,2},{3,19},{19,3},{4,20},{20... | collective-permute-start | bytes 786440 | tf_op jit(solution)/shard_map/ppermute | solution.py:27
  104.2 6.3 %collective-permute-start.7 = (bf16[256,512]{1,0:T(8,128)(2,1)S(1)}, bf16[256,512]{1,0:T(8,128)(2,1)S(1)}, u32[]{:S(2)}, u32[]{:S(2)}) collective-permute-start(bf16[256,512]{1,0:T(8,128)(2,1)S(1)} %collective-permute-done.5.across), channel_id=1, source_target_pairs={{0,16},{16,0},{1,17},{17,1},{2,18},{18,2},{3,19},{19,3},{4,20},{20... | collective-permute-start | bytes 786440 | tf_op jit(solution)/shard_map/ppermute | solution.py:27
  111.0 10.9 %collective-permute-start.8 = (bf16[256,512]{1,0:T(8,128)(2,1)S(1)}, bf16[256,512]{1,0:T(8,128)(2,1)S(1)}, u32[]{:S(2)}, u32[]{:S(2)}) collective-permute-start(bf16[256,512]{1,0:T(8,128)(2,1)S(1)} %mix.1.own), channel_id=1, source_target_pairs={{0,8},{8,0},{1,9},{9,1},{2,10},{10,2},{3,11},{11,3},{4,12},{12,4},... | collective-permute-start | bytes 786440 | tf_op jit(solution)/shard_map/ppermute | solution.py:27
  115.3 9.9 %collective-permute-start.9 = (bf16[256,512]{1,0:T(8,128)(2,1)S(1)}, bf16[256,512]{1,0:T(8,128)(2,1)S(1)}, u32[]{:S(2)}, u32[]{:S(2)}) collective-permute-start(bf16[256,512]{1,0:T(8,128)(2,1)S(1)} %mix.1.own), channel_id=1, source_target_pairs={{0,16},{16,0},{1,17},{17,1},{2,18},{18,2},{3,19},{19,3},{4,20},{20... | collective-permute-start | bytes 786440 | tf_op jit(solution)/shard_map/ppermute | solution.py:27
  121.9 4.3 %collective-permute-start.10 = (bf16[256,512]{1,0:T(8,128)(2,1)S(1)}, bf16[256,512]{1,0:T(8,128)(2,1)S(1)}, u32[]{:S(2)}, u32[]{:S(2)}) collective-permute-start(bf16[256,512]{1,0:T(8,128)(2,1)S(1)} %collective-permute-done.8.across), channel_id=1, source_target_pairs={{0,16},{16,0},{1,17},{17,1},{2,18},{18,2},{3,19},{19,3},{4,20},{20... | collective-permute-start | bytes 786440 | tf_op jit(solution)/shard_map/ppermute | solution.py:27
  130.5 3.8 %collective-permute-start.11 = (bf16[1024,256]{1,0:T(8,128)(2,1)S(1)}, bf16[1024,256]{1,0:T(8,128)(2,1)S(1)}, u32[]{:S(2)}, u32[]{:S(2)}) collective-permute-start(bf16[1024,256]{1,0:T(8,128)(2,1)S(1)} %get-tuple-element.36), channel_id=1, source_target_pairs={{0,16},{16,0},{1,17},{17,1},{2,18},{18,2},{3,19},{19,3},{4,20},{20... | collective-permute-start | bytes 1572872 | tf_op jit(solution)/shard_map/ppermute | solution.py:27
Sparse Core Ops, SparseCore 0:
  9.4 50.0 all-gather.4
  61.6 61.2 all-gather.6

commit v14 on v13

--- a/solution.py
+++ b/solution.py
@@ -261,15 +261,6 @@
     out[...] = (res[...].astype(F32) + mixed).astype(BF)
 
 
-def norm_kernel(own, across, beside, far, gain, near, here, there, whole):
-    place_blocks(own, across, beside, far, whole)
-    half = here.shape[1]
-    near[...] = whole[:, :half]
-    for c, normed in ((0, here), (1, there)):
-        cols = slice(half * c, half * (c + 1))
-        normed[...] = norm_rows(whole[:, cols].astype(F32), gain[...])
-
-
 def feed_forward(normed, w, hidden, ready):
     for z in range(0, 8, 2):
         ready(z // 2)
@@ -287,7 +278,11 @@
         yield k, slice(LANES * k, LANES * (k + 2)), 0.5 * value
 
 
-def give_kernel(normed, blocks, give, w, hidden, sems):
+def give_kernel(
+    own, across, beside, far, gain, blocks,
+    give, w, near, here,
+    whole, there, hidden, sems,
+):
     loads = [
         pltpu.make_async_copy(
             blocks.at[2 * i : 2 * i + 2, 0:8], w.at[2 * i : 2 * i + 2, 0:8], sems.at[i]
@@ -297,7 +292,13 @@
     loads.append(pltpu.make_async_copy(blocks.at[:, 8:16], w.at[:, 8:16], sems.at[4]))
     for copy in loads:
         copy.start()
-    for _, rows, value in feed_forward(normed, w, hidden, lambda i: loads[i].wait()):
+    place_blocks(own, across, beside, far, whole)
+    half = here.shape[1]
+    near[...] = whole[:, :half]
+    for c, normed in ((0, here), (1, there)):
+        cols = slice(half * c, half * (c + 1))
+        normed[...] = norm_rows(whole[:, cols].astype(F32), gain[...])
+    for _, rows, value in feed_forward(there, w, hidden, lambda i: loads[i].wait()):
         give[rows, :] = value.astype(BF)
 
 
@@ -447,24 +448,25 @@
         compiler_params=PARAMS,
         name="mix",
     )(*group_gather(activated), first, res)
-    near, here, there = pl.pallas_call(
-        norm_kernel,
-        out_shape=(shape((full, run), BF),) * 3,
-        in_specs=[VMEM] * 5,
-        out_specs=(VMEM,) * 3,
-        scratch_shapes=[pltpu.VMEM((full, 2 * run), BF)],
-        compiler_params=PARAMS,
-        name="norm",
-    )(*group_gather(block), ln_ff_gain[:, None])
-    give, blocks = pl.pallas_call(
+    give, blocks, near, here = pl.pallas_call(
         give_kernel,
-        out_shape=(shape((full, run), BF), shape((nz, 16, LANES, LANES), BF)),
-        in_specs=[VMEM, HBM],
-        out_specs=(VMEM,) * 2,
-        scratch_shapes=[pltpu.VMEM((full, run), BF), pltpu.SemaphoreType.DMA((5,))],
+        out_shape=(
+            shape((full, run), BF),
+            shape((nz, 16, LANES, LANES), BF),
+            shape((full, run), BF),
+            shape((full, run), BF),
+        ),
+        in_specs=[VMEM] * 5 + [HBM],
+        out_specs=(VMEM,) * 4,
+        scratch_shapes=[
+            pltpu.VMEM((full, 2 * run), BF),
+            pltpu.VMEM((full, run), BF),
+            pltpu.VMEM((full, run), BF),
+            pltpu.SemaphoreType.DMA((5,)),
+        ],
         compiler_params=PARAMS,
         name="give",
-    )(there, *in_hbm(blocks))
+    )(*group_gather(block), ln_ff_gain[:, None], *in_hbm(blocks))
     keep = pl.pallas_call(
         keep_kernel,
         out_shape=shape((full, run), F32),

time: 162 us -> 162 us (level)
  transfers between devices with their start and end apart: 15 -> 15, of which waited for: 9 -> 9; matrix products, arithmetic and copies ran while one was open for 0% -> 0% of each run, Pallas kernels for 7% -> 6%
where the time goes in v14:
time: 162 us; the launch traced here: 160 us
  starting transfers between devices  58.2 us (36%)
  blocking collectives  44.8 us (28%)
  waiting for transfers between devices  24.8 us (15%)
  Pallas kernels  16.4 us (10%)
  between operations  13.6 us (8%)
  local copies, waits for them, and re-layouts  2.53 us (2%)
    ppermute x10, starting transfers between devices, swap(): return lax.ppermute(x, axis, [(0, 1), (1, 0)])  39.3 us
    all_to_all x1, blocking collectives, body(): lax.all_to_all(keep.reshape(2 * nz, width, run), (XHI, Z), 0, 0, tiled=True)  18.8 us
    all_to_all x1, blocking collectives, body(): stats = lax.all_to_all(stats, (XLO, Y), 0, 0, tiled=True)  15.5 us
    ppermute x10, waiting for transfers between devices, swap(): return lax.ppermute(x, axis, [(0, 1), (1, 0)])  12.2 us
    all_to_all x1, waiting for transfers between devices, body(): parts = lax.all_to_all(parts, Z, 0, 0, tiled=True)  11.6 us
    all_to_all x1, blocking collectives, body(): stats = lax.all_to_all(stats, Z, 0, 0, tiled=True)  10.5 us
    all_to_all x1, starting transfers between devices, body(): parts = lax.all_to_all(parts, Z, 0, 0, tiled=True)  8.79 us
    ppermute x1, starting transfers between devices, body(): right = lax.ppermute(head, (XLO, Y, CORE), [(j, i) for i, j in up])  5.48 us
  transfers between devices with their start and end apart: 15, of which 9 were waited for; matrix products, arithmetic and copies ran while one was open for 0% of the time, Pallas kernels for 6%

profile of v14, /device:TPU:1, one launch (start us, length us, event | category | flops | bytes accessed | tf_op | source)
XLA Modules:
  0.0 160.5 jit_solution(17330474219489279179)
XLA Ops:
  6.5 1.7 %weights.1 = (bf16[112,1024]{1,0:T(8,128)(2,1)}, bf16[64,2048]{1,0:T(8,128)(2,1)S(1)}, bf16[64,128]{1,0:T(8,128)(2,1)S(1)}, bf16[64,128]{1,0:T(8,128)(2,1)S(1)}) custom-call(bf16[2,64,1024]{2,1,0:T(8,128)(2,1)} %bitcast.15, bf16[64,1024]{1,0:T(8,128)(2,1)} %bitcast.17, f32[31,64]{1,0:T(8,128)} %depth.1, f32[1,64]{1,0:T(1,128)} %bitcast.20, ...), custom_call_target="tpu_custom_call" | custom-call | tf_op jit(solution)/shard_map/weights/pallas_call | solution.py:336
  8.3 4.6 %collective-permute-start = (bf16[64,128]{1,0:T(8,128)(2,1)S(1)}, bf16[64,128]{1,0:T(8,128)(2,1)S(1)}, u32[]{:S(2)}, u32[]{:S(2)}) collective-permute-start(bf16[64,128]{1,0:T(8,128)(2,1)S(1)} %get-tuple-element.21), channel_id=1, source_target_pairs={{0,16},{16,32},{32,48},{48,64},{64,80},{80,96},{96,112},{112,128},... | collective-permute-start | bytes 49160 | tf_op jit(solution)/shard_map/ppermute | solution.py:368
  12.9 5.5 %collective-permute-start.1 = (bf16[64,128]{1,0:T(8,128)(2,1)S(1)}, bf16[64,128]{1,0:T(8,128)(2,1)S(1)}, u32[]{:S(2)}, u32[]{:S(2)}) collective-permute-start(bf16[64,128]{1,0:T(8,128)(2,1)S(1)} %get-tuple-element.22), channel_id=1, source_target_pairs={{16,0},{32,16},{48,32},{64,48},{80,64},{96,80},{112,96},{128,112},... | collective-permute-start | bytes 49160 | tf_op jit(solution)/shard_map/ppermute | solution.py:369
  18.4 0.8 collective-permute-done.1.right
  19.2 0.9 pack.1
  20.1 8.8 %all-to-all-start = ((bf16[8,144,128]{2,1,0:T(8,128)(2,1)}), bf16[8,144,128]{2,1,0:T(8,128)(2,1)S(1)}, u32[]{:S(2)}, u32[]{:S(2)}) async-start(bf16[8,144,128]{2,1,0:T(8,128)(2,1)} %pack.1), calls=%async_computation | async-start | bytes 589824 | tf_op jit(solution)/shard_map/all_to_all | solution.py:378
  28.9 1.0 copy-done.1
  30.0 1.0 copy-done.2
  31.0 1.0 blocks.1
  32.0 11.6 %all-to-all-done.own = bf16[8,144,128]{2,1,0:T(8,128)(2,1)S(1)} async-done(((bf16[8,144,128]{2,1,0:T(8,128)(2,1)}), bf16[8,144,128]{2,1,0:T(8,128)(2,1)S(1)}, u32[]{:S(2)}, u32[]{:S(2)}) %all-to-all-start) | async-done | bytes 294944 | tf_op jit(solution)/shard_map/all_to_all | solution.py:378
  43.7 4.7 %collective-permute-start.2 = (bf16[8,144,128]{2,1,0:T(8,128)(2,1)S(1)}, bf16[8,144,128]{2,1,0:T(8,128)(2,1)S(1)}, u32[]{:S(2)}, u32[]{:S(2)}) collective-permute-start(bf16[8,144,128]{2,1,0:T(8,128)(2,1)S(1)} %all-to-all-done.own), channel_id=1, source_target_pairs={{0,8},{8,0},{1,9},{9,1},{2,10},{10,2},{3,11},{11,3},{4,12},{12,4},... | collective-permute-start | bytes 884744 | tf_op jit(solution)/shard_map/ppermute | solution.py:27
  48.3 1.9 %collective-permute-start.3 = (bf16[8,144,128]{2,1,0:T(8,128)(2,1)S(1)}, bf16[8,144,128]{2,1,0:T(8,128)(2,1)S(1)}, u32[]{:S(2)}, u32[]{:S(2)}) collective-permute-start(bf16[8,144,128]{2,1,0:T(8,128)(2,1)S(1)} %all-to-all-done.own), channel_id=1, source_target_pairs={{0,16},{16,0},{1,17},{17,1},{2,18},{18,2},{3,19},{19,3},{4,20},{20... | collective-permute-start | bytes 884744 | tf_op jit(solution)/shard_map/ppermute | solution.py:27
  50.3 4.6 %collective-permute-done.2.across = bf16[8,144,128]{2,1,0:T(8,128)(2,1)S(1)} collective-permute-done((bf16[8,144,128]{2,1,0:T(8,128)(2,1)S(1)}, bf16[8,144,128]{2,1,0:T(8,128)(2,1)S(1)}, u32[]{:S(2)}, u32[]{:S(2)}) %collective-permute-start.2) | collective-permute-done | bytes 294944 | tf_op jit(solution)/shard_map/ppermute | solution.py:27
  54.9 1.9 %collective-permute-start.4 = (bf16[8,144,128]{2,1,0:T(8,128)(2,1)S(1)}, bf16[8,144,128]{2,1,0:T(8,128)(2,1)S(1)}, u32[]{:S(2)}, u32[]{:S(2)}) collective-permute-start(bf16[8,144,128]{2,1,0:T(8,128)(2,1)S(1)} %collective-permute-done.2.across), channel_id=1, source_target_pairs={{0,16},{16,0},{1,17},{17,1},{2,18},{18,2},{3,19},{19,3},{4,20},{20... | collective-permute-start | bytes 884744 | tf_op jit(solution)/shard_map/ppermute | solution.py:27
  57.1 1.3 collective-permute-done.4.far
  58.4 1.0 gather.1
  59.5 5.0 %conv.1 = (f32[512,256]{1,0:T(8,128)S(1)}, f32[16,4,128]{2,1,0:T(4,128)S(1)}, f32[8,256]{1,0:T(8,128)S(1)}) custom-call(bf16[1024,640]{1,0:T(8,128)(2,1)S(1)} %get-tuple-element.24.normed, bf16[8,112,1024]{2,1,0:T(8,128)(2,1)} %bitcast.11), custom_call_target="tpu_custom_call" | custom-call | tf_op jit(solution)/shard_map/conv/pallas_call | solution.py:401
  64.5 15.5 %all_to_all.20.stats = f32[16,4,128]{2,1,0:T(4,128)S(1)} all-to-all(f32[16,4,128]{2,1,0:T(4,128)S(1)} %get-tuple-element.27), channel_id=1, replica_groups=mesh['xlo'=2,'y'=8,'core'=2,'xhi'=2,'z'=8] {'xlo','y'}, dimensions={0} | all-to-all | bytes 65536 | tf_op jit(solution)/shard_map/all_to_all | solution.py:419
  80.0 10.5 %all_to_all.21.stats = f32[8,4,128]{2,1,0:T(4,128)S(1)} all-to-all(f32[8,4,128]{2,1,0:T(4,128)S(1)} %merge.1), channel_id=1, replica_groups=mesh['xlo'=2,'y'=8,'core'=2,'xhi'=2,'z'=8] {'z'}, dimensions={0} | all-to-all | bytes 32768 | tf_op jit(solution)/shard_map/all_to_all | solution.py:428
  90.7 4.4 %collective-permute-start.5 = (bf16[256,512]{1,0:T(8,128)(2,1)S(1)}, bf16[256,512]{1,0:T(8,128)(2,1)S(1)}, u32[]{:S(2)}, u32[]{:S(2)}) collective-permute-start(bf16[256,512]{1,0:T(8,128)(2,1)S(1)} %bn.1.own), channel_id=1, source_target_pairs={{0,8},{8,0},{1,9},{9,1},{2,10},{10,2},{3,11},{11,3},{4,12},{12,4},... | collective-permute-start | bytes 786440 | tf_op jit(solution)/shard_map/ppermute | solution.py:27
  95.1 9.1 %collective-permute-start.6 = (bf16[256,512]{1,0:T(8,128)(2,1)S(1)}, bf16[256,512]{1,0:T(8,128)(2,1)S(1)}, u32[]{:S(2)}, u32[]{:S(2)}) collective-permute-start(bf16[256,512]{1,0:T(8,128)(2,1)S(1)} %bn.1.own), channel_id=1, source_target_pairs={{0,16},{16,0},{1,17},{17,1},{2,18},{18,2},{3,19},{19,3},{4,20},{20... | collective-permute-start | bytes 786440 | tf_op jit(solution)/shard_map/ppermute | solution.py:27
  104.2 5.1 %collective-permute-start.7 = (bf16[256,512]{1,0:T(8,128)(2,1)S(1)}, bf16[256,512]{1,0:T(8,128)(2,1)S(1)}, u32[]{:S(2)}, u32[]{:S(2)}) collective-permute-start(bf16[256,512]{1,0:T(8,128)(2,1)S(1)} %collective-permute-done.5.across), channel_id=1, source_target_pairs={{0,16},{16,0},{1,17},{17,1},{2,18},{18,2},{3,19},{19,3},{4,20},{20... | collective-permute-start | bytes 786440 | tf_op jit(solution)/shard_map/ppermute | solution.py:27
  109.3 1.1 collective-permute-done.7.far
  111.0 4.3 %collective-permute-start.8 = (bf16[256,512]{1,0:T(8,128)(2,1)S(1)}, bf16[256,512]{1,0:T(8,128)(2,1)S(1)}, u32[]{:S(2)}, u32[]{:S(2)}) collective-permute-start(bf16[256,512]{1,0:T(8,128)(2,1)S(1)} %mix.1.own), channel_id=1, source_target_pairs={{0,8},{8,0},{1,9},{9,1},{2,10},{10,2},{3,11},{11,3},{4,12},{12,4},... | collective-permute-start | bytes 786440 | tf_op jit(solution)/shard_map/ppermute | solution.py:27
  115.3 2.6 %collective-permute-start.9 = (bf16[256,512]{1,0:T(8,128)(2,1)S(1)}, bf16[256,512]{1,0:T(8,128)(2,1)S(1)}, u32[]{:S(2)}, u32[]{:S(2)}) collective-permute-start(bf16[256,512]{1,0:T(8,128)(2,1)S(1)} %mix.1.own), channel_id=1, source_target_pairs={{0,16},{16,0},{1,17},{17,1},{2,18},{18,2},{3,19},{19,3},{4,20},{20... | collective-permute-start | bytes 786440 | tf_op jit(solution)/shard_map/ppermute | solution.py:27
  117.9 4.0 %collective-permute-done.8.across = bf16[256,512]{1,0:T(8,128)(2,1)S(1)} collective-permute-done((bf16[256,512]{1,0:T(8,128)(2,1)S(1)}, bf16[256,512]{1,0:T(8,128)(2,1)S(1)}, u32[]{:S(2)}, u32[]{:S(2)}) %collective-permute-start.8) | collective-permute-done | bytes 262176 | tf_op jit(solution)/shard_map/ppermute | solution.py:27
  121.9 3.1 %collective-permute-start.10 = (bf16[256,512]{1,0:T(8,128)(2,1)S(1)}, bf16[256,512]{1,0:T(8,128)(2,1)S(1)}, u32[]{:S(2)}, u32[]{:S(2)}) collective-permute-start(bf16[256,512]{1,0:T(8,128)(2,1)S(1)} %collective-permute-done.8.across), channel_id=1, source_target_pairs={{0,16},{16,0},{1,17},{17,1},{2,18},{18,2},{3,19},{19,3},{4,20},{20... | collective-permute-start | bytes 786440 | tf_op jit(solution)/shard_map/ppermute | solution.py:27
  125.2 0.9 collective-permute-done.10.far
  126.1 4.0 %give.1 = (bf16[1024,256]{1,0:T(8,128)(2,1)S(1)}, bf16[8,16,128,128]{3,2,1,0:T(8,128)(2,1)S(1)}, bf16[1024,256]{1,0:T(8,128)(2,1)S(1)}, bf16[1024,256]{1,0:T(8,128)(2,1)S(1)}) custom-call(bf16[256,512]{1,0:T(8,128)(2,1)S(1)} %mix.1.own, bf16[256,512]{1,0:T(8,128)(2,1)S(1)} %collective-permute-done.8.across, ...), custom_call_target="tpu_custom_call" | custom-call | tf_op jit(solution)/shard_map/give/pallas_call | solution.py:451
  130.2 2.3 %collective-permute-start.11 = (bf16[1024,256]{1,0:T(8,128)(2,1)S(1)}, bf16[1024,256]{1,0:T(8,128)(2,1)S(1)}, u32[]{:S(2)}, u32[]{:S(2)}) collective-permute-start(bf16[1024,256]{1,0:T(8,128)(2,1)S(1)} %get-tuple-element.34), channel_id=1, source_target_pairs={{0,16},{16,0},{1,17},{17,1},{2,18},{18,2},{3,19},{19,3},{4,20},{20... | collective-permute-start | bytes 1572872 | tf_op jit(solution)/shard_map/ppermute | solution.py:27
  132.4 1.2 keep.1
  134.1 18.8 %all_to_all.22.parts = bf16[16,64,256]{2,1,0:T(8,128)(2,1)S(1)} all-to-all(bf16[16,64,256]{2,1,0:T(8,128)(2,1)S(1)} %bitcast.14), channel_id=1, replica_groups=mesh['xlo'=2,'y'=8,'core'=2,'xhi'=2,'z'=8] {'xhi','z'}, dimensions={0} | all-to-all | bytes 1048576 | tf_op jit(solution)/shard_map/all_to_all | solution.py:483
  (27 shorter events, 2.6 us)
Async XLA Ops:
  6.5 50.3 %copy-start.3 = (f32[1024]{0:T(1024)S(1)}, f32[1024]{0:T(1024)}, u32[]{:S(2)}) copy-start(f32[1024]{0:T(1024)} %param.11) | copy-start | bytes 12292
  6.5 53.0 %all-gather.5.cloned.1.call-start = ((), (), s32[]{:S(2)}) async-start(), calls=%async_computation.4 | async-start | bytes 2064384 | tf_op jit(solution)/shard_map/all_gather | solution.py:364
  8.3 10.1 %collective-permute-start = (bf16[64,128]{1,0:T(8,128)(2,1)S(1)}, bf16[64,128]{1,0:T(8,128)(2,1)S(1)}, u32[]{:S(2)}, u32[]{:S(2)}) collective-permute-start(bf16[64,128]{1,0:T(8,128)(2,1)S(1)} %get-tuple-element.21), channel_id=1, source_target_pairs={{0,16},{16,32},{32,48},{48,64},{64,80},{80,96},{96,112},{112,128},... | collective-permute-start | bytes 49160 | tf_op jit(solution)/shard_map/ppermute | solution.py:368
  12.9 6.3 %collective-permute-start.1 = (bf16[64,128]{1,0:T(8,128)(2,1)S(1)}, bf16[64,128]{1,0:T(8,128)(2,1)S(1)}, u32[]{:S(2)}, u32[]{:S(2)}) collective-permute-start(bf16[64,128]{1,0:T(8,128)(2,1)S(1)} %get-tuple-element.22), channel_id=1, source_target_pairs={{16,0},{32,16},{48,32},{64,48},{80,64},{96,80},{112,96},{128,112},... | collective-permute-start | bytes 49160 | tf_op jit(solution)/shard_map/ppermute | solution.py:369
  20.1 23.6 %all-to-all-start = ((bf16[8,144,128]{2,1,0:T(8,128)(2,1)}), bf16[8,144,128]{2,1,0:T(8,128)(2,1)S(1)}, u32[]{:S(2)}, u32[]{:S(2)}) async-start(bf16[8,144,128]{2,1,0:T(8,128)(2,1)} %pack.1), calls=%async_computation | async-start | bytes 589824 | tf_op jit(solution)/shard_map/all_to_all | solution.py:378
  28.9 97.3 %all-gather.7.cloned.1.call-start = ((), (), s32[]{:S(2)}) async-start(), calls=%async_computation.5 | async-start | bytes 4718592 | tf_op jit(solution)/shard_map/all_gather | solution.py:389
  28.9 1.0 copy-start.1
  30.0 1.0 copy-start.2
  43.7 11.2 %collective-permute-start.2 = (bf16[8,144,128]{2,1,0:T(8,128)(2,1)S(1)}, bf16[8,144,128]{2,1,0:T(8,128)(2,1)S(1)}, u32[]{:S(2)}, u32[]{:S(2)}) collective-permute-start(bf16[8,144,128]{2,1,0:T(8,128)(2,1)S(1)} %all-to-all-done.own), channel_id=1, source_target_pairs={{0,8},{8,0},{1,9},{9,1},{2,10},{10,2},{3,11},{11,3},{4,12},{12,4},... | collective-permute-start | bytes 884744 | tf_op jit(solution)/shard_map/ppermute | solution.py:27
  48.3 8.7 %collective-permute-start.3 = (bf16[8,144,128]{2,1,0:T(8,128)(2,1)S(1)}, bf16[8,144,128]{2,1,0:T(8,128)(2,1)S(1)}, u32[]{:S(2)}, u32[]{:S(2)}) collective-permute-start(bf16[8,144,128]{2,1,0:T(8,128)(2,1)S(1)} %all-to-all-done.own), channel_id=1, source_target_pairs={{0,16},{16,0},{1,17},{17,1},{2,18},{18,2},{3,19},{19,3},{4,20},{20... | collective-permute-start | bytes 884744 | tf_op jit(solution)/shard_map/ppermute | solution.py:27
  54.9 3.5 %collective-permute-start.4 = (bf16[8,144,128]{2,1,0:T(8,128)(2,1)S(1)}, bf16[8,144,128]{2,1,0:T(8,128)(2,1)S(1)}, u32[]{:S(2)}, u32[]{:S(2)}) collective-permute-start(bf16[8,144,128]{2,1,0:T(8,128)(2,1)S(1)} %collective-permute-done.2.across), channel_id=1, source_target_pairs={{0,16},{16,0},{1,17},{17,1},{2,18},{18,2},{3,19},{19,3},{4,20},{20... | collective-permute-start | bytes 884744 | tf_op jit(solution)/shard_map/ppermute | solution.py:27
  57.0 67.9 %copy-start.4 = (f32[1024]{0:T(1024)S(1)}, f32[1024]{0:T(1024)}, u32[]{:S(2)}) copy-start(f32[1024]{0:T(1024)} %param.17) | copy-start | bytes 12292
  59.5 50.9 %copy-start = (bf16[896,1024]{1,0:T(8,128)(2,1)S(1)}, bf16[896,1024]{1,0:T(8,128)(2,1)}, u32[]{:S(2)}) copy-start(bf16[896,1024]{1,0:T(8,128)(2,1)} %all-gather.5.cloned.1.call-done) | copy-start | bytes 5505028
  90.7 13.5 %collective-permute-start.5 = (bf16[256,512]{1,0:T(8,128)(2,1)S(1)}, bf16[256,512]{1,0:T(8,128)(2,1)S(1)}, u32[]{:S(2)}, u32[]{:S(2)}) collective-permute-start(bf16[256,512]{1,0:T(8,128)(2,1)S(1)} %bn.1.own), channel_id=1, source_target_pairs={{0,8},{8,0},{1,9},{9,1},{2,10},{10,2},{3,11},{11,3},{4,12},{12,4},... | collective-permute-start | bytes 786440 | tf_op jit(solution)/shard_map/ppermute | solution.py:27
  95.1 14.2 %collective-permute-start.6 = (bf16[256,512]{1,0:T(8,128)(2,1)S(1)}, bf16[256,512]{1,0:T(8,128)(2,1)S(1)}, u32[]{:S(2)}, u32[]{:S(2)}) collective-permute-start(bf16[256,512]{1,0:T(8,128)(2,1)S(1)} %bn.1.own), channel_id=1, source_target_pairs={{0,16},{16,0},{1,17},{17,1},{2,18},{18,2},{3,19},{19,3},{4,20},{20... | collective-permute-start | bytes 786440 | tf_op jit(solution)/shard_map/ppermute | solution.py:27
  104.2 6.3 %collective-permute-start.7 = (bf16[256,512]{1,0:T(8,128)(2,1)S(1)}, bf16[256,512]{1,0:T(8,128)(2,1)S(1)}, u32[]{:S(2)}, u32[]{:S(2)}) collective-permute-start(bf16[256,512]{1,0:T(8,128)(2,1)S(1)} %collective-permute-done.5.across), channel_id=1, source_target_pairs={{0,16},{16,0},{1,17},{17,1},{2,18},{18,2},{3,19},{19,3},{4,20},{20... | collective-permute-start | bytes 786440 | tf_op jit(solution)/shard_map/ppermute | solution.py:27
  111.0 10.9 %collective-permute-start.8 = (bf16[256,512]{1,0:T(8,128)(2,1)S(1)}, bf16[256,512]{1,0:T(8,128)(2,1)S(1)}, u32[]{:S(2)}, u32[]{:S(2)}) collective-permute-start(bf16[256,512]{1,0:T(8,128)(2,1)S(1)} %mix.1.own), channel_id=1, source_target_pairs={{0,8},{8,0},{1,9},{9,1},{2,10},{10,2},{3,11},{11,3},{4,12},{12,4},... | collective-permute-start | bytes 786440 | tf_op jit(solution)/shard_map/ppermute | solution.py:27
  115.3 9.9 %collective-permute-start.9 = (bf16[256,512]{1,0:T(8,128)(2,1)S(1)}, bf16[256,512]{1,0:T(8,128)(2,1)S(1)}, u32[]{:S(2)}, u32[]{:S(2)}) collective-permute-start(bf16[256,512]{1,0:T(8,128)(2,1)S(1)} %mix.1.own), channel_id=1, source_target_pairs={{0,16},{16,0},{1,17},{17,1},{2,18},{18,2},{3,19},{19,3},{4,20},{20... | collective-permute-start | bytes 786440 | tf_op jit(solution)/shard_map/ppermute | solution.py:27
  121.9 4.3 %collective-permute-start.10 = (bf16[256,512]{1,0:T(8,128)(2,1)S(1)}, bf16[256,512]{1,0:T(8,128)(2,1)S(1)}, u32[]{:S(2)}, u32[]{:S(2)}) collective-permute-start(bf16[256,512]{1,0:T(8,128)(2,1)S(1)} %collective-permute-done.8.across), channel_id=1, source_target_pairs={{0,16},{16,0},{1,17},{17,1},{2,18},{18,2},{3,19},{19,3},{4,20},{20... | collective-permute-start | bytes 786440 | tf_op jit(solution)/shard_map/ppermute | solution.py:27
  130.2 3.8 %collective-permute-start.11 = (bf16[1024,256]{1,0:T(8,128)(2,1)S(1)}, bf16[1024,256]{1,0:T(8,128)(2,1)S(1)}, u32[]{:S(2)}, u32[]{:S(2)}) collective-permute-start(bf16[1024,256]{1,0:T(8,128)(2,1)S(1)} %get-tuple-element.34), channel_id=1, source_target_pairs={{0,16},{16,0},{1,17},{17,1},{2,18},{18,2},{3,19},{19,3},{4,20},{20... | collective-permute-start | bytes 1572872 | tf_op jit(solution)/shard_map/ppermute | solution.py:27
Sparse Core Ops, SparseCore 0:
  9.4 50.0 all-gather.4
  61.6 61.2 all-gather.6
